TPU v7x, 32 devices: a whole 2x2x4 slice. The times are simulated.
32 devices in a mesh: path: 8 (over y, x, core), shard: 4 (over z).
Axes of the slice: x: 2, y: 2, z: 4, core: 2. Of those that a mesh axis runs over, the one named last changes fastest.
Arguments:
- path_params: bfloat16 [8, 16, 32, 4096], P('path', None, 'shard'), may hold values from -6 to 6
- global_params: float32 [128, 32, 4096], P('path', 'shard'), may hold values from -6 to 6
- momentum: float32 [128, 32, 4096], P('path', 'shard'), may hold values from -6 to 6
- module_ids: int32 [8, 16], replicated, may hold values from 0 to 127, as said below
- token_counts: int32 [8, 16], replicated, may hold values from 16 to 256
Outputs:
- new_global: float32 [128, 32, 4096], P('path', 'shard')
- new_momentum: float32 [128, 32, 4096], P('path', 'shard')
- path_modules: bfloat16 [8, 16, 32, 4096], P('path', None, 'shard')
Inputs may be any that keep to these rules, and one draw needn't show every extreme that they name: `module_ids`: each row names 16 different modules. Among the modules of one row, at most 2 lie in any one block of 16 consecutive module numbers, and every row has exactly 2 in some block.
All inputs are finite; a program needn't handle non-finite values.
Results may differ from a plain program's by a relative error of at most 0.0004.
Values may be sent and summed in bfloat16 or wider, within the bound.
No kernel may reach another device: no remote copies, remote signals or barrier semaphores. Data moves between devices by JAX's collectives and lax.ppermute only.
A program may use at most 128 MiB of HBM per device.

v0:
```python
import jax
import jax.numpy as jnp
from jax import lax
from jax.sharding import PartitionSpec as P

CAP = 2


outer_momentum = 0.9
outer_rate = 0.7


def on_device(path_params, global_params, momentum, module_ids, token_counts):
    paths, held = module_ids.shape
    owned = global_params.shape[0]
    rows = path_params.shape[2]
    width = path_params.shape[3]
    span = rows * width
    owner = lax.axis_index("path")
    local = path_params.reshape(held, span)
    counts = token_counts.astype(jnp.float32)
    targets = owner * owned + jnp.arange(owned, dtype=jnp.int32)
    match = module_ids[None, :, :] == targets[:, None, None]
    total = jnp.sum(jnp.where(match, counts[None, :, :], 0.0), axis=(1, 2))
    groups = module_ids // owned
    places = jnp.arange(held, dtype=jnp.int32)
    before = (groups[:, None, :] == groups[:, :, None]) & (places[None, :] < places[:, None])[
        None, :, :
    ]
    earlier = jnp.sum(before.astype(jnp.int32), axis=2)
    my_ids = lax.dynamic_index_in_dim(module_ids, owner, 0, keepdims=False)
    my_group = lax.dynamic_index_in_dim(groups, owner, 0, keepdims=False)
    my_earlier = lax.dynamic_index_in_dim(earlier, owner, 0, keepdims=False)
    slot_owner = jnp.arange(paths * CAP, dtype=jnp.int32) // CAP
    slot_rank = jnp.arange(paths * CAP, dtype=jnp.int32) % CAP
    ranks = jnp.arange(CAP, dtype=jnp.int32)
    slot_match = match[:, :, None, :] & (earlier[None, :, None, :] == ranks[None, None, :, None])
    select = (
        (my_group[None, :] == slot_owner[:, None]) & (my_earlier[None, :] == slot_rank[:, None])
    ).astype(jnp.bfloat16)
    outgoing = (
        jnp.dot(select, local, preferred_element_type=jnp.float32)
        .astype(jnp.bfloat16)
        .reshape(paths, CAP, span)
    )
    incoming = lax.all_to_all(outgoing, "path", split_axis=0, concat_axis=0, tiled=True)
    weights = jnp.sum(jnp.where(slot_match, counts[None, :, None, :], 0.0), axis=3)
    summed = jnp.dot(
        weights.reshape(owned, paths * CAP).astype(jnp.bfloat16),
        incoming.reshape(paths * CAP, span),
        preferred_element_type=jnp.float32,
    )
    params = global_params.reshape(owned, span)
    past = momentum.reshape(owned, span)
    raw = (total[:, None] * params - summed) / jnp.maximum(total, 1.0)[:, None]
    squares = lax.psum(jnp.sum(raw * raw, axis=1), "shard")
    mean_square = squares / (span * lax.axis_size("shard"))
    factor = jnp.minimum(1.0, 1.0 / jnp.sqrt(mean_square + 1e-06))
    delta = raw * factor[:, None]
    velocity = outer_momentum * past + delta
    updated = params - outer_rate * (outer_momentum * velocity + delta)
    rounded = updated.astype(jnp.bfloat16)
    piece = lax.all_gather(rounded, "path", axis=0, tiled=True)
    count = piece.shape[0]
    onehot = (my_ids[:, None] == jnp.arange(count, dtype=jnp.int32)[None, :]).astype(jnp.bfloat16)
    received = jnp.dot(onehot, piece, preferred_element_type=jnp.float32)
    path_out = received.astype(jnp.bfloat16).reshape(1, held, rows, width)
    return (updated.reshape(global_params.shape), velocity.reshape(momentum.shape), path_out)


def solution(mesh):
    placed = (
        P("path", None, "shard", None),
        P("path", "shard", None),
        P("path", "shard", None),
        P(),
        P(),
    )
    return jax.shard_map(
        on_device,
        mesh=mesh,
        in_specs=placed,
        out_specs=(
            P("path", "shard", None),
            P("path", "shard", None),
            P("path", None, "shard", None),
        ),
        check_vma=False,
    )
```

profile of v0, /device:TPU:1, one launch (start us, length us, event | category | flops | bytes accessed | tf_op | source)
XLA Modules:
  0.0 115.7 jit_solution(9688414508435627718)
XLA Ops:
  7.2 0.7 add_select_fusion
  7.9 1.8 %copy.16 = bf16[2,8,8,4096]{3,1,2,0:T(8,128)(2,1)S(1)} copy(bf16[2,8,8,4096]{3,2,1,0:T(8,128)(2,1)} %bitcast.40) | data formatting | bytes 2097152
  9.7 0.3 convert_reduce_fusion
  10.0 0.5 convolution_convert_fusion.1
  10.5 0.0 copy-start.3
  10.5 1.5 %reshape.91 = bf16[8,2,32768]{2,1,0:T(2,128)(2,1)} reshape(bf16[16,32768]{1,0:T(8,128)(2,1)S(1)} %convolution_convert_fusion.1) | data formatting | bytes 2097152 | tf_op jit(solution)/shard_map/reshape | solution.py:44
  12.0 5.2 %all-to-all-start = ((bf16[8,2,32768]{2,1,0:T(2,128)(2,1)}), bf16[8,2,32768]{2,1,0:T(2,128)(2,1)S(1)}, u32[]{:S(2)}, u32[]{:S(2)}) async-start(bf16[8,2,32768]{2,1,0:T(2,128)(2,1)} %reshape.91), calls=%async_computation | async-start | bytes 2097152 | tf_op jit(solution)/shard_map/all_to_all | solution.py:46
  17.3 0.1 broadcast_compare_fusion
  17.4 0.1 select_reduce_fusion
  17.5 0.1 copy.12
  17.6 3.0 %copy.14 = f32[2,8,8,4096]{3,1,2,0:T(8,128)S(1)} copy(f32[2,8,8,4096]{3,2,1,0:T(8,128)} %bitcast.37) | data formatting | bytes 4194304
  20.6 0.2 broadcast_multiply_fusion
  20.8 2.5 %copy.15 = f32[2,8,8,4096]{3,1,2,0:T(8,128)} copy(f32[2,8,8,4096]{3,2,1,0:T(8,128)S(1)} %bitcast.29) | data formatting | bytes 4194304
  23.3 0.3 select_reduce_fusion.1
  23.6 5.6 %all-to-all-done = bf16[8,2,32768]{2,1,0:T(2,128)(2,1)S(1)} async-done(((bf16[8,2,32768]{2,1,0:T(2,128)(2,1)}), bf16[8,2,32768]{2,1,0:T(2,128)(2,1)S(1)}, u32[]{:S(2)}, u32[]{:S(2)}) %all-to-all-start) | async-done | bytes 1048608 | tf_op jit(solution)/shard_map/all_to_all | solution.py:46
  29.2 2.3 %multiply_reduce_fusion = (f32[16]{0:T(128)S(1)}, f32[16,32768]{1,0:T(8,128)}) fusion(f32[16]{0:T(128)S(1)} %broadcast_maximum_fusion, bf16[16,8,2]{0,1,2:T(8,128)(2,1)S(1)} %copy.12, bf16[8,2,32768]{2,1,0:T(2,128)(2,1)S(1)} %all-to-all-done, f32[16,32768]{1,0:T(8,128)S(1)} %bitcast.30, f32[16]{0:T(128)S(1)} %select_reduce_fusion.1), kind=kOutput, calls=%fused_computation.6 | convolution fusion | flops 19398640 | bytes 5243584 | tf_op jit(solution)/shard_map/dot_general | solution.py:48
  31.4 10.0 %psum.7 = f32[16]{0:T(128)S(1)} all-reduce(f32[16]{0:T(128)S(1)} %get-tuple-element.6), channel_id=1, replica_groups=mesh['path'=8,'shard'=4] {'shard'}, use_global_device_ids=true, to_apply=%region_4.5 | all-reduce | flops 16 | bytes 128 | tf_op jit(solution)/shard_map/psum | solution.py:56
  41.5 5.1 %fusion.17 = (bf16[16,32768]{1,0:T(8,128)(2,1)}, f32[16,32768]{1,0:T(8,128)}, f32[16,32768]{1,0:T(8,128)}) fusion(f32[16,32768]{1,0:T(8,128)S(1)} %bitcast.31, f32[16,32768]{1,0:T(8,128)} %bitcast.32, f32[16,32768]{1,0:T(8,128)} %get-tuple-element.7, f32[16]{0:T(128)S(1)} %rsqrt_minimum_fusion), kind=kLoop, calls=%fused_computation.47 | loop fusion | flops 3670016 | bytes 11534400 | tf_op jit(solution)/shard_map/convert_element_type | solution.py:62
  46.6 0.0 all-gather.2.cloned.1.call-update
  46.6 4.3 %copy.17 = f32[2,8,8,4096]{3,2,1,0:T(8,128)} copy(f32[2,8,8,4096]{3,1,2,0:T(8,128)} %bitcast.34) | data formatting | bytes 4194304
  50.9 2.5 %copy.18 = f32[2,8,8,4096]{3,2,1,0:T(8,128)} copy(f32[2,8,8,4096]{3,1,2,0:T(8,128)S(1)} %bitcast.33) | data formatting | bytes 4194304
  53.5 49.2 %all-gather.2.cloned.1.call-done = bf16[128,32768]{1,0:T(8,128)(2,1)} async-done(((bf16[16,32768]{1,0:T(8,128)(2,1)}), bf16[128,32768]{1,0:T(8,128)(2,1)}) %all-gather.2.cloned.1.call-update) | async-done | bytes 8388624 | tf_op jit(solution)/shard_map/all_gather | solution.py:63
  102.7 4.6 %convolution_convert_fusion = bf16[16,32768]{1,0:T(8,128)(2,1)S(1)} fusion(bf16[128,32768]{1,0:T(8,128)(2,1)} %all-gather.2.cloned.1.call-done, s32[16]{0:T(128)S(1)} %fusion.16), kind=kOutput, calls=%fused_computation.3 | convolution fusion | flops 134744064 | bytes 9437248 | tf_op jit(solution)/shard_map/dot_general | solution.py:66
  107.3 1.6 %copy.19 = bf16[2,8,8,4096]{3,2,1,0:T(8,128)(2,1)} copy(bf16[2,8,8,4096]{3,1,2,0:T(8,128)(2,1)S(1)} %bitcast.35) | data formatting | bytes 2097152
  (17 shorter events, 0.1 us)
Async XLA Ops:
  10.5 6.8 %copy-start.3 = (s32[8,16]{1,0:T(8,128)S(1)}, s32[8,16]{1,0:T(8,128)}, u32[]{:S(2)}) copy-start(s32[8,16]{1,0:T(8,128)} %param.9) | copy-start | bytes 1540
  10.5 6.8 %copy-start.2 = (s32[8,16]{1,0:T(8,128)S(1)}, s32[8,16]{1,0:T(8,128)}, u32[]{:S(2)}) copy-start(s32[8,16]{1,0:T(8,128)} %param.8) | copy-start | bytes 1540
  12.0 17.2 %all-to-all-start = ((bf16[8,2,32768]{2,1,0:T(2,128)(2,1)}), bf16[8,2,32768]{2,1,0:T(2,128)(2,1)S(1)}, u32[]{:S(2)}, u32[]{:S(2)}) async-start(bf16[8,2,32768]{2,1,0:T(2,128)(2,1)} %reshape.91), calls=%async_computation | async-start | bytes 2097152 | tf_op jit(solution)/shard_map/all_to_all | solution.py:46
  17.2 85.5 %all-gather.2.cloned.1.call-start = ((), (), s32[]{:S(2)}) async-start(), calls=%async_computation.1 | async-start | bytes 9437184 | tf_op jit(solution)/shard_map/all_gather | solution.py:63
  17.6 3.0 %copy-start.1 = (f32[16,8,4096]{2,1,0:T(8,128)S(1)}, f32[16,8,4096]{2,1,0:T(8,128)}, u32[]{:S(2)}) copy-start(f32[16,8,4096]{2,1,0:T(8,128)} %param.7) | copy-start | bytes 6291460
  46.6 4.3 %copy-start = (f32[16,32768]{1,0:T(8,128)S(1)}, f32[16,32768]{1,0:T(8,128)}, u32[]{:S(2)}) copy-start(f32[16,32768]{1,0:T(8,128)} %get-tuple-element.5) | copy-start | bytes 6291460
Sparse Core Ops, SparseCore 0:
  46.7 55.8 all-gather.1
where the time goes:
time: 116 us
  waiting for transfers between devices  54.8 us (47%)
  local copies, waits for them, and re-layouts  17.3 us (15%)
  between operations  14.2 us (12%)
  blocking collectives  10 us (9%)
  matrix products  7.36 us (6%)
  other arithmetic  6.82 us (6%)
  starting transfers between devices  5.23 us (5%)
    all_gather x1, waiting for transfers between devices, on_device(): piece = lax.all_gather(rounded, 'path', axis=0, tiled=True)  49.2 us
    unnamed x14, local copies, waits for them, and re-layouts  15.7 us
    psum x1, blocking collectives, on_device(): squares = lax.psum(jnp.sum(raw * raw, axis=1), 'shard')  10 us
    all_to_all x1, waiting for transfers between devices, on_device(): lax.all_to_all(outgoing, 'path', split_axis=0, concat_axis=0, tiled=True)  5.58 us
    all_to_all x1, starting transfers between devices, on_device(): lax.all_to_all(outgoing, 'path', split_axis=0, concat_axis=0, tiled=True)  5.22 us
    convert_element_type x1, other arithmetic, on_device(): rounded = updated.astype(jnp.bfloat16)  5.11 us
    dot_general x1, matrix products, on_device(): received = jnp.dot(onehot, piece, preferred_element_type=jnp.float32)  4.62 us
  transfers between devices with their start and end apart: 2, of which 2 were waited for; matrix products, arithmetic and copies ran while one was open for 11% of the time, Pallas kernels for 0%

commit v1 on v0

v1 whole, which is shorter than its diff:
```python
import functools

import jax
import jax.numpy as jnp
from jax import lax
from jax.experimental import pallas as pl
from jax.experimental.pallas import tpu as pltpu
from jax.sharding import PartitionSpec as P

CAP = 2
CHUNK = 1024
outer_momentum = 0.9
outer_rate = 0.7

SMEM = pl.BlockSpec(memory_space=pltpu.SMEM)
VMEM = pl.BlockSpec(memory_space=pltpu.VMEM)
ANY = pl.BlockSpec(memory_space=pl.ANY)


def in_vmem(x):
    return pltpu.with_memory_space_constraint(x, pltpu.VMEM)


def chunks(width):
    step = CHUNK if width % CHUNK == 0 else width
    return [pl.ds(at, step) for at in range(0, width, step)]


def pack_kernel(paths, owned, me_ref, ids_ref, local_ref, places_ref, *rest):
    pieces, (seen, sems) = rest[:paths], rest[paths:]
    me = me_ref[0]
    held = ids_ref.shape[1]

    def clear(i, _):
        places_ref[i] = jnp.int32(-1)
        return 0

    def reset(i, _):
        seen[i] = jnp.int32(0)
        return 0

    def place(k, _):
        group = ids_ref[me, k] // owned
        rank = seen[group]
        seen[group] = rank + 1
        places_ref[group * CAP + rank] = k
        return 0

    lax.fori_loop(0, paths * CAP, clear, 0)
    lax.fori_loop(0, paths, reset, 0)
    lax.fori_loop(0, held, place, 0)
    copies = []
    for d in list(range(1, paths)) + [0]:
        for r in range(CAP):
            k = jnp.maximum(places_ref[(me ^ d) * CAP + r], 0)
            copy = pltpu.make_async_copy(
                local_ref.at[k], pieces[d].at[r], sems.at[d * CAP + r]
            )
            copy.start()
            copies.append(copy)
    for copy in copies:
        copy.wait()


def early_kernel(
    paths, me_ref, ids_ref, counts_ref, own_ref, params_ref, past_ref,
    module_ref, weight_ref, total_ref, acc_ref, base_ref,
):
    me = me_ref[0]
    owned, _, width = params_ref.shape
    held = ids_ref.shape[1]

    def clear(i, _):
        module_ref[i] = jnp.int32(0)
        weight_ref[i] = jnp.float32(0.0)
        return 0

    def reset(i, _):
        total_ref[i] = jnp.float32(0.0)
        return 0

    lax.fori_loop(0, paths * CAP, clear, 0)
    lax.fori_loop(0, owned, reset, 0)

    def one(i, rank):
        path, k = i // held, i % held
        rank = jnp.where(k == 0, 0, rank)
        at = ids_ref[path, k] - me * owned
        mine = (at >= 0) & (at < owned)

        @pl.when(mine)
        def _():
            count = counts_ref[path, k]
            module_ref[path * CAP + rank] = at
            weight_ref[path * CAP + rank] = count
            total_ref[at] = total_ref[at] + count

        return jnp.where(mine, rank + 1, rank)

    lax.fori_loop(0, paths * held, one, jnp.int32(0))

    def fill(m, _):
        for c in chunks(width):
            params = params_ref[m, :, c]
            acc_ref[m, :, c] = total_ref[m] * params
            base_ref[m, :, c] = params - (outer_rate * outer_momentum**2) * past_ref[m, :, c]
        return 0

    lax.fori_loop(0, owned, fill, 0)
    subtract(me, [own_ref], [0], module_ref, weight_ref, acc_ref)


def subtract(me, pieces, distances, module_ref, weight_ref, acc_ref):
    width = acc_ref.shape[2]
    for piece, d in zip(pieces, distances, strict=True):
        for r in range(CAP):
            slot = (me ^ d) * CAP + r
            m, weight = module_ref[slot], weight_ref[slot]
            for c in chunks(width):
                acc_ref[m, :, c] = acc_ref[m, :, c] - weight * piece[r, :, c].astype(jnp.float32)


def combine_kernel(paths, me_ref, module_ref, weight_ref, total_ref, acc_in, *rest):
    pieces, (acc_ref, squares_ref) = rest[: paths - 1], rest[paths - 1 :]
    subtract(me_ref[0], pieces, range(1, paths), module_ref, weight_ref, acc_ref)
    owned, rows, width = acc_ref.shape
    for m in range(owned):
        inverse = 1.0 / jnp.maximum(jnp.full((rows, 128), total_ref[m], jnp.float32), 1.0)
        added = jnp.zeros((rows, 128), jnp.float32)
        for at in range(0, width, 128):
            raw = acc_ref[m, :, pl.ds(at, 128)] * inverse
            added = added + raw * raw
        squares_ref[pl.ds(m, 1), :] = jnp.sum(added, axis=0, keepdims=True)


def scales(entries, total, squares):
    inverse = 1.0 / jnp.maximum(total, 1.0)
    mean = jnp.sum(squares, axis=1, keepdims=True) / entries
    factor = jnp.minimum(1.0, 1.0 / jnp.sqrt(mean + 1e-06))
    return inverse * factor


def send_kernel(paths, shards, me_ref, module_ref, total_ref, acc_ref, base_ref, *rest):
    squares, (scale_ref, *pieces) = rest[:shards], rest[shards:]
    me = me_ref[0]
    owned, rows, width = acc_ref.shape
    summed = squares[0][...]
    for other in squares[1:]:
        summed = summed + other[...]
    total = jnp.concatenate(
        [jnp.full((1, 128), total_ref[m], jnp.float32) for m in range(owned)], axis=0
    )
    scale = scales(rows * width * shards, total, summed)
    for m in range(owned):
        scale_ref[m] = jnp.broadcast_to(scale[m : m + 1, :], (rows, 128))
    rate = outer_rate * (1.0 + outer_momentum)
    for d in list(range(1, paths)) + [0]:
        for r in range(CAP):
            m = module_ref[(me ^ d) * CAP + r]
            step = rate * scale_ref[m][:, :1]
            for c in chunks(width):
                pieces[d][r, :, c] = (base_ref[m, :, c] - step * acc_ref[m, :, c]).astype(
                    jnp.bfloat16
                )


def store_kernel(scale_ref, acc_ref, base_ref, past_ref, updated_ref, velocity_ref):
    rate = outer_rate * (1.0 + outer_momentum)
    scale = scale_ref[0][:, :1]
    for c in chunks(acc_ref.shape[2]):
        delta = scale * acc_ref[0, :, c]
        updated_ref[0, :, c] = base_ref[0, :, c] - rate * delta
        velocity_ref[0, :, c] = outer_momentum * past_ref[0, :, c] + delta


def unpack_kernel(paths, me_ref, places_ref, *rest):
    pieces, (out_ref, sems) = rest[:paths], rest[paths:]
    me = me_ref[0]
    for wait in (False, True):
        for d in range(paths):
            for r in range(CAP):
                k = places_ref[(me ^ d) * CAP + r]

                @pl.when(k >= 0)
                def _():
                    copy = pltpu.make_async_copy(
                        pieces[d].at[r], out_ref.at[0, k], sems.at[d * CAP + r]
                    )
                    if wait:
                        copy.wait()
                    else:
                        copy.start()


def on_device(path_params, global_params, momentum, module_ids, token_counts):
    paths, held = module_ids.shape
    owned, rows, width = global_params.shape
    shards = lax.axis_size("shard")
    me = lax.axis_index("path").astype(jnp.int32).reshape(1)
    counts = token_counts.astype(jnp.float32)
    slots = paths * CAP
    piece = jax.ShapeDtypeStruct((CAP, rows, width), jnp.bfloat16)
    module = jax.ShapeDtypeStruct((owned, rows, width), jnp.float32)
    limits = pltpu.CompilerParams(vmem_limit_bytes=32 * 1024 * 1024)

    def exchange(pieces):
        return [
            lax.ppermute(pieces[d], "path", [(i, i ^ d) for i in range(paths)])
            for d in range(1, paths)
        ]

    places, *packed = pl.pallas_call(
        functools.partial(pack_kernel, paths, owned),
        out_shape=[jax.ShapeDtypeStruct((slots,), jnp.int32)] + [piece] * paths,
        in_specs=[SMEM, SMEM, ANY],
        out_specs=[SMEM] + [ANY] * paths,
        scratch_shapes=[pltpu.SMEM((paths,), jnp.int32), pltpu.SemaphoreType.DMA((slots,))],
        name="pack",
    )(me, module_ids, path_params.reshape(held, rows, width))
    arrived = exchange(packed)
    table, weights, total, acc, base = pl.pallas_call(
        functools.partial(early_kernel, paths),
        out_shape=[
            jax.ShapeDtypeStruct((slots,), jnp.int32),
            jax.ShapeDtypeStruct((slots,), jnp.float32),
            jax.ShapeDtypeStruct((owned,), jnp.float32),
            pltpu.VMEM(module.shape, module.dtype),
            pltpu.VMEM(module.shape, module.dtype),
        ],
        in_specs=[SMEM] * 3 + [VMEM] * 3,
        out_specs=[SMEM] * 3 + [VMEM] * 2,
        compiler_params=limits,
        cost_estimate=pl.CostEstimate(flops=10**6, bytes_accessed=12 * 2**20, transcendentals=0),
        name="early",
    )(me, module_ids, counts, packed[0], global_params, momentum)
    acc, squares = pl.pallas_call(
        functools.partial(combine_kernel, paths),
        out_shape=[
            pltpu.VMEM(module.shape, module.dtype),
            jax.ShapeDtypeStruct((owned, 128), jnp.float32),
        ],
        in_specs=[SMEM] * 4 + [VMEM] * paths,
        out_specs=[VMEM] * 2,
        input_output_aliases={4: 0},
        compiler_params=limits,
        name="combine",
    )(me, table, weights, total, in_vmem(acc), *arrived)
    parts = [squares] + [
        lax.ppermute(squares, "shard", [(i, (i + d) % shards) for i in range(shards)])
        for d in range(1, shards)
    ]
    scale, *outgoing = pl.pallas_call(
        functools.partial(send_kernel, paths, shards),
        out_shape=[jax.ShapeDtypeStruct((owned, rows, 128), jnp.float32)] + [piece] * paths,
        in_specs=[SMEM] * 3 + [VMEM] * (2 + shards),
        out_specs=[VMEM] * (1 + paths),
        compiler_params=limits,
        name="send",
    )(me, table, total, in_vmem(acc), in_vmem(base), *parts)
    returned = exchange(outgoing)
    block = pl.BlockSpec((1, rows, width), lambda m: (m, 0, 0))
    updated, velocity = pl.pallas_call(
        store_kernel,
        out_shape=[module] * 2,
        grid=(owned,),
        in_specs=[pl.BlockSpec((1, rows, 128), lambda m: (m, 0, 0))] + [block] * 3,
        out_specs=[block] * 2,
        compiler_params=limits,
        cost_estimate=pl.CostEstimate(flops=10**6, bytes_accessed=12 * 2**20, transcendentals=0),
        name="store",
    )(scale, acc, base, momentum)
    path_out = pl.pallas_call(
        functools.partial(unpack_kernel, paths),
        out_shape=jax.ShapeDtypeStruct(path_params.shape, path_params.dtype),
        in_specs=[SMEM] * 2 + [ANY] * paths,
        out_specs=ANY,
        scratch_shapes=[pltpu.SemaphoreType.DMA((slots,))],
        name="unpack",
    )(me, places, outgoing[0], *returned)
    return updated, velocity, path_out


def solution(mesh):
    placed = (
        P("path", None, "shard", None),
        P("path", "shard", None),
        P("path", "shard", None),
        P(),
        P(),
    )
    return jax.shard_map(
        on_device,
        mesh=mesh,
        in_specs=placed,
        out_specs=(
            P("path", "shard", None),
            P("path", "shard", None),
            P("path", None, "shard", None),
        ),
        check_vma=False,
    )
```

time: 116 us -> 115 us (level)
  Pallas kernels: 0 us -> 81.3 us
  waiting for transfers between devices: 54.8 us -> 3.83 us
  starting transfers between devices: 5.23 us -> 22.4 us
  between operations: 14.2 us -> 0.79 us
  local copies, waits for them, and re-layouts: 17.3 us -> 5.52 us
  blocking collectives: 10 us -> 0 us
  matrix products: 7.36 us -> 0 us
  other arithmetic: 6.82 us -> 0.69 us
    pallas_call x0 -> x6, Pallas kernels: none -> 81.3 us  [the longest x1 34.7 us: on_device(): pl.pallas_call(functools.partial(pack_kernel, paths, owned), out_shape=[j...]
    all_gather x1 -> x0, waiting for transfers between devices: 49.2 us -> none  [on_device(): piece = lax.all_gather(rounded, 'path', axis=0, tiled=True)]
    ppermute x0 -> x17, starting transfers between devices: none -> 22.4 us  [the longest x14 17.7 us: exchange(): lax.ppermute(pieces[d], 'path', [(i, i ^ d) for i in range(paths)])]
    unnamed x14 -> x26, local copies, waits for them, and re-layouts: 15.7 us -> 5.52 us
    psum x1 -> x0, blocking collectives: 10 us -> none  [on_device(): squares = lax.psum(jnp.sum(raw * raw, axis=1), 'shard')]
    dot_general x3 -> x0, matrix products: 7.36 us -> none  [the longest x1 4.62 us: on_device(): received = jnp.dot(onehot, piece, preferred_element_type=jnp.float32)]
    all_to_all x1 -> x0, waiting for transfers between devices: 5.58 us -> none  [on_device(): lax.all_to_all(outgoing, 'path', split_axis=0, concat_axis=0, tiled=True)]
    all_to_all x1 -> x0, starting transfers between devices: 5.22 us -> none  [on_device(): lax.all_to_all(outgoing, 'path', split_axis=0, concat_axis=0, tiled=True)]
  transfers between devices with their start and end apart: 2 -> 17, of which waited for: 2 -> 4; matrix products, arithmetic and copies ran while one was open for 11% -> 1% of each run, Pallas kernels for 0% -> 10%
where the time goes in v1:
time: 115 us
  Pallas kernels  81.3 us (71%)
  starting transfers between devices  22.4 us (19%)
  local copies, waits for them, and re-layouts  5.52 us (5%)
  waiting for transfers between devices  3.83 us (3%)
    pallas_call x1, Pallas kernels, on_device(): pl.pallas_call(functools.partial(pack_kernel, paths, owned), out_shape=[j...  34.7 us
    pallas_call x1, Pallas kernels, on_device(): pl.pallas_call(functools.partial(unpack_kernel, paths), out_shape=jax.Sha...  33.7 us
    ppermute x14, starting transfers between devices, exchange(): lax.ppermute(pieces[d], 'path', [(i, i ^ d) for i in range(paths)])  17.7 us
    pallas_call x1, Pallas kernels, on_device(): pl.pallas_call(store_kernel, out_shape=[module] * 2, grid=(owned,), in_sp...  6.41 us
    unnamed x26, local copies, waits for them, and re-layouts  5.52 us
    ppermute x3, starting transfers between devices, on_device(): lax.ppermute(squares, 'shard', [(i, (i + d) % shards) for i in range(shar...  4.72 us
    pallas_call x1, Pallas kernels, on_device(): pl.pallas_call(functools.partial(early_kernel, paths), out_shape=[jax.Sha...  4.54 us
    ppermute x14, waiting for transfers between devices, exchange(): lax.ppermute(pieces[d], 'path', [(i, i ^ d) for i in range(paths)])  2.4 us
  transfers between devices with their start and end apart: 17, of which 4 were waited for; matrix products, arithmetic and copies ran while one was open for 1% of the time, Pallas kernels for 10%

profile of v1, /device:TPU:1, one launch (start us, length us, event | category | flops | bytes accessed | tf_op | source)
XLA Modules:
  0.0 114.6 jit_solution(14348837858453595105)
XLA Ops:
  0.6 34.7 %pack.1 = (s32[16]{0:T(128)}, bf16[2,8,4096]{2,1,0:T(8,128)(2,1)}, bf16[2,8,4096]{2,1,0:T(8,128)(2,1)}, bf16[2,8,4096]{2,1,0:T(8,128)(2,1)}, bf16[2,8,4096]{2,1,...) custom-call(s32[1]{0:T(128)} %bitcast.me_ref, ...), custom_call_target="tpu_custom_call" | custom-call | tf_op jit(solution)/shard_map/pack/pallas_call | solution.py:212
  35.5 2.7 %collective-permute-start.1 = (bf16[2,8,4096]{2,1,0:T(8,128)(2,1)}, bf16[2,8,4096]{2,1,0:T(8,128)(2,1)S(1)}, u32[]{:S(2)}, u32[]{:S(2)}) collective-permute-start(bf16[2,8,4096]{2,1,0:T(8,128)(2,1)} %get-tuple-element.36), channel_id=1, source_target_pairs={{0,8},{4,12},{8,0},{12,4},{16,24},{20,28},{24,16},{28,20},{1,9},{5... | collective-permute-start | bytes 393224 | tf_op jit(solution)/shard_map/ppermute | solution.py:208
  38.2 1.7 %collective-permute-start.3 = (bf16[2,8,4096]{2,1,0:T(8,128)(2,1)}, bf16[2,8,4096]{2,1,0:T(8,128)(2,1)S(1)}, u32[]{:S(2)}, u32[]{:S(2)}) collective-permute-start(bf16[2,8,4096]{2,1,0:T(8,128)(2,1)} %get-tuple-element.38), channel_id=1, source_target_pairs={{0,16},{4,20},{8,24},{12,28},{16,0},{20,4},{24,8},{28,12},{1,17},{... | collective-permute-start | bytes 393224 | tf_op jit(solution)/shard_map/ppermute | solution.py:208
  40.2 2.4 %collective-permute-start.5 = (bf16[2,8,4096]{2,1,0:T(8,128)(2,1)}, bf16[2,8,4096]{2,1,0:T(8,128)(2,1)S(1)}, u32[]{:S(2)}, u32[]{:S(2)}) collective-permute-start(bf16[2,8,4096]{2,1,0:T(8,128)(2,1)} %get-tuple-element.40), channel_id=1, source_target_pairs={{0,24},{4,28},{8,16},{12,20},{16,8},{20,12},{24,0},{28,4},{1,25},{... | collective-permute-start | bytes 393224 | tf_op jit(solution)/shard_map/ppermute | solution.py:208
  42.6 3.0 %collective-permute-start.6 = (bf16[2,8,4096]{2,1,0:T(8,128)(2,1)}, bf16[2,8,4096]{2,1,0:T(8,128)(2,1)S(1)}, u32[]{:S(2)}, u32[]{:S(2)}) collective-permute-start(bf16[2,8,4096]{2,1,0:T(8,128)(2,1)} %get-tuple-element.41), channel_id=1, source_target_pairs={{0,28},{4,24},{8,20},{12,16},{16,12},{20,8},{24,4},{28,0},{1,29},{... | collective-permute-start | bytes 393224 | tf_op jit(solution)/shard_map/ppermute | solution.py:208
  45.6 0.7 convert_element_type.3.counts_ref
  46.3 1.6 %copy-done = f32[16,8,4096]{2,1,0:T(8,128)S(1)} copy-done((f32[16,8,4096]{2,1,0:T(8,128)S(1)}, f32[16,8,4096]{2,1,0:T(8,128)}, u32[]{:S(2)}) %copy-start) | copy-done | bytes 2097176
  47.9 1.6 %copy-done.2 = f32[16,8,4096]{2,1,0:T(8,128)S(1)} copy-done((f32[16,8,4096]{2,1,0:T(8,128)S(1)}, f32[16,8,4096]{2,1,0:T(8,128)}, u32[]{:S(2)}) %copy-start.2) | copy-done | bytes 2097176
  49.5 0.9 copy-done.3
  51.0 4.5 %early.1 = (s32[16]{0:T(128)S(1)}, f32[16]{0:T(128)S(1)}, f32[16]{0:T(128)S(1)}, f32[16,8,4096]{2,1,0:T(8,128)S(1)}, f32[16,8,4096]{2,1,0:T(8,128)S(1)}) custom-call(s32[1]{0:T(128)} %bitcast.me_ref, s32[8,16]{1,0:T(8,128)S(1)} %copy-done.5, f32[8,16]{1,0:T(8,128)S(1)} %convert_element_type.3.counts_ref, bf16[2,8,4096]{2,1,0:T(8,128)(2,1)S(1)} %copy-done.3, ...), custom_call_target="tpu_custom_call" | custom-call | flops 1000000 | bytes 12582912 | tf_op jit(solution)/shard_map/early/pallas_call | solution.py:221
  55.7 1.0 combine.1
  56.6 1.3 %collective-permute-start.7 = (f32[16,128]{1,0:T(8,128)S(1)}, f32[16,128]{1,0:T(8,128)S(1)}, u32[]{:S(2)}, u32[]{:S(2)}) collective-permute-start(f32[16,128]{1,0:T(8,128)S(1)} %get-tuple-element.44.rest_0_), channel_id=1, source_target_pairs={{0,1},{1,2},{2,3},{3,0},{4,5},{5,6},{6,7},{7,4},{8,9},{9,10},{10,1... | collective-permute-start | bytes 24584 | tf_op jit(solution)/shard_map/ppermute | solution.py:249
  58.0 2.3 %collective-permute-start.8 = (f32[16,128]{1,0:T(8,128)S(1)}, f32[16,128]{1,0:T(8,128)S(1)}, u32[]{:S(2)}, u32[]{:S(2)}) collective-permute-start(f32[16,128]{1,0:T(8,128)S(1)} %get-tuple-element.44.rest_0_), channel_id=1, source_target_pairs={{0,2},{1,3},{2,0},{3,1},{4,6},{5,7},{6,4},{7,5},{8,10},{9,11},{10,... | collective-permute-start | bytes 24584 | tf_op jit(solution)/shard_map/ppermute | solution.py:249
  60.3 1.1 collective-permute-start.9
  61.7 1.1 collective-permute-done.9.rest_3_
  62.8 1.0 send.1
  63.8 1.0 collective-permute-start.10
  65.1 1.4 %collective-permute-start.12 = (bf16[2,8,4096]{2,1,0:T(8,128)(2,1)S(1)}, bf16[2,8,4096]{2,1,0:T(8,128)(2,1)S(1)}, u32[]{:S(2)}, u32[]{:S(2)}) collective-permute-start(bf16[2,8,4096]{2,1,0:T(8,128)(2,1)S(1)} %get-tuple-element.52), channel_id=1, source_target_pairs={{0,12},{4,8},{8,4},{12,0},{16,28},{20,24},{24,20},{28,16},{1,13},{... | collective-permute-start | bytes 393224 | tf_op jit(solution)/shard_map/ppermute | solution.py:208
  66.7 1.6 %collective-permute-start.14 = (bf16[2,8,4096]{2,1,0:T(8,128)(2,1)S(1)}, bf16[2,8,4096]{2,1,0:T(8,128)(2,1)S(1)}, u32[]{:S(2)}, u32[]{:S(2)}) collective-permute-start(bf16[2,8,4096]{2,1,0:T(8,128)(2,1)S(1)} %get-tuple-element.54), channel_id=1, source_target_pairs={{0,20},{4,16},{8,28},{12,24},{16,4},{20,0},{24,12},{28,8},{1,21},{... | collective-permute-start | bytes 393224 | tf_op jit(solution)/shard_map/ppermute | solution.py:208
  68.3 0.9 collective-permute-start.15
  69.9 2.1 %collective-permute-start.16 = (bf16[2,8,4096]{2,1,0:T(8,128)(2,1)S(1)}, bf16[2,8,4096]{2,1,0:T(8,128)(2,1)S(1)}, u32[]{:S(2)}, u32[]{:S(2)}) collective-permute-start(bf16[2,8,4096]{2,1,0:T(8,128)(2,1)S(1)} %get-tuple-element.56), channel_id=1, source_target_pairs={{0,28},{4,24},{8,20},{12,16},{16,12},{20,8},{24,4},{28,0},{1,29},{... | collective-permute-start | bytes 393224 | tf_op jit(solution)/shard_map/ppermute | solution.py:208
  72.0 6.4 %store.1 = (f32[16,8,4096]{2,1,0:T(8,128)}, f32[16,8,4096]{2,1,0:T(8,128)}) custom-call(f32[16,8,128]{2,1,0:T(8,128)S(1)} %get-tuple-element.45.scale_ref, f32[16,8,4096]{2,1,0:T(8,128)S(1)} %get-tuple-element.42.acc_ref, f32[16,8,4096]{2,1,0:T(8,128)S(1)} %get-tuple-element.43.base_ref, f32[16,8,4096]{2,1,0:T(8,128)S(1)} %copy-done.1), custom_call_target="tpu_custom_call" | custom-call | flops 1000000 | bytes 12582912 | tf_op jit(solution)/shard_map/store/pallas_call | solution.py:262
  78.4 1.7 %collective-permute-done.14.rest_5_ = bf16[2,8,4096]{2,1,0:T(8,128)(2,1)S(1)} collective-permute-done((bf16[2,8,4096]{2,1,0:T(8,128)(2,1)S(1)}, bf16[2,8,4096]{2,1,0:T(8,128)(2,1)S(1)}, u32[]{:S(2)}, u32[]{:S(2)}) %collective-permute-start.14) | collective-permute-done | bytes 131104 | tf_op jit(solution)/shard_map/ppermute | solution.py:208
  80.9 33.7 %unpack.1 = bf16[1,16,8,4096]{3,2,1,0:T(8,128)(2,1)} custom-call(s32[1]{0:T(128)} %bitcast.me_ref, s32[16]{0:T(128)} %get-tuple-element.48.places_ref, bf16[2,8,4096]{2,1,0:T(8,128)(2,1)} %copy-done.4, bf16[2,8,4096]{2,1,0:T(8,128)(2,1)} %copy-done.6, bf16[2,8,4096]{2,1,0:T(8,128)(2,1)} %copy-done.7, bf16[2,8,4096]{2,1,0:T(8,128)(2,1)} %copy-done.8, ...), custom_call_target="tpu_custom_call" | custom-call | tf_op jit(solution)/shard_map/unpack/pallas_call | solution.py:272
  (43 shorter events, 3.4 us)
Async XLA Ops:
  35.4 4.8 %collective-permute-start = (bf16[2,8,4096]{2,1,0:T(8,128)(2,1)}, bf16[2,8,4096]{2,1,0:T(8,128)(2,1)S(1)}, u32[]{:S(2)}, u32[]{:S(2)}) collective-permute-start(bf16[2,8,4096]{2,1,0:T(8,128)(2,1)} %get-tuple-element.35), channel_id=1, source_target_pairs={{0,4},{4,0},{8,12},{12,8},{16,20},{20,16},{24,28},{28,24},{1,5},{5... | collective-permute-start | bytes 393224 | tf_op jit(solution)/shard_map/ppermute | solution.py:208
  35.5 7.1 %collective-permute-start.1 = (bf16[2,8,4096]{2,1,0:T(8,128)(2,1)}, bf16[2,8,4096]{2,1,0:T(8,128)(2,1)S(1)}, u32[]{:S(2)}, u32[]{:S(2)}) collective-permute-start(bf16[2,8,4096]{2,1,0:T(8,128)(2,1)} %get-tuple-element.36), channel_id=1, source_target_pairs={{0,8},{4,12},{8,0},{12,4},{16,24},{20,28},{24,16},{28,20},{1,9},{5... | collective-permute-start | bytes 393224 | tf_op jit(solution)/shard_map/ppermute | solution.py:208
  38.2 17.4 %collective-permute-start.2 = (bf16[2,8,4096]{2,1,0:T(8,128)(2,1)}, bf16[2,8,4096]{2,1,0:T(8,128)(2,1)S(1)}, u32[]{:S(2)}, u32[]{:S(2)}) collective-permute-start(bf16[2,8,4096]{2,1,0:T(8,128)(2,1)} %get-tuple-element.37), channel_id=1, source_target_pairs={{0,12},{4,8},{8,4},{12,0},{16,28},{20,24},{24,20},{28,16},{1,13},{... | collective-permute-start | bytes 393224 | tf_op jit(solution)/shard_map/ppermute | solution.py:208
  38.2 17.4 %collective-permute-start.3 = (bf16[2,8,4096]{2,1,0:T(8,128)(2,1)}, bf16[2,8,4096]{2,1,0:T(8,128)(2,1)S(1)}, u32[]{:S(2)}, u32[]{:S(2)}) collective-permute-start(bf16[2,8,4096]{2,1,0:T(8,128)(2,1)} %get-tuple-element.38), channel_id=1, source_target_pairs={{0,16},{4,20},{8,24},{12,28},{16,0},{20,4},{24,8},{28,12},{1,17},{... | collective-permute-start | bytes 393224 | tf_op jit(solution)/shard_map/ppermute | solution.py:208
  39.9 15.7 %collective-permute-start.4 = (bf16[2,8,4096]{2,1,0:T(8,128)(2,1)}, bf16[2,8,4096]{2,1,0:T(8,128)(2,1)S(1)}, u32[]{:S(2)}, u32[]{:S(2)}) collective-permute-start(bf16[2,8,4096]{2,1,0:T(8,128)(2,1)} %get-tuple-element.39), channel_id=1, source_target_pairs={{0,20},{4,16},{8,28},{12,24},{16,4},{20,0},{24,12},{28,8},{1,21},{... | collective-permute-start | bytes 393224 | tf_op jit(solution)/shard_map/ppermute | solution.py:208
  40.2 15.4 %collective-permute-start.5 = (bf16[2,8,4096]{2,1,0:T(8,128)(2,1)}, bf16[2,8,4096]{2,1,0:T(8,128)(2,1)S(1)}, u32[]{:S(2)}, u32[]{:S(2)}) collective-permute-start(bf16[2,8,4096]{2,1,0:T(8,128)(2,1)} %get-tuple-element.40), channel_id=1, source_target_pairs={{0,24},{4,28},{8,16},{12,20},{16,8},{20,12},{24,0},{28,4},{1,25},{... | collective-permute-start | bytes 393224 | tf_op jit(solution)/shard_map/ppermute | solution.py:208
  42.6 13.0 %collective-permute-start.6 = (bf16[2,8,4096]{2,1,0:T(8,128)(2,1)}, bf16[2,8,4096]{2,1,0:T(8,128)(2,1)S(1)}, u32[]{:S(2)}, u32[]{:S(2)}) collective-permute-start(bf16[2,8,4096]{2,1,0:T(8,128)(2,1)} %get-tuple-element.41), channel_id=1, source_target_pairs={{0,28},{4,24},{8,20},{12,16},{16,12},{20,8},{24,4},{28,0},{1,29},{... | collective-permute-start | bytes 393224 | tf_op jit(solution)/shard_map/ppermute | solution.py:208
  46.3 1.6 %copy-start = (f32[16,8,4096]{2,1,0:T(8,128)S(1)}, f32[16,8,4096]{2,1,0:T(8,128)}, u32[]{:S(2)}) copy-start(f32[16,8,4096]{2,1,0:T(8,128)} %past_ref.3) | copy-start | bytes 6291460
  56.6 4.7 %collective-permute-start.7 = (f32[16,128]{1,0:T(8,128)S(1)}, f32[16,128]{1,0:T(8,128)S(1)}, u32[]{:S(2)}, u32[]{:S(2)}) collective-permute-start(f32[16,128]{1,0:T(8,128)S(1)} %get-tuple-element.44.rest_0_), channel_id=1, source_target_pairs={{0,1},{1,2},{2,3},{3,0},{4,5},{5,6},{6,7},{7,4},{8,9},{9,10},{10,1... | collective-permute-start | bytes 24584 | tf_op jit(solution)/shard_map/ppermute | solution.py:249
  58.0 3.7 %collective-permute-start.8 = (f32[16,128]{1,0:T(8,128)S(1)}, f32[16,128]{1,0:T(8,128)S(1)}, u32[]{:S(2)}, u32[]{:S(2)}) collective-permute-start(f32[16,128]{1,0:T(8,128)S(1)} %get-tuple-element.44.rest_0_), channel_id=1, source_target_pairs={{0,2},{1,3},{2,0},{3,1},{4,6},{5,7},{6,4},{7,5},{8,10},{9,11},{10,... | collective-permute-start | bytes 24584 | tf_op jit(solution)/shard_map/ppermute | solution.py:249
  60.3 2.5 %collective-permute-start.9 = (f32[16,128]{1,0:T(8,128)S(1)}, f32[16,128]{1,0:T(8,128)S(1)}, u32[]{:S(2)}, u32[]{:S(2)}) collective-permute-start(f32[16,128]{1,0:T(8,128)S(1)} %get-tuple-element.44.rest_0_), channel_id=1, source_target_pairs={{0,3},{1,0},{2,1},{3,2},{4,7},{5,4},{6,5},{7,6},{8,11},{9,8},{10,9... | collective-permute-start | bytes 24584 | tf_op jit(solution)/shard_map/ppermute | solution.py:249
  62.8 9.2 %copy-start.1 = (f32[16,8,4096]{2,1,0:T(8,128)S(1)}, f32[16,8,4096]{2,1,0:T(8,128)}, u32[]{:S(2)}) copy-start(f32[16,8,4096]{2,1,0:T(8,128)} %past_ref.3) | copy-start | bytes 6291460
  63.8 14.6 %copy-start.4 = (bf16[2,8,4096]{2,1,0:T(8,128)(2,1)}, bf16[2,8,4096]{2,1,0:T(8,128)(2,1)S(1)}, u32[]{:S(2)}) copy-start(bf16[2,8,4096]{2,1,0:T(8,128)(2,1)S(1)} %get-tuple-element.49.rest_0_) | copy-start | bytes 393220
  63.8 4.5 %collective-permute-start.10 = (bf16[2,8,4096]{2,1,0:T(8,128)(2,1)S(1)}, bf16[2,8,4096]{2,1,0:T(8,128)(2,1)S(1)}, u32[]{:S(2)}, u32[]{:S(2)}) collective-permute-start(bf16[2,8,4096]{2,1,0:T(8,128)(2,1)S(1)} %get-tuple-element.50), channel_id=1, source_target_pairs={{0,4},{4,0},{8,12},{12,8},{16,20},{20,16},{24,28},{28,24},{1,5},{5... | collective-permute-start | bytes 393224 | tf_op jit(solution)/shard_map/ppermute | solution.py:208
  64.8 5.1 %collective-permute-start.11 = (bf16[2,8,4096]{2,1,0:T(8,128)(2,1)S(1)}, bf16[2,8,4096]{2,1,0:T(8,128)(2,1)S(1)}, u32[]{:S(2)}, u32[]{:S(2)}) collective-permute-start(bf16[2,8,4096]{2,1,0:T(8,128)(2,1)S(1)} %get-tuple-element.51), channel_id=1, source_target_pairs={{0,8},{4,12},{8,0},{12,4},{16,24},{20,28},{24,16},{28,20},{1,9},{5... | collective-permute-start | bytes 393224 | tf_op jit(solution)/shard_map/ppermute | solution.py:208
  65.1 13.3 %collective-permute-start.12 = (bf16[2,8,4096]{2,1,0:T(8,128)(2,1)S(1)}, bf16[2,8,4096]{2,1,0:T(8,128)(2,1)S(1)}, u32[]{:S(2)}, u32[]{:S(2)}) collective-permute-start(bf16[2,8,4096]{2,1,0:T(8,128)(2,1)S(1)} %get-tuple-element.52), channel_id=1, source_target_pairs={{0,12},{4,8},{8,4},{12,0},{16,28},{20,24},{24,20},{28,16},{1,13},{... | collective-permute-start | bytes 393224 | tf_op jit(solution)/shard_map/ppermute | solution.py:208
  66.5 11.9 %collective-permute-start.13 = (bf16[2,8,4096]{2,1,0:T(8,128)(2,1)S(1)}, bf16[2,8,4096]{2,1,0:T(8,128)(2,1)S(1)}, u32[]{:S(2)}, u32[]{:S(2)}) collective-permute-start(bf16[2,8,4096]{2,1,0:T(8,128)(2,1)S(1)} %get-tuple-element.53), channel_id=1, source_target_pairs={{0,16},{4,20},{8,24},{12,28},{16,0},{20,4},{24,8},{28,12},{1,17},{... | collective-permute-start | bytes 393224 | tf_op jit(solution)/shard_map/ppermute | solution.py:208
  66.7 13.4 %collective-permute-start.14 = (bf16[2,8,4096]{2,1,0:T(8,128)(2,1)S(1)}, bf16[2,8,4096]{2,1,0:T(8,128)(2,1)S(1)}, u32[]{:S(2)}, u32[]{:S(2)}) collective-permute-start(bf16[2,8,4096]{2,1,0:T(8,128)(2,1)S(1)} %get-tuple-element.54), channel_id=1, source_target_pairs={{0,20},{4,16},{8,28},{12,24},{16,4},{20,0},{24,12},{28,8},{1,21},{... | collective-permute-start | bytes 393224 | tf_op jit(solution)/shard_map/ppermute | solution.py:208
  68.3 10.1 %copy-start.6 = (bf16[2,8,4096]{2,1,0:T(8,128)(2,1)}, bf16[2,8,4096]{2,1,0:T(8,128)(2,1)S(1)}, u32[]{:S(2)}) copy-start(bf16[2,8,4096]{2,1,0:T(8,128)(2,1)S(1)} %collective-permute-done.10.rest_1_) | copy-start | bytes 393220
  68.3 11.9 %collective-permute-start.15 = (bf16[2,8,4096]{2,1,0:T(8,128)(2,1)S(1)}, bf16[2,8,4096]{2,1,0:T(8,128)(2,1)S(1)}, u32[]{:S(2)}, u32[]{:S(2)}) collective-permute-start(bf16[2,8,4096]{2,1,0:T(8,128)(2,1)S(1)} %get-tuple-element.55), channel_id=1, source_target_pairs={{0,24},{4,28},{8,16},{12,20},{16,8},{20,12},{24,0},{28,4},{1,25},{... | collective-permute-start | bytes 393224 | tf_op jit(solution)/shard_map/ppermute | solution.py:208
  69.9 8.5 %copy-start.7 = (bf16[2,8,4096]{2,1,0:T(8,128)(2,1)}, bf16[2,8,4096]{2,1,0:T(8,128)(2,1)S(1)}, u32[]{:S(2)}) copy-start(bf16[2,8,4096]{2,1,0:T(8,128)(2,1)S(1)} %collective-permute-done.11.rest_2_) | copy-start | bytes 393220
  69.9 10.3 %collective-permute-start.16 = (bf16[2,8,4096]{2,1,0:T(8,128)(2,1)S(1)}, bf16[2,8,4096]{2,1,0:T(8,128)(2,1)S(1)}, u32[]{:S(2)}, u32[]{:S(2)}) collective-permute-start(bf16[2,8,4096]{2,1,0:T(8,128)(2,1)S(1)} %get-tuple-element.56), channel_id=1, source_target_pairs={{0,28},{4,24},{8,20},{12,16},{16,12},{20,8},{24,4},{28,0},{1,29},{... | collective-permute-start | bytes 393224 | tf_op jit(solution)/shard_map/ppermute | solution.py:208
  78.4 1.8 %copy-start.8 = (bf16[2,8,4096]{2,1,0:T(8,128)(2,1)}, bf16[2,8,4096]{2,1,0:T(8,128)(2,1)S(1)}, u32[]{:S(2)}) copy-start(bf16[2,8,4096]{2,1,0:T(8,128)(2,1)S(1)} %collective-permute-done.12.rest_3_) | copy-start | bytes 393220
  78.4 1.8 %copy-start.9 = (bf16[2,8,4096]{2,1,0:T(8,128)(2,1)}, bf16[2,8,4096]{2,1,0:T(8,128)(2,1)S(1)}, u32[]{:S(2)}) copy-start(bf16[2,8,4096]{2,1,0:T(8,128)(2,1)S(1)} %collective-permute-done.13.rest_4_) | copy-start | bytes 393220
  (6 other events, 5.3 us)

commit v2 on v1

--- a/solution.py
+++ b/solution.py
@@ -9,6 +9,7 @@
 
 CAP = 2
 CHUNK = 1024
+PARTS = 4
 outer_momentum = 0.9
 outer_rate = 0.7
 
@@ -63,50 +64,61 @@
 
 
 def early_kernel(
-    paths, me_ref, ids_ref, counts_ref, own_ref, params_ref, past_ref,
-    module_ref, weight_ref, total_ref, acc_ref, base_ref,
+    paths, me_ref, ids_ref, counts_ref, own_ref, params_hbm, past_hbm,
+    module_ref, weight_ref, total_ref, acc_ref, base_ref, params_ref, past_ref, sems,
 ):
     me = me_ref[0]
-    owned, _, width = params_ref.shape
+    owned, _, width = acc_ref.shape
     held = ids_ref.shape[1]
-
-    def clear(i, _):
-        module_ref[i] = jnp.int32(0)
-        weight_ref[i] = jnp.float32(0.0)
-        return 0
+    part = owned // PARTS
+
+    def copies(i):
+        at = pl.ds(i * part, part)
+        return [
+            pltpu.make_async_copy(hbm.at[at], ref.at[at], sems.at[n, i])
+            for n, (hbm, ref) in enumerate(((params_hbm, params_ref), (past_hbm, past_ref)))
+        ]
+
+    for i in range(PARTS):
+        for copy in copies(i):
+            copy.start()
 
     def reset(i, _):
         total_ref[i] = jnp.float32(0.0)
         return 0
 
-    lax.fori_loop(0, paths * CAP, clear, 0)
+    def one(path, _):
+        first = path * (CAP + 1)
+        for r in range(CAP):
+            module_ref[first + r] = jnp.int32(0)
+            weight_ref[first + r] = jnp.float32(0.0)
+        rank = jnp.int32(0)
+        for k in range(held):
+            at = ids_ref[path, k] - me * owned
+            mine = (at >= 0) & (at < owned)
+            slot = first + jnp.where(mine, rank, CAP)
+            module_ref[slot] = at
+            weight_ref[slot] = counts_ref[path, k]
+            rank = rank + mine.astype(jnp.int32)
+        for r in range(CAP):
+            at = module_ref[first + r]
+            total_ref[at] = total_ref[at] + weight_ref[first + r]
+        return 0
+
     lax.fori_loop(0, owned, reset, 0)
-
-    def one(i, rank):
-        path, k = i // held, i % held
-        rank = jnp.where(k == 0, 0, rank)
-        at = ids_ref[path, k] - me * owned
-        mine = (at >= 0) & (at < owned)
-
-        @pl.when(mine)
-        def _():
-            count = counts_ref[path, k]
-            module_ref[path * CAP + rank] = at
-            weight_ref[path * CAP + rank] = count
-            total_ref[at] = total_ref[at] + count
-
-        return jnp.where(mine, rank + 1, rank)
-
-    lax.fori_loop(0, paths * held, one, jnp.int32(0))
-
-    def fill(m, _):
-        for c in chunks(width):
-            params = params_ref[m, :, c]
-            acc_ref[m, :, c] = total_ref[m] * params
-            base_ref[m, :, c] = params - (outer_rate * outer_momentum**2) * past_ref[m, :, c]
-        return 0
-
-    lax.fori_loop(0, owned, fill, 0)
+    lax.fori_loop(0, paths, one, 0)
+    for i in range(PARTS):
+        for copy in copies(i):
+            copy.wait()
+
+        def fill(m, _):
+            for c in chunks(width):
+                params = params_ref[m, :, c]
+                acc_ref[m, :, c] = total_ref[m] * params
+                base_ref[m, :, c] = params - (outer_rate * outer_momentum**2) * past_ref[m, :, c]
+            return 0
+
+        lax.fori_loop(i * part, (i + 1) * part, fill, 0)
     subtract(me, [own_ref], [0], module_ref, weight_ref, acc_ref)
 
 
@@ -114,7 +126,7 @@
     width = acc_ref.shape[2]
     for piece, d in zip(pieces, distances, strict=True):
         for r in range(CAP):
-            slot = (me ^ d) * CAP + r
+            slot = (me ^ d) * (CAP + 1) + r
             m, weight = module_ref[slot], weight_ref[slot]
             for c in chunks(width):
                 acc_ref[m, :, c] = acc_ref[m, :, c] - weight * piece[r, :, c].astype(jnp.float32)
@@ -156,7 +168,7 @@
     rate = outer_rate * (1.0 + outer_momentum)
     for d in list(range(1, paths)) + [0]:
         for r in range(CAP):
-            m = module_ref[(me ^ d) * CAP + r]
+            m = module_ref[(me ^ d) * (CAP + 1) + r]
             step = rate * scale_ref[m][:, :1]
             for c in chunks(width):
                 pieces[d][r, :, c] = (base_ref[m, :, c] - step * acc_ref[m, :, c]).astype(
@@ -199,7 +211,7 @@
     me = lax.axis_index("path").astype(jnp.int32).reshape(1)
     counts = token_counts.astype(jnp.float32)
     slots = paths * CAP
-    piece = jax.ShapeDtypeStruct((CAP, rows, width), jnp.bfloat16)
+    piece = pltpu.VMEM((CAP, rows, width), jnp.bfloat16)
     module = jax.ShapeDtypeStruct((owned, rows, width), jnp.float32)
     limits = pltpu.CompilerParams(vmem_limit_bytes=32 * 1024 * 1024)
 
@@ -213,7 +225,7 @@
         functools.partial(pack_kernel, paths, owned),
         out_shape=[jax.ShapeDtypeStruct((slots,), jnp.int32)] + [piece] * paths,
         in_specs=[SMEM, SMEM, ANY],
-        out_specs=[SMEM] + [ANY] * paths,
+        out_specs=[SMEM] + [VMEM] * paths,
         scratch_shapes=[pltpu.SMEM((paths,), jnp.int32), pltpu.SemaphoreType.DMA((slots,))],
         name="pack",
     )(me, module_ids, path_params.reshape(held, rows, width))
@@ -221,18 +233,23 @@
     table, weights, total, acc, base = pl.pallas_call(
         functools.partial(early_kernel, paths),
         out_shape=[
-            jax.ShapeDtypeStruct((slots,), jnp.int32),
-            jax.ShapeDtypeStruct((slots,), jnp.float32),
+            jax.ShapeDtypeStruct((paths * (CAP + 1),), jnp.int32),
+            jax.ShapeDtypeStruct((paths * (CAP + 1),), jnp.float32),
             jax.ShapeDtypeStruct((owned,), jnp.float32),
             pltpu.VMEM(module.shape, module.dtype),
             pltpu.VMEM(module.shape, module.dtype),
         ],
-        in_specs=[SMEM] * 3 + [VMEM] * 3,
+        in_specs=[SMEM] * 3 + [VMEM] + [ANY] * 2,
         out_specs=[SMEM] * 3 + [VMEM] * 2,
+        scratch_shapes=[
+            pltpu.VMEM(module.shape, module.dtype),
+            pltpu.VMEM(module.shape, module.dtype),
+            pltpu.SemaphoreType.DMA((2, PARTS)),
+        ],
         compiler_params=limits,
         cost_estimate=pl.CostEstimate(flops=10**6, bytes_accessed=12 * 2**20, transcendentals=0),
         name="early",
-    )(me, module_ids, counts, packed[0], global_params, momentum)
+    )(me, module_ids, counts, in_vmem(packed[0]), global_params, momentum)
     acc, squares = pl.pallas_call(
         functools.partial(combine_kernel, paths),
         out_shape=[
@@ -244,10 +261,10 @@
         input_output_aliases={4: 0},
         compiler_params=limits,
         name="combine",
-    )(me, table, weights, total, in_vmem(acc), *arrived)
+    )(me, table, weights, total, in_vmem(acc), *[in_vmem(x) for x in arrived])
     parts = [squares] + [
         lax.ppermute(squares, "shard", [(i, (i + d) % shards) for i in range(shards)])
-        for d in range(1, shards)
+        for d in sorted(range(1, shards), key=lambda d: (d != 2, d))
     ]
     scale, *outgoing = pl.pallas_call(
         functools.partial(send_kernel, paths, shards),
@@ -272,11 +289,11 @@
     path_out = pl.pallas_call(
         functools.partial(unpack_kernel, paths),
         out_shape=jax.ShapeDtypeStruct(path_params.shape, path_params.dtype),
-        in_specs=[SMEM] * 2 + [ANY] * paths,
+        in_specs=[SMEM] * 2 + [VMEM] * paths,
         out_specs=ANY,
         scratch_shapes=[pltpu.SemaphoreType.DMA((slots,))],
         name="unpack",
-    )(me, places, outgoing[0], *returned)
+    )(me, places, *[in_vmem(x) for x in [outgoing[0], *returned]])
     return updated, velocity, path_out
 
 

time: 115 us -> 48.5 us (0.42)
  Pallas kernels: 81.3 us -> 16.1 us
  starting transfers between devices: 22.4 us -> 25.2 us
  waiting for transfers between devices: 3.83 us -> 1.55 us
  local copies, waits for them, and re-layouts: 5.52 us -> 3.87 us
    pallas_call x1, Pallas kernels: 33.7 us -> 1.76 us  [on_device(): pl.pallas_call(functools.partial(unpack_kernel, paths), out_shape=jax.Sha...]
    pallas_call x1, Pallas kernels: 34.7 us -> 3.11 us  [on_device(): pl.pallas_call(functools.partial(pack_kernel, paths, owned), out_shape=[j...]
    ppermute x14, waiting for transfers between devices: 2.4 us -> 0.51 us  [exchange(): lax.ppermute(pieces[d], 'path', [(i, i ^ d) for i in range(paths)])]
    ppermute x14, starting transfers between devices: 17.7 us -> 19.6 us  [exchange(): lax.ppermute(pieces[d], 'path', [(i, i ^ d) for i in range(paths)])]
    pallas_call x1, Pallas kernels: 4.54 us -> 2.81 us  [on_device(): pl.pallas_call(functools.partial(early_kernel, paths), out_shape=[jax.Sha...]
    unnamed x26 -> x8, local copies, waits for them, and re-layouts: 5.52 us -> 3.87 us
  transfers between devices with their start and end apart: 17 -> 17, of which waited for: 4 -> 2; matrix products, arithmetic and copies ran while one was open for 1% -> 1% of each run, Pallas kernels for 10% -> 19%
where the time goes in v2:
time: 48.5 us; the launch traced here: 48.1 us
  starting transfers between devices  25.2 us (52%)
  Pallas kernels  16.1 us (33%)
  local copies, waits for them, and re-layouts  3.87 us (8%)
  waiting for transfers between devices  1.55 us (3%)
  between operations  0.72 us (1%)
  other arithmetic  0.69 us (1%)
    ppermute x14, starting transfers between devices, exchange(): lax.ppermute(pieces[d], 'path', [(i, i ^ d) for i in range(paths)])  19.6 us
    pallas_call x1, Pallas kernels, on_device(): pl.pallas_call(store_kernel, out_shape=[module] * 2, grid=(owned,), in_sp...  6.41 us
    ppermute x3, starting transfers between devices, on_device(): lax.ppermute(squares, 'shard', [(i, (i + d) % shards) for i in range(shar...  5.64 us
    unnamed x8, local copies, waits for them, and re-layouts  3.87 us
    pallas_call x1, Pallas kernels, on_device(): pl.pallas_call(functools.partial(pack_kernel, paths, owned), out_shape=[j...  3.11 us
    pallas_call x1, Pallas kernels, on_device(): pl.pallas_call(functools.partial(early_kernel, paths), out_shape=[jax.Sha...  2.81 us
    pallas_call x1, Pallas kernels, on_device(): pl.pallas_call(functools.partial(unpack_kernel, paths), out_shape=jax.Sha...  1.76 us
    ppermute x3, waiting for transfers between devices, on_device(): lax.ppermute(squares, 'shard', [(i, (i + d) % shards) for i in range(shar...  1.04 us
  transfers between devices with their start and end apart: 17, of which 2 were waited for; matrix products, arithmetic and copies ran while one was open for 1% of the time, Pallas kernels for 19%

profile of v2, /device:TPU:1, one launch (start us, length us, event | category | flops | bytes accessed | tf_op | source)
XLA Modules:
  0.0 48.1 jit_solution(6726150833585361475)
XLA Ops:
  0.6 3.1 %pack.1 = (s32[16]{0:T(128)}, bf16[2,8,4096]{2,1,0:T(8,128)(2,1)S(1)}, bf16[2,8,4096]{2,1,0:T(8,128)(2,1)S(1)}, bf16[2,8,4096]{2,1,0:T(8,128)(2,1)S(1)}, bf16[2,...) custom-call(s32[1]{0:T(128)} %bitcast.me_ref, ...), custom_call_target="tpu_custom_call" | custom-call | tf_op jit(solution)/shard_map/pack/pallas_call | solution.py:224
  3.9 2.7 %collective-permute-start.1 = (bf16[2,8,4096]{2,1,0:T(8,128)(2,1)S(1)}, bf16[2,8,4096]{2,1,0:T(8,128)(2,1)S(1)}, u32[]{:S(2)}, u32[]{:S(2)}) collective-permute-start(bf16[2,8,4096]{2,1,0:T(8,128)(2,1)S(1)} %get-tuple-element.36), channel_id=1, source_target_pairs={{0,8},{4,12},{8,0},{12,4},{16,24},{20,28},{24,16},{28,20},{1,9},{5... | collective-permute-start | bytes 393224 | tf_op jit(solution)/shard_map/ppermute | solution.py:220
  6.6 1.7 %collective-permute-start.3 = (bf16[2,8,4096]{2,1,0:T(8,128)(2,1)S(1)}, bf16[2,8,4096]{2,1,0:T(8,128)(2,1)S(1)}, u32[]{:S(2)}, u32[]{:S(2)}) collective-permute-start(bf16[2,8,4096]{2,1,0:T(8,128)(2,1)S(1)} %get-tuple-element.38), channel_id=1, source_target_pairs={{0,16},{4,20},{8,24},{12,28},{16,0},{20,4},{24,8},{28,12},{1,17},{... | collective-permute-start | bytes 393224 | tf_op jit(solution)/shard_map/ppermute | solution.py:220
  8.6 2.4 %collective-permute-start.5 = (bf16[2,8,4096]{2,1,0:T(8,128)(2,1)S(1)}, bf16[2,8,4096]{2,1,0:T(8,128)(2,1)S(1)}, u32[]{:S(2)}, u32[]{:S(2)}) collective-permute-start(bf16[2,8,4096]{2,1,0:T(8,128)(2,1)S(1)} %get-tuple-element.40), channel_id=1, source_target_pairs={{0,24},{4,28},{8,16},{12,20},{16,8},{20,12},{24,0},{28,4},{1,25},{... | collective-permute-start | bytes 393224 | tf_op jit(solution)/shard_map/ppermute | solution.py:220
  11.0 2.7 %collective-permute-start.6 = (bf16[2,8,4096]{2,1,0:T(8,128)(2,1)S(1)}, bf16[2,8,4096]{2,1,0:T(8,128)(2,1)S(1)}, u32[]{:S(2)}, u32[]{:S(2)}) collective-permute-start(bf16[2,8,4096]{2,1,0:T(8,128)(2,1)S(1)} %get-tuple-element.41), channel_id=1, source_target_pairs={{0,28},{4,24},{8,20},{12,16},{16,12},{20,8},{24,4},{28,0},{1,29},{... | collective-permute-start | bytes 393224 | tf_op jit(solution)/shard_map/ppermute | solution.py:220
  13.7 0.7 %convert_element_type.3.counts_ref = f32[8,16]{1,0:T(8,128)S(1)} convert(s32[8,16]{1,0:T(8,128)} %param.9) | non-fusion elementwise | flops 128 | bytes 1024 | tf_op jit(solution)/shard_map/convert_element_type | solution.py:212
  14.4 1.6 %copy-done = f32[16,8,4096]{2,1,0:T(8,128)S(1)} copy-done((f32[16,8,4096]{2,1,0:T(8,128)S(1)}, f32[16,8,4096]{2,1,0:T(8,128)}, u32[]{:S(2)}) %copy-start) | copy-done | bytes 2097176
  16.0 1.6 %copy-done.2 = f32[16,8,4096]{2,1,0:T(8,128)S(1)} copy-done((f32[16,8,4096]{2,1,0:T(8,128)S(1)}, f32[16,8,4096]{2,1,0:T(8,128)}, u32[]{:S(2)}) %copy-start.2) | copy-done | bytes 2097176
  17.6 0.7 %copy-done.3 = s32[8,16]{1,0:T(8,128)S(1)} copy-done((s32[8,16]{1,0:T(8,128)S(1)}, s32[8,16]{1,0:T(8,128)}, u32[]{:S(2)}) %copy-start.3) | copy-done | bytes 536
  18.3 2.8 %early.1 = (s32[24]{0:T(128)S(1)}, f32[24]{0:T(128)S(1)}, f32[16]{0:T(128)S(1)}, f32[16,8,4096]{2,1,0:T(8,128)S(1)}, f32[16,8,4096]{2,1,0:T(8,128)S(1)}) custom-call(s32[1]{0:T(128)} %bitcast.me_ref, s32[8,16]{1,0:T(8,128)S(1)} %copy-done.3, f32[8,16]{1,0:T(8,128)S(1)} %convert_element_type.3.counts_ref, bf16[2,8,4096]{2,1,0:T(8,128)(2,1)S(1)} %get-tuple-element.30.own_ref, ...), custom_call_target="tpu_custom_call" | custom-call | flops 1000000 | bytes 12582912 | tf_op jit(solution)/shard_map/early/pallas_call | solution.py:233
  21.2 1.0 %combine.1 = (f32[16,8,4096]{2,1,0:T(8,128)S(1)}, f32[16,128]{1,0:T(8,128)S(1)}) custom-call(s32[1]{0:T(128)} %bitcast.me_ref, s32[24]{0:T(128)S(1)} %get-tuple-element.31.module_ref, f32[24]{0:T(128)S(1)} %get-tuple-element.33.weight_ref, f32[16]{0:T(128)S(1)} %get-tuple-element.32.total_ref, ...), custom_call_target="tpu_custom_call", output_to_operand_aliasing={{0}: (4, {})} | custom-call | tf_op jit(solution)/shard_map/combine/pallas_call | solution.py:253
  22.2 2.4 %collective-permute-start.7 = (f32[16,128]{1,0:T(8,128)S(1)}, f32[16,128]{1,0:T(8,128)S(1)}, u32[]{:S(2)}, u32[]{:S(2)}) collective-permute-start(f32[16,128]{1,0:T(8,128)S(1)} %get-tuple-element.44.rest_0_), channel_id=1, source_target_pairs={{0,2},{1,3},{2,0},{3,1},{4,6},{5,7},{6,4},{7,5},{8,10},{9,11},{10,... | collective-permute-start | bytes 24584 | tf_op jit(solution)/shard_map/ppermute | solution.py:266
  24.5 1.3 %collective-permute-start.8 = (f32[16,128]{1,0:T(8,128)S(1)}, f32[16,128]{1,0:T(8,128)S(1)}, u32[]{:S(2)}, u32[]{:S(2)}) collective-permute-start(f32[16,128]{1,0:T(8,128)S(1)} %get-tuple-element.44.rest_0_), channel_id=1, source_target_pairs={{0,1},{1,2},{2,3},{3,0},{4,5},{5,6},{6,7},{7,4},{8,9},{9,10},{10,1... | collective-permute-start | bytes 24584 | tf_op jit(solution)/shard_map/ppermute | solution.py:266
  25.8 2.0 %collective-permute-start.9 = (f32[16,128]{1,0:T(8,128)S(1)}, f32[16,128]{1,0:T(8,128)S(1)}, u32[]{:S(2)}, u32[]{:S(2)}) collective-permute-start(f32[16,128]{1,0:T(8,128)S(1)} %get-tuple-element.44.rest_0_), channel_id=1, source_target_pairs={{0,3},{1,0},{2,1},{3,2},{4,7},{5,4},{6,5},{7,6},{8,11},{9,8},{10,9... | collective-permute-start | bytes 24584 | tf_op jit(solution)/shard_map/ppermute | solution.py:266
  27.8 1.0 %collective-permute-done.8.rest_2_ = f32[16,128]{1,0:T(8,128)S(1)} collective-permute-done((f32[16,128]{1,0:T(8,128)S(1)}, f32[16,128]{1,0:T(8,128)S(1)}, u32[]{:S(2)}, u32[]{:S(2)}) %collective-permute-start.8) | collective-permute-done | bytes 8224 | tf_op jit(solution)/shard_map/ppermute | solution.py:266
  28.8 1.0 %send.1 = (f32[16,8,128]{2,1,0:T(8,128)S(1)}, bf16[2,8,4096]{2,1,0:T(8,128)(2,1)S(1)}, bf16[2,8,4096]{2,1,0:T(8,128)(2,1)S(1)}, bf16[2,8,4096]{2,1,0:T(8,128)(2,...) custom-call(s32[1]{0:T(128)} %bitcast.me_ref, ...), custom_call_target="tpu_custom_call" | custom-call | tf_op jit(solution)/shard_map/send/pallas_call | solution.py:269
  29.8 1.1 %collective-permute-start.10 = (bf16[2,8,4096]{2,1,0:T(8,128)(2,1)S(1)}, bf16[2,8,4096]{2,1,0:T(8,128)(2,1)S(1)}, u32[]{:S(2)}, u32[]{:S(2)}) collective-permute-start(bf16[2,8,4096]{2,1,0:T(8,128)(2,1)S(1)} %get-tuple-element.50), channel_id=1, source_target_pairs={{0,4},{4,0},{8,12},{12,8},{16,20},{20,16},{24,28},{28,24},{1,5},{5... | collective-permute-start | bytes 393224 | tf_op jit(solution)/shard_map/ppermute | solution.py:220
  31.0 1.3 %collective-permute-start.11 = (bf16[2,8,4096]{2,1,0:T(8,128)(2,1)S(1)}, bf16[2,8,4096]{2,1,0:T(8,128)(2,1)S(1)}, u32[]{:S(2)}, u32[]{:S(2)}) collective-permute-start(bf16[2,8,4096]{2,1,0:T(8,128)(2,1)S(1)} %get-tuple-element.51), channel_id=1, source_target_pairs={{0,8},{4,12},{8,0},{12,4},{16,24},{20,28},{24,16},{28,20},{1,9},{5... | collective-permute-start | bytes 393224 | tf_op jit(solution)/shard_map/ppermute | solution.py:220
  32.7 1.3 %collective-permute-start.13 = (bf16[2,8,4096]{2,1,0:T(8,128)(2,1)S(1)}, bf16[2,8,4096]{2,1,0:T(8,128)(2,1)S(1)}, u32[]{:S(2)}, u32[]{:S(2)}) collective-permute-start(bf16[2,8,4096]{2,1,0:T(8,128)(2,1)S(1)} %get-tuple-element.53), channel_id=1, source_target_pairs={{0,16},{4,20},{8,24},{12,28},{16,0},{20,4},{24,8},{28,12},{1,17},{... | collective-permute-start | bytes 393224 | tf_op jit(solution)/shard_map/ppermute | solution.py:220
  33.9 0.5 %collective-permute-start.14 = (bf16[2,8,4096]{2,1,0:T(8,128)(2,1)S(1)}, bf16[2,8,4096]{2,1,0:T(8,128)(2,1)S(1)}, u32[]{:S(2)}, u32[]{:S(2)}) collective-permute-start(bf16[2,8,4096]{2,1,0:T(8,128)(2,1)S(1)} %get-tuple-element.54), channel_id=1, source_target_pairs={{0,20},{4,16},{8,28},{12,24},{16,4},{20,0},{24,12},{28,8},{1,21},{... | collective-permute-start | bytes 393224 | tf_op jit(solution)/shard_map/ppermute | solution.py:220
  34.5 2.2 %collective-permute-start.15 = (bf16[2,8,4096]{2,1,0:T(8,128)(2,1)S(1)}, bf16[2,8,4096]{2,1,0:T(8,128)(2,1)S(1)}, u32[]{:S(2)}, u32[]{:S(2)}) collective-permute-start(bf16[2,8,4096]{2,1,0:T(8,128)(2,1)S(1)} %get-tuple-element.55), channel_id=1, source_target_pairs={{0,24},{4,28},{8,16},{12,20},{16,8},{20,12},{24,0},{28,4},{1,25},{... | collective-permute-start | bytes 393224 | tf_op jit(solution)/shard_map/ppermute | solution.py:220
  36.7 2.7 %collective-permute-start.16 = (bf16[2,8,4096]{2,1,0:T(8,128)(2,1)S(1)}, bf16[2,8,4096]{2,1,0:T(8,128)(2,1)S(1)}, u32[]{:S(2)}, u32[]{:S(2)}) collective-permute-start(bf16[2,8,4096]{2,1,0:T(8,128)(2,1)S(1)} %get-tuple-element.56), channel_id=1, source_target_pairs={{0,28},{4,24},{8,20},{12,16},{16,12},{20,8},{24,4},{28,0},{1,29},{... | collective-permute-start | bytes 393224 | tf_op jit(solution)/shard_map/ppermute | solution.py:220
  39.4 6.4 %store.1 = (f32[16,8,4096]{2,1,0:T(8,128)}, f32[16,8,4096]{2,1,0:T(8,128)}) custom-call(f32[16,8,128]{2,1,0:T(8,128)S(1)} %get-tuple-element.45.scale_ref, f32[16,8,4096]{2,1,0:T(8,128)S(1)} %get-tuple-element.42.acc_ref, f32[16,8,4096]{2,1,0:T(8,128)S(1)} %get-tuple-element.43.base_ref, f32[16,8,4096]{2,1,0:T(8,128)S(1)} %copy-done.1), custom_call_target="tpu_custom_call" | custom-call | flops 1000000 | bytes 12582912 | tf_op jit(solution)/shard_map/store/pallas_call | solution.py:279
  46.3 1.8 %unpack.1 = bf16[1,16,8,4096]{3,2,1,0:T(8,128)(2,1)} custom-call(s32[1]{0:T(128)} %bitcast.me_ref, s32[16]{0:T(128)} %get-tuple-element.48.places_ref, bf16[2,8,4096]{2,1,0:T(8,128)(2,1)S(1)} %get-tuple-element.49.rest_0_, bf16[2,8,4096]{2,1,0:T(8,128)(2,1)S(1)} %collective-permute-done.10.rest_1_, bf16[2,8,4096]{2,1,0:T(8,128)(2,1)S(1)} %collective-permute-done.11.rest_2_, ...), custom_call_target="tpu_custom_call" | custom-call | tf_op jit(solution)/shard_map/unpack/pallas_call | solution.py:289
  (25 shorter events, 1.5 us)
Async XLA Ops:
  3.7 4.8 %collective-permute-start = (bf16[2,8,4096]{2,1,0:T(8,128)(2,1)S(1)}, bf16[2,8,4096]{2,1,0:T(8,128)(2,1)S(1)}, u32[]{:S(2)}, u32[]{:S(2)}) collective-permute-start(bf16[2,8,4096]{2,1,0:T(8,128)(2,1)S(1)} %get-tuple-element.35), channel_id=1, source_target_pairs={{0,4},{4,0},{8,12},{12,8},{16,20},{20,16},{24,28},{28,24},{1,5},{5... | collective-permute-start | bytes 393224 | tf_op jit(solution)/shard_map/ppermute | solution.py:220
  3.9 7.1 %collective-permute-start.1 = (bf16[2,8,4096]{2,1,0:T(8,128)(2,1)S(1)}, bf16[2,8,4096]{2,1,0:T(8,128)(2,1)S(1)}, u32[]{:S(2)}, u32[]{:S(2)}) collective-permute-start(bf16[2,8,4096]{2,1,0:T(8,128)(2,1)S(1)} %get-tuple-element.36), channel_id=1, source_target_pairs={{0,8},{4,12},{8,0},{12,4},{16,24},{20,28},{24,16},{28,20},{1,9},{5... | collective-permute-start | bytes 393224 | tf_op jit(solution)/shard_map/ppermute | solution.py:220
  6.5 14.6 %collective-permute-start.2 = (bf16[2,8,4096]{2,1,0:T(8,128)(2,1)S(1)}, bf16[2,8,4096]{2,1,0:T(8,128)(2,1)S(1)}, u32[]{:S(2)}, u32[]{:S(2)}) collective-permute-start(bf16[2,8,4096]{2,1,0:T(8,128)(2,1)S(1)} %get-tuple-element.37), channel_id=1, source_target_pairs={{0,12},{4,8},{8,4},{12,0},{16,28},{20,24},{24,20},{28,16},{1,13},{... | collective-permute-start | bytes 393224 | tf_op jit(solution)/shard_map/ppermute | solution.py:220
  6.6 14.5 %collective-permute-start.3 = (bf16[2,8,4096]{2,1,0:T(8,128)(2,1)S(1)}, bf16[2,8,4096]{2,1,0:T(8,128)(2,1)S(1)}, u32[]{:S(2)}, u32[]{:S(2)}) collective-permute-start(bf16[2,8,4096]{2,1,0:T(8,128)(2,1)S(1)} %get-tuple-element.38), channel_id=1, source_target_pairs={{0,16},{4,20},{8,24},{12,28},{16,0},{20,4},{24,8},{28,12},{1,17},{... | collective-permute-start | bytes 393224 | tf_op jit(solution)/shard_map/ppermute | solution.py:220
  8.3 12.9 %collective-permute-start.4 = (bf16[2,8,4096]{2,1,0:T(8,128)(2,1)S(1)}, bf16[2,8,4096]{2,1,0:T(8,128)(2,1)S(1)}, u32[]{:S(2)}, u32[]{:S(2)}) collective-permute-start(bf16[2,8,4096]{2,1,0:T(8,128)(2,1)S(1)} %get-tuple-element.39), channel_id=1, source_target_pairs={{0,20},{4,16},{8,28},{12,24},{16,4},{20,0},{24,12},{28,8},{1,21},{... | collective-permute-start | bytes 393224 | tf_op jit(solution)/shard_map/ppermute | solution.py:220
  8.6 12.6 %collective-permute-start.5 = (bf16[2,8,4096]{2,1,0:T(8,128)(2,1)S(1)}, bf16[2,8,4096]{2,1,0:T(8,128)(2,1)S(1)}, u32[]{:S(2)}, u32[]{:S(2)}) collective-permute-start(bf16[2,8,4096]{2,1,0:T(8,128)(2,1)S(1)} %get-tuple-element.40), channel_id=1, source_target_pairs={{0,24},{4,28},{8,16},{12,20},{16,8},{20,12},{24,0},{28,4},{1,25},{... | collective-permute-start | bytes 393224 | tf_op jit(solution)/shard_map/ppermute | solution.py:220
  11.0 10.2 %collective-permute-start.6 = (bf16[2,8,4096]{2,1,0:T(8,128)(2,1)S(1)}, bf16[2,8,4096]{2,1,0:T(8,128)(2,1)S(1)}, u32[]{:S(2)}, u32[]{:S(2)}) collective-permute-start(bf16[2,8,4096]{2,1,0:T(8,128)(2,1)S(1)} %get-tuple-element.41), channel_id=1, source_target_pairs={{0,28},{4,24},{8,20},{12,16},{16,12},{20,8},{24,4},{28,0},{1,29},{... | collective-permute-start | bytes 393224 | tf_op jit(solution)/shard_map/ppermute | solution.py:220
  14.4 1.6 %copy-start = (f32[16,8,4096]{2,1,0:T(8,128)S(1)}, f32[16,8,4096]{2,1,0:T(8,128)}, u32[]{:S(2)}) copy-start(f32[16,8,4096]{2,1,0:T(8,128)} %past_ref.1) | copy-start | bytes 6291460
  16.0 1.6 %copy-start.2 = (f32[16,8,4096]{2,1,0:T(8,128)S(1)}, f32[16,8,4096]{2,1,0:T(8,128)}, u32[]{:S(2)}) copy-start(f32[16,8,4096]{2,1,0:T(8,128)} %params_hbm.1) | copy-start | bytes 6291460
  17.6 0.7 %copy-start.3 = (s32[8,16]{1,0:T(8,128)S(1)}, s32[8,16]{1,0:T(8,128)}, u32[]{:S(2)}) copy-start(s32[8,16]{1,0:T(8,128)} %ids_ref.3) | copy-start | bytes 1540
  22.2 5.6 %collective-permute-start.7 = (f32[16,128]{1,0:T(8,128)S(1)}, f32[16,128]{1,0:T(8,128)S(1)}, u32[]{:S(2)}, u32[]{:S(2)}) collective-permute-start(f32[16,128]{1,0:T(8,128)S(1)} %get-tuple-element.44.rest_0_), channel_id=1, source_target_pairs={{0,2},{1,3},{2,0},{3,1},{4,6},{5,7},{6,4},{7,5},{8,10},{9,11},{10,... | collective-permute-start | bytes 24584 | tf_op jit(solution)/shard_map/ppermute | solution.py:266
  24.5 4.3 %collective-permute-start.8 = (f32[16,128]{1,0:T(8,128)S(1)}, f32[16,128]{1,0:T(8,128)S(1)}, u32[]{:S(2)}, u32[]{:S(2)}) collective-permute-start(f32[16,128]{1,0:T(8,128)S(1)} %get-tuple-element.44.rest_0_), channel_id=1, source_target_pairs={{0,1},{1,2},{2,3},{3,0},{4,5},{5,6},{6,7},{7,4},{8,9},{9,10},{10,1... | collective-permute-start | bytes 24584 | tf_op jit(solution)/shard_map/ppermute | solution.py:266
  25.8 3.0 %collective-permute-start.9 = (f32[16,128]{1,0:T(8,128)S(1)}, f32[16,128]{1,0:T(8,128)S(1)}, u32[]{:S(2)}, u32[]{:S(2)}) collective-permute-start(f32[16,128]{1,0:T(8,128)S(1)} %get-tuple-element.44.rest_0_), channel_id=1, source_target_pairs={{0,3},{1,0},{2,1},{3,2},{4,7},{5,4},{6,5},{7,6},{8,11},{9,8},{10,9... | collective-permute-start | bytes 24584 | tf_op jit(solution)/shard_map/ppermute | solution.py:266
  28.8 10.6 %copy-start.1 = (f32[16,8,4096]{2,1,0:T(8,128)S(1)}, f32[16,8,4096]{2,1,0:T(8,128)}, u32[]{:S(2)}) copy-start(f32[16,8,4096]{2,1,0:T(8,128)} %past_ref.1) | copy-start | bytes 6291460
  29.8 4.6 %collective-permute-start.10 = (bf16[2,8,4096]{2,1,0:T(8,128)(2,1)S(1)}, bf16[2,8,4096]{2,1,0:T(8,128)(2,1)S(1)}, u32[]{:S(2)}, u32[]{:S(2)}) collective-permute-start(bf16[2,8,4096]{2,1,0:T(8,128)(2,1)S(1)} %get-tuple-element.50), channel_id=1, source_target_pairs={{0,4},{4,0},{8,12},{12,8},{16,20},{20,16},{24,28},{28,24},{1,5},{5... | collective-permute-start | bytes 393224 | tf_op jit(solution)/shard_map/ppermute | solution.py:220
  31.0 5.7 %collective-permute-start.11 = (bf16[2,8,4096]{2,1,0:T(8,128)(2,1)S(1)}, bf16[2,8,4096]{2,1,0:T(8,128)(2,1)S(1)}, u32[]{:S(2)}, u32[]{:S(2)}) collective-permute-start(bf16[2,8,4096]{2,1,0:T(8,128)(2,1)S(1)} %get-tuple-element.51), channel_id=1, source_target_pairs={{0,8},{4,12},{8,0},{12,4},{16,24},{20,28},{24,16},{28,20},{1,9},{5... | collective-permute-start | bytes 393224 | tf_op jit(solution)/shard_map/ppermute | solution.py:220
  32.2 13.6 %collective-permute-start.12 = (bf16[2,8,4096]{2,1,0:T(8,128)(2,1)S(1)}, bf16[2,8,4096]{2,1,0:T(8,128)(2,1)S(1)}, u32[]{:S(2)}, u32[]{:S(2)}) collective-permute-start(bf16[2,8,4096]{2,1,0:T(8,128)(2,1)S(1)} %get-tuple-element.52), channel_id=1, source_target_pairs={{0,12},{4,8},{8,4},{12,0},{16,28},{20,24},{24,20},{28,16},{1,13},{... | collective-permute-start | bytes 393224 | tf_op jit(solution)/shard_map/ppermute | solution.py:220
  32.7 13.2 %collective-permute-start.13 = (bf16[2,8,4096]{2,1,0:T(8,128)(2,1)S(1)}, bf16[2,8,4096]{2,1,0:T(8,128)(2,1)S(1)}, u32[]{:S(2)}, u32[]{:S(2)}) collective-permute-start(bf16[2,8,4096]{2,1,0:T(8,128)(2,1)S(1)} %get-tuple-element.53), channel_id=1, source_target_pairs={{0,16},{4,20},{8,24},{12,28},{16,0},{20,4},{24,8},{28,12},{1,17},{... | collective-permute-start | bytes 393224 | tf_op jit(solution)/shard_map/ppermute | solution.py:220
  33.9 12.4 %collective-permute-start.14 = (bf16[2,8,4096]{2,1,0:T(8,128)(2,1)S(1)}, bf16[2,8,4096]{2,1,0:T(8,128)(2,1)S(1)}, u32[]{:S(2)}, u32[]{:S(2)}) collective-permute-start(bf16[2,8,4096]{2,1,0:T(8,128)(2,1)S(1)} %get-tuple-element.54), channel_id=1, source_target_pairs={{0,20},{4,16},{8,28},{12,24},{16,4},{20,0},{24,12},{28,8},{1,21},{... | collective-permute-start | bytes 393224 | tf_op jit(solution)/shard_map/ppermute | solution.py:220
  34.5 11.9 %collective-permute-start.15 = (bf16[2,8,4096]{2,1,0:T(8,128)(2,1)S(1)}, bf16[2,8,4096]{2,1,0:T(8,128)(2,1)S(1)}, u32[]{:S(2)}, u32[]{:S(2)}) collective-permute-start(bf16[2,8,4096]{2,1,0:T(8,128)(2,1)S(1)} %get-tuple-element.55), channel_id=1, source_target_pairs={{0,24},{4,28},{8,16},{12,20},{16,8},{20,12},{24,0},{28,4},{1,25},{... | collective-permute-start | bytes 393224 | tf_op jit(solution)/shard_map/ppermute | solution.py:220
  36.7 9.7 %collective-permute-start.16 = (bf16[2,8,4096]{2,1,0:T(8,128)(2,1)S(1)}, bf16[2,8,4096]{2,1,0:T(8,128)(2,1)S(1)}, u32[]{:S(2)}, u32[]{:S(2)}) collective-permute-start(bf16[2,8,4096]{2,1,0:T(8,128)(2,1)S(1)} %get-tuple-element.56), channel_id=1, source_target_pairs={{0,28},{4,24},{8,20},{12,16},{16,12},{20,8},{24,4},{28,0},{1,29},{... | collective-permute-start | bytes 393224 | tf_op jit(solution)/shard_map/ppermute | solution.py:220

commit v3 on v2

v3 whole, which is shorter than its diff:
```python
import functools

import jax
import jax.numpy as jnp
from jax import lax
from jax.experimental import pallas as pl
from jax.experimental.pallas import tpu as pltpu
from jax.sharding import PartitionSpec as P

CAP = 2
CHUNK = 1024
PARTS = 4
outer_momentum = 0.9
outer_rate = 0.7

SMEM = pl.BlockSpec(memory_space=pltpu.SMEM)
VMEM = pl.BlockSpec(memory_space=pltpu.VMEM)
ANY = pl.BlockSpec(memory_space=pl.ANY)


def in_vmem(*arrays):
    return [pltpu.with_memory_space_constraint(x, pltpu.VMEM) for x in arrays]


def in_hbm(*arrays):
    return [pltpu.with_memory_space_constraint(x, pltpu.HBM) for x in arrays]


def chunks(width):
    step = CHUNK if width % CHUNK == 0 else width
    return [pl.ds(at, step) for at in range(0, width, step)]


def pack_kernel(paths, owned, order, me_ref, ids_ref, local_ref, places_ref, *rest):
    pieces, (seen, sems) = rest[:paths], rest[paths:]
    me = me_ref[0]
    for i in range(paths):
        seen[i] = jnp.int32(0)
    for i in range(paths * CAP):
        places_ref[i] = jnp.int32(-1)
    for k in range(ids_ref.shape[1]):
        group = lax.div(ids_ref[me, k], jnp.int32(owned))
        rank = seen[group]
        seen[group] = rank + 1
        places_ref[group * CAP + rank] = jnp.int32(k)
    copies = []
    for d in order:
        for r in range(CAP):
            k = jnp.maximum(places_ref[(me ^ d) * CAP + r], 0)
            copy = pltpu.make_async_copy(
                local_ref.at[k], pieces[d].at[r], sems.at[d * CAP + r]
            )
            copy.start()
            copies.append(copy)
    for copy in copies:
        copy.wait()


def find_slots(me, owned, ids_ref, counts_ref, module_ref, weight_ref, total_ref):
    paths, held = ids_ref.shape

    def reset(i, _):
        total_ref[i] = jnp.float32(0.0)
        return 0

    def one(path, _):
        first = path * (CAP + 1)
        for r in range(CAP):
            module_ref[first + r] = jnp.int32(0)
            weight_ref[first + r] = jnp.float32(0.0)
        rank = jnp.int32(0)
        for k in range(held):
            at = ids_ref[path, k] - me * owned
            mine = (at >= 0) & (at < owned)
            slot = first + jnp.where(mine, rank, CAP)
            module_ref[slot] = at
            weight_ref[slot] = counts_ref[path, k].astype(jnp.float32)
            rank = rank + mine.astype(jnp.int32)
        for r in range(CAP):
            at = module_ref[first + r]
            total_ref[at] = total_ref[at] + weight_ref[first + r]
        return 0

    lax.fori_loop(0, owned, reset, 0)
    lax.fori_loop(0, paths, one, 0)


def subtract(me, pieces, distances, module_ref, weight_ref, acc_ref):
    width = acc_ref.shape[2]
    for piece, d in zip(pieces, distances, strict=True):
        for r in range(CAP):
            slot = (me ^ d) * (CAP + 1) + r
            m, weight = module_ref[slot], weight_ref[slot]
            for c in chunks(width):
                acc_ref[m, :, c] = acc_ref[m, :, c] - weight * piece[r, :, c].astype(jnp.float32)


def prepare(me, own_ref, params_hbm, past_hbm, tables, acc_ref, base_ref, params_ref, past_ref, sems, find):
    owned, _, width = acc_ref.shape
    part = owned // PARTS

    def copies(i):
        at = pl.ds(i * part, part)
        return [
            pltpu.make_async_copy(hbm.at[at], ref.at[at], sems.at[n, i])
            for n, (hbm, ref) in enumerate(((params_hbm, params_ref), (past_hbm, past_ref)))
        ]

    for i in range(PARTS):
        for copy in copies(i):
            copy.start()
    find()
    module_ref, weight_ref, total_ref = tables
    for i in range(PARTS):
        for copy in copies(i):
            copy.wait()

        def fill(m, _):
            for c in chunks(width):
                params = params_ref[m, :, c]
                acc_ref[m, :, c] = total_ref[m] * params
                base_ref[m, :, c] = params - (outer_rate * outer_momentum**2) * past_ref[m, :, c]
            return 0

        lax.fori_loop(i * part, (i + 1) * part, fill, 0)
    subtract(me, [own_ref], [0], module_ref, weight_ref, acc_ref)


def before_kernel(me_ref, ids_ref, counts_ref, own_ref, params_hbm, past_hbm, *rest):
    acc_ref, base_ref, *_, module_ref, weight_ref, total_ref, params_ref, past_ref, sems = rest[
        (len(rest) - 8) // 2 :
    ]
    me = me_ref[0]
    tables = module_ref, weight_ref, total_ref

    @pl.when(lax.rem(me, 2) == 1)
    def _():
        find = functools.partial(find_slots, me, acc_ref.shape[0], ids_ref, counts_ref, *tables)
        prepare(
            me, own_ref, params_hbm, past_hbm, tables, acc_ref, base_ref, params_ref, past_ref, sems, find
        )


def beside_kernel(
    me_ref, ids_ref, counts_ref, own_ref, params_hbm, past_hbm, _acc, _base,
    module_ref, weight_ref, total_ref, acc_ref, base_ref, params_ref, past_ref, sems,
):
    me = me_ref[0]
    tables = module_ref, weight_ref, total_ref
    find = functools.partial(find_slots, me, acc_ref.shape[0], ids_ref, counts_ref, *tables)

    @pl.when(lax.rem(me, 2) == 1)
    def _():
        find()

    @pl.when(lax.rem(me, 2) == 0)
    def _():
        prepare(
            me, own_ref, params_hbm, past_hbm, tables, acc_ref, base_ref, params_ref, past_ref, sems, find
        )


def combine_kernel(paths, me_ref, module_ref, weight_ref, total_ref, acc_in, *rest):
    pieces, (acc_ref, squares_ref) = rest[: paths - 1], rest[paths - 1 :]
    subtract(me_ref[0], pieces, range(1, paths), module_ref, weight_ref, acc_ref)
    owned, rows, width = acc_ref.shape
    for m in range(owned):
        inverse = 1.0 / jnp.maximum(jnp.full((rows, 128), total_ref[m], jnp.float32), 1.0)
        added = jnp.zeros((rows, 128), jnp.float32)
        for at in range(0, width, 128):
            raw = acc_ref[m, :, pl.ds(at, 128)] * inverse
            added = added + raw * raw
        squares_ref[pl.ds(m, 1), :] = jnp.sum(added, axis=0, keepdims=True)


def scales(entries, total, squares):
    inverse = 1.0 / jnp.maximum(total, 1.0)
    mean = jnp.sum(squares, axis=1, keepdims=True) / entries
    factor = jnp.minimum(1.0, 1.0 / jnp.sqrt(mean + 1e-06))
    return inverse * factor


def send_kernel(paths, shards, me_ref, module_ref, total_ref, acc_ref, base_ref, *rest):
    squares, (scale_ref, *pieces) = rest[:shards], rest[shards:]
    me = me_ref[0]
    owned, rows, width = acc_ref.shape
    summed = squares[0][...]
    for other in squares[1:]:
        summed = summed + other[...]
    total = jnp.concatenate(
        [jnp.full((1, 128), total_ref[m], jnp.float32) for m in range(owned)], axis=0
    )
    scale = scales(rows * width * shards, total, summed)
    for m in range(owned):
        scale_ref[m] = jnp.broadcast_to(scale[m : m + 1, :], (rows, 128))
    rate = outer_rate * (1.0 + outer_momentum)
    for d in range(paths):
        for r in range(CAP):
            m = module_ref[(me ^ d) * (CAP + 1) + r]
            step = rate * scale_ref[m][:, :1]
            for c in chunks(width):
                pieces[d][r, :, c] = (base_ref[m, :, c] - step * acc_ref[m, :, c]).astype(
                    jnp.bfloat16
                )


def store_kernel(
    scale_ref, acc_ref, base_ref, past_ref, updated_hbm, velocity_hbm, updated_ref, velocity_ref, sems
):
    rate = outer_rate * (1.0 + outer_momentum)
    owned, _, width = acc_ref.shape
    part = owned // PARTS

    def copies(i):
        at = pl.ds(i * part, part)
        return [
            pltpu.make_async_copy(ref.at[at], hbm.at[at], sems.at[n, i])
            for n, (ref, hbm) in enumerate(
                ((updated_ref, updated_hbm), (velocity_ref, velocity_hbm))
            )
        ]

    for i in range(PARTS):

        def fill(m, _):
            scale = scale_ref[m][:, :1]
            for c in chunks(width):
                delta = scale * acc_ref[m, :, c]
                updated_ref[m, :, c] = base_ref[m, :, c] - rate * delta
                velocity_ref[m, :, c] = outer_momentum * past_ref[m, :, c] + delta
            return 0

        lax.fori_loop(i * part, (i + 1) * part, fill, 0)
        for copy in copies(i):
            copy.start()
    for i in range(PARTS):
        for copy in copies(i):
            copy.wait()


def unpack_kernel(paths, me_ref, places_ref, *rest):
    pieces, (out_ref, sems) = rest[:paths], rest[paths:]
    me = me_ref[0]
    for wait in (False, True):
        for d in range(paths):
            for r in range(CAP):
                k = places_ref[(me ^ d) * CAP + r]

                @pl.when(k >= 0)
                def _():
                    copy = pltpu.make_async_copy(
                        pieces[d].at[r], out_ref.at[0, k], sems.at[d * CAP + r]
                    )
                    if wait:
                        copy.wait()
                    else:
                        copy.start()


def on_device(path_params, global_params, momentum, module_ids, token_counts):
    paths, held = module_ids.shape
    owned, rows, width = global_params.shape
    shards = lax.axis_size("shard")
    me = lax.axis_index("path").astype(jnp.int32).reshape(1)
    module_ids, counts = in_hbm(module_ids, token_counts)
    slots = paths * CAP
    piece = pltpu.VMEM((CAP, rows, width), jnp.bfloat16)
    module = jax.ShapeDtypeStruct((owned, rows, width), jnp.float32)
    held_module = pltpu.VMEM(module.shape, module.dtype)
    tables = [
        jax.ShapeDtypeStruct((paths * (CAP + 1),), jnp.int32),
        jax.ShapeDtypeStruct((paths * (CAP + 1),), jnp.float32),
        jax.ShapeDtypeStruct((owned,), jnp.float32),
    ]
    room = [
        pltpu.VMEM(module.shape, module.dtype),
        pltpu.VMEM(module.shape, module.dtype),
        pltpu.SemaphoreType.DMA((2, PARTS)),
    ]
    limits = pltpu.CompilerParams(vmem_limit_bytes=24 * 1024 * 1024)
    far = sorted(range(2, paths, 2), key=lambda d: (-d.bit_count(), d))

    def to(x, d):
        return lax.ppermute(x, "path", [(i, i ^ d) for i in range(paths)])

    order = [d ^ 1 for d in far] + far + [1, 0]
    places, *packed = pl.pallas_call(
        functools.partial(pack_kernel, paths, owned, order),
        out_shape=[jax.ShapeDtypeStruct((slots,), jnp.int32)] + [piece] * paths,
        in_specs=[SMEM, SMEM, ANY],
        out_specs=[SMEM] + [VMEM] * paths,
        scratch_shapes=[pltpu.SMEM((paths,), jnp.int32), pltpu.SemaphoreType.DMA((slots,))],
        name="pack",
    )(me, module_ids, *in_hbm(path_params.reshape(held, rows, width)))

    through = [packed[d] for d in far] + [to(packed[d ^ 1], 1) for d in far]
    fixed = 6
    acc, base, *passed = pl.pallas_call(
        before_kernel,
        out_shape=[held_module] * 2 + [piece] * len(through),
        in_specs=[SMEM] * 3 + [VMEM] + [ANY] * 2 + [VMEM] * len(through),
        out_specs=[VMEM] * (2 + len(through)),
        input_output_aliases={fixed + i: 2 + i for i in range(len(through))},
        scratch_shapes=[
            pltpu.SMEM(tables[0].shape, jnp.int32),
            pltpu.SMEM(tables[1].shape, jnp.float32),
            pltpu.SMEM(tables[2].shape, jnp.float32),
        ]
        + room,
        compiler_params=limits,
        name="before",
    )(
        me, module_ids, counts, *in_vmem(packed[0]), *in_hbm(global_params, momentum),
        *in_vmem(*through),
    )
    arrived = {}
    for d, x in zip(far, passed[: len(far)], strict=True):
        arrived[d] = to(x, d)
    for d, x in zip(far, passed[len(far) :], strict=True):
        arrived[d ^ 1] = to(x, d)
    arrived[1] = to(packed[1], 1)
    table, weights, total, acc, base = pl.pallas_call(
        beside_kernel,
        out_shape=tables + [held_module] * 2,
        in_specs=[SMEM] * 3 + [VMEM] + [ANY] * 2 + [VMEM] * 2,
        out_specs=[SMEM] * 3 + [VMEM] * 2,
        input_output_aliases={fixed: 3, fixed + 1: 4},
        scratch_shapes=room,
        compiler_params=limits,
        cost_estimate=pl.CostEstimate(flops=10**6, bytes_accessed=12 * 2**20, transcendentals=0),
        name="beside",
    )(
        me, module_ids, counts, *in_vmem(packed[0]), *in_hbm(global_params, momentum),
        *in_vmem(acc, base),
    )
    acc, squares = pl.pallas_call(
        functools.partial(combine_kernel, paths),
        out_shape=[held_module, jax.ShapeDtypeStruct((owned, 128), jnp.float32)],
        in_specs=[SMEM] * 4 + [VMEM] * paths,
        out_specs=[VMEM] * 2,
        input_output_aliases={4: 0},
        compiler_params=limits,
        name="combine",
    )(me, table, weights, total, *in_vmem(acc, *[arrived[d] for d in range(1, paths)]))
    parts = [squares] + [
        lax.ppermute(squares, "shard", [(i, (i + d) % shards) for i in range(shards)])
        for d in sorted(range(1, shards), key=lambda d: (d != 2, d))
    ]
    scale, *outgoing = pl.pallas_call(
        functools.partial(send_kernel, paths, shards),
        out_shape=[jax.ShapeDtypeStruct((owned, rows, 128), jnp.float32)] + [piece] * paths,
        in_specs=[SMEM] * 3 + [VMEM] * (2 + shards),
        out_specs=[VMEM] * (1 + paths),
        compiler_params=limits,
        name="send",
    )(me, table, total, *in_vmem(acc, base), *parts)
    relayed = {d: to(outgoing[d ^ 1], d) for d in far}
    returned = {0: outgoing[0]}
    for d in far:
        returned[d] = to(outgoing[d], d)
    returned[1] = to(outgoing[1], 1)
    for d in far:
        returned[d ^ 1] = to(relayed[d], 1)
    updated, velocity = pl.pallas_call(
        store_kernel,
        out_shape=[module] * 2,
        in_specs=[VMEM] * 4,
        out_specs=[ANY] * 2,
        scratch_shapes=room,
        compiler_params=limits,
        cost_estimate=pl.CostEstimate(flops=10**6, bytes_accessed=12 * 2**20, transcendentals=0),
        name="store",
    )(scale, *in_vmem(acc, base), momentum)
    path_out = pl.pallas_call(
        functools.partial(unpack_kernel, paths),
        out_shape=jax.ShapeDtypeStruct(path_params.shape, path_params.dtype),
        in_specs=[SMEM] * 2 + [VMEM] * paths,
        out_specs=ANY,
        scratch_shapes=[pltpu.SemaphoreType.DMA((slots,))],
        name="unpack",
    )(me, places, *in_vmem(*[returned[d] for d in range(paths)]))
    return updated, velocity, path_out


def solution(mesh):
    placed = (
        P("path", None, "shard", None),
        P("path", "shard", None),
        P("path", "shard", None),
        P(),
        P(),
    )
    return jax.shard_map(
        on_device,
        mesh=mesh,
        in_specs=placed,
        out_specs=(
            P("path", "shard", None),
            P("path", "shard", None),
            P("path", None, "shard", None),
        ),
        check_vma=False,
    )
```

time: 48.5 us -> 50.7 us (1.045)
  waiting for transfers between devices: 1.55 us -> 6.24 us
  local copies, waits for them, and re-layouts: 3.87 us -> 0.01 us
  starting transfers between devices: 25.2 us -> 28.7 us
  Pallas kernels: 16.1 us -> 14.4 us
  other arithmetic: 0.69 us -> 0 us
    ppermute x14 -> x20, waiting for transfers between devices: 0.51 us -> 5.2 us  [to(): return lax.ppermute(x, 'path', [(i, i ^ d) for i in range(paths)])]
    unnamed x8 -> x2, local copies, waits for them, and re-layouts: 3.87 us -> 0.01 us
    ppermute x14 -> x20, starting transfers between devices: 19.6 us -> 22.6 us  [to(): return lax.ppermute(x, 'path', [(i, i ^ d) for i in range(paths)])]
    pallas_call x4 -> x5, Pallas kernels: 13.3 us -> 11.7 us  [the longest x1 3.13 us: on_device(): pl.pallas_call(before_kernel, out_shape=[held_module] * 2 + [piece] * len...]
    convert_element_type x1 -> x0, other arithmetic: 0.69 us -> none  [on_device(): counts = token_counts.astype(jnp.float32)]
  transfers between devices with their start and end apart: 17 -> 23, of which waited for: 2 -> 6; matrix products, arithmetic and copies ran while one was open for 1% -> 0% of each run, Pallas kernels for 19% -> 16%
where the time goes in v3:
time: 50.7 us; the launch traced here: 50 us
  starting transfers between devices  28.7 us (57%)
  Pallas kernels  14.4 us (28%)
  waiting for transfers between devices  6.24 us (12%)
  between operations  0.75 us (1%)
    ppermute x20, starting transfers between devices, to(): return lax.ppermute(x, 'path', [(i, i ^ d) for i in range(paths)])  22.6 us
    ppermute x3, starting transfers between devices, on_device(): lax.ppermute(squares, 'shard', [(i, (i + d) % shards) for i in range(shar...  6.09 us
    ppermute x20, waiting for transfers between devices, to(): return lax.ppermute(x, 'path', [(i, i ^ d) for i in range(paths)])  5.2 us
    pallas_call x1, Pallas kernels, on_device(): pl.pallas_call(before_kernel, out_shape=[held_module] * 2 + [piece] * len...  3.13 us
    pallas_call x1, Pallas kernels, on_device(): pl.pallas_call(functools.partial(pack_kernel, paths, owned, order), out_s...  2.72 us
    pallas_call x1, Pallas kernels, on_device(): pl.pallas_call(store_kernel, out_shape=[module] * 2, in_specs=[VMEM] * 4,...  2.52 us
    pallas_call x1, Pallas kernels, on_device(): pl.pallas_call(beside_kernel, out_shape=tables + [held_module] * 2, in_sp...  2.35 us
    pallas_call x1, Pallas kernels, on_device(): pl.pallas_call(functools.partial(unpack_kernel, paths), out_shape=jax.Sha...  1.76 us
  transfers between devices with their start and end apart: 23, of which 6 were waited for; matrix products, arithmetic and copies ran while one was open for 0% of the time, Pallas kernels for 16%

profile of v3, /device:TPU:1, one launch (start us, length us, event | category | flops | bytes accessed | tf_op | source)
XLA Modules:
  0.0 50.0 jit_solution(16129387975178500707)
XLA Ops:
  0.6 2.7 %pack.1 = (s32[16]{0:T(128)}, bf16[2,8,4096]{2,1,0:T(8,128)(2,1)S(1)}, bf16[2,8,4096]{2,1,0:T(8,128)(2,1)S(1)}, bf16[2,8,4096]{2,1,0:T(8,128)(2,1)S(1)}, bf16[2,...) custom-call(s32[1]{0:T(128)} %bitcast.me_ref, ...), custom_call_target="tpu_custom_call" | custom-call | tf_op jit(solution)/shard_map/pack/pallas_call | solution.py:287
  5.3 3.1 %before.1 = (f32[16,8,4096]{2,1,0:T(8,128)S(1)}, f32[16,8,4096]{2,1,0:T(8,128)S(1)}, bf16[2,8,4096]{2,1,0:T(8,128)(2,1)S(1)}, bf16[2,8,4096]{2,1,0:T(8,128)(2,1)...) custom-call(s32[1]{0:T(128)} %bitcast.me_ref, ...), custom_call_target="tpu_custom_call", output_to_operand_aliasing={{2}: (6, {}), {3}: (7, {}), {4}: (8, {}), {5}: (9, {}), {6}... | custom-call | tf_op jit(solution)/shard_map/before/pallas_call | solution.py:298
  8.4 2.5 %collective-permute-start.4 = (bf16[2,8,4096]{2,1,0:T(8,128)(2,1)S(1)}, bf16[2,8,4096]{2,1,0:T(8,128)(2,1)S(1)}, u32[]{:S(2)}, u32[]{:S(2)}) collective-permute-start(bf16[2,8,4096]{2,1,0:T(8,128)(2,1)S(1)} %get-tuple-element.52), channel_id=1, source_target_pairs={{0,8},{4,12},{8,0},{12,4},{16,24},{20,28},{24,16},{28,20},{1,9},{5... | collective-permute-start | bytes 393224 | tf_op jit(solution)/shard_map/ppermute | solution.py:284
  11.0 1.4 %collective-permute-start.6 = (bf16[2,8,4096]{2,1,0:T(8,128)(2,1)S(1)}, bf16[2,8,4096]{2,1,0:T(8,128)(2,1)S(1)}, u32[]{:S(2)}, u32[]{:S(2)}) collective-permute-start(bf16[2,8,4096]{2,1,0:T(8,128)(2,1)S(1)} %get-tuple-element.54), channel_id=1, source_target_pairs={{0,16},{4,20},{8,24},{12,28},{16,0},{20,4},{24,8},{28,12},{1,17},{... | collective-permute-start | bytes 393224 | tf_op jit(solution)/shard_map/ppermute | solution.py:284
  12.4 2.4 %collective-permute-start.8 = (bf16[2,8,4096]{2,1,0:T(8,128)(2,1)S(1)}, bf16[2,8,4096]{2,1,0:T(8,128)(2,1)S(1)}, u32[]{:S(2)}, u32[]{:S(2)}) collective-permute-start(bf16[2,8,4096]{2,1,0:T(8,128)(2,1)S(1)} %get-tuple-element.56), channel_id=1, source_target_pairs={{0,24},{4,28},{8,16},{12,20},{16,8},{20,12},{24,0},{28,4},{1,25},{... | collective-permute-start | bytes 393224 | tf_op jit(solution)/shard_map/ppermute | solution.py:284
  14.8 2.6 %collective-permute-start.9 = (bf16[2,8,4096]{2,1,0:T(8,128)(2,1)S(1)}, bf16[2,8,4096]{2,1,0:T(8,128)(2,1)S(1)}, u32[]{:S(2)}, u32[]{:S(2)}) collective-permute-start(bf16[2,8,4096]{2,1,0:T(8,128)(2,1)S(1)} %get-tuple-element.57), channel_id=1, source_target_pairs={{0,24},{4,28},{8,16},{12,20},{16,8},{20,12},{24,0},{28,4},{1,25},{... | collective-permute-start | bytes 393224 | tf_op jit(solution)/shard_map/ppermute | solution.py:284
  17.4 2.3 %beside.1 = (s32[24]{0:T(128)S(1)}, f32[24]{0:T(128)S(1)}, f32[16]{0:T(128)S(1)}, f32[16,8,4096]{2,1,0:T(8,128)S(1)}, f32[16,8,4096]{2,1,0:T(8,128)S(1)}) custom-call(s32[1]{0:T(128)} %bitcast.me_ref, s32[8,16]{1,0:T(8,128)} %ids_ref.5, s32[8,16]{1,0:T(8,128)} %counts_ref.3, ...), custom_call_target="tpu_custom_call", output_to_operand_aliasing={{3}: (6, {}), {4}: (7, {})} | custom-call | flops 1000000 | bytes 12582912 | tf_op jit(solution)/shard_map/beside/pallas_call | solution.py:322
  19.8 3.6 %collective-permute-done.7.rest_4_ = bf16[2,8,4096]{2,1,0:T(8,128)(2,1)S(1)} collective-permute-done((bf16[2,8,4096]{2,1,0:T(8,128)(2,1)S(1)}, bf16[2,8,4096]{2,1,0:T(8,128)(2,1)S(1)}, u32[]{:S(2)}, u32[]{:S(2)}) %collective-permute-start.7) | collective-permute-done | bytes 131104 | tf_op jit(solution)/shard_map/ppermute | solution.py:284
  23.4 1.0 %combine.1 = (f32[16,8,4096]{2,1,0:T(8,128)S(1)}, f32[16,128]{1,0:T(8,128)S(1)}) custom-call(s32[1]{0:T(128)} %bitcast.me_ref, s32[24]{0:T(128)S(1)} %get-tuple-element.47.module_ref, f32[24]{0:T(128)S(1)} %get-tuple-element.49.weight_ref, f32[16]{0:T(128)S(1)} %get-tuple-element.48.total_ref, ...), custom_call_target="tpu_custom_call", output_to_operand_aliasing={{0}: (4, {})} | custom-call | tf_op jit(solution)/shard_map/combine/pallas_call | solution.py:336
  24.4 2.8 %collective-permute-start.10 = (f32[16,128]{1,0:T(8,128)S(1)}, f32[16,128]{1,0:T(8,128)S(1)}, u32[]{:S(2)}, u32[]{:S(2)}) collective-permute-start(f32[16,128]{1,0:T(8,128)S(1)} %get-tuple-element.60.rest_0_), channel_id=1, source_target_pairs={{0,2},{1,3},{2,0},{3,1},{4,6},{5,7},{6,4},{7,5},{8,10},{9,11},{10,... | collective-permute-start | bytes 24584 | tf_op jit(solution)/shard_map/ppermute | solution.py:346
  27.2 1.3 %collective-permute-start.11 = (f32[16,128]{1,0:T(8,128)S(1)}, f32[16,128]{1,0:T(8,128)S(1)}, u32[]{:S(2)}, u32[]{:S(2)}) collective-permute-start(f32[16,128]{1,0:T(8,128)S(1)} %get-tuple-element.60.rest_0_), channel_id=1, source_target_pairs={{0,1},{1,2},{2,3},{3,0},{4,5},{5,6},{6,7},{7,4},{8,9},{9,10},{10,1... | collective-permute-start | bytes 24584 | tf_op jit(solution)/shard_map/ppermute | solution.py:346
  28.5 2.0 %collective-permute-start.12 = (f32[16,128]{1,0:T(8,128)S(1)}, f32[16,128]{1,0:T(8,128)S(1)}, u32[]{:S(2)}, u32[]{:S(2)}) collective-permute-start(f32[16,128]{1,0:T(8,128)S(1)} %get-tuple-element.60.rest_0_), channel_id=1, source_target_pairs={{0,3},{1,0},{2,1},{3,2},{4,7},{5,4},{6,5},{7,6},{8,11},{9,8},{10,9... | collective-permute-start | bytes 24584 | tf_op jit(solution)/shard_map/ppermute | solution.py:346
  30.5 1.0 %collective-permute-done.11.rest_2_ = f32[16,128]{1,0:T(8,128)S(1)} collective-permute-done((f32[16,128]{1,0:T(8,128)S(1)}, f32[16,128]{1,0:T(8,128)S(1)}, u32[]{:S(2)}, u32[]{:S(2)}) %collective-permute-start.11) | collective-permute-done | bytes 8224 | tf_op jit(solution)/shard_map/ppermute | solution.py:346
  31.5 0.9 %send.1 = (f32[16,8,128]{2,1,0:T(8,128)S(1)}, bf16[2,8,4096]{2,1,0:T(8,128)(2,1)S(1)}, bf16[2,8,4096]{2,1,0:T(8,128)(2,1)S(1)}, bf16[2,8,4096]{2,1,0:T(8,128)(2,...) custom-call(s32[1]{0:T(128)} %bitcast.me_ref, ...), custom_call_target="tpu_custom_call" | custom-call | tf_op jit(solution)/shard_map/send/pallas_call | solution.py:349
  32.5 1.3 %collective-permute-start.15 = (bf16[2,8,4096]{2,1,0:T(8,128)(2,1)S(1)}, bf16[2,8,4096]{2,1,0:T(8,128)(2,1)S(1)}, u32[]{:S(2)}, u32[]{:S(2)}) collective-permute-start(bf16[2,8,4096]{2,1,0:T(8,128)(2,1)S(1)} %get-tuple-element.68), channel_id=1, source_target_pairs={{0,8},{4,12},{8,0},{12,4},{16,24},{20,28},{24,16},{28,20},{1,9},{5... | collective-permute-start | bytes 393224 | tf_op jit(solution)/shard_map/ppermute | solution.py:284
  33.7 1.2 %collective-permute-start.18 = (bf16[2,8,4096]{2,1,0:T(8,128)(2,1)S(1)}, bf16[2,8,4096]{2,1,0:T(8,128)(2,1)S(1)}, u32[]{:S(2)}, u32[]{:S(2)}) collective-permute-start(bf16[2,8,4096]{2,1,0:T(8,128)(2,1)S(1)} %get-tuple-element.70), channel_id=1, source_target_pairs={{0,16},{4,20},{8,24},{12,28},{16,0},{20,4},{24,8},{28,12},{1,17},{... | collective-permute-start | bytes 393224 | tf_op jit(solution)/shard_map/ppermute | solution.py:284
  35.2 1.6 %collective-permute-start.13 = (bf16[2,8,4096]{2,1,0:T(8,128)(2,1)S(1)}, bf16[2,8,4096]{2,1,0:T(8,128)(2,1)S(1)}, u32[]{:S(2)}, u32[]{:S(2)}) collective-permute-start(bf16[2,8,4096]{2,1,0:T(8,128)(2,1)S(1)} %get-tuple-element.66), channel_id=1, source_target_pairs={{0,4},{4,0},{8,12},{12,8},{16,20},{20,16},{24,28},{28,24},{1,5},{5... | collective-permute-start | bytes 393224 | tf_op jit(solution)/shard_map/ppermute | solution.py:284
  36.8 1.7 %collective-permute-start.14 = (bf16[2,8,4096]{2,1,0:T(8,128)(2,1)S(1)}, bf16[2,8,4096]{2,1,0:T(8,128)(2,1)S(1)}, u32[]{:S(2)}, u32[]{:S(2)}) collective-permute-start(bf16[2,8,4096]{2,1,0:T(8,128)(2,1)S(1)} %get-tuple-element.67), channel_id=1, source_target_pairs={{0,8},{4,12},{8,0},{12,4},{16,24},{20,28},{24,16},{28,20},{1,9},{5... | collective-permute-start | bytes 393224 | tf_op jit(solution)/shard_map/ppermute | solution.py:284
  38.5 1.2 %collective-permute-start.17 = (bf16[2,8,4096]{2,1,0:T(8,128)(2,1)S(1)}, bf16[2,8,4096]{2,1,0:T(8,128)(2,1)S(1)}, u32[]{:S(2)}, u32[]{:S(2)}) collective-permute-start(bf16[2,8,4096]{2,1,0:T(8,128)(2,1)S(1)} %get-tuple-element.69), channel_id=1, source_target_pairs={{0,16},{4,20},{8,24},{12,28},{16,0},{20,4},{24,8},{28,12},{1,17},{... | collective-permute-start | bytes 393224 | tf_op jit(solution)/shard_map/ppermute | solution.py:284
  39.7 0.7 %collective-permute-done.21 = bf16[2,8,4096]{2,1,0:T(8,128)(2,1)S(1)} collective-permute-done((bf16[2,8,4096]{2,1,0:T(8,128)(2,1)S(1)}, bf16[2,8,4096]{2,1,0:T(8,128)(2,1)S(1)}, u32[]{:S(2)}, u32[]{:S(2)}) %collective-permute-start.21) | collective-permute-done | bytes 131104 | tf_op jit(solution)/shard_map/ppermute | solution.py:284
  40.4 3.5 %collective-permute-start.16 = (bf16[2,8,4096]{2,1,0:T(8,128)(2,1)S(1)}, bf16[2,8,4096]{2,1,0:T(8,128)(2,1)S(1)}, u32[]{:S(2)}, u32[]{:S(2)}) collective-permute-start(bf16[2,8,4096]{2,1,0:T(8,128)(2,1)S(1)} %collective-permute-done.15), channel_id=1, source_target_pairs={{0,4},{4,0},{8,12},{12,8},{16,20},{20,16},{24,28},{28,24},{1,5},{5... | collective-permute-start | bytes 393224 | tf_op jit(solution)/shard_map/ppermute | solution.py:284
  44.0 1.7 %collective-permute-start.22 = (bf16[2,8,4096]{2,1,0:T(8,128)(2,1)S(1)}, bf16[2,8,4096]{2,1,0:T(8,128)(2,1)S(1)}, u32[]{:S(2)}, u32[]{:S(2)}) collective-permute-start(bf16[2,8,4096]{2,1,0:T(8,128)(2,1)S(1)} %collective-permute-done.21), channel_id=1, source_target_pairs={{0,4},{4,0},{8,12},{12,8},{16,20},{20,16},{24,28},{28,24},{1,5},{5... | collective-permute-start | bytes 393224 | tf_op jit(solution)/shard_map/ppermute | solution.py:284
  45.7 2.5 %store.1 = (f32[16,8,4096]{2,1,0:T(8,128)}, f32[16,8,4096]{2,1,0:T(8,128)}) custom-call(f32[16,8,128]{2,1,0:T(8,128)S(1)} %get-tuple-element.61.scale_ref, f32[16,8,4096]{2,1,0:T(8,128)S(1)} %get-tuple-element.58.acc_ref, f32[16,8,4096]{2,1,0:T(8,128)S(1)} %get-tuple-element.59.base_ref, f32[16,8,4096]{2,1,0:T(8,128)S(1)} %copy-done), custom_call_target="tpu_custom_call" | custom-call | flops 1000000 | bytes 12582912 | tf_op jit(solution)/shard_map/store/pallas_call | solution.py:364
  48.3 1.8 %unpack.1 = bf16[1,16,8,4096]{3,2,1,0:T(8,128)(2,1)} custom-call(s32[1]{0:T(128)} %bitcast.me_ref, s32[16]{0:T(128)} %get-tuple-element.64.places_ref, bf16[2,8,4096]{2,1,0:T(8,128)(2,1)S(1)} %get-tuple-element.65.rest_0_, bf16[2,8,4096]{2,1,0:T(8,128)(2,1)S(1)} %collective-permute-done.13.rest_1_, bf16[2,8,4096]{2,1,0:T(8,128)(2,1)S(1)} %collective-permute-done.14.rest_2_, ...), custom_call_target="tpu_custom_call" | custom-call | tf_op jit(solution)/shard_map/unpack/pallas_call | solution.py:374
  (31 shorter events, 2.3 us)
Async XLA Ops:
  3.4 1.4 %collective-permute-start = (bf16[2,8,4096]{2,1,0:T(8,128)(2,1)S(1)}, bf16[2,8,4096]{2,1,0:T(8,128)(2,1)S(1)}, u32[]{:S(2)}, u32[]{:S(2)}) collective-permute-start(bf16[2,8,4096]{2,1,0:T(8,128)(2,1)S(1)} %get-tuple-element.42), channel_id=1, source_target_pairs={{0,4},{4,0},{8,12},{12,8},{16,20},{20,16},{24,28},{28,24},{1,5},{5... | collective-permute-start | bytes 393224 | tf_op jit(solution)/shard_map/ppermute | solution.py:284
  3.5 1.5 %collective-permute-start.1 = (bf16[2,8,4096]{2,1,0:T(8,128)(2,1)S(1)}, bf16[2,8,4096]{2,1,0:T(8,128)(2,1)S(1)}, u32[]{:S(2)}, u32[]{:S(2)}) collective-permute-start(bf16[2,8,4096]{2,1,0:T(8,128)(2,1)S(1)} %get-tuple-element.43), channel_id=1, source_target_pairs={{0,4},{4,0},{8,12},{12,8},{16,20},{20,16},{24,28},{28,24},{1,5},{5... | collective-permute-start | bytes 393224 | tf_op jit(solution)/shard_map/ppermute | solution.py:284
  3.9 1.3 %collective-permute-start.2 = (bf16[2,8,4096]{2,1,0:T(8,128)(2,1)S(1)}, bf16[2,8,4096]{2,1,0:T(8,128)(2,1)S(1)}, u32[]{:S(2)}, u32[]{:S(2)}) collective-permute-start(bf16[2,8,4096]{2,1,0:T(8,128)(2,1)S(1)} %get-tuple-element.44), channel_id=1, source_target_pairs={{0,4},{4,0},{8,12},{12,8},{16,20},{20,16},{24,28},{28,24},{1,5},{5... | collective-permute-start | bytes 393224 | tf_op jit(solution)/shard_map/ppermute | solution.py:284
  4.0 8.4 %collective-permute-start.3 = (bf16[2,8,4096]{2,1,0:T(8,128)(2,1)S(1)}, bf16[2,8,4096]{2,1,0:T(8,128)(2,1)S(1)}, u32[]{:S(2)}, u32[]{:S(2)}) collective-permute-start(bf16[2,8,4096]{2,1,0:T(8,128)(2,1)S(1)} %get-tuple-element.51), channel_id=1, source_target_pairs={{0,4},{4,0},{8,12},{12,8},{16,20},{20,16},{24,28},{28,24},{1,5},{5... | collective-permute-start | bytes 393224 | tf_op jit(solution)/shard_map/ppermute | solution.py:284
  8.4 6.4 %collective-permute-start.4 = (bf16[2,8,4096]{2,1,0:T(8,128)(2,1)S(1)}, bf16[2,8,4096]{2,1,0:T(8,128)(2,1)S(1)}, u32[]{:S(2)}, u32[]{:S(2)}) collective-permute-start(bf16[2,8,4096]{2,1,0:T(8,128)(2,1)S(1)} %get-tuple-element.52), channel_id=1, source_target_pairs={{0,8},{4,12},{8,0},{12,4},{16,24},{20,28},{24,16},{28,20},{1,9},{5... | collective-permute-start | bytes 393224 | tf_op jit(solution)/shard_map/ppermute | solution.py:284
  10.9 8.9 %collective-permute-start.5 = (bf16[2,8,4096]{2,1,0:T(8,128)(2,1)S(1)}, bf16[2,8,4096]{2,1,0:T(8,128)(2,1)S(1)}, u32[]{:S(2)}, u32[]{:S(2)}) collective-permute-start(bf16[2,8,4096]{2,1,0:T(8,128)(2,1)S(1)} %get-tuple-element.53), channel_id=1, source_target_pairs={{0,8},{4,12},{8,0},{12,4},{16,24},{20,28},{24,16},{28,20},{1,9},{5... | collective-permute-start | bytes 393224 | tf_op jit(solution)/shard_map/ppermute | solution.py:284
  11.0 8.8 %collective-permute-start.6 = (bf16[2,8,4096]{2,1,0:T(8,128)(2,1)S(1)}, bf16[2,8,4096]{2,1,0:T(8,128)(2,1)S(1)}, u32[]{:S(2)}, u32[]{:S(2)}) collective-permute-start(bf16[2,8,4096]{2,1,0:T(8,128)(2,1)S(1)} %get-tuple-element.54), channel_id=1, source_target_pairs={{0,16},{4,20},{8,24},{12,28},{16,0},{20,4},{24,8},{28,12},{1,17},{... | collective-permute-start | bytes 393224 | tf_op jit(solution)/shard_map/ppermute | solution.py:284
  12.4 11.0 %collective-permute-start.7 = (bf16[2,8,4096]{2,1,0:T(8,128)(2,1)S(1)}, bf16[2,8,4096]{2,1,0:T(8,128)(2,1)S(1)}, u32[]{:S(2)}, u32[]{:S(2)}) collective-permute-start(bf16[2,8,4096]{2,1,0:T(8,128)(2,1)S(1)} %get-tuple-element.55), channel_id=1, source_target_pairs={{0,16},{4,20},{8,24},{12,28},{16,0},{20,4},{24,8},{28,12},{1,17},{... | collective-permute-start | bytes 393224 | tf_op jit(solution)/shard_map/ppermute | solution.py:284
  12.4 11.0 %collective-permute-start.8 = (bf16[2,8,4096]{2,1,0:T(8,128)(2,1)S(1)}, bf16[2,8,4096]{2,1,0:T(8,128)(2,1)S(1)}, u32[]{:S(2)}, u32[]{:S(2)}) collective-permute-start(bf16[2,8,4096]{2,1,0:T(8,128)(2,1)S(1)} %get-tuple-element.56), channel_id=1, source_target_pairs={{0,24},{4,28},{8,16},{12,20},{16,8},{20,12},{24,0},{28,4},{1,25},{... | collective-permute-start | bytes 393224 | tf_op jit(solution)/shard_map/ppermute | solution.py:284
  14.8 8.6 %collective-permute-start.9 = (bf16[2,8,4096]{2,1,0:T(8,128)(2,1)S(1)}, bf16[2,8,4096]{2,1,0:T(8,128)(2,1)S(1)}, u32[]{:S(2)}, u32[]{:S(2)}) collective-permute-start(bf16[2,8,4096]{2,1,0:T(8,128)(2,1)S(1)} %get-tuple-element.57), channel_id=1, source_target_pairs={{0,24},{4,28},{8,16},{12,20},{16,8},{20,12},{24,0},{28,4},{1,25},{... | collective-permute-start | bytes 393224 | tf_op jit(solution)/shard_map/ppermute | solution.py:284
  24.4 6.1 %collective-permute-start.10 = (f32[16,128]{1,0:T(8,128)S(1)}, f32[16,128]{1,0:T(8,128)S(1)}, u32[]{:S(2)}, u32[]{:S(2)}) collective-permute-start(f32[16,128]{1,0:T(8,128)S(1)} %get-tuple-element.60.rest_0_), channel_id=1, source_target_pairs={{0,2},{1,3},{2,0},{3,1},{4,6},{5,7},{6,4},{7,5},{8,10},{9,11},{10,... | collective-permute-start | bytes 24584 | tf_op jit(solution)/shard_map/ppermute | solution.py:346
  27.2 4.3 %collective-permute-start.11 = (f32[16,128]{1,0:T(8,128)S(1)}, f32[16,128]{1,0:T(8,128)S(1)}, u32[]{:S(2)}, u32[]{:S(2)}) collective-permute-start(f32[16,128]{1,0:T(8,128)S(1)} %get-tuple-element.60.rest_0_), channel_id=1, source_target_pairs={{0,1},{1,2},{2,3},{3,0},{4,5},{5,6},{6,7},{7,4},{8,9},{9,10},{10,1... | collective-permute-start | bytes 24584 | tf_op jit(solution)/shard_map/ppermute | solution.py:346
  28.5 3.0 %collective-permute-start.12 = (f32[16,128]{1,0:T(8,128)S(1)}, f32[16,128]{1,0:T(8,128)S(1)}, u32[]{:S(2)}, u32[]{:S(2)}) collective-permute-start(f32[16,128]{1,0:T(8,128)S(1)} %get-tuple-element.60.rest_0_), channel_id=1, source_target_pairs={{0,3},{1,0},{2,1},{3,2},{4,7},{5,4},{6,5},{7,6},{8,11},{9,8},{10,9... | collective-permute-start | bytes 24584 | tf_op jit(solution)/shard_map/ppermute | solution.py:346
  31.5 14.2 %copy-start = (f32[16,8,4096]{2,1,0:T(8,128)S(1)}, f32[16,8,4096]{2,1,0:T(8,128)}, u32[]{:S(2)}) copy-start(f32[16,8,4096]{2,1,0:T(8,128)} %past_ref.1) | copy-start | bytes 6291460
  32.5 6.0 %collective-permute-start.15 = (bf16[2,8,4096]{2,1,0:T(8,128)(2,1)S(1)}, bf16[2,8,4096]{2,1,0:T(8,128)(2,1)S(1)}, u32[]{:S(2)}, u32[]{:S(2)}) collective-permute-start(bf16[2,8,4096]{2,1,0:T(8,128)(2,1)S(1)} %get-tuple-element.68), channel_id=1, source_target_pairs={{0,8},{4,12},{8,0},{12,4},{16,24},{20,28},{24,16},{28,20},{1,9},{5... | collective-permute-start | bytes 393224 | tf_op jit(solution)/shard_map/ppermute | solution.py:284
  33.7 6.0 %collective-permute-start.18 = (bf16[2,8,4096]{2,1,0:T(8,128)(2,1)S(1)}, bf16[2,8,4096]{2,1,0:T(8,128)(2,1)S(1)}, u32[]{:S(2)}, u32[]{:S(2)}) collective-permute-start(bf16[2,8,4096]{2,1,0:T(8,128)(2,1)S(1)} %get-tuple-element.70), channel_id=1, source_target_pairs={{0,16},{4,20},{8,24},{12,28},{16,0},{20,4},{24,8},{28,12},{1,17},{... | collective-permute-start | bytes 393224 | tf_op jit(solution)/shard_map/ppermute | solution.py:284
  35.0 5.5 %collective-permute-start.21 = (bf16[2,8,4096]{2,1,0:T(8,128)(2,1)S(1)}, bf16[2,8,4096]{2,1,0:T(8,128)(2,1)S(1)}, u32[]{:S(2)}, u32[]{:S(2)}) collective-permute-start(bf16[2,8,4096]{2,1,0:T(8,128)(2,1)S(1)} %get-tuple-element.72), channel_id=1, source_target_pairs={{0,24},{4,28},{8,16},{12,20},{16,8},{20,12},{24,0},{28,4},{1,25},{... | collective-permute-start | bytes 393224 | tf_op jit(solution)/shard_map/ppermute | solution.py:284
  35.2 8.8 %collective-permute-start.13 = (bf16[2,8,4096]{2,1,0:T(8,128)(2,1)S(1)}, bf16[2,8,4096]{2,1,0:T(8,128)(2,1)S(1)}, u32[]{:S(2)}, u32[]{:S(2)}) collective-permute-start(bf16[2,8,4096]{2,1,0:T(8,128)(2,1)S(1)} %get-tuple-element.66), channel_id=1, source_target_pairs={{0,4},{4,0},{8,12},{12,8},{16,20},{20,16},{24,28},{28,24},{1,5},{5... | collective-permute-start | bytes 393224 | tf_op jit(solution)/shard_map/ppermute | solution.py:284
  36.8 7.2 %collective-permute-start.14 = (bf16[2,8,4096]{2,1,0:T(8,128)(2,1)S(1)}, bf16[2,8,4096]{2,1,0:T(8,128)(2,1)S(1)}, u32[]{:S(2)}, u32[]{:S(2)}) collective-permute-start(bf16[2,8,4096]{2,1,0:T(8,128)(2,1)S(1)} %get-tuple-element.67), channel_id=1, source_target_pairs={{0,8},{4,12},{8,0},{12,4},{16,24},{20,28},{24,16},{28,20},{1,9},{5... | collective-permute-start | bytes 393224 | tf_op jit(solution)/shard_map/ppermute | solution.py:284
  38.5 9.8 %collective-permute-start.17 = (bf16[2,8,4096]{2,1,0:T(8,128)(2,1)S(1)}, bf16[2,8,4096]{2,1,0:T(8,128)(2,1)S(1)}, u32[]{:S(2)}, u32[]{:S(2)}) collective-permute-start(bf16[2,8,4096]{2,1,0:T(8,128)(2,1)S(1)} %get-tuple-element.69), channel_id=1, source_target_pairs={{0,16},{4,20},{8,24},{12,28},{16,0},{20,4},{24,8},{28,12},{1,17},{... | collective-permute-start | bytes 393224 | tf_op jit(solution)/shard_map/ppermute | solution.py:284
  39.7 8.6 %collective-permute-start.20 = (bf16[2,8,4096]{2,1,0:T(8,128)(2,1)S(1)}, bf16[2,8,4096]{2,1,0:T(8,128)(2,1)S(1)}, u32[]{:S(2)}, u32[]{:S(2)}) collective-permute-start(bf16[2,8,4096]{2,1,0:T(8,128)(2,1)S(1)} %get-tuple-element.71), channel_id=1, source_target_pairs={{0,24},{4,28},{8,16},{12,20},{16,8},{20,12},{24,0},{28,4},{1,25},{... | collective-permute-start | bytes 393224 | tf_op jit(solution)/shard_map/ppermute | solution.py:284
  40.4 7.8 %collective-permute-start.16 = (bf16[2,8,4096]{2,1,0:T(8,128)(2,1)S(1)}, bf16[2,8,4096]{2,1,0:T(8,128)(2,1)S(1)}, u32[]{:S(2)}, u32[]{:S(2)}) collective-permute-start(bf16[2,8,4096]{2,1,0:T(8,128)(2,1)S(1)} %collective-permute-done.15), channel_id=1, source_target_pairs={{0,4},{4,0},{8,12},{12,8},{16,20},{20,16},{24,28},{28,24},{1,5},{5... | collective-permute-start | bytes 393224 | tf_op jit(solution)/shard_map/ppermute | solution.py:284
  44.0 4.3 %collective-permute-start.19 = (bf16[2,8,4096]{2,1,0:T(8,128)(2,1)S(1)}, bf16[2,8,4096]{2,1,0:T(8,128)(2,1)S(1)}, u32[]{:S(2)}, u32[]{:S(2)}) collective-permute-start(bf16[2,8,4096]{2,1,0:T(8,128)(2,1)S(1)} %collective-permute-done.18), channel_id=1, source_target_pairs={{0,4},{4,0},{8,12},{12,8},{16,20},{20,16},{24,28},{28,24},{1,5},{5... | collective-permute-start | bytes 393224 | tf_op jit(solution)/shard_map/ppermute | solution.py:284
  44.0 4.3 %collective-permute-start.22 = (bf16[2,8,4096]{2,1,0:T(8,128)(2,1)S(1)}, bf16[2,8,4096]{2,1,0:T(8,128)(2,1)S(1)}, u32[]{:S(2)}, u32[]{:S(2)}) collective-permute-start(bf16[2,8,4096]{2,1,0:T(8,128)(2,1)S(1)} %collective-permute-done.21), channel_id=1, source_target_pairs={{0,4},{4,0},{8,12},{12,8},{16,20},{20,16},{24,28},{28,24},{1,5},{5... | collective-permute-start | bytes 393224 | tf_op jit(solution)/shard_map/ppermute | solution.py:284

commit v4 on v3

--- a/solution.py
+++ b/solution.py
@@ -126,38 +126,16 @@
     subtract(me, [own_ref], [0], module_ref, weight_ref, acc_ref)
 
 
-def before_kernel(me_ref, ids_ref, counts_ref, own_ref, params_hbm, past_hbm, *rest):
-    acc_ref, base_ref, *_, module_ref, weight_ref, total_ref, params_ref, past_ref, sems = rest[
-        (len(rest) - 8) // 2 :
-    ]
-    me = me_ref[0]
-    tables = module_ref, weight_ref, total_ref
-
-    @pl.when(lax.rem(me, 2) == 1)
-    def _():
-        find = functools.partial(find_slots, me, acc_ref.shape[0], ids_ref, counts_ref, *tables)
-        prepare(
-            me, own_ref, params_hbm, past_hbm, tables, acc_ref, base_ref, params_ref, past_ref, sems, find
-        )
-
-
-def beside_kernel(
-    me_ref, ids_ref, counts_ref, own_ref, params_hbm, past_hbm, _acc, _base,
+def early_kernel(
+    me_ref, ids_ref, counts_ref, own_ref, params_hbm, past_hbm,
     module_ref, weight_ref, total_ref, acc_ref, base_ref, params_ref, past_ref, sems,
 ):
     me = me_ref[0]
     tables = module_ref, weight_ref, total_ref
     find = functools.partial(find_slots, me, acc_ref.shape[0], ids_ref, counts_ref, *tables)
-
-    @pl.when(lax.rem(me, 2) == 1)
-    def _():
-        find()
-
-    @pl.when(lax.rem(me, 2) == 0)
-    def _():
-        prepare(
-            me, own_ref, params_hbm, past_hbm, tables, acc_ref, base_ref, params_ref, past_ref, sems, find
-        )
+    prepare(
+        me, own_ref, params_hbm, past_hbm, tables, acc_ref, base_ref, params_ref, past_ref, sems, find
+    )
 
 
 def combine_kernel(paths, me_ref, module_ref, weight_ref, total_ref, acc_in, *rest):
@@ -278,14 +256,16 @@
         pltpu.SemaphoreType.DMA((2, PARTS)),
     ]
     limits = pltpu.CompilerParams(vmem_limit_bytes=24 * 1024 * 1024)
-    far = sorted(range(2, paths, 2), key=lambda d: (-d.bit_count(), d))
-
-    def to(x, d):
-        return lax.ppermute(x, "path", [(i, i ^ d) for i in range(paths)])
-
-    order = [d ^ 1 for d in far] + far + [1, 0]
+    order = sorted(range(1, paths), key=lambda d: (-(d // 2).bit_count(), d % 2, d))
+
+    def exchange(pieces):
+        moved = {
+            d: lax.ppermute(pieces[d], "path", [(i, i ^ d) for i in range(paths)]) for d in order
+        }
+        return [moved[d] for d in range(1, paths)]
+
     places, *packed = pl.pallas_call(
-        functools.partial(pack_kernel, paths, owned, order),
+        functools.partial(pack_kernel, paths, owned, [*order, 0]),
         out_shape=[jax.ShapeDtypeStruct((slots,), jnp.int32)] + [piece] * paths,
         in_specs=[SMEM, SMEM, ANY],
         out_specs=[SMEM] + [VMEM] * paths,
@@ -293,46 +273,17 @@
         name="pack",
     )(me, module_ids, *in_hbm(path_params.reshape(held, rows, width)))
 
-    through = [packed[d] for d in far] + [to(packed[d ^ 1], 1) for d in far]
-    fixed = 6
-    acc, base, *passed = pl.pallas_call(
-        before_kernel,
-        out_shape=[held_module] * 2 + [piece] * len(through),
-        in_specs=[SMEM] * 3 + [VMEM] + [ANY] * 2 + [VMEM] * len(through),
-        out_specs=[VMEM] * (2 + len(through)),
-        input_output_aliases={fixed + i: 2 + i for i in range(len(through))},
-        scratch_shapes=[
-            pltpu.SMEM(tables[0].shape, jnp.int32),
-            pltpu.SMEM(tables[1].shape, jnp.float32),
-            pltpu.SMEM(tables[2].shape, jnp.float32),
-        ]
-        + room,
-        compiler_params=limits,
-        name="before",
-    )(
-        me, module_ids, counts, *in_vmem(packed[0]), *in_hbm(global_params, momentum),
-        *in_vmem(*through),
-    )
-    arrived = {}
-    for d, x in zip(far, passed[: len(far)], strict=True):
-        arrived[d] = to(x, d)
-    for d, x in zip(far, passed[len(far) :], strict=True):
-        arrived[d ^ 1] = to(x, d)
-    arrived[1] = to(packed[1], 1)
+    arrived = exchange(packed)
     table, weights, total, acc, base = pl.pallas_call(
-        beside_kernel,
+        early_kernel,
         out_shape=tables + [held_module] * 2,
-        in_specs=[SMEM] * 3 + [VMEM] + [ANY] * 2 + [VMEM] * 2,
+        in_specs=[SMEM] * 3 + [VMEM] + [ANY] * 2,
         out_specs=[SMEM] * 3 + [VMEM] * 2,
-        input_output_aliases={fixed: 3, fixed + 1: 4},
         scratch_shapes=room,
         compiler_params=limits,
         cost_estimate=pl.CostEstimate(flops=10**6, bytes_accessed=12 * 2**20, transcendentals=0),
-        name="beside",
-    )(
-        me, module_ids, counts, *in_vmem(packed[0]), *in_hbm(global_params, momentum),
-        *in_vmem(acc, base),
-    )
+        name="early",
+    )(me, module_ids, counts, *in_vmem(packed[0]), *in_hbm(global_params, momentum))
     acc, squares = pl.pallas_call(
         functools.partial(combine_kernel, paths),
         out_shape=[held_module, jax.ShapeDtypeStruct((owned, 128), jnp.float32)],
@@ -341,7 +292,7 @@
         input_output_aliases={4: 0},
         compiler_params=limits,
         name="combine",
-    )(me, table, weights, total, *in_vmem(acc, *[arrived[d] for d in range(1, paths)]))
+    )(me, table, weights, total, *in_vmem(acc, *arrived))
     parts = [squares] + [
         lax.ppermute(squares, "shard", [(i, (i + d) % shards) for i in range(shards)])
         for d in sorted(range(1, shards), key=lambda d: (d != 2, d))
@@ -354,13 +305,7 @@
         compiler_params=limits,
         name="send",
     )(me, table, total, *in_vmem(acc, base), *parts)
-    relayed = {d: to(outgoing[d ^ 1], d) for d in far}
-    returned = {0: outgoing[0]}
-    for d in far:
-        returned[d] = to(outgoing[d], d)
-    returned[1] = to(outgoing[1], 1)
-    for d in far:
-        returned[d ^ 1] = to(relayed[d], 1)
+    returned = [outgoing[0], *exchange(outgoing)]
     updated, velocity = pl.pallas_call(
         store_kernel,
         out_shape=[module] * 2,
@@ -378,7 +323,7 @@
         out_specs=ANY,
         scratch_shapes=[pltpu.SemaphoreType.DMA((slots,))],
         name="unpack",
-    )(me, places, *in_vmem(*[returned[d] for d in range(paths)]))
+    )(me, places, *in_vmem(*returned))
     return updated, velocity, path_out
 
 

time: 50.7 us -> 48 us (0.947)
  starting transfers between devices: 28.7 us -> 25.9 us
  waiting for transfers between devices: 6.24 us -> 8.42 us
  Pallas kernels: 14.4 us -> 12.6 us
    ppermute x20 -> x14, starting transfers between devices: 22.6 us -> 20.1 us  [exchange(): lax.ppermute(pieces[d], 'path', [(i, i ^ d) for i in range(paths)])]
    ppermute x20 -> x14, waiting for transfers between devices: 5.2 us -> 7.39 us  [exchange(): lax.ppermute(pieces[d], 'path', [(i, i ^ d) for i in range(paths)])]
    pallas_call x3 -> x2, Pallas kernels: 8.2 us -> 6.42 us  [the longest x1 3.7 us: on_device(): pl.pallas_call(early_kernel, out_shape=tables + [held_module] * 2, in_spe...]
  transfers between devices with their start and end apart: 23 -> 17, of which waited for: 6 -> 3; matrix products, arithmetic and copies ran while one was open for 0% -> 0% of each run, Pallas kernels for 16% -> 13%
where the time goes in v4:
time: 48 us; the launch traced here: 47.6 us
  starting transfers between devices  25.9 us (54%)
  Pallas kernels  12.6 us (26%)
  waiting for transfers between devices  8.42 us (18%)
  between operations  0.71 us (1%)
    ppermute x14, starting transfers between devices, exchange(): lax.ppermute(pieces[d], 'path', [(i, i ^ d) for i in range(paths)])  20.1 us
    ppermute x14, waiting for transfers between devices, exchange(): lax.ppermute(pieces[d], 'path', [(i, i ^ d) for i in range(paths)])  7.39 us
    ppermute x3, starting transfers between devices, on_device(): lax.ppermute(squares, 'shard', [(i, (i + d) % shards) for i in range(shar...  5.86 us
    pallas_call x1, Pallas kernels, on_device(): pl.pallas_call(early_kernel, out_shape=tables + [held_module] * 2, in_spe...  3.7 us
    pallas_call x1, Pallas kernels, on_device(): pl.pallas_call(functools.partial(pack_kernel, paths, owned, [*order, 0]),...  2.72 us
    pallas_call x1, Pallas kernels, on_device(): pl.pallas_call(store_kernel, out_shape=[module] * 2, in_specs=[VMEM] * 4,...  2.52 us
    pallas_call x1, Pallas kernels, on_device(): pl.pallas_call(functools.partial(unpack_kernel, paths), out_shape=jax.Sha...  1.76 us
    ppermute x3, waiting for transfers between devices, on_device(): lax.ppermute(squares, 'shard', [(i, (i + d) % shards) for i in range(shar...  1.04 us
  transfers between devices with their start and end apart: 17, of which 3 were waited for; matrix products, arithmetic and copies ran while one was open for 0% of the time, Pallas kernels for 13%

profile of v4, /device:TPU:1, one launch (start us, length us, event | category | flops | bytes accessed | tf_op | source)
XLA Modules:
  0.0 47.6 jit_solution(3871813124485567585)
XLA Ops:
  0.6 2.7 %pack.1 = (s32[16]{0:T(128)}, bf16[2,8,4096]{2,1,0:T(8,128)(2,1)S(1)}, bf16[2,8,4096]{2,1,0:T(8,128)(2,1)S(1)}, bf16[2,8,4096]{2,1,0:T(8,128)(2,1)S(1)}, bf16[2,...) custom-call(s32[1]{0:T(128)} %bitcast.me_ref, ...), custom_call_target="tpu_custom_call" | custom-call | tf_op jit(solution)/shard_map/pack/pallas_call | solution.py:267
  3.5 2.7 %collective-permute-start.1 = (bf16[2,8,4096]{2,1,0:T(8,128)(2,1)S(1)}, bf16[2,8,4096]{2,1,0:T(8,128)(2,1)S(1)}, u32[]{:S(2)}, u32[]{:S(2)}) collective-permute-start(bf16[2,8,4096]{2,1,0:T(8,128)(2,1)S(1)} %get-tuple-element.36), channel_id=1, source_target_pairs={{0,8},{4,12},{8,0},{12,4},{16,24},{20,28},{24,16},{28,20},{1,9},{5... | collective-permute-start | bytes 393224 | tf_op jit(solution)/shard_map/ppermute | solution.py:263
  6.2 1.7 %collective-permute-start.3 = (bf16[2,8,4096]{2,1,0:T(8,128)(2,1)S(1)}, bf16[2,8,4096]{2,1,0:T(8,128)(2,1)S(1)}, u32[]{:S(2)}, u32[]{:S(2)}) collective-permute-start(bf16[2,8,4096]{2,1,0:T(8,128)(2,1)S(1)} %get-tuple-element.38), channel_id=1, source_target_pairs={{0,16},{4,20},{8,24},{12,28},{16,0},{20,4},{24,8},{28,12},{1,17},{... | collective-permute-start | bytes 393224 | tf_op jit(solution)/shard_map/ppermute | solution.py:263
  7.9 0.3 collective-permute-start.4
  8.2 2.4 %collective-permute-start.5 = (bf16[2,8,4096]{2,1,0:T(8,128)(2,1)S(1)}, bf16[2,8,4096]{2,1,0:T(8,128)(2,1)S(1)}, u32[]{:S(2)}, u32[]{:S(2)}) collective-permute-start(bf16[2,8,4096]{2,1,0:T(8,128)(2,1)S(1)} %get-tuple-element.40), channel_id=1, source_target_pairs={{0,24},{4,28},{8,16},{12,20},{16,8},{20,12},{24,0},{28,4},{1,25},{... | collective-permute-start | bytes 393224 | tf_op jit(solution)/shard_map/ppermute | solution.py:263
  10.6 2.7 %collective-permute-start.6 = (bf16[2,8,4096]{2,1,0:T(8,128)(2,1)S(1)}, bf16[2,8,4096]{2,1,0:T(8,128)(2,1)S(1)}, u32[]{:S(2)}, u32[]{:S(2)}) collective-permute-start(bf16[2,8,4096]{2,1,0:T(8,128)(2,1)S(1)} %get-tuple-element.41), channel_id=1, source_target_pairs={{0,28},{4,24},{8,20},{12,16},{16,12},{20,8},{24,4},{28,0},{1,29},{... | collective-permute-start | bytes 393224 | tf_op jit(solution)/shard_map/ppermute | solution.py:263
  13.4 3.7 %early.1 = (s32[24]{0:T(128)S(1)}, f32[24]{0:T(128)S(1)}, f32[16]{0:T(128)S(1)}, f32[16,8,4096]{2,1,0:T(8,128)S(1)}, f32[16,8,4096]{2,1,0:T(8,128)S(1)}) custom-call(s32[1]{0:T(128)} %bitcast.me_ref, s32[8,16]{1,0:T(8,128)} %ids_ref.3, s32[8,16]{1,0:T(8,128)} %counts_ref.1, bf16[2,8,4096]{2,1,0:T(8,128)(2,1)S(1)} %get-tuple-element.30.own_ref, ...), custom_call_target="tpu_custom_call" | custom-call | flops 1000000 | bytes 12582912 | tf_op jit(solution)/shard_map/early/pallas_call | solution.py:277
  17.1 3.0 %collective-permute-done.4.rest_4_ = bf16[2,8,4096]{2,1,0:T(8,128)(2,1)S(1)} collective-permute-done((bf16[2,8,4096]{2,1,0:T(8,128)(2,1)S(1)}, bf16[2,8,4096]{2,1,0:T(8,128)(2,1)S(1)}, u32[]{:S(2)}, u32[]{:S(2)}) %collective-permute-start.4) | collective-permute-done | bytes 131104 | tf_op jit(solution)/shard_map/ppermute | solution.py:263
  20.1 1.0 %combine.1 = (f32[16,8,4096]{2,1,0:T(8,128)S(1)}, f32[16,128]{1,0:T(8,128)S(1)}) custom-call(s32[1]{0:T(128)} %bitcast.me_ref, s32[24]{0:T(128)S(1)} %get-tuple-element.31.module_ref, f32[24]{0:T(128)S(1)} %get-tuple-element.33.weight_ref, f32[16]{0:T(128)S(1)} %get-tuple-element.32.total_ref, ...), custom_call_target="tpu_custom_call", output_to_operand_aliasing={{0}: (4, {})} | custom-call | tf_op jit(solution)/shard_map/combine/pallas_call | solution.py:287
  21.1 2.6 %collective-permute-start.7 = (f32[16,128]{1,0:T(8,128)S(1)}, f32[16,128]{1,0:T(8,128)S(1)}, u32[]{:S(2)}, u32[]{:S(2)}) collective-permute-start(f32[16,128]{1,0:T(8,128)S(1)} %get-tuple-element.44.rest_0_), channel_id=1, source_target_pairs={{0,2},{1,3},{2,0},{3,1},{4,6},{5,7},{6,4},{7,5},{8,10},{9,11},{10,... | collective-permute-start | bytes 24584 | tf_op jit(solution)/shard_map/ppermute | solution.py:297
  23.7 1.3 %collective-permute-start.8 = (f32[16,128]{1,0:T(8,128)S(1)}, f32[16,128]{1,0:T(8,128)S(1)}, u32[]{:S(2)}, u32[]{:S(2)}) collective-permute-start(f32[16,128]{1,0:T(8,128)S(1)} %get-tuple-element.44.rest_0_), channel_id=1, source_target_pairs={{0,1},{1,2},{2,3},{3,0},{4,5},{5,6},{6,7},{7,4},{8,9},{9,10},{10,1... | collective-permute-start | bytes 24584 | tf_op jit(solution)/shard_map/ppermute | solution.py:297
  25.0 2.0 %collective-permute-start.9 = (f32[16,128]{1,0:T(8,128)S(1)}, f32[16,128]{1,0:T(8,128)S(1)}, u32[]{:S(2)}, u32[]{:S(2)}) collective-permute-start(f32[16,128]{1,0:T(8,128)S(1)} %get-tuple-element.44.rest_0_), channel_id=1, source_target_pairs={{0,3},{1,0},{2,1},{3,2},{4,7},{5,4},{6,5},{7,6},{8,11},{9,8},{10,9... | collective-permute-start | bytes 24584 | tf_op jit(solution)/shard_map/ppermute | solution.py:297
  26.9 1.0 %collective-permute-done.8.rest_2_ = f32[16,128]{1,0:T(8,128)S(1)} collective-permute-done((f32[16,128]{1,0:T(8,128)S(1)}, f32[16,128]{1,0:T(8,128)S(1)}, u32[]{:S(2)}, u32[]{:S(2)}) %collective-permute-start.8) | collective-permute-done | bytes 8224 | tf_op jit(solution)/shard_map/ppermute | solution.py:297
  28.0 0.9 %send.1 = (f32[16,8,128]{2,1,0:T(8,128)S(1)}, bf16[2,8,4096]{2,1,0:T(8,128)(2,1)S(1)}, bf16[2,8,4096]{2,1,0:T(8,128)(2,1)S(1)}, bf16[2,8,4096]{2,1,0:T(8,128)(2,...) custom-call(s32[1]{0:T(128)} %bitcast.me_ref, ...), custom_call_target="tpu_custom_call" | custom-call | tf_op jit(solution)/shard_map/send/pallas_call | solution.py:300
  28.9 1.6 %collective-permute-start.10 = (bf16[2,8,4096]{2,1,0:T(8,128)(2,1)S(1)}, bf16[2,8,4096]{2,1,0:T(8,128)(2,1)S(1)}, u32[]{:S(2)}, u32[]{:S(2)}) collective-permute-start(bf16[2,8,4096]{2,1,0:T(8,128)(2,1)S(1)} %get-tuple-element.50), channel_id=1, source_target_pairs={{0,4},{4,0},{8,12},{12,8},{16,20},{20,16},{24,28},{28,24},{1,5},{5... | collective-permute-start | bytes 393224 | tf_op jit(solution)/shard_map/ppermute | solution.py:263
  30.5 1.2 %collective-permute-start.11 = (bf16[2,8,4096]{2,1,0:T(8,128)(2,1)S(1)}, bf16[2,8,4096]{2,1,0:T(8,128)(2,1)S(1)}, u32[]{:S(2)}, u32[]{:S(2)}) collective-permute-start(bf16[2,8,4096]{2,1,0:T(8,128)(2,1)S(1)} %get-tuple-element.51), channel_id=1, source_target_pairs={{0,8},{4,12},{8,0},{12,4},{16,24},{20,28},{24,16},{28,20},{1,9},{5... | collective-permute-start | bytes 393224 | tf_op jit(solution)/shard_map/ppermute | solution.py:263
  31.8 0.5 %collective-permute-start.12 = (bf16[2,8,4096]{2,1,0:T(8,128)(2,1)S(1)}, bf16[2,8,4096]{2,1,0:T(8,128)(2,1)S(1)}, u32[]{:S(2)}, u32[]{:S(2)}) collective-permute-start(bf16[2,8,4096]{2,1,0:T(8,128)(2,1)S(1)} %get-tuple-element.52), channel_id=1, source_target_pairs={{0,12},{4,8},{8,4},{12,0},{16,28},{20,24},{24,20},{28,16},{1,13},{... | collective-permute-start | bytes 393224 | tf_op jit(solution)/shard_map/ppermute | solution.py:263
  32.2 1.2 %collective-permute-start.13 = (bf16[2,8,4096]{2,1,0:T(8,128)(2,1)S(1)}, bf16[2,8,4096]{2,1,0:T(8,128)(2,1)S(1)}, u32[]{:S(2)}, u32[]{:S(2)}) collective-permute-start(bf16[2,8,4096]{2,1,0:T(8,128)(2,1)S(1)} %get-tuple-element.53), channel_id=1, source_target_pairs={{0,16},{4,20},{8,24},{12,28},{16,0},{20,4},{24,8},{28,12},{1,17},{... | collective-permute-start | bytes 393224 | tf_op jit(solution)/shard_map/ppermute | solution.py:263
  33.5 0.6 %collective-permute-start.14 = (bf16[2,8,4096]{2,1,0:T(8,128)(2,1)S(1)}, bf16[2,8,4096]{2,1,0:T(8,128)(2,1)S(1)}, u32[]{:S(2)}, u32[]{:S(2)}) collective-permute-start(bf16[2,8,4096]{2,1,0:T(8,128)(2,1)S(1)} %get-tuple-element.54), channel_id=1, source_target_pairs={{0,20},{4,16},{8,28},{12,24},{16,4},{20,0},{24,12},{28,8},{1,21},{... | collective-permute-start | bytes 393224 | tf_op jit(solution)/shard_map/ppermute | solution.py:263
  34.0 2.2 %collective-permute-start.15 = (bf16[2,8,4096]{2,1,0:T(8,128)(2,1)S(1)}, bf16[2,8,4096]{2,1,0:T(8,128)(2,1)S(1)}, u32[]{:S(2)}, u32[]{:S(2)}) collective-permute-start(bf16[2,8,4096]{2,1,0:T(8,128)(2,1)S(1)} %get-tuple-element.55), channel_id=1, source_target_pairs={{0,24},{4,28},{8,16},{12,20},{16,8},{20,12},{24,0},{28,4},{1,25},{... | collective-permute-start | bytes 393224 | tf_op jit(solution)/shard_map/ppermute | solution.py:263
  36.2 2.7 %collective-permute-start.16 = (bf16[2,8,4096]{2,1,0:T(8,128)(2,1)S(1)}, bf16[2,8,4096]{2,1,0:T(8,128)(2,1)S(1)}, u32[]{:S(2)}, u32[]{:S(2)}) collective-permute-start(bf16[2,8,4096]{2,1,0:T(8,128)(2,1)S(1)} %get-tuple-element.56), channel_id=1, source_target_pairs={{0,28},{4,24},{8,20},{12,16},{16,12},{20,8},{24,4},{28,0},{1,29},{... | collective-permute-start | bytes 393224 | tf_op jit(solution)/shard_map/ppermute | solution.py:263
  39.0 2.5 %store.1 = (f32[16,8,4096]{2,1,0:T(8,128)}, f32[16,8,4096]{2,1,0:T(8,128)}) custom-call(f32[16,8,128]{2,1,0:T(8,128)S(1)} %get-tuple-element.45.scale_ref, f32[16,8,4096]{2,1,0:T(8,128)S(1)} %get-tuple-element.42.acc_ref, f32[16,8,4096]{2,1,0:T(8,128)S(1)} %get-tuple-element.43.base_ref, f32[16,8,4096]{2,1,0:T(8,128)S(1)} %copy-done), custom_call_target="tpu_custom_call" | custom-call | flops 1000000 | bytes 12582912 | tf_op jit(solution)/shard_map/store/pallas_call | solution.py:309
  41.5 4.4 %collective-permute-done.14.rest_5_ = bf16[2,8,4096]{2,1,0:T(8,128)(2,1)S(1)} collective-permute-done((bf16[2,8,4096]{2,1,0:T(8,128)(2,1)S(1)}, bf16[2,8,4096]{2,1,0:T(8,128)(2,1)S(1)}, u32[]{:S(2)}, u32[]{:S(2)}) %collective-permute-start.14) | collective-permute-done | bytes 131104 | tf_op jit(solution)/shard_map/ppermute | solution.py:263
  45.9 1.8 %unpack.1 = bf16[1,16,8,4096]{3,2,1,0:T(8,128)(2,1)} custom-call(s32[1]{0:T(128)} %bitcast.me_ref, s32[16]{0:T(128)} %get-tuple-element.48.places_ref, bf16[2,8,4096]{2,1,0:T(8,128)(2,1)S(1)} %get-tuple-element.49.rest_0_, bf16[2,8,4096]{2,1,0:T(8,128)(2,1)S(1)} %collective-permute-done.10.rest_1_, bf16[2,8,4096]{2,1,0:T(8,128)(2,1)S(1)} %collective-permute-done.11.rest_2_, ...), custom_call_target="tpu_custom_call" | custom-call | tf_op jit(solution)/shard_map/unpack/pallas_call | solution.py:319
  (18 shorter events, 0.2 us)
Async XLA Ops:
  3.4 4.8 %collective-permute-start = (bf16[2,8,4096]{2,1,0:T(8,128)(2,1)S(1)}, bf16[2,8,4096]{2,1,0:T(8,128)(2,1)S(1)}, u32[]{:S(2)}, u32[]{:S(2)}) collective-permute-start(bf16[2,8,4096]{2,1,0:T(8,128)(2,1)S(1)} %get-tuple-element.35), channel_id=1, source_target_pairs={{0,4},{4,0},{8,12},{12,8},{16,20},{20,16},{24,28},{28,24},{1,5},{5... | collective-permute-start | bytes 393224 | tf_op jit(solution)/shard_map/ppermute | solution.py:263
  3.5 7.1 %collective-permute-start.1 = (bf16[2,8,4096]{2,1,0:T(8,128)(2,1)S(1)}, bf16[2,8,4096]{2,1,0:T(8,128)(2,1)S(1)}, u32[]{:S(2)}, u32[]{:S(2)}) collective-permute-start(bf16[2,8,4096]{2,1,0:T(8,128)(2,1)S(1)} %get-tuple-element.36), channel_id=1, source_target_pairs={{0,8},{4,12},{8,0},{12,4},{16,24},{20,28},{24,16},{28,20},{1,9},{5... | collective-permute-start | bytes 393224 | tf_op jit(solution)/shard_map/ppermute | solution.py:263
  6.2 10.9 %collective-permute-start.2 = (bf16[2,8,4096]{2,1,0:T(8,128)(2,1)S(1)}, bf16[2,8,4096]{2,1,0:T(8,128)(2,1)S(1)}, u32[]{:S(2)}, u32[]{:S(2)}) collective-permute-start(bf16[2,8,4096]{2,1,0:T(8,128)(2,1)S(1)} %get-tuple-element.37), channel_id=1, source_target_pairs={{0,12},{4,8},{8,4},{12,0},{16,28},{20,24},{24,20},{28,16},{1,13},{... | collective-permute-start | bytes 393224 | tf_op jit(solution)/shard_map/ppermute | solution.py:263
  6.2 10.9 %collective-permute-start.3 = (bf16[2,8,4096]{2,1,0:T(8,128)(2,1)S(1)}, bf16[2,8,4096]{2,1,0:T(8,128)(2,1)S(1)}, u32[]{:S(2)}, u32[]{:S(2)}) collective-permute-start(bf16[2,8,4096]{2,1,0:T(8,128)(2,1)S(1)} %get-tuple-element.38), channel_id=1, source_target_pairs={{0,16},{4,20},{8,24},{12,28},{16,0},{20,4},{24,8},{28,12},{1,17},{... | collective-permute-start | bytes 393224 | tf_op jit(solution)/shard_map/ppermute | solution.py:263
  7.9 12.2 %collective-permute-start.4 = (bf16[2,8,4096]{2,1,0:T(8,128)(2,1)S(1)}, bf16[2,8,4096]{2,1,0:T(8,128)(2,1)S(1)}, u32[]{:S(2)}, u32[]{:S(2)}) collective-permute-start(bf16[2,8,4096]{2,1,0:T(8,128)(2,1)S(1)} %get-tuple-element.39), channel_id=1, source_target_pairs={{0,20},{4,16},{8,28},{12,24},{16,4},{20,0},{24,12},{28,8},{1,21},{... | collective-permute-start | bytes 393224 | tf_op jit(solution)/shard_map/ppermute | solution.py:263
  8.2 11.9 %collective-permute-start.5 = (bf16[2,8,4096]{2,1,0:T(8,128)(2,1)S(1)}, bf16[2,8,4096]{2,1,0:T(8,128)(2,1)S(1)}, u32[]{:S(2)}, u32[]{:S(2)}) collective-permute-start(bf16[2,8,4096]{2,1,0:T(8,128)(2,1)S(1)} %get-tuple-element.40), channel_id=1, source_target_pairs={{0,24},{4,28},{8,16},{12,20},{16,8},{20,12},{24,0},{28,4},{1,25},{... | collective-permute-start | bytes 393224 | tf_op jit(solution)/shard_map/ppermute | solution.py:263
  10.6 9.5 %collective-permute-start.6 = (bf16[2,8,4096]{2,1,0:T(8,128)(2,1)S(1)}, bf16[2,8,4096]{2,1,0:T(8,128)(2,1)S(1)}, u32[]{:S(2)}, u32[]{:S(2)}) collective-permute-start(bf16[2,8,4096]{2,1,0:T(8,128)(2,1)S(1)} %get-tuple-element.41), channel_id=1, source_target_pairs={{0,28},{4,24},{8,20},{12,16},{16,12},{20,8},{24,4},{28,0},{1,29},{... | collective-permute-start | bytes 393224 | tf_op jit(solution)/shard_map/ppermute | solution.py:263
  21.1 5.9 %collective-permute-start.7 = (f32[16,128]{1,0:T(8,128)S(1)}, f32[16,128]{1,0:T(8,128)S(1)}, u32[]{:S(2)}, u32[]{:S(2)}) collective-permute-start(f32[16,128]{1,0:T(8,128)S(1)} %get-tuple-element.44.rest_0_), channel_id=1, source_target_pairs={{0,2},{1,3},{2,0},{3,1},{4,6},{5,7},{6,4},{7,5},{8,10},{9,11},{10,... | collective-permute-start | bytes 24584 | tf_op jit(solution)/shard_map/ppermute | solution.py:297
  23.7 4.3 %collective-permute-start.8 = (f32[16,128]{1,0:T(8,128)S(1)}, f32[16,128]{1,0:T(8,128)S(1)}, u32[]{:S(2)}, u32[]{:S(2)}) collective-permute-start(f32[16,128]{1,0:T(8,128)S(1)} %get-tuple-element.44.rest_0_), channel_id=1, source_target_pairs={{0,1},{1,2},{2,3},{3,0},{4,5},{5,6},{6,7},{7,4},{8,9},{9,10},{10,1... | collective-permute-start | bytes 24584 | tf_op jit(solution)/shard_map/ppermute | solution.py:297
  25.0 3.0 %collective-permute-start.9 = (f32[16,128]{1,0:T(8,128)S(1)}, f32[16,128]{1,0:T(8,128)S(1)}, u32[]{:S(2)}, u32[]{:S(2)}) collective-permute-start(f32[16,128]{1,0:T(8,128)S(1)} %get-tuple-element.44.rest_0_), channel_id=1, source_target_pairs={{0,3},{1,0},{2,1},{3,2},{4,7},{5,4},{6,5},{7,6},{8,11},{9,8},{10,9... | collective-permute-start | bytes 24584 | tf_op jit(solution)/shard_map/ppermute | solution.py:297
  28.0 11.0 %copy-start = (f32[16,8,4096]{2,1,0:T(8,128)S(1)}, f32[16,8,4096]{2,1,0:T(8,128)}, u32[]{:S(2)}) copy-start(f32[16,8,4096]{2,1,0:T(8,128)} %past_ref.1) | copy-start | bytes 6291460
  28.9 5.2 %collective-permute-start.10 = (bf16[2,8,4096]{2,1,0:T(8,128)(2,1)S(1)}, bf16[2,8,4096]{2,1,0:T(8,128)(2,1)S(1)}, u32[]{:S(2)}, u32[]{:S(2)}) collective-permute-start(bf16[2,8,4096]{2,1,0:T(8,128)(2,1)S(1)} %get-tuple-element.50), channel_id=1, source_target_pairs={{0,4},{4,0},{8,12},{12,8},{16,20},{20,16},{24,28},{28,24},{1,5},{5... | collective-permute-start | bytes 393224 | tf_op jit(solution)/shard_map/ppermute | solution.py:263
  30.5 5.7 %collective-permute-start.11 = (bf16[2,8,4096]{2,1,0:T(8,128)(2,1)S(1)}, bf16[2,8,4096]{2,1,0:T(8,128)(2,1)S(1)}, u32[]{:S(2)}, u32[]{:S(2)}) collective-permute-start(bf16[2,8,4096]{2,1,0:T(8,128)(2,1)S(1)} %get-tuple-element.51), channel_id=1, source_target_pairs={{0,8},{4,12},{8,0},{12,4},{16,24},{20,28},{24,16},{28,20},{1,9},{5... | collective-permute-start | bytes 393224 | tf_op jit(solution)/shard_map/ppermute | solution.py:263
  31.8 9.7 %collective-permute-start.12 = (bf16[2,8,4096]{2,1,0:T(8,128)(2,1)S(1)}, bf16[2,8,4096]{2,1,0:T(8,128)(2,1)S(1)}, u32[]{:S(2)}, u32[]{:S(2)}) collective-permute-start(bf16[2,8,4096]{2,1,0:T(8,128)(2,1)S(1)} %get-tuple-element.52), channel_id=1, source_target_pairs={{0,12},{4,8},{8,4},{12,0},{16,28},{20,24},{24,20},{28,16},{1,13},{... | collective-permute-start | bytes 393224 | tf_op jit(solution)/shard_map/ppermute | solution.py:263
  32.2 9.3 %collective-permute-start.13 = (bf16[2,8,4096]{2,1,0:T(8,128)(2,1)S(1)}, bf16[2,8,4096]{2,1,0:T(8,128)(2,1)S(1)}, u32[]{:S(2)}, u32[]{:S(2)}) collective-permute-start(bf16[2,8,4096]{2,1,0:T(8,128)(2,1)S(1)} %get-tuple-element.53), channel_id=1, source_target_pairs={{0,16},{4,20},{8,24},{12,28},{16,0},{20,4},{24,8},{28,12},{1,17},{... | collective-permute-start | bytes 393224 | tf_op jit(solution)/shard_map/ppermute | solution.py:263
  33.5 12.4 %collective-permute-start.14 = (bf16[2,8,4096]{2,1,0:T(8,128)(2,1)S(1)}, bf16[2,8,4096]{2,1,0:T(8,128)(2,1)S(1)}, u32[]{:S(2)}, u32[]{:S(2)}) collective-permute-start(bf16[2,8,4096]{2,1,0:T(8,128)(2,1)S(1)} %get-tuple-element.54), channel_id=1, source_target_pairs={{0,20},{4,16},{8,28},{12,24},{16,4},{20,0},{24,12},{28,8},{1,21},{... | collective-permute-start | bytes 393224 | tf_op jit(solution)/shard_map/ppermute | solution.py:263
  34.0 11.9 %collective-permute-start.15 = (bf16[2,8,4096]{2,1,0:T(8,128)(2,1)S(1)}, bf16[2,8,4096]{2,1,0:T(8,128)(2,1)S(1)}, u32[]{:S(2)}, u32[]{:S(2)}) collective-permute-start(bf16[2,8,4096]{2,1,0:T(8,128)(2,1)S(1)} %get-tuple-element.55), channel_id=1, source_target_pairs={{0,24},{4,28},{8,16},{12,20},{16,8},{20,12},{24,0},{28,4},{1,25},{... | collective-permute-start | bytes 393224 | tf_op jit(solution)/shard_map/ppermute | solution.py:263
  36.2 9.7 %collective-permute-start.16 = (bf16[2,8,4096]{2,1,0:T(8,128)(2,1)S(1)}, bf16[2,8,4096]{2,1,0:T(8,128)(2,1)S(1)}, u32[]{:S(2)}, u32[]{:S(2)}) collective-permute-start(bf16[2,8,4096]{2,1,0:T(8,128)(2,1)S(1)} %get-tuple-element.56), channel_id=1, source_target_pairs={{0,28},{4,24},{8,20},{12,16},{16,12},{20,8},{24,4},{28,0},{1,29},{... | collective-permute-start | bytes 393224 | tf_op jit(solution)/shard_map/ppermute | solution.py:263

commit v5 on v4

v5 whole, which is shorter than its diff:
```python
import functools

import jax
import jax.numpy as jnp
from jax import lax
from jax.experimental import pallas as pl
from jax.experimental.pallas import tpu as pltpu
from jax.sharding import PartitionSpec as P

CAP = 2
CHUNK = 1024
PARTS = 4
outer_momentum = 0.9
outer_rate = 0.7

SMEM = pl.BlockSpec(memory_space=pltpu.SMEM)
VMEM = pl.BlockSpec(memory_space=pltpu.VMEM)
ANY = pl.BlockSpec(memory_space=pl.ANY)


def in_vmem(*arrays):
    return [pltpu.with_memory_space_constraint(x, pltpu.VMEM) for x in arrays]


def in_hbm(*arrays):
    return [pltpu.with_memory_space_constraint(x, pltpu.HBM) for x in arrays]


def chunks(width):
    step = CHUNK if width % CHUNK == 0 else width
    return [pl.ds(at, step) for at in range(0, width, step)]


def fetches(me, sent, local_ref, places_ref, sems):
    found = []
    for n, (d, parity, piece) in enumerate(sent):
        wanted = True if parity is None else lax.rem(me ^ d, 2) == parity
        for r in range(CAP):
            k = jnp.maximum(places_ref[(me ^ d) * CAP + r], 0)
            copy = pltpu.make_async_copy(local_ref.at[k], piece.at[r], sems.at[n * CAP + r])
            found.append((wanted, copy))
    return found


def run(wanted, act):
    if wanted is True:
        act()
    else:
        pl.when(wanted)(act)


def pack_kernel(
    owned, sent, me_ref, ids_ref, counts_ref, local_ref,
    places_ref, module_ref, weight_ref, total_ref, *rest,
):
    pieces, (seen, sems) = rest[:-2], rest[-2:]
    me = me_ref[0]
    paths, held = ids_ref.shape
    for i in range(paths):
        seen[i] = jnp.int32(0)
    for i in range(paths * CAP):
        places_ref[i] = jnp.int32(-1)
    for k in range(held):
        group = lax.div(ids_ref[me, k], jnp.int32(owned))
        rank = seen[group]
        seen[group] = rank + 1
        places_ref[group * CAP + rank] = jnp.int32(k)
    sent = [(*s, p) for s, p in zip(sent, pieces, strict=True)]
    copies = fetches(me, sent, local_ref, places_ref, sems)
    for wanted, copy in copies:
        run(wanted, copy.start)
    find_slots(me, owned, ids_ref, counts_ref, module_ref, weight_ref, total_ref)
    for wanted, copy in copies:
        run(wanted, copy.wait)


def find_slots(me, owned, ids_ref, counts_ref, module_ref, weight_ref, total_ref):
    paths, held = ids_ref.shape

    def reset(i, _):
        total_ref[i] = jnp.float32(0.0)
        return 0

    def one(path, _):
        first = path * (CAP + 1)
        for r in range(CAP):
            module_ref[first + r] = jnp.int32(0)
            weight_ref[first + r] = jnp.float32(0.0)
        rank = jnp.int32(0)
        for k in range(held):
            at = ids_ref[path, k] - me * owned
            mine = (at >= 0) & (at < owned)
            slot = first + jnp.where(mine, rank, CAP)
            module_ref[slot] = at
            weight_ref[slot] = counts_ref[path, k].astype(jnp.float32)
            rank = rank + mine.astype(jnp.int32)
        for r in range(CAP):
            at = module_ref[first + r]
            total_ref[at] = total_ref[at] + weight_ref[first + r]
        return 0

    lax.fori_loop(0, owned, reset, 0)
    lax.fori_loop(0, paths, one, 0)


def subtract(me, pieces, distances, module_ref, weight_ref, acc_ref):
    width = acc_ref.shape[2]
    for piece, d in zip(pieces, distances, strict=True):
        for r in range(CAP):
            slot = (me ^ d) * (CAP + 1) + r
            m, weight = module_ref[slot], weight_ref[slot]
            for c in chunks(width):
                acc_ref[m, :, c] = acc_ref[m, :, c] - weight * piece[r, :, c].astype(jnp.float32)


def combine(parity, me, distances, pieces, tables, params_hbm, acc_ref, squares_ref, params_ref, sems):
    module_ref, weight_ref, total_ref = tables
    owned, rows, width = acc_ref.shape
    part = owned // PARTS

    def copy(i):
        at = pl.ds(i * part, part)
        return pltpu.make_async_copy(params_hbm.at[at], params_ref.at[at], sems.at[i])

    @pl.when(lax.rem(me, 2) == parity)
    def _():
        for i in range(PARTS):
            copy(i).start()

        def clear(m, _):
            acc_ref[m] = jnp.zeros((rows, width), jnp.float32)
            return 0

        lax.fori_loop(0, owned, clear, 0)
        subtract(me, pieces, distances, module_ref, weight_ref, acc_ref)
        for m in range(owned):
            if m % part == 0:
                copy(m // part).wait()
            total = jnp.full((rows, 128), total_ref[m], jnp.float32)
            inverse = 1.0 / jnp.maximum(total, 1.0)
            added = jnp.zeros((rows, 128), jnp.float32)
            for at in range(0, width, 128):
                c = pl.ds(at, 128)
                acc = acc_ref[m, :, c] + total * params_ref[m, :, c]
                acc_ref[m, :, c] = acc
                raw = acc * inverse
                added = added + raw * raw
            squares_ref[pl.ds(m, 1), :] = jnp.sum(added, axis=0, keepdims=True)


def first_combine_kernel(
    distances, sent, me_ref, module_ref, weight_ref, total_ref, places_ref, local_ref, params_hbm, *rest
):
    n = len(distances)
    arrived, (acc_ref, squares_ref, *pieces), room = rest[:n], rest[n:-3], rest[-3:]
    params_room, params_sems, sems = room
    me = me_ref[0]
    sent = [(*s, p) for s, p in zip(sent, pieces, strict=True)]
    copies = fetches(me, sent, local_ref, places_ref, sems)
    for wanted, copy in copies:
        run(wanted, copy.start)
    for wanted, copy in copies:
        run(wanted, copy.wait)
    tables = module_ref, weight_ref, total_ref
    combine(
        0, me, distances, arrived, tables, params_hbm, acc_ref, squares_ref, params_room, params_sems
    )


def second_combine_kernel(
    distances, me_ref, module_ref, weight_ref, total_ref, acc_in, params_hbm, *rest
):
    arrived, (acc_ref, squares_ref, *room) = rest[:-4], rest[-4:]
    tables = module_ref, weight_ref, total_ref
    combine(1, me_ref[0], distances, arrived, tables, params_hbm, acc_ref, squares_ref, *room)


def scales(entries, total, squares):
    inverse = 1.0 / jnp.maximum(total, 1.0)
    mean = jnp.sum(squares, axis=1, keepdims=True) / entries
    factor = jnp.minimum(1.0, 1.0 / jnp.sqrt(mean + 1e-06))
    return inverse * factor


def step(scale, acc, params, past):
    delta = scale * acc
    velocity = outer_momentum * past + delta
    return params - outer_rate * (outer_momentum * velocity + delta), velocity


def send_kernel(
    order, shards, me_ref, module_ref, total_ref, acc_ref, params_ref, past_ref, *rest
):
    even, odd, (scale_ref, *pieces) = rest[:shards], rest[shards : 2 * shards], rest[2 * shards :]
    me = me_ref[0]
    owned, rows, width = acc_ref.shape
    is_odd = lax.rem(me, 2) == 1
    summed = jnp.where(is_odd, odd[0][...], even[0][...])
    for a, b in zip(even[1:], odd[1:], strict=True):
        summed = summed + jnp.where(is_odd, b[...], a[...])
    total = jnp.concatenate(
        [jnp.full((1, 128), total_ref[m], jnp.float32) for m in range(owned)], axis=0
    )
    scale = scales(rows * width * shards, total, summed)
    for m in range(owned):
        scale_ref[m] = jnp.broadcast_to(scale[m : m + 1, :], (rows, 128))
    for d, piece in zip(order, pieces, strict=True):
        for r in range(CAP):
            m = module_ref[(me ^ d) * (CAP + 1) + r]
            scale_m = scale_ref[m][:, :1]
            for c in chunks(width):
                updated, _ = step(
                    scale_m, acc_ref[m, :, c], params_ref[m, :, c], past_ref[m, :, c]
                )
                piece[r, :, c] = updated.astype(jnp.bfloat16)


def store_kernel(
    scale_ref, acc_ref, params_ref, past_ref, updated_hbm, velocity_hbm, updated_ref, velocity_ref, sems
):
    owned, _, width = acc_ref.shape
    part = owned // PARTS

    def copies(i):
        at = pl.ds(i * part, part)
        return [
            pltpu.make_async_copy(ref.at[at], hbm.at[at], sems.at[n, i])
            for n, (ref, hbm) in enumerate(
                ((updated_ref, updated_hbm), (velocity_ref, velocity_hbm))
            )
        ]

    for i in range(PARTS):

        def fill(m, _):
            scale = scale_ref[m][:, :1]
            for c in chunks(width):
                updated_ref[m, :, c], velocity_ref[m, :, c] = step(
                    scale, acc_ref[m, :, c], params_ref[m, :, c], past_ref[m, :, c]
                )
            return 0

        lax.fori_loop(i * part, (i + 1) * part, fill, 0)
        for copy in copies(i):
            copy.start()
    for i in range(PARTS):
        for copy in copies(i):
            copy.wait()


def unpack_kernel(order, me_ref, places_ref, *rest):
    pieces, (out_ref, sems) = rest[:-2], rest[-2:]
    me = me_ref[0]
    for wait in (False, True):
        for d, piece in zip(order, pieces, strict=True):
            for r in range(CAP):
                k = places_ref[(me ^ d) * CAP + r]

                @pl.when(k >= 0)
                def _():
                    copy = pltpu.make_async_copy(
                        piece.at[r], out_ref.at[0, k], sems.at[d * CAP + r]
                    )
                    if wait:
                        copy.wait()
                    else:
                        copy.start()


def on_device(path_params, global_params, momentum, module_ids, token_counts):
    paths, held = module_ids.shape
    owned, rows, width = global_params.shape
    shards = lax.axis_size("shard")
    me = lax.axis_index("path").astype(jnp.int32).reshape(1)
    module_ids, counts = in_hbm(module_ids, token_counts)
    slots = paths * CAP
    piece = pltpu.VMEM((CAP, rows, width), jnp.bfloat16)
    module = jax.ShapeDtypeStruct((owned, rows, width), jnp.float32)
    held_module = pltpu.VMEM(module.shape, module.dtype)
    tables = [
        jax.ShapeDtypeStruct((paths * (CAP + 1),), jnp.int32),
        jax.ShapeDtypeStruct((paths * (CAP + 1),), jnp.float32),
        jax.ShapeDtypeStruct((owned,), jnp.float32),
    ]
    room = [
        pltpu.VMEM(module.shape, module.dtype),
        pltpu.VMEM(module.shape, module.dtype),
        pltpu.SemaphoreType.DMA((2, PARTS)),
    ]
    limits = pltpu.CompilerParams(vmem_limit_bytes=24 * 1024 * 1024)
    far = sorted(range(2, paths, 2), key=lambda d: (-d.bit_count(), d))
    order = far + [d + 1 for d in far] + [1]
    local, params = in_hbm(path_params.reshape(held, rows, width), global_params)

    first = [(d, 0) for d in far] + [(d, None) for d in order[len(far) :]] + [(0, None)]
    third = [(d, 1) for d in far]

    def to_parity(x, d, parity):
        return lax.ppermute(
            x, "path", [(i, i ^ d) for i in range(paths) if (i ^ d) % 2 == parity]
        )

    def sems(sent):
        return pltpu.SemaphoreType.DMA((len(sent) * CAP,))

    places, table, weights, total, *packed = pl.pallas_call(
        functools.partial(pack_kernel, owned, first),
        out_shape=[jax.ShapeDtypeStruct((slots,), jnp.int32)] + tables + [piece] * len(first),
        in_specs=[SMEM] * 3 + [ANY],
        out_specs=[SMEM] * 4 + [VMEM] * len(first),
        scratch_shapes=[pltpu.SMEM((paths,), jnp.int32), sems(first)],
        name="pack",
    )(me, module_ids, counts, local)
    own = packed[-1]
    arrived = [to_parity(x, d, 0) for d, x in zip(order, packed)]
    acc, squares, *repacked = pl.pallas_call(
        functools.partial(first_combine_kernel, [*order, 0], third),
        out_shape=[held_module, jax.ShapeDtypeStruct((owned, 128), jnp.float32)]
        + [piece] * len(third),
        in_specs=[SMEM] * 5 + [ANY] * 2 + [VMEM] * (1 + len(order)),
        out_specs=[VMEM] * (2 + len(third)),
        scratch_shapes=[
            pltpu.VMEM(module.shape, module.dtype),
            pltpu.SemaphoreType.DMA((PARTS,)),
            sems(third),
        ],
        compiler_params=limits,
        name="combine",
    )(me, table, weights, total, places, local, params, *in_vmem(*arrived, own))
    late = order[len(far) :] + far
    arrived = [to_parity(x, d, 1) for d, x in zip(late, packed[len(far) : -1] + repacked)]

    def gather(x, parity):
        turns = sorted(range(1, shards), key=lambda d: (d != 2, d))
        return [x] + [
            lax.ppermute(
                x,
                ("path", "shard"),
                [
                    (p * shards + i, p * shards + (i + d) % shards)
                    for p in range(parity, paths, 2)
                    for i in range(shards)
                ],
            )
            for d in turns
        ]

    parts = gather(squares, 0)
    acc, squares = pl.pallas_call(
        functools.partial(second_combine_kernel, [*late, 0]),
        out_shape=[held_module, jax.ShapeDtypeStruct((owned, 128), jnp.float32)],
        in_specs=[SMEM] * 4 + [VMEM] + [ANY] + [VMEM] * (1 + len(late)),
        out_specs=[VMEM] * 2,
        input_output_aliases={4: 0},
        scratch_shapes=[
            pltpu.VMEM(module.shape, module.dtype),
            pltpu.SemaphoreType.DMA((PARTS,)),
        ],
        compiler_params=limits,
        name="combine",
    )(me, table, weights, total, *in_vmem(acc), params, *in_vmem(*arrived, own))
    parts += gather(squares, 1)
    scale, *outgoing = pl.pallas_call(
        functools.partial(send_kernel, [*order, 0], shards),
        out_shape=[jax.ShapeDtypeStruct((owned, rows, 128), jnp.float32)] + [piece] * paths,
        in_specs=[SMEM] * 3 + [VMEM] * (3 + 2 * shards),
        out_specs=[VMEM] * (1 + paths),
        compiler_params=limits,
        name="send",
    )(me, table, total, *in_vmem(acc), global_params, momentum, *parts)
    returned = [
        lax.ppermute(x, "path", [(i, i ^ d) for i in range(paths)])
        for d, x in zip(order, outgoing)
    ] + [outgoing[-1]]
    updated, velocity = pl.pallas_call(
        store_kernel,
        out_shape=[module] * 2,
        in_specs=[VMEM] * 4,
        out_specs=[ANY] * 2,
        scratch_shapes=room,
        compiler_params=limits,
        cost_estimate=pl.CostEstimate(flops=10**6, bytes_accessed=12 * 2**20, transcendentals=0),
        name="store",
    )(scale, *in_vmem(acc), global_params, momentum)
    path_out = pl.pallas_call(
        functools.partial(unpack_kernel, [*order, 0]),
        out_shape=jax.ShapeDtypeStruct(path_params.shape, path_params.dtype),
        in_specs=[SMEM] * 2 + [VMEM] * paths,
        out_specs=ANY,
        scratch_shapes=[pltpu.SemaphoreType.DMA((slots,))],
        name="unpack",
    )(me, places, *in_vmem(*returned))
    return updated, velocity, path_out


def solution(mesh):
    placed = (
        P("path", None, "shard", None),
        P("path", "shard", None),
        P("path", "shard", None),
        P(),
        P(),
    )
    return jax.shard_map(
        on_device,
        mesh=mesh,
        in_specs=placed,
        out_specs=(
            P("path", "shard", None),
            P("path", "shard", None),
            P("path", None, "shard", None),
        ),
        check_vma=False,
    )
```

time: 48 us -> 73.8 us (1.54)
  starting transfers between devices: 25.9 us -> 49.1 us
  local copies, waits for them, and re-layouts: 0.01 us -> 2.63 us
  waiting for transfers between devices: 8.42 us -> 7.61 us
    ppermute x17 -> x27, starting transfers between devices: 25.9 us -> 49.1 us  [the longest x14 32.2 us: to_parity(): lax.ppermute(x, 'path', [(i, i ^ d) for i in range(paths) if (i ^ d) % 2...]
    unnamed x2 -> x16, local copies, waits for them, and re-layouts: 0.01 us -> 2.63 us
    ppermute x17 -> x27, waiting for transfers between devices: 8.42 us -> 7.61 us  [the longest x7 4.11 us: on_device(): lax.ppermute(x, 'path', [(i, i ^ d) for i in range(paths)])]
  transfers between devices with their start and end apart: 17 -> 27, of which waited for: 3 -> 6; matrix products, arithmetic and copies ran while one was open for 0% -> 0% of each run, Pallas kernels for 13% -> 9%
where the time goes in v5:
time: 73.8 us; the launch traced here: 72.9 us
  starting transfers between devices  49.1 us (67%)
  Pallas kernels  12.5 us (17%)
  waiting for transfers between devices  7.61 us (10%)
  local copies, waits for them, and re-layouts  2.63 us (4%)
  between operations  1 us (1%)
    ppermute x14, starting transfers between devices, to_parity(): lax.ppermute(x, 'path', [(i, i ^ d) for i in range(paths) if (i ^ d) % 2...  32.2 us
    ppermute x6, starting transfers between devices, gather(): lax.ppermute(x, ('path', 'shard'), [(p * shards + i, p * shards + (i + d)...  11.5 us
    ppermute x7, starting transfers between devices, on_device(): lax.ppermute(x, 'path', [(i, i ^ d) for i in range(paths)])  5.37 us
    ppermute x7, waiting for transfers between devices, on_device(): lax.ppermute(x, 'path', [(i, i ^ d) for i in range(paths)])  4.11 us
    ppermute x6, waiting for transfers between devices, gather(): lax.ppermute(x, ('path', 'shard'), [(p * shards + i, p * shards + (i + d)...  2.92 us
    pallas_call x1, Pallas kernels, on_device(): pl.pallas_call(functools.partial(pack_kernel, owned, first), out_shape=[j...  2.71 us
    pallas_call x1, Pallas kernels, on_device(): pl.pallas_call(store_kernel, out_shape=[module] * 2, in_specs=[VMEM] * 4,...  2.64 us
    unnamed x16, local copies, waits for them, and re-layouts  2.63 us
  transfers between devices with their start and end apart: 27, of which 6 were waited for; matrix products, arithmetic and copies ran while one was open for 0% of the time, Pallas kernels for 9%

profile of v5, /device:TPU:1, one launch (start us, length us, event | category | flops | bytes accessed | tf_op | source)
XLA Modules:
  0.0 72.9 jit_solution(1761225480089146288)
XLA Ops:
  0.6 2.7 %pack.1 = (s32[16]{0:T(128)}, s32[24]{0:T(128)}, f32[24]{0:T(128)}, f32[16]{0:T(128)}, bf16[2,8,4096]{2,1,0:T(8,128)(2,1)S(1)}, /*index=5*/bf16[2,8,4096]{2,1,0:...) custom-call(s32[1]{0:T(128)} %bitcast.me_ref, ...), custom_call_target="tpu_custom_call" | custom-call | tf_op jit(solution)/shard_map/pack/pallas_call | solution.py:306
  5.4 12.8 %collective-permute-start.3 = (bf16[2,8,4096]{2,1,0:T(8,128)(2,1)S(1)}, bf16[2,8,4096]{2,1,0:T(8,128)(2,1)S(1)}, u32[]{:S(2)}, u32[]{:S(2)}) collective-permute-start(bf16[2,8,4096]{2,1,0:T(8,128)(2,1)S(1)} %get-tuple-element.40), channel_id=1, source_target_pairs={{4,24},{12,16},{20,8},{28,0},{5,25},{13,17},{21,9},{29,1},{6,26},{... | collective-permute-start | bytes 393224 | tf_op jit(solution)/shard_map/ppermute | solution.py:299
  18.2 1.3 %collective-permute-start.4 = (bf16[2,8,4096]{2,1,0:T(8,128)(2,1)S(1)}, bf16[2,8,4096]{2,1,0:T(8,128)(2,1)S(1)}, u32[]{:S(2)}, u32[]{:S(2)}) collective-permute-start(bf16[2,8,4096]{2,1,0:T(8,128)(2,1)S(1)} %get-tuple-element.41), channel_id=1, source_target_pairs={{4,8},{12,0},{20,24},{28,16},{5,9},{13,1},{21,25},{29,17},{6,10},{... | collective-permute-start | bytes 393224 | tf_op jit(solution)/shard_map/ppermute | solution.py:299
  19.5 1.3 %collective-permute-start.5 = (bf16[2,8,4096]{2,1,0:T(8,128)(2,1)S(1)}, bf16[2,8,4096]{2,1,0:T(8,128)(2,1)S(1)}, u32[]{:S(2)}, u32[]{:S(2)}) collective-permute-start(bf16[2,8,4096]{2,1,0:T(8,128)(2,1)S(1)} %get-tuple-element.42), channel_id=1, source_target_pairs={{4,16},{12,24},{20,0},{28,8},{5,17},{13,25},{21,1},{29,9},{6,18},{... | collective-permute-start | bytes 393224 | tf_op jit(solution)/shard_map/ppermute | solution.py:299
  20.8 1.3 %collective-permute-start.6 = (bf16[2,8,4096]{2,1,0:T(8,128)(2,1)S(1)}, bf16[2,8,4096]{2,1,0:T(8,128)(2,1)S(1)}, u32[]{:S(2)}, u32[]{:S(2)}) collective-permute-start(bf16[2,8,4096]{2,1,0:T(8,128)(2,1)S(1)} %get-tuple-element.43), channel_id=1, source_target_pairs={{4,0},{12,8},{20,16},{28,24},{5,1},{13,9},{21,17},{29,25},{6,2},{1... | collective-permute-start | bytes 393224 | tf_op jit(solution)/shard_map/ppermute | solution.py:299
  22.1 1.3 %collective-permute-start.7 = (bf16[2,8,4096]{2,1,0:T(8,128)(2,1)S(1)}, bf16[2,8,4096]{2,1,0:T(8,128)(2,1)S(1)}, u32[]{:S(2)}, u32[]{:S(2)}) collective-permute-start(bf16[2,8,4096]{2,1,0:T(8,128)(2,1)S(1)} %get-tuple-element.40), channel_id=1, source_target_pairs={{0,28},{8,20},{16,12},{24,4},{1,29},{9,21},{17,13},{25,5},{2,30},{... | collective-permute-start | bytes 393224 | tf_op jit(solution)/shard_map/ppermute | solution.py:299
  23.4 1.3 %collective-permute-start.8 = (bf16[2,8,4096]{2,1,0:T(8,128)(2,1)S(1)}, bf16[2,8,4096]{2,1,0:T(8,128)(2,1)S(1)}, u32[]{:S(2)}, u32[]{:S(2)}) collective-permute-start(bf16[2,8,4096]{2,1,0:T(8,128)(2,1)S(1)} %get-tuple-element.41), channel_id=1, source_target_pairs={{0,12},{8,4},{16,28},{24,20},{1,13},{9,5},{17,29},{25,21},{2,14},{... | collective-permute-start | bytes 393224 | tf_op jit(solution)/shard_map/ppermute | solution.py:299
  24.7 1.3 %collective-permute-start.9 = (bf16[2,8,4096]{2,1,0:T(8,128)(2,1)S(1)}, bf16[2,8,4096]{2,1,0:T(8,128)(2,1)S(1)}, u32[]{:S(2)}, u32[]{:S(2)}) collective-permute-start(bf16[2,8,4096]{2,1,0:T(8,128)(2,1)S(1)} %get-tuple-element.42), channel_id=1, source_target_pairs={{0,20},{8,28},{16,4},{24,12},{1,21},{9,29},{17,5},{25,13},{2,22},{... | collective-permute-start | bytes 393224 | tf_op jit(solution)/shard_map/ppermute | solution.py:299
  26.0 1.3 %collective-permute-start.10 = (bf16[2,8,4096]{2,1,0:T(8,128)(2,1)S(1)}, bf16[2,8,4096]{2,1,0:T(8,128)(2,1)S(1)}, u32[]{:S(2)}, u32[]{:S(2)}) collective-permute-start(bf16[2,8,4096]{2,1,0:T(8,128)(2,1)S(1)} %get-tuple-element.43), channel_id=1, source_target_pairs={{0,4},{8,12},{16,20},{24,28},{1,5},{9,13},{17,21},{25,29},{2,6},{1... | collective-permute-start | bytes 393224 | tf_op jit(solution)/shard_map/ppermute | solution.py:299
  30.0 1.7 %combine.2 = (f32[16,8,4096]{2,1,0:T(8,128)S(1)}, f32[16,128]{1,0:T(8,128)S(1)}, bf16[2,8,4096]{2,1,0:T(8,128)(2,1)S(1)}, bf16[2,8,4096]{2,1,0:T(8,128)(2,1)S(1)}, bf16[2,8,4096]{2,1,0:T(8,128)(2,1)S(1)}) custom-call(s32[1]{0:T(128)} %bitcast.me_ref, s32[24]{0:T(128)S(1)} %copy-done.2, f32[24]{0:T(128)S(1)} %copy-done.6, f32[16]{0:T(128)S(1)} %copy-done.4, ...), custom_call_target="tpu_custom_call" | custom-call | tf_op jit(solution)/shard_map/combine/pallas_call | solution.py:316
  31.7 2.2 %collective-permute-start.11 = (bf16[2,8,4096]{2,1,0:T(8,128)(2,1)S(1)}, bf16[2,8,4096]{2,1,0:T(8,128)(2,1)S(1)}, u32[]{:S(2)}, u32[]{:S(2)}) collective-permute-start(bf16[2,8,4096]{2,1,0:T(8,128)(2,1)S(1)} %get-tuple-element.46), channel_id=1, source_target_pairs={{4,28},{12,20},{20,12},{28,4},{5,29},{13,21},{21,13},{29,5},{6,30}... | collective-permute-start | bytes 393224 | tf_op jit(solution)/shard_map/ppermute | solution.py:299
  33.8 3.1 %collective-permute-start.12 = (bf16[2,8,4096]{2,1,0:T(8,128)(2,1)S(1)}, bf16[2,8,4096]{2,1,0:T(8,128)(2,1)S(1)}, u32[]{:S(2)}, u32[]{:S(2)}) collective-permute-start(bf16[2,8,4096]{2,1,0:T(8,128)(2,1)S(1)} %get-tuple-element.47), channel_id=1, source_target_pairs={{4,12},{12,4},{20,28},{28,20},{5,13},{13,5},{21,29},{29,21},{6,14}... | collective-permute-start | bytes 393224 | tf_op jit(solution)/shard_map/ppermute | solution.py:299
  37.0 3.1 %collective-permute-start.13 = (bf16[2,8,4096]{2,1,0:T(8,128)(2,1)S(1)}, bf16[2,8,4096]{2,1,0:T(8,128)(2,1)S(1)}, u32[]{:S(2)}, u32[]{:S(2)}) collective-permute-start(bf16[2,8,4096]{2,1,0:T(8,128)(2,1)S(1)} %get-tuple-element.48), channel_id=1, source_target_pairs={{4,20},{12,28},{20,4},{28,12},{5,21},{13,29},{21,5},{29,13},{6,22}... | collective-permute-start | bytes 393224 | tf_op jit(solution)/shard_map/ppermute | solution.py:299
  42.7 2.5 %combine.3 = (f32[16,8,4096]{2,1,0:T(8,128)S(1)}, f32[16,128]{1,0:T(8,128)S(1)}) custom-call(s32[1]{0:T(128)} %bitcast.me_ref, s32[24]{0:T(128)S(1)} %copy-done.3, f32[24]{0:T(128)S(1)} %copy-done.6, f32[16]{0:T(128)S(1)} %copy-done.5, f32[16,8,4096]{2,1,0:T(8,128)S(1)} %get-tuple-element.45.acc_in, ...), custom_call_target="tpu_custom_call", output_to_operand_aliasing={{0}: (4, {})} | custom-call | tf_op jit(solution)/shard_map/combine/pallas_call | solution.py:349
  45.2 5.2 %collective-permute-start.19 = (f32[16,128]{1,0:T(8,128)S(1)}, f32[16,128]{1,0:T(8,128)S(1)}, u32[]{:S(2)}, u32[]{:S(2)}) collective-permute-start(f32[16,128]{1,0:T(8,128)S(1)} %get-tuple-element.51.rest_4_), channel_id=1, source_target_pairs={{4,7},{5,4},{6,5},{7,6},{12,15},{13,12},{14,13},{15,14},{20,23},{2... | collective-permute-start | bytes 24584 | tf_op jit(solution)/shard_map/ppermute | solution.py:336
  50.5 1.9 %collective-permute-start.18 = (f32[16,128]{1,0:T(8,128)S(1)}, f32[16,128]{1,0:T(8,128)S(1)}, u32[]{:S(2)}, u32[]{:S(2)}) collective-permute-start(f32[16,128]{1,0:T(8,128)S(1)} %get-tuple-element.51.rest_4_), channel_id=1, source_target_pairs={{4,5},{5,6},{6,7},{7,4},{12,13},{13,14},{14,15},{15,12},{20,21},{2... | collective-permute-start | bytes 24584 | tf_op jit(solution)/shard_map/ppermute | solution.py:336
  52.4 2.3 %collective-permute-start.17 = (f32[16,128]{1,0:T(8,128)S(1)}, f32[16,128]{1,0:T(8,128)S(1)}, u32[]{:S(2)}, u32[]{:S(2)}) collective-permute-start(f32[16,128]{1,0:T(8,128)S(1)} %get-tuple-element.51.rest_4_), channel_id=1, source_target_pairs={{4,6},{5,7},{6,4},{7,5},{12,14},{13,15},{14,12},{15,13},{20,22},{2... | collective-permute-start | bytes 24584 | tf_op jit(solution)/shard_map/ppermute | solution.py:336
  54.8 1.9 %collective-permute-done.18.rest_6_ = f32[16,128]{1,0:T(8,128)S(1)} collective-permute-done((f32[16,128]{1,0:T(8,128)S(1)}, f32[16,128]{1,0:T(8,128)S(1)}, u32[]{:S(2)}, u32[]{:S(2)}) %collective-permute-start.18) | collective-permute-done | bytes 8224 | tf_op jit(solution)/shard_map/ppermute | solution.py:336
  57.7 1.3 %send.1 = (f32[16,8,128]{2,1,0:T(8,128)S(1)}, bf16[2,8,4096]{2,1,0:T(8,128)(2,1)S(1)}, bf16[2,8,4096]{2,1,0:T(8,128)(2,1)S(1)}, bf16[2,8,4096]{2,1,0:T(8,128)(2,...) custom-call(s32[1]{0:T(128)} %bitcast.me_ref, ...), custom_call_target="tpu_custom_call" | custom-call | tf_op jit(solution)/shard_map/send/pallas_call | solution.py:363
  59.0 1.5 %collective-permute-start.20 = (bf16[2,8,4096]{2,1,0:T(8,128)(2,1)S(1)}, bf16[2,8,4096]{2,1,0:T(8,128)(2,1)S(1)}, u32[]{:S(2)}, u32[]{:S(2)}) collective-permute-start(bf16[2,8,4096]{2,1,0:T(8,128)(2,1)S(1)} %get-tuple-element.55), channel_id=1, source_target_pairs={{0,24},{4,28},{8,16},{12,20},{16,8},{20,12},{24,0},{28,4},{1,25},{... | collective-permute-start | bytes 393224 | tf_op jit(solution)/shard_map/ppermute | solution.py:372
  61.7 2.6 %collective-permute-start.24 = (bf16[2,8,4096]{2,1,0:T(8,128)(2,1)S(1)}, bf16[2,8,4096]{2,1,0:T(8,128)(2,1)S(1)}, u32[]{:S(2)}, u32[]{:S(2)}) collective-permute-start(bf16[2,8,4096]{2,1,0:T(8,128)(2,1)S(1)} %get-tuple-element.59), channel_id=1, source_target_pairs={{0,12},{4,8},{8,4},{12,0},{16,28},{20,24},{24,20},{28,16},{1,13},{... | collective-permute-start | bytes 393224 | tf_op jit(solution)/shard_map/ppermute | solution.py:372
  65.5 2.6 %store.1 = (f32[16,8,4096]{2,1,0:T(8,128)}, f32[16,8,4096]{2,1,0:T(8,128)}) custom-call(f32[16,8,128]{2,1,0:T(8,128)S(1)} %get-tuple-element.52.scale_ref, f32[16,8,4096]{2,1,0:T(8,128)S(1)} %get-tuple-element.49.acc_ref, f32[16,8,4096]{2,1,0:T(8,128)S(1)} %copy-done, f32[16,8,4096]{2,1,0:T(8,128)S(1)} %copy-done.1), custom_call_target="tpu_custom_call" | custom-call | flops 1000000 | bytes 12582912 | tf_op jit(solution)/shard_map/store/pallas_call | solution.py:375
  68.5 2.6 %collective-permute-done.24.rest_4_ = bf16[2,8,4096]{2,1,0:T(8,128)(2,1)S(1)} collective-permute-done((bf16[2,8,4096]{2,1,0:T(8,128)(2,1)S(1)}, bf16[2,8,4096]{2,1,0:T(8,128)(2,1)S(1)}, u32[]{:S(2)}, u32[]{:S(2)}) %collective-permute-start.24) | collective-permute-done | bytes 131104 | tf_op jit(solution)/shard_map/ppermute | solution.py:372
  71.1 1.8 %unpack.1 = bf16[1,16,8,4096]{3,2,1,0:T(8,128)(2,1)} custom-call(s32[1]{0:T(128)} %bitcast.me_ref, s32[16]{0:T(128)} %get-tuple-element.36.places_ref, bf16[2,8,4096]{2,1,0:T(8,128)(2,1)S(1)} %collective-permute-done.20.rest_0_, bf16[2,8,4096]{2,1,0:T(8,128)(2,1)S(1)} %collective-permute-done.21.rest_1_, ...), custom_call_target="tpu_custom_call" | custom-call | tf_op jit(solution)/shard_map/unpack/pallas_call | solution.py:385
  (52 shorter events, 10.9 us)
Async XLA Ops:
  3.4 16.1 %collective-permute-start = (bf16[2,8,4096]{2,1,0:T(8,128)(2,1)S(1)}, bf16[2,8,4096]{2,1,0:T(8,128)(2,1)S(1)}, u32[]{:S(2)}, u32[]{:S(2)}) collective-permute-start(bf16[2,8,4096]{2,1,0:T(8,128)(2,1)S(1)} %get-tuple-element.37), channel_id=1, source_target_pairs={{0,24},{8,16},{16,8},{24,0},{1,25},{9,17},{17,9},{25,1},{2,26},{10... | collective-permute-start | bytes 393224 | tf_op jit(solution)/shard_map/ppermute | solution.py:299
  4.0 16.8 %collective-permute-start.1 = (bf16[2,8,4096]{2,1,0:T(8,128)(2,1)S(1)}, bf16[2,8,4096]{2,1,0:T(8,128)(2,1)S(1)}, u32[]{:S(2)}, u32[]{:S(2)}) collective-permute-start(bf16[2,8,4096]{2,1,0:T(8,128)(2,1)S(1)} %get-tuple-element.38), channel_id=1, source_target_pairs={{0,8},{8,0},{16,24},{24,16},{1,9},{9,1},{17,25},{25,17},{2,10},{10... | collective-permute-start | bytes 393224 | tf_op jit(solution)/shard_map/ppermute | solution.py:299
  4.7 17.4 %collective-permute-start.2 = (bf16[2,8,4096]{2,1,0:T(8,128)(2,1)S(1)}, bf16[2,8,4096]{2,1,0:T(8,128)(2,1)S(1)}, u32[]{:S(2)}, u32[]{:S(2)}) collective-permute-start(bf16[2,8,4096]{2,1,0:T(8,128)(2,1)S(1)} %get-tuple-element.39), channel_id=1, source_target_pairs={{0,16},{8,24},{16,0},{24,8},{1,17},{9,25},{17,1},{25,9},{2,18},{10... | collective-permute-start | bytes 393224 | tf_op jit(solution)/shard_map/ppermute | solution.py:299
  5.4 18.0 %collective-permute-start.3 = (bf16[2,8,4096]{2,1,0:T(8,128)(2,1)S(1)}, bf16[2,8,4096]{2,1,0:T(8,128)(2,1)S(1)}, u32[]{:S(2)}, u32[]{:S(2)}) collective-permute-start(bf16[2,8,4096]{2,1,0:T(8,128)(2,1)S(1)} %get-tuple-element.40), channel_id=1, source_target_pairs={{4,24},{12,16},{20,8},{28,0},{5,25},{13,17},{21,9},{29,1},{6,26},{... | collective-permute-start | bytes 393224 | tf_op jit(solution)/shard_map/ppermute | solution.py:299
  18.2 6.6 %collective-permute-start.4 = (bf16[2,8,4096]{2,1,0:T(8,128)(2,1)S(1)}, bf16[2,8,4096]{2,1,0:T(8,128)(2,1)S(1)}, u32[]{:S(2)}, u32[]{:S(2)}) collective-permute-start(bf16[2,8,4096]{2,1,0:T(8,128)(2,1)S(1)} %get-tuple-element.41), channel_id=1, source_target_pairs={{4,8},{12,0},{20,24},{28,16},{5,9},{13,1},{21,25},{29,17},{6,10},{... | collective-permute-start | bytes 393224 | tf_op jit(solution)/shard_map/ppermute | solution.py:299
  19.5 6.6 %collective-permute-start.5 = (bf16[2,8,4096]{2,1,0:T(8,128)(2,1)S(1)}, bf16[2,8,4096]{2,1,0:T(8,128)(2,1)S(1)}, u32[]{:S(2)}, u32[]{:S(2)}) collective-permute-start(bf16[2,8,4096]{2,1,0:T(8,128)(2,1)S(1)} %get-tuple-element.42), channel_id=1, source_target_pairs={{4,16},{12,24},{20,0},{28,8},{5,17},{13,25},{21,1},{29,9},{6,18},{... | collective-permute-start | bytes 393224 | tf_op jit(solution)/shard_map/ppermute | solution.py:299
  20.8 6.5 %collective-permute-start.6 = (bf16[2,8,4096]{2,1,0:T(8,128)(2,1)S(1)}, bf16[2,8,4096]{2,1,0:T(8,128)(2,1)S(1)}, u32[]{:S(2)}, u32[]{:S(2)}) collective-permute-start(bf16[2,8,4096]{2,1,0:T(8,128)(2,1)S(1)} %get-tuple-element.43), channel_id=1, source_target_pairs={{4,0},{12,8},{20,16},{28,24},{5,1},{13,9},{21,17},{29,25},{6,2},{1... | collective-permute-start | bytes 393224 | tf_op jit(solution)/shard_map/ppermute | solution.py:299
  22.1 11.7 %collective-permute-start.7 = (bf16[2,8,4096]{2,1,0:T(8,128)(2,1)S(1)}, bf16[2,8,4096]{2,1,0:T(8,128)(2,1)S(1)}, u32[]{:S(2)}, u32[]{:S(2)}) collective-permute-start(bf16[2,8,4096]{2,1,0:T(8,128)(2,1)S(1)} %get-tuple-element.40), channel_id=1, source_target_pairs={{0,28},{8,20},{16,12},{24,4},{1,29},{9,21},{17,13},{25,5},{2,30},{... | collective-permute-start | bytes 393224 | tf_op jit(solution)/shard_map/ppermute | solution.py:299
  23.4 13.5 %collective-permute-start.8 = (bf16[2,8,4096]{2,1,0:T(8,128)(2,1)S(1)}, bf16[2,8,4096]{2,1,0:T(8,128)(2,1)S(1)}, u32[]{:S(2)}, u32[]{:S(2)}) collective-permute-start(bf16[2,8,4096]{2,1,0:T(8,128)(2,1)S(1)} %get-tuple-element.41), channel_id=1, source_target_pairs={{0,12},{8,4},{16,28},{24,20},{1,13},{9,5},{17,29},{25,21},{2,14},{... | collective-permute-start | bytes 393224 | tf_op jit(solution)/shard_map/ppermute | solution.py:299
  24.7 15.3 %collective-permute-start.9 = (bf16[2,8,4096]{2,1,0:T(8,128)(2,1)S(1)}, bf16[2,8,4096]{2,1,0:T(8,128)(2,1)S(1)}, u32[]{:S(2)}, u32[]{:S(2)}) collective-permute-start(bf16[2,8,4096]{2,1,0:T(8,128)(2,1)S(1)} %get-tuple-element.42), channel_id=1, source_target_pairs={{0,20},{8,28},{16,4},{24,12},{1,21},{9,29},{17,5},{25,13},{2,22},{... | collective-permute-start | bytes 393224 | tf_op jit(solution)/shard_map/ppermute | solution.py:299
  26.0 14.7 %collective-permute-start.10 = (bf16[2,8,4096]{2,1,0:T(8,128)(2,1)S(1)}, bf16[2,8,4096]{2,1,0:T(8,128)(2,1)S(1)}, u32[]{:S(2)}, u32[]{:S(2)}) collective-permute-start(bf16[2,8,4096]{2,1,0:T(8,128)(2,1)S(1)} %get-tuple-element.43), channel_id=1, source_target_pairs={{0,4},{8,12},{16,20},{24,28},{1,5},{9,13},{17,21},{25,29},{2,6},{1... | collective-permute-start | bytes 393224 | tf_op jit(solution)/shard_map/ppermute | solution.py:299
  31.7 9.8 %collective-permute-start.11 = (bf16[2,8,4096]{2,1,0:T(8,128)(2,1)S(1)}, bf16[2,8,4096]{2,1,0:T(8,128)(2,1)S(1)}, u32[]{:S(2)}, u32[]{:S(2)}) collective-permute-start(bf16[2,8,4096]{2,1,0:T(8,128)(2,1)S(1)} %get-tuple-element.46), channel_id=1, source_target_pairs={{4,28},{12,20},{20,12},{28,4},{5,29},{13,21},{21,13},{29,5},{6,30}... | collective-permute-start | bytes 393224 | tf_op jit(solution)/shard_map/ppermute | solution.py:299
  33.8 8.3 %collective-permute-start.12 = (bf16[2,8,4096]{2,1,0:T(8,128)(2,1)S(1)}, bf16[2,8,4096]{2,1,0:T(8,128)(2,1)S(1)}, u32[]{:S(2)}, u32[]{:S(2)}) collective-permute-start(bf16[2,8,4096]{2,1,0:T(8,128)(2,1)S(1)} %get-tuple-element.47), channel_id=1, source_target_pairs={{4,12},{12,4},{20,28},{28,20},{5,13},{13,5},{21,29},{29,21},{6,14}... | collective-permute-start | bytes 393224 | tf_op jit(solution)/shard_map/ppermute | solution.py:299
  37.0 5.7 %collective-permute-start.13 = (bf16[2,8,4096]{2,1,0:T(8,128)(2,1)S(1)}, bf16[2,8,4096]{2,1,0:T(8,128)(2,1)S(1)}, u32[]{:S(2)}, u32[]{:S(2)}) collective-permute-start(bf16[2,8,4096]{2,1,0:T(8,128)(2,1)S(1)} %get-tuple-element.48), channel_id=1, source_target_pairs={{4,20},{12,28},{20,4},{28,12},{5,21},{13,29},{21,5},{29,13},{6,22}... | collective-permute-start | bytes 393224 | tf_op jit(solution)/shard_map/ppermute | solution.py:299
  40.1 12.3 %collective-permute-start.16 = (f32[16,128]{1,0:T(8,128)S(1)}, f32[16,128]{1,0:T(8,128)S(1)}, u32[]{:S(2)}, u32[]{:S(2)}) collective-permute-start(f32[16,128]{1,0:T(8,128)S(1)} %get-tuple-element.50.rest_0_), channel_id=1, source_target_pairs={{0,3},{1,0},{2,1},{3,2},{8,11},{9,8},{10,9},{11,10},{16,19},{17,16... | collective-permute-start | bytes 24584 | tf_op jit(solution)/shard_map/ppermute | solution.py:336
  40.8 14.0 %collective-permute-start.15 = (f32[16,128]{1,0:T(8,128)S(1)}, f32[16,128]{1,0:T(8,128)S(1)}, u32[]{:S(2)}, u32[]{:S(2)}) collective-permute-start(f32[16,128]{1,0:T(8,128)S(1)} %get-tuple-element.50.rest_0_), channel_id=1, source_target_pairs={{0,1},{1,2},{2,3},{3,0},{8,9},{9,10},{10,11},{11,8},{16,17},{17,18... | collective-permute-start | bytes 24584 | tf_op jit(solution)/shard_map/ppermute | solution.py:336
  41.4 13.3 %collective-permute-start.14 = (f32[16,128]{1,0:T(8,128)S(1)}, f32[16,128]{1,0:T(8,128)S(1)}, u32[]{:S(2)}, u32[]{:S(2)}) collective-permute-start(f32[16,128]{1,0:T(8,128)S(1)} %get-tuple-element.50.rest_0_), channel_id=1, source_target_pairs={{0,2},{1,3},{2,0},{3,1},{8,10},{9,11},{10,8},{11,9},{16,18},{17,19... | collective-permute-start | bytes 24584 | tf_op jit(solution)/shard_map/ppermute | solution.py:336
  45.2 9.6 %collective-permute-start.19 = (f32[16,128]{1,0:T(8,128)S(1)}, f32[16,128]{1,0:T(8,128)S(1)}, u32[]{:S(2)}, u32[]{:S(2)}) collective-permute-start(f32[16,128]{1,0:T(8,128)S(1)} %get-tuple-element.51.rest_4_), channel_id=1, source_target_pairs={{4,7},{5,4},{6,5},{7,6},{12,15},{13,12},{14,13},{15,14},{20,23},{2... | collective-permute-start | bytes 24584 | tf_op jit(solution)/shard_map/ppermute | solution.py:336
  50.5 6.2 %collective-permute-start.18 = (f32[16,128]{1,0:T(8,128)S(1)}, f32[16,128]{1,0:T(8,128)S(1)}, u32[]{:S(2)}, u32[]{:S(2)}) collective-permute-start(f32[16,128]{1,0:T(8,128)S(1)} %get-tuple-element.51.rest_4_), channel_id=1, source_target_pairs={{4,5},{5,6},{6,7},{7,4},{12,13},{13,14},{14,15},{15,12},{20,21},{2... | collective-permute-start | bytes 24584 | tf_op jit(solution)/shard_map/ppermute | solution.py:336
  61.4 6.7 %collective-permute-start.22 = (bf16[2,8,4096]{2,1,0:T(8,128)(2,1)S(1)}, bf16[2,8,4096]{2,1,0:T(8,128)(2,1)S(1)}, u32[]{:S(2)}, u32[]{:S(2)}) collective-permute-start(bf16[2,8,4096]{2,1,0:T(8,128)(2,1)S(1)} %get-tuple-element.57), channel_id=1, source_target_pairs={{0,16},{4,20},{8,24},{12,28},{16,0},{20,4},{24,8},{28,12},{1,17},{... | collective-permute-start | bytes 393224 | tf_op jit(solution)/shard_map/ppermute | solution.py:372
  61.7 6.8 %collective-permute-start.23 = (bf16[2,8,4096]{2,1,0:T(8,128)(2,1)S(1)}, bf16[2,8,4096]{2,1,0:T(8,128)(2,1)S(1)}, u32[]{:S(2)}, u32[]{:S(2)}) collective-permute-start(bf16[2,8,4096]{2,1,0:T(8,128)(2,1)S(1)} %get-tuple-element.58), channel_id=1, source_target_pairs={{0,28},{4,24},{8,20},{12,16},{16,12},{20,8},{24,4},{28,0},{1,29},{... | collective-permute-start | bytes 393224 | tf_op jit(solution)/shard_map/ppermute | solution.py:372
  61.7 9.4 %collective-permute-start.24 = (bf16[2,8,4096]{2,1,0:T(8,128)(2,1)S(1)}, bf16[2,8,4096]{2,1,0:T(8,128)(2,1)S(1)}, u32[]{:S(2)}, u32[]{:S(2)}) collective-permute-start(bf16[2,8,4096]{2,1,0:T(8,128)(2,1)S(1)} %get-tuple-element.59), channel_id=1, source_target_pairs={{0,12},{4,8},{8,4},{12,0},{16,28},{20,24},{24,20},{28,16},{1,13},{... | collective-permute-start | bytes 393224 | tf_op jit(solution)/shard_map/ppermute | solution.py:372
  64.3 6.8 %collective-permute-start.25 = (bf16[2,8,4096]{2,1,0:T(8,128)(2,1)S(1)}, bf16[2,8,4096]{2,1,0:T(8,128)(2,1)S(1)}, u32[]{:S(2)}, u32[]{:S(2)}) collective-permute-start(bf16[2,8,4096]{2,1,0:T(8,128)(2,1)S(1)} %get-tuple-element.60), channel_id=1, source_target_pairs={{0,20},{4,16},{8,28},{12,24},{16,4},{20,0},{24,12},{28,8},{1,21},{... | collective-permute-start | bytes 393224 | tf_op jit(solution)/shard_map/ppermute | solution.py:372
  65.5 5.7 %collective-permute-start.26 = (bf16[2,8,4096]{2,1,0:T(8,128)(2,1)S(1)}, bf16[2,8,4096]{2,1,0:T(8,128)(2,1)S(1)}, u32[]{:S(2)}, u32[]{:S(2)}) collective-permute-start(bf16[2,8,4096]{2,1,0:T(8,128)(2,1)S(1)} %get-tuple-element.61), channel_id=1, source_target_pairs={{0,4},{4,0},{8,12},{12,8},{16,20},{20,16},{24,28},{28,24},{1,5},{5... | collective-permute-start | bytes 393224 | tf_op jit(solution)/shard_map/ppermute | solution.py:372
  (11 other events, 73.6 us)

commit v6 on v4

--- a/solution.py
+++ b/solution.py
@@ -31,9 +31,10 @@
     return [pl.ds(at, step) for at in range(0, width, step)]
 
 
-def pack_kernel(paths, owned, order, me_ref, ids_ref, local_ref, places_ref, *rest):
-    pieces, (seen, sems) = rest[:paths], rest[paths:]
+def pack_kernel(owned, order, me_ref, ids_ref, local_ref, places_ref, *rest):
+    pieces, (seen, sems) = rest[:-2], rest[-2:]
     me = me_ref[0]
+    paths = len(order)
     for i in range(paths):
         seen[i] = jnp.int32(0)
     for i in range(paths * CAP):
@@ -44,11 +45,11 @@
         seen[group] = rank + 1
         places_ref[group * CAP + rank] = jnp.int32(k)
     copies = []
-    for d in order:
+    for d, piece in zip(order, pieces, strict=True):
         for r in range(CAP):
             k = jnp.maximum(places_ref[(me ^ d) * CAP + r], 0)
             copy = pltpu.make_async_copy(
-                local_ref.at[k], pieces[d].at[r], sems.at[d * CAP + r]
+                local_ref.at[k], piece.at[r], sems.at[d * CAP + r]
             )
             copy.start()
             copies.append(copy)
@@ -138,9 +139,9 @@
     )
 
 
-def combine_kernel(paths, me_ref, module_ref, weight_ref, total_ref, acc_in, *rest):
-    pieces, (acc_ref, squares_ref) = rest[: paths - 1], rest[paths - 1 :]
-    subtract(me_ref[0], pieces, range(1, paths), module_ref, weight_ref, acc_ref)
+def combine_kernel(order, me_ref, module_ref, weight_ref, total_ref, acc_in, *rest):
+    pieces, (acc_ref, squares_ref) = rest[:-2], rest[-2:]
+    subtract(me_ref[0], pieces, order, module_ref, weight_ref, acc_ref)
     owned, rows, width = acc_ref.shape
     for m in range(owned):
         inverse = 1.0 / jnp.maximum(jnp.full((rows, 128), total_ref[m], jnp.float32), 1.0)
@@ -158,7 +159,7 @@
     return inverse * factor
 
 
-def send_kernel(paths, shards, me_ref, module_ref, total_ref, acc_ref, base_ref, *rest):
+def send_kernel(order, shards, me_ref, module_ref, total_ref, acc_ref, base_ref, *rest):
     squares, (scale_ref, *pieces) = rest[:shards], rest[shards:]
     me = me_ref[0]
     owned, rows, width = acc_ref.shape
@@ -172,12 +173,12 @@
     for m in range(owned):
         scale_ref[m] = jnp.broadcast_to(scale[m : m + 1, :], (rows, 128))
     rate = outer_rate * (1.0 + outer_momentum)
-    for d in range(paths):
+    for d, piece in zip(order, pieces, strict=True):
         for r in range(CAP):
             m = module_ref[(me ^ d) * (CAP + 1) + r]
             step = rate * scale_ref[m][:, :1]
             for c in chunks(width):
-                pieces[d][r, :, c] = (base_ref[m, :, c] - step * acc_ref[m, :, c]).astype(
+                piece[r, :, c] = (base_ref[m, :, c] - step * acc_ref[m, :, c]).astype(
                     jnp.bfloat16
                 )
 
@@ -216,18 +217,18 @@
             copy.wait()
 
 
-def unpack_kernel(paths, me_ref, places_ref, *rest):
-    pieces, (out_ref, sems) = rest[:paths], rest[paths:]
+def unpack_kernel(order, me_ref, places_ref, *rest):
+    pieces, (out_ref, sems) = rest[:-2], rest[-2:]
     me = me_ref[0]
     for wait in (False, True):
-        for d in range(paths):
+        for d, piece in zip(order, pieces, strict=True):
             for r in range(CAP):
                 k = places_ref[(me ^ d) * CAP + r]
 
                 @pl.when(k >= 0)
                 def _():
                     copy = pltpu.make_async_copy(
-                        pieces[d].at[r], out_ref.at[0, k], sems.at[d * CAP + r]
+                        piece.at[r], out_ref.at[0, k], sems.at[d * CAP + r]
                     )
                     if wait:
                         copy.wait()
@@ -256,16 +257,17 @@
         pltpu.SemaphoreType.DMA((2, PARTS)),
     ]
     limits = pltpu.CompilerParams(vmem_limit_bytes=24 * 1024 * 1024)
-    order = sorted(range(1, paths), key=lambda d: (-(d // 2).bit_count(), d % 2, d))
+    far = sorted(range(2, paths, 2), key=lambda d: (-d.bit_count(), -d))
+    order = far + [d + 1 for d in far] + [1]
 
     def exchange(pieces):
-        moved = {
-            d: lax.ppermute(pieces[d], "path", [(i, i ^ d) for i in range(paths)]) for d in order
-        }
-        return [moved[d] for d in range(1, paths)]
+        return [
+            lax.ppermute(x, "path", [(i, i ^ d) for i in range(paths)])
+            for d, x in zip(order, pieces)
+        ]
 
     places, *packed = pl.pallas_call(
-        functools.partial(pack_kernel, paths, owned, [*order, 0]),
+        functools.partial(pack_kernel, owned, [*order, 0]),
         out_shape=[jax.ShapeDtypeStruct((slots,), jnp.int32)] + [piece] * paths,
         in_specs=[SMEM, SMEM, ANY],
         out_specs=[SMEM] + [VMEM] * paths,
@@ -283,9 +285,9 @@
         compiler_params=limits,
         cost_estimate=pl.CostEstimate(flops=10**6, bytes_accessed=12 * 2**20, transcendentals=0),
         name="early",
-    )(me, module_ids, counts, *in_vmem(packed[0]), *in_hbm(global_params, momentum))
+    )(me, module_ids, counts, *in_vmem(packed[-1]), *in_hbm(global_params, momentum))
     acc, squares = pl.pallas_call(
-        functools.partial(combine_kernel, paths),
+        functools.partial(combine_kernel, order),
         out_shape=[held_module, jax.ShapeDtypeStruct((owned, 128), jnp.float32)],
         in_specs=[SMEM] * 4 + [VMEM] * paths,
         out_specs=[VMEM] * 2,
@@ -298,14 +300,14 @@
         for d in sorted(range(1, shards), key=lambda d: (d != 2, d))
     ]
     scale, *outgoing = pl.pallas_call(
-        functools.partial(send_kernel, paths, shards),
+        functools.partial(send_kernel, [*order, 0], shards),
         out_shape=[jax.ShapeDtypeStruct((owned, rows, 128), jnp.float32)] + [piece] * paths,
         in_specs=[SMEM] * 3 + [VMEM] * (2 + shards),
         out_specs=[VMEM] * (1 + paths),
         compiler_params=limits,
         name="send",
     )(me, table, total, *in_vmem(acc, base), *parts)
-    returned = [outgoing[0], *exchange(outgoing)]
+    returned = [*exchange(outgoing), outgoing[-1]]
     updated, velocity = pl.pallas_call(
         store_kernel,
         out_shape=[module] * 2,
@@ -317,7 +319,7 @@
         name="store",
     )(scale, *in_vmem(acc, base), momentum)
     path_out = pl.pallas_call(
-        functools.partial(unpack_kernel, paths),
+        functools.partial(unpack_kernel, [*order, 0]),
         out_shape=jax.ShapeDtypeStruct(path_params.shape, path_params.dtype),
         in_specs=[SMEM] * 2 + [VMEM] * paths,
         out_specs=ANY,

time: 48 us -> 45.5 us (0.948)
  waiting for transfers between devices: 8.42 us -> 2.35 us
  starting transfers between devices: 25.9 us -> 29.5 us
    ppermute x14, waiting for transfers between devices: 7.39 us -> 1.31 us  [exchange(): lax.ppermute(x, 'path', [(i, i ^ d) for i in range(paths)])]
    ppermute x14, starting transfers between devices: 20.1 us -> 24.9 us  [exchange(): lax.ppermute(x, 'path', [(i, i ^ d) for i in range(paths)])]
    ppermute x3, starting transfers between devices: 5.86 us -> 4.6 us  [on_device(): lax.ppermute(squares, 'shard', [(i, (i + d) % shards) for i in range(shar...]
  transfers between devices with their start and end apart: 17 -> 17, of which waited for: 3 -> 2; matrix products, arithmetic and copies ran while one was open for 0% -> 0% of each run, Pallas kernels for 13% -> 14%
where the time goes in v6:
time: 45.5 us; the launch traced here: 45.2 us
  starting transfers between devices  29.5 us (65%)
  Pallas kernels  12.6 us (28%)
  waiting for transfers between devices  2.35 us (5%)
  between operations  0.76 us (2%)
    ppermute x14, starting transfers between devices, exchange(): lax.ppermute(x, 'path', [(i, i ^ d) for i in range(paths)])  24.9 us
    ppermute x3, starting transfers between devices, on_device(): lax.ppermute(squares, 'shard', [(i, (i + d) % shards) for i in range(shar...  4.6 us
    pallas_call x1, Pallas kernels, on_device(): pl.pallas_call(early_kernel, out_shape=tables + [held_module] * 2, in_spe...  3.7 us
    pallas_call x1, Pallas kernels, on_device(): pl.pallas_call(functools.partial(pack_kernel, owned, [*order, 0]), out_sh...  2.72 us
    pallas_call x1, Pallas kernels, on_device(): pl.pallas_call(store_kernel, out_shape=[module] * 2, in_specs=[VMEM] * 4,...  2.52 us
    pallas_call x1, Pallas kernels, on_device(): pl.pallas_call(functools.partial(unpack_kernel, [*order, 0]), out_shape=j...  1.76 us
    ppermute x14, waiting for transfers between devices, exchange(): lax.ppermute(x, 'path', [(i, i ^ d) for i in range(paths)])  1.31 us
    ppermute x3, waiting for transfers between devices, on_device(): lax.ppermute(squares, 'shard', [(i, (i + d) % shards) for i in range(shar...  1.04 us
  transfers between devices with their start and end apart: 17, of which 2 were waited for; matrix products, arithmetic and copies ran while one was open for 0% of the time, Pallas kernels for 14%

profile of v6, /device:TPU:1, one launch (start us, length us, event | category | flops | bytes accessed | tf_op | source)
XLA Modules:
  0.0 45.2 jit_solution(18404273686802875779)
XLA Ops:
  0.6 2.7 %pack.1 = (s32[16]{0:T(128)}, bf16[2,8,4096]{2,1,0:T(8,128)(2,1)S(1)}, bf16[2,8,4096]{2,1,0:T(8,128)(2,1)S(1)}, bf16[2,8,4096]{2,1,0:T(8,128)(2,1)S(1)}, bf16[2,...) custom-call(s32[1]{0:T(128)} %bitcast.me_ref, ...), custom_call_target="tpu_custom_call" | custom-call | tf_op jit(solution)/shard_map/pack/pallas_call | solution.py:269
  3.4 3.1 %collective-permute-start = (bf16[2,8,4096]{2,1,0:T(8,128)(2,1)S(1)}, bf16[2,8,4096]{2,1,0:T(8,128)(2,1)S(1)}, u32[]{:S(2)}, u32[]{:S(2)}) collective-permute-start(bf16[2,8,4096]{2,1,0:T(8,128)(2,1)S(1)} %get-tuple-element.35), channel_id=1, source_target_pairs={{0,24},{4,28},{8,16},{12,20},{16,8},{20,12},{24,0},{28,4},{1,25},{... | collective-permute-start | bytes 393224 | tf_op jit(solution)/shard_map/ppermute | solution.py:265
  6.4 0.2 collective-permute-start.1
  6.6 0.1 collective-permute-start.2
  6.8 3.7 %collective-permute-start.3 = (bf16[2,8,4096]{2,1,0:T(8,128)(2,1)S(1)}, bf16[2,8,4096]{2,1,0:T(8,128)(2,1)S(1)}, u32[]{:S(2)}, u32[]{:S(2)}) collective-permute-start(bf16[2,8,4096]{2,1,0:T(8,128)(2,1)S(1)} %get-tuple-element.38), channel_id=1, source_target_pairs={{0,28},{4,24},{8,20},{12,16},{16,12},{20,8},{24,4},{28,0},{1,29},{... | collective-permute-start | bytes 393224 | tf_op jit(solution)/shard_map/ppermute | solution.py:265
  10.5 0.0 collective-permute-start.4
  10.5 0.0 collective-permute-done.rest_0_
  10.5 2.8 %collective-permute-start.5 = (bf16[2,8,4096]{2,1,0:T(8,128)(2,1)S(1)}, bf16[2,8,4096]{2,1,0:T(8,128)(2,1)S(1)}, u32[]{:S(2)}, u32[]{:S(2)}) collective-permute-start(bf16[2,8,4096]{2,1,0:T(8,128)(2,1)S(1)} %get-tuple-element.40), channel_id=1, source_target_pairs={{0,12},{4,8},{8,4},{12,0},{16,28},{20,24},{24,20},{28,16},{1,13},{... | collective-permute-start | bytes 393224 | tf_op jit(solution)/shard_map/ppermute | solution.py:265
  13.3 1.3 %collective-permute-done.1.rest_1_ = bf16[2,8,4096]{2,1,0:T(8,128)(2,1)S(1)} collective-permute-done((bf16[2,8,4096]{2,1,0:T(8,128)(2,1)S(1)}, bf16[2,8,4096]{2,1,0:T(8,128)(2,1)S(1)}, u32[]{:S(2)}, u32[]{:S(2)}) %collective-permute-start.1) | collective-permute-done | bytes 131104 | tf_op jit(solution)/shard_map/ppermute | solution.py:265
  14.6 1.8 %collective-permute-start.6 = (bf16[2,8,4096]{2,1,0:T(8,128)(2,1)S(1)}, bf16[2,8,4096]{2,1,0:T(8,128)(2,1)S(1)}, u32[]{:S(2)}, u32[]{:S(2)}) collective-permute-start(bf16[2,8,4096]{2,1,0:T(8,128)(2,1)S(1)} %get-tuple-element.41), channel_id=1, source_target_pairs={{0,4},{4,0},{8,12},{12,8},{16,20},{20,16},{24,28},{28,24},{1,5},{5... | collective-permute-start | bytes 393224 | tf_op jit(solution)/shard_map/ppermute | solution.py:265
  16.4 3.7 %early.1 = (s32[24]{0:T(128)S(1)}, f32[24]{0:T(128)S(1)}, f32[16]{0:T(128)S(1)}, f32[16,8,4096]{2,1,0:T(8,128)S(1)}, f32[16,8,4096]{2,1,0:T(8,128)S(1)}) custom-call(s32[1]{0:T(128)} %bitcast.me_ref, s32[8,16]{1,0:T(8,128)} %ids_ref.3, s32[8,16]{1,0:T(8,128)} %counts_ref.1, bf16[2,8,4096]{2,1,0:T(8,128)(2,1)S(1)} %get-tuple-element.30.own_ref, ...), custom_call_target="tpu_custom_call" | custom-call | flops 1000000 | bytes 12582912 | tf_op jit(solution)/shard_map/early/pallas_call | solution.py:279
  20.2 1.0 %combine.1 = (f32[16,8,4096]{2,1,0:T(8,128)S(1)}, f32[16,128]{1,0:T(8,128)S(1)}) custom-call(s32[1]{0:T(128)} %bitcast.me_ref, s32[24]{0:T(128)S(1)} %get-tuple-element.31.module_ref, f32[24]{0:T(128)S(1)} %get-tuple-element.33.weight_ref, f32[16]{0:T(128)S(1)} %get-tuple-element.32.total_ref, ...), custom_call_target="tpu_custom_call", output_to_operand_aliasing={{0}: (4, {})} | custom-call | tf_op jit(solution)/shard_map/combine/pallas_call | solution.py:289
  21.2 1.3 %collective-permute-start.7 = (f32[16,128]{1,0:T(8,128)S(1)}, f32[16,128]{1,0:T(8,128)S(1)}, u32[]{:S(2)}, u32[]{:S(2)}) collective-permute-start(f32[16,128]{1,0:T(8,128)S(1)} %get-tuple-element.44.rest_0_), channel_id=1, source_target_pairs={{0,2},{1,3},{2,0},{3,1},{4,6},{5,7},{6,4},{7,5},{8,10},{9,11},{10,... | collective-permute-start | bytes 24584 | tf_op jit(solution)/shard_map/ppermute | solution.py:299
  22.5 1.3 %collective-permute-start.8 = (f32[16,128]{1,0:T(8,128)S(1)}, f32[16,128]{1,0:T(8,128)S(1)}, u32[]{:S(2)}, u32[]{:S(2)}) collective-permute-start(f32[16,128]{1,0:T(8,128)S(1)} %get-tuple-element.44.rest_0_), channel_id=1, source_target_pairs={{0,1},{1,2},{2,3},{3,0},{4,5},{5,6},{6,7},{7,4},{8,9},{9,10},{10,1... | collective-permute-start | bytes 24584 | tf_op jit(solution)/shard_map/ppermute | solution.py:299
  23.8 2.0 %collective-permute-start.9 = (f32[16,128]{1,0:T(8,128)S(1)}, f32[16,128]{1,0:T(8,128)S(1)}, u32[]{:S(2)}, u32[]{:S(2)}) collective-permute-start(f32[16,128]{1,0:T(8,128)S(1)} %get-tuple-element.44.rest_0_), channel_id=1, source_target_pairs={{0,3},{1,0},{2,1},{3,2},{4,7},{5,4},{6,5},{7,6},{8,11},{9,8},{10,9... | collective-permute-start | bytes 24584 | tf_op jit(solution)/shard_map/ppermute | solution.py:299
  25.8 1.0 %collective-permute-done.8.rest_2_ = f32[16,128]{1,0:T(8,128)S(1)} collective-permute-done((f32[16,128]{1,0:T(8,128)S(1)}, f32[16,128]{1,0:T(8,128)S(1)}, u32[]{:S(2)}, u32[]{:S(2)}) %collective-permute-start.8) | collective-permute-done | bytes 8224 | tf_op jit(solution)/shard_map/ppermute | solution.py:299
  26.8 0.9 %send.1 = (f32[16,8,128]{2,1,0:T(8,128)S(1)}, bf16[2,8,4096]{2,1,0:T(8,128)(2,1)S(1)}, bf16[2,8,4096]{2,1,0:T(8,128)(2,1)S(1)}, bf16[2,8,4096]{2,1,0:T(8,128)(2,...) custom-call(s32[1]{0:T(128)} %bitcast.me_ref, ...), custom_call_target="tpu_custom_call" | custom-call | tf_op jit(solution)/shard_map/send/pallas_call | solution.py:302
  27.7 2.7 %collective-permute-start.10 = (bf16[2,8,4096]{2,1,0:T(8,128)(2,1)S(1)}, bf16[2,8,4096]{2,1,0:T(8,128)(2,1)S(1)}, u32[]{:S(2)}, u32[]{:S(2)}) collective-permute-start(bf16[2,8,4096]{2,1,0:T(8,128)(2,1)S(1)} %get-tuple-element.49), channel_id=1, source_target_pairs={{0,24},{4,28},{8,16},{12,20},{16,8},{20,12},{24,0},{28,4},{1,25},{... | collective-permute-start | bytes 393224 | tf_op jit(solution)/shard_map/ppermute | solution.py:265
  30.4 0.4 collective-permute-start.12
  30.8 4.4 %collective-permute-start.13 = (bf16[2,8,4096]{2,1,0:T(8,128)(2,1)S(1)}, bf16[2,8,4096]{2,1,0:T(8,128)(2,1)S(1)}, u32[]{:S(2)}, u32[]{:S(2)}) collective-permute-start(bf16[2,8,4096]{2,1,0:T(8,128)(2,1)S(1)} %get-tuple-element.52), channel_id=1, source_target_pairs={{0,28},{4,24},{8,20},{12,16},{16,12},{20,8},{24,4},{28,0},{1,29},{... | collective-permute-start | bytes 393224 | tf_op jit(solution)/shard_map/ppermute | solution.py:265
  35.2 2.3 %collective-permute-start.15 = (bf16[2,8,4096]{2,1,0:T(8,128)(2,1)S(1)}, bf16[2,8,4096]{2,1,0:T(8,128)(2,1)S(1)}, u32[]{:S(2)}, u32[]{:S(2)}) collective-permute-start(bf16[2,8,4096]{2,1,0:T(8,128)(2,1)S(1)} %get-tuple-element.54), channel_id=1, source_target_pairs={{0,12},{4,8},{8,4},{12,0},{16,28},{20,24},{24,20},{28,16},{1,13},{... | collective-permute-start | bytes 393224 | tf_op jit(solution)/shard_map/ppermute | solution.py:265
  37.4 3.4 %collective-permute-start.16 = (bf16[2,8,4096]{2,1,0:T(8,128)(2,1)S(1)}, bf16[2,8,4096]{2,1,0:T(8,128)(2,1)S(1)}, u32[]{:S(2)}, u32[]{:S(2)}) collective-permute-start(bf16[2,8,4096]{2,1,0:T(8,128)(2,1)S(1)} %get-tuple-element.55), channel_id=1, source_target_pairs={{0,4},{4,0},{8,12},{12,8},{16,20},{20,16},{24,28},{28,24},{1,5},{5... | collective-permute-start | bytes 393224 | tf_op jit(solution)/shard_map/ppermute | solution.py:265
  40.9 2.5 %store.1 = (f32[16,8,4096]{2,1,0:T(8,128)}, f32[16,8,4096]{2,1,0:T(8,128)}) custom-call(f32[16,8,128]{2,1,0:T(8,128)S(1)} %get-tuple-element.45.scale_ref, f32[16,8,4096]{2,1,0:T(8,128)S(1)} %get-tuple-element.42.acc_ref, f32[16,8,4096]{2,1,0:T(8,128)S(1)} %get-tuple-element.43.base_ref, f32[16,8,4096]{2,1,0:T(8,128)S(1)} %copy-done), custom_call_target="tpu_custom_call" | custom-call | flops 1000000 | bytes 12582912 | tf_op jit(solution)/shard_map/store/pallas_call | solution.py:311
  43.5 1.8 %unpack.1 = bf16[1,16,8,4096]{3,2,1,0:T(8,128)(2,1)} custom-call(s32[1]{0:T(128)} %bitcast.me_ref, s32[16]{0:T(128)} %get-tuple-element.48.places_ref, bf16[2,8,4096]{2,1,0:T(8,128)(2,1)S(1)} %collective-permute-done.10.rest_0_, bf16[2,8,4096]{2,1,0:T(8,128)(2,1)S(1)} %collective-permute-done.11.rest_1_, ...), custom_call_target="tpu_custom_call" | custom-call | tf_op jit(solution)/shard_map/unpack/pallas_call | solution.py:321
  (18 shorter events, 0.0 us)
Async XLA Ops:
  3.4 7.1 %collective-permute-start = (bf16[2,8,4096]{2,1,0:T(8,128)(2,1)S(1)}, bf16[2,8,4096]{2,1,0:T(8,128)(2,1)S(1)}, u32[]{:S(2)}, u32[]{:S(2)}) collective-permute-start(bf16[2,8,4096]{2,1,0:T(8,128)(2,1)S(1)} %get-tuple-element.35), channel_id=1, source_target_pairs={{0,24},{4,28},{8,16},{12,20},{16,8},{20,12},{24,0},{28,4},{1,25},{... | collective-permute-start | bytes 393224 | tf_op jit(solution)/shard_map/ppermute | solution.py:265
  6.4 8.2 %collective-permute-start.1 = (bf16[2,8,4096]{2,1,0:T(8,128)(2,1)S(1)}, bf16[2,8,4096]{2,1,0:T(8,128)(2,1)S(1)}, u32[]{:S(2)}, u32[]{:S(2)}) collective-permute-start(bf16[2,8,4096]{2,1,0:T(8,128)(2,1)S(1)} %get-tuple-element.36), channel_id=1, source_target_pairs={{0,16},{4,20},{8,24},{12,28},{16,0},{20,4},{24,8},{28,12},{1,17},{... | collective-permute-start | bytes 393224 | tf_op jit(solution)/shard_map/ppermute | solution.py:265
  6.6 13.5 %collective-permute-start.2 = (bf16[2,8,4096]{2,1,0:T(8,128)(2,1)S(1)}, bf16[2,8,4096]{2,1,0:T(8,128)(2,1)S(1)}, u32[]{:S(2)}, u32[]{:S(2)}) collective-permute-start(bf16[2,8,4096]{2,1,0:T(8,128)(2,1)S(1)} %get-tuple-element.37), channel_id=1, source_target_pairs={{0,8},{4,12},{8,0},{12,4},{16,24},{20,28},{24,16},{28,20},{1,9},{5... | collective-permute-start | bytes 393224 | tf_op jit(solution)/shard_map/ppermute | solution.py:265
  6.8 13.4 %collective-permute-start.3 = (bf16[2,8,4096]{2,1,0:T(8,128)(2,1)S(1)}, bf16[2,8,4096]{2,1,0:T(8,128)(2,1)S(1)}, u32[]{:S(2)}, u32[]{:S(2)}) collective-permute-start(bf16[2,8,4096]{2,1,0:T(8,128)(2,1)S(1)} %get-tuple-element.38), channel_id=1, source_target_pairs={{0,28},{4,24},{8,20},{12,16},{16,12},{20,8},{24,4},{28,0},{1,29},{... | collective-permute-start | bytes 393224 | tf_op jit(solution)/shard_map/ppermute | solution.py:265
  10.5 9.7 %collective-permute-start.4 = (bf16[2,8,4096]{2,1,0:T(8,128)(2,1)S(1)}, bf16[2,8,4096]{2,1,0:T(8,128)(2,1)S(1)}, u32[]{:S(2)}, u32[]{:S(2)}) collective-permute-start(bf16[2,8,4096]{2,1,0:T(8,128)(2,1)S(1)} %get-tuple-element.39), channel_id=1, source_target_pairs={{0,20},{4,16},{8,28},{12,24},{16,4},{20,0},{24,12},{28,8},{1,21},{... | collective-permute-start | bytes 393224 | tf_op jit(solution)/shard_map/ppermute | solution.py:265
  10.5 9.7 %collective-permute-start.5 = (bf16[2,8,4096]{2,1,0:T(8,128)(2,1)S(1)}, bf16[2,8,4096]{2,1,0:T(8,128)(2,1)S(1)}, u32[]{:S(2)}, u32[]{:S(2)}) collective-permute-start(bf16[2,8,4096]{2,1,0:T(8,128)(2,1)S(1)} %get-tuple-element.40), channel_id=1, source_target_pairs={{0,12},{4,8},{8,4},{12,0},{16,28},{20,24},{24,20},{28,16},{1,13},{... | collective-permute-start | bytes 393224 | tf_op jit(solution)/shard_map/ppermute | solution.py:265
  14.6 5.6 %collective-permute-start.6 = (bf16[2,8,4096]{2,1,0:T(8,128)(2,1)S(1)}, bf16[2,8,4096]{2,1,0:T(8,128)(2,1)S(1)}, u32[]{:S(2)}, u32[]{:S(2)}) collective-permute-start(bf16[2,8,4096]{2,1,0:T(8,128)(2,1)S(1)} %get-tuple-element.41), channel_id=1, source_target_pairs={{0,4},{4,0},{8,12},{12,8},{16,20},{20,16},{24,28},{28,24},{1,5},{5... | collective-permute-start | bytes 393224 | tf_op jit(solution)/shard_map/ppermute | solution.py:265
  21.2 4.6 %collective-permute-start.7 = (f32[16,128]{1,0:T(8,128)S(1)}, f32[16,128]{1,0:T(8,128)S(1)}, u32[]{:S(2)}, u32[]{:S(2)}) collective-permute-start(f32[16,128]{1,0:T(8,128)S(1)} %get-tuple-element.44.rest_0_), channel_id=1, source_target_pairs={{0,2},{1,3},{2,0},{3,1},{4,6},{5,7},{6,4},{7,5},{8,10},{9,11},{10,... | collective-permute-start | bytes 24584 | tf_op jit(solution)/shard_map/ppermute | solution.py:299
  22.5 4.3 %collective-permute-start.8 = (f32[16,128]{1,0:T(8,128)S(1)}, f32[16,128]{1,0:T(8,128)S(1)}, u32[]{:S(2)}, u32[]{:S(2)}) collective-permute-start(f32[16,128]{1,0:T(8,128)S(1)} %get-tuple-element.44.rest_0_), channel_id=1, source_target_pairs={{0,1},{1,2},{2,3},{3,0},{4,5},{5,6},{6,7},{7,4},{8,9},{9,10},{10,1... | collective-permute-start | bytes 24584 | tf_op jit(solution)/shard_map/ppermute | solution.py:299
  23.8 3.0 %collective-permute-start.9 = (f32[16,128]{1,0:T(8,128)S(1)}, f32[16,128]{1,0:T(8,128)S(1)}, u32[]{:S(2)}, u32[]{:S(2)}) collective-permute-start(f32[16,128]{1,0:T(8,128)S(1)} %get-tuple-element.44.rest_0_), channel_id=1, source_target_pairs={{0,3},{1,0},{2,1},{3,2},{4,7},{5,4},{6,5},{7,6},{8,11},{9,8},{10,9... | collective-permute-start | bytes 24584 | tf_op jit(solution)/shard_map/ppermute | solution.py:299
  26.8 14.1 %copy-start = (f32[16,8,4096]{2,1,0:T(8,128)S(1)}, f32[16,8,4096]{2,1,0:T(8,128)}, u32[]{:S(2)}) copy-start(f32[16,8,4096]{2,1,0:T(8,128)} %past_ref.1) | copy-start | bytes 6291460
  27.7 7.4 %collective-permute-start.10 = (bf16[2,8,4096]{2,1,0:T(8,128)(2,1)S(1)}, bf16[2,8,4096]{2,1,0:T(8,128)(2,1)S(1)}, u32[]{:S(2)}, u32[]{:S(2)}) collective-permute-start(bf16[2,8,4096]{2,1,0:T(8,128)(2,1)S(1)} %get-tuple-element.49), channel_id=1, source_target_pairs={{0,24},{4,28},{8,16},{12,20},{16,8},{20,12},{24,0},{28,4},{1,25},{... | collective-permute-start | bytes 393224 | tf_op jit(solution)/shard_map/ppermute | solution.py:265
  30.4 7.0 %collective-permute-start.11 = (bf16[2,8,4096]{2,1,0:T(8,128)(2,1)S(1)}, bf16[2,8,4096]{2,1,0:T(8,128)(2,1)S(1)}, u32[]{:S(2)}, u32[]{:S(2)}) collective-permute-start(bf16[2,8,4096]{2,1,0:T(8,128)(2,1)S(1)} %get-tuple-element.50), channel_id=1, source_target_pairs={{0,16},{4,20},{8,24},{12,28},{16,0},{20,4},{24,8},{28,12},{1,17},{... | collective-permute-start | bytes 393224 | tf_op jit(solution)/shard_map/ppermute | solution.py:265
  30.4 13.0 %collective-permute-start.12 = (bf16[2,8,4096]{2,1,0:T(8,128)(2,1)S(1)}, bf16[2,8,4096]{2,1,0:T(8,128)(2,1)S(1)}, u32[]{:S(2)}, u32[]{:S(2)}) collective-permute-start(bf16[2,8,4096]{2,1,0:T(8,128)(2,1)S(1)} %get-tuple-element.51), channel_id=1, source_target_pairs={{0,8},{4,12},{8,0},{12,4},{16,24},{20,28},{24,16},{28,20},{1,9},{5... | collective-permute-start | bytes 393224 | tf_op jit(solution)/shard_map/ppermute | solution.py:265
  30.8 12.6 %collective-permute-start.13 = (bf16[2,8,4096]{2,1,0:T(8,128)(2,1)S(1)}, bf16[2,8,4096]{2,1,0:T(8,128)(2,1)S(1)}, u32[]{:S(2)}, u32[]{:S(2)}) collective-permute-start(bf16[2,8,4096]{2,1,0:T(8,128)(2,1)S(1)} %get-tuple-element.52), channel_id=1, source_target_pairs={{0,28},{4,24},{8,20},{12,16},{16,12},{20,8},{24,4},{28,0},{1,29},{... | collective-permute-start | bytes 393224 | tf_op jit(solution)/shard_map/ppermute | solution.py:265
  35.2 8.3 %collective-permute-start.14 = (bf16[2,8,4096]{2,1,0:T(8,128)(2,1)S(1)}, bf16[2,8,4096]{2,1,0:T(8,128)(2,1)S(1)}, u32[]{:S(2)}, u32[]{:S(2)}) collective-permute-start(bf16[2,8,4096]{2,1,0:T(8,128)(2,1)S(1)} %get-tuple-element.53), channel_id=1, source_target_pairs={{0,20},{4,16},{8,28},{12,24},{16,4},{20,0},{24,12},{28,8},{1,21},{... | collective-permute-start | bytes 393224 | tf_op jit(solution)/shard_map/ppermute | solution.py:265
  35.2 8.3 %collective-permute-start.15 = (bf16[2,8,4096]{2,1,0:T(8,128)(2,1)S(1)}, bf16[2,8,4096]{2,1,0:T(8,128)(2,1)S(1)}, u32[]{:S(2)}, u32[]{:S(2)}) collective-permute-start(bf16[2,8,4096]{2,1,0:T(8,128)(2,1)S(1)} %get-tuple-element.54), channel_id=1, source_target_pairs={{0,12},{4,8},{8,4},{12,0},{16,28},{20,24},{24,20},{28,16},{1,13},{... | collective-permute-start | bytes 393224 | tf_op jit(solution)/shard_map/ppermute | solution.py:265
  37.4 6.0 %collective-permute-start.16 = (bf16[2,8,4096]{2,1,0:T(8,128)(2,1)S(1)}, bf16[2,8,4096]{2,1,0:T(8,128)(2,1)S(1)}, u32[]{:S(2)}, u32[]{:S(2)}) collective-permute-start(bf16[2,8,4096]{2,1,0:T(8,128)(2,1)S(1)} %get-tuple-element.55), channel_id=1, source_target_pairs={{0,4},{4,0},{8,12},{12,8},{16,20},{20,16},{24,28},{28,24},{1,5},{5... | collective-permute-start | bytes 393224 | tf_op jit(solution)/shard_map/ppermute | solution.py:265

commit v7 on v6

--- a/solution.py
+++ b/solution.py
@@ -22,6 +22,10 @@
     return [pltpu.with_memory_space_constraint(x, pltpu.VMEM) for x in arrays]
 
 
+def in_smem(*arrays):
+    return [pltpu.with_memory_space_constraint(x, pltpu.SMEM) for x in arrays]
+
+
 def in_hbm(*arrays):
     return [pltpu.with_memory_space_constraint(x, pltpu.HBM) for x in arrays]
 
@@ -31,9 +35,9 @@
     return [pl.ds(at, step) for at in range(0, width, step)]
 
 
-def pack_kernel(owned, order, me_ref, ids_ref, local_ref, places_ref, *rest):
+def pack_kernel(owned, order, ids_ref, local_ref, places_ref, *rest):
     pieces, (seen, sems) = rest[:-2], rest[-2:]
-    me = me_ref[0]
+    me = lax.axis_index("path").astype(jnp.int32)
     paths = len(order)
     for i in range(paths):
         seen[i] = jnp.int32(0)
@@ -128,10 +132,10 @@
 
 
 def early_kernel(
-    me_ref, ids_ref, counts_ref, own_ref, params_hbm, past_hbm,
+    ids_ref, counts_ref, own_ref, params_hbm, past_hbm,
     module_ref, weight_ref, total_ref, acc_ref, base_ref, params_ref, past_ref, sems,
 ):
-    me = me_ref[0]
+    me = lax.axis_index("path").astype(jnp.int32)
     tables = module_ref, weight_ref, total_ref
     find = functools.partial(find_slots, me, acc_ref.shape[0], ids_ref, counts_ref, *tables)
     prepare(
@@ -139,9 +143,10 @@
     )
 
 
-def combine_kernel(order, me_ref, module_ref, weight_ref, total_ref, acc_in, *rest):
+def combine_kernel(order, module_ref, weight_ref, total_ref, acc_in, *rest):
     pieces, (acc_ref, squares_ref) = rest[:-2], rest[-2:]
-    subtract(me_ref[0], pieces, order, module_ref, weight_ref, acc_ref)
+    me = lax.axis_index("path").astype(jnp.int32)
+    subtract(me, pieces, order, module_ref, weight_ref, acc_ref)
     owned, rows, width = acc_ref.shape
     for m in range(owned):
         inverse = 1.0 / jnp.maximum(jnp.full((rows, 128), total_ref[m], jnp.float32), 1.0)
@@ -159,9 +164,9 @@
     return inverse * factor
 
 
-def send_kernel(order, shards, me_ref, module_ref, total_ref, acc_ref, base_ref, *rest):
+def send_kernel(order, shards, module_ref, total_ref, acc_ref, base_ref, *rest):
     squares, (scale_ref, *pieces) = rest[:shards], rest[shards:]
-    me = me_ref[0]
+    me = lax.axis_index("path").astype(jnp.int32)
     owned, rows, width = acc_ref.shape
     summed = squares[0][...]
     for other in squares[1:]:
@@ -217,9 +222,9 @@
             copy.wait()
 
 
-def unpack_kernel(order, me_ref, places_ref, *rest):
+def unpack_kernel(order, places_ref, *rest):
     pieces, (out_ref, sems) = rest[:-2], rest[-2:]
-    me = me_ref[0]
+    me = lax.axis_index("path").astype(jnp.int32)
     for wait in (False, True):
         for d, piece in zip(order, pieces, strict=True):
             for r in range(CAP):
@@ -240,16 +245,15 @@
     paths, held = module_ids.shape
     owned, rows, width = global_params.shape
     shards = lax.axis_size("shard")
-    me = lax.axis_index("path").astype(jnp.int32).reshape(1)
     module_ids, counts = in_hbm(module_ids, token_counts)
     slots = paths * CAP
     piece = pltpu.VMEM((CAP, rows, width), jnp.bfloat16)
     module = jax.ShapeDtypeStruct((owned, rows, width), jnp.float32)
     held_module = pltpu.VMEM(module.shape, module.dtype)
     tables = [
-        jax.ShapeDtypeStruct((paths * (CAP + 1),), jnp.int32),
-        jax.ShapeDtypeStruct((paths * (CAP + 1),), jnp.float32),
-        jax.ShapeDtypeStruct((owned,), jnp.float32),
+        pltpu.SMEM((paths * (CAP + 1),), jnp.int32),
+        pltpu.SMEM((paths * (CAP + 1),), jnp.float32),
+        pltpu.SMEM((owned,), jnp.float32),
     ]
     room = [
         pltpu.VMEM(module.shape, module.dtype),
@@ -258,7 +262,7 @@
     ]
     limits = pltpu.CompilerParams(vmem_limit_bytes=24 * 1024 * 1024)
     far = sorted(range(2, paths, 2), key=lambda d: (-d.bit_count(), -d))
-    order = far + [d + 1 for d in far] + [1]
+    order = far + [d + 1 for d in far[::-1]] + [1]
 
     def exchange(pieces):
         return [
@@ -268,33 +272,33 @@
 
     places, *packed = pl.pallas_call(
         functools.partial(pack_kernel, owned, [*order, 0]),
-        out_shape=[jax.ShapeDtypeStruct((slots,), jnp.int32)] + [piece] * paths,
-        in_specs=[SMEM, SMEM, ANY],
+        out_shape=[pltpu.SMEM((slots,), jnp.int32)] + [piece] * paths,
+        in_specs=[SMEM, ANY],
         out_specs=[SMEM] + [VMEM] * paths,
         scratch_shapes=[pltpu.SMEM((paths,), jnp.int32), pltpu.SemaphoreType.DMA((slots,))],
         name="pack",
-    )(me, module_ids, *in_hbm(path_params.reshape(held, rows, width)))
+    )(module_ids, *in_hbm(path_params.reshape(held, rows, width)))
 
     arrived = exchange(packed)
     table, weights, total, acc, base = pl.pallas_call(
         early_kernel,
         out_shape=tables + [held_module] * 2,
-        in_specs=[SMEM] * 3 + [VMEM] + [ANY] * 2,
+        in_specs=[SMEM] * 2 + [VMEM] + [ANY] * 2,
         out_specs=[SMEM] * 3 + [VMEM] * 2,
         scratch_shapes=room,
         compiler_params=limits,
         cost_estimate=pl.CostEstimate(flops=10**6, bytes_accessed=12 * 2**20, transcendentals=0),
         name="early",
-    )(me, module_ids, counts, *in_vmem(packed[-1]), *in_hbm(global_params, momentum))
+    )(module_ids, counts, *in_vmem(packed[-1]), *in_hbm(global_params, momentum))
     acc, squares = pl.pallas_call(
         functools.partial(combine_kernel, order),
         out_shape=[held_module, jax.ShapeDtypeStruct((owned, 128), jnp.float32)],
-        in_specs=[SMEM] * 4 + [VMEM] * paths,
+        in_specs=[SMEM] * 3 + [VMEM] * paths,
         out_specs=[VMEM] * 2,
-        input_output_aliases={4: 0},
+        input_output_aliases={3: 0},
         compiler_params=limits,
         name="combine",
-    )(me, table, weights, total, *in_vmem(acc, *arrived))
+    )(*in_smem(table, weights, total), *in_vmem(acc, *arrived))
     parts = [squares] + [
         lax.ppermute(squares, "shard", [(i, (i + d) % shards) for i in range(shards)])
         for d in sorted(range(1, shards), key=lambda d: (d != 2, d))
@@ -302,11 +306,11 @@
     scale, *outgoing = pl.pallas_call(
         functools.partial(send_kernel, [*order, 0], shards),
         out_shape=[jax.ShapeDtypeStruct((owned, rows, 128), jnp.float32)] + [piece] * paths,
-        in_specs=[SMEM] * 3 + [VMEM] * (2 + shards),
+        in_specs=[SMEM] * 2 + [VMEM] * (2 + shards),
         out_specs=[VMEM] * (1 + paths),
         compiler_params=limits,
         name="send",
-    )(me, table, total, *in_vmem(acc, base), *parts)
+    )(*in_smem(table, total), *in_vmem(acc, base), *parts)
     returned = [*exchange(outgoing), outgoing[-1]]
     updated, velocity = pl.pallas_call(
         store_kernel,
@@ -321,11 +325,11 @@
     path_out = pl.pallas_call(
         functools.partial(unpack_kernel, [*order, 0]),
         out_shape=jax.ShapeDtypeStruct(path_params.shape, path_params.dtype),
-        in_specs=[SMEM] * 2 + [VMEM] * paths,
+        in_specs=[SMEM] + [VMEM] * paths,
         out_specs=ANY,
         scratch_shapes=[pltpu.SemaphoreType.DMA((slots,))],
         name="unpack",
-    )(me, places, *in_vmem(*returned))
+    )(*in_smem(places), *in_vmem(*returned))
     return updated, velocity, path_out
 
 

time: 45.5 us -> 42.6 us (0.936)
  Pallas kernels: 12.6 us -> 9.76 us
  starting transfers between devices: 29.5 us -> 27.3 us
  waiting for transfers between devices: 2.35 us -> 4.54 us
    ppermute x14, starting transfers between devices: 24.9 us -> 21.5 us  [exchange(): lax.ppermute(x, 'path', [(i, i ^ d) for i in range(paths)])]
    ppermute x14, waiting for transfers between devices: 1.31 us -> 3.51 us  [exchange(): lax.ppermute(x, 'path', [(i, i ^ d) for i in range(paths)])]
    ppermute x3, starting transfers between devices: 4.6 us -> 5.75 us  [on_device(): lax.ppermute(squares, 'shard', [(i, (i + d) % shards) for i in range(shar...]
    pallas_call x1, Pallas kernels: 1.76 us -> 1.09 us  [on_device(): pl.pallas_call(functools.partial(unpack_kernel, [*order, 0]), out_shape=j...]
    pallas_call x1, Pallas kernels: 3.7 us -> 3.13 us  [on_device(): pl.pallas_call(early_kernel, out_shape=tables + [held_module] * 2, in_spe...]
    pallas_call x1, Pallas kernels: 0.91 us -> 0.37 us  [on_device(): pl.pallas_call(functools.partial(send_kernel, [*order, 0], shards), out_s...]
    pallas_call x1, Pallas kernels: 0.99 us -> 0.45 us  [on_device(): pl.pallas_call(functools.partial(combine_kernel, order), out_shape=[held_...]
    pallas_call x1, Pallas kernels: 2.72 us -> 2.21 us  [on_device(): pl.pallas_call(functools.partial(pack_kernel, owned, [*order, 0]), out_sh...]
  transfers between devices with their start and end apart: 17 -> 17, of which waited for: 2 -> 3; matrix products, arithmetic and copies ran while one was open for 0% -> 0% of each run, Pallas kernels for 14% -> 13%
where the time goes in v7:
time: 42.6 us; the launch traced here: 42.3 us
  starting transfers between devices  27.3 us (64%)
  Pallas kernels  9.76 us (23%)
  waiting for transfers between devices  4.54 us (11%)
  between operations  0.73 us (2%)
    ppermute x14, starting transfers between devices, exchange(): lax.ppermute(x, 'path', [(i, i ^ d) for i in range(paths)])  21.5 us
    ppermute x3, starting transfers between devices, on_device(): lax.ppermute(squares, 'shard', [(i, (i + d) % shards) for i in range(shar...  5.75 us
    ppermute x14, waiting for transfers between devices, exchange(): lax.ppermute(x, 'path', [(i, i ^ d) for i in range(paths)])  3.51 us
    pallas_call x1, Pallas kernels, on_device(): pl.pallas_call(early_kernel, out_shape=tables + [held_module] * 2, in_spe...  3.13 us
    pallas_call x1, Pallas kernels, on_device(): pl.pallas_call(store_kernel, out_shape=[module] * 2, in_specs=[VMEM] * 4,...  2.52 us
    pallas_call x1, Pallas kernels, on_device(): pl.pallas_call(functools.partial(pack_kernel, owned, [*order, 0]), out_sh...  2.21 us
    pallas_call x1, Pallas kernels, on_device(): pl.pallas_call(functools.partial(unpack_kernel, [*order, 0]), out_shape=j...  1.09 us
    ppermute x3, waiting for transfers between devices, on_device(): lax.ppermute(squares, 'shard', [(i, (i + d) % shards) for i in range(shar...  1.04 us
  transfers between devices with their start and end apart: 17, of which 3 were waited for; matrix products, arithmetic and copies ran while one was open for 0% of the time, Pallas kernels for 13%

profile of v7, /device:TPU:1, one launch (start us, length us, event | category | flops | bytes accessed | tf_op | source)
XLA Modules:
  0.0 42.3 jit_solution(15010327666333089670)
XLA Ops:
  0.6 2.2 %pack.1 = (s32[16]{0:T(128)S(4)}, bf16[2,8,4096]{2,1,0:T(8,128)(2,1)S(1)}, bf16[2,8,4096]{2,1,0:T(8,128)(2,1)S(1)}, bf16[2,8,4096]{2,1,0:T(8,128)(2,1)S(1)}, bf1...) custom-call(s32[8,16]{1,0:T(8,128)} %ids_ref.3, ...), custom_call_target="tpu_custom_call" | custom-call | tf_op jit(solution)/shard_map/pack/pallas_call | solution.py:273
  2.8 3.1 %collective-permute-start = (bf16[2,8,4096]{2,1,0:T(8,128)(2,1)S(1)}, bf16[2,8,4096]{2,1,0:T(8,128)(2,1)S(1)}, u32[]{:S(2)}, u32[]{:S(2)}) collective-permute-start(bf16[2,8,4096]{2,1,0:T(8,128)(2,1)S(1)} %get-tuple-element.35), channel_id=1, source_target_pairs={{0,24},{4,28},{8,16},{12,20},{16,8},{20,12},{24,0},{28,4},{1,25},{... | collective-permute-start | bytes 393224 | tf_op jit(solution)/shard_map/ppermute | solution.py:269
  5.9 0.2 collective-permute-start.1
  6.1 0.1 collective-permute-start.2
  6.3 2.7 %collective-permute-start.3 = (bf16[2,8,4096]{2,1,0:T(8,128)(2,1)S(1)}, bf16[2,8,4096]{2,1,0:T(8,128)(2,1)S(1)}, u32[]{:S(2)}, u32[]{:S(2)}) collective-permute-start(bf16[2,8,4096]{2,1,0:T(8,128)(2,1)S(1)} %get-tuple-element.38), channel_id=1, source_target_pairs={{0,12},{4,8},{8,4},{12,0},{16,28},{20,24},{24,20},{28,16},{1,13},{... | collective-permute-start | bytes 393224 | tf_op jit(solution)/shard_map/ppermute | solution.py:269
  9.0 0.1 collective-permute-start.4
  9.1 4.6 %collective-permute-start.5 = (bf16[2,8,4096]{2,1,0:T(8,128)(2,1)S(1)}, bf16[2,8,4096]{2,1,0:T(8,128)(2,1)S(1)}, u32[]{:S(2)}, u32[]{:S(2)}) collective-permute-start(bf16[2,8,4096]{2,1,0:T(8,128)(2,1)S(1)} %get-tuple-element.40), channel_id=1, source_target_pairs={{0,28},{4,24},{8,20},{12,16},{16,12},{20,8},{24,4},{28,0},{1,29},{... | collective-permute-start | bytes 393224 | tf_op jit(solution)/shard_map/ppermute | solution.py:269
  13.8 3.1 %early.1 = (s32[24]{0:T(128)S(4)}, f32[24]{0:T(128)S(4)}, f32[16]{0:T(128)S(4)}, f32[16,8,4096]{2,1,0:T(8,128)S(1)}, f32[16,8,4096]{2,1,0:T(8,128)S(1)}) custom-call(s32[8,16]{1,0:T(8,128)} %ids_ref.3, s32[8,16]{1,0:T(8,128)} %counts_ref.1, bf16[2,8,4096]{2,1,0:T(8,128)(2,1)S(1)} %get-tuple-element.30.own_ref, f32[16,8,4096]{2,1,0:T(8,128)} %params_hbm.1, ...), custom_call_target="tpu_custom_call" | custom-call | flops 1000000 | bytes 12582912 | tf_op jit(solution)/shard_map/early/pallas_call | solution.py:283
  16.9 1.3 %collective-permute-done.5.rest_5_ = bf16[2,8,4096]{2,1,0:T(8,128)(2,1)S(1)} collective-permute-done((bf16[2,8,4096]{2,1,0:T(8,128)(2,1)S(1)}, bf16[2,8,4096]{2,1,0:T(8,128)(2,1)S(1)}, u32[]{:S(2)}, u32[]{:S(2)}) %collective-permute-start.5) | collective-permute-done | bytes 131104 | tf_op jit(solution)/shard_map/ppermute | solution.py:269
  18.2 0.5 %combine.1 = (f32[16,8,4096]{2,1,0:T(8,128)S(1)}, f32[16,128]{1,0:T(8,128)S(1)}) custom-call(s32[24]{0:T(128)S(4)} %get-tuple-element.31.module_ref, f32[24]{0:T(128)S(4)} %get-tuple-element.33.weight_ref, f32[16]{0:T(128)S(4)} %get-tuple-element.32.total_ref, f32[16,8,4096]{2,1,0:T(8,128)S(1)} %get-tuple-element.34.acc_in, ...), custom_call_target="tpu_custom_call", output_to_operand_aliasing={{0}: (3, {})} | custom-call | tf_op jit(solution)/shard_map/combine/pallas_call | solution.py:293
  18.6 2.5 %collective-permute-start.7 = (f32[16,128]{1,0:T(8,128)S(1)}, f32[16,128]{1,0:T(8,128)S(1)}, u32[]{:S(2)}, u32[]{:S(2)}) collective-permute-start(f32[16,128]{1,0:T(8,128)S(1)} %get-tuple-element.44.rest_0_), channel_id=1, source_target_pairs={{0,2},{1,3},{2,0},{3,1},{4,6},{5,7},{6,4},{7,5},{8,10},{9,11},{10,... | collective-permute-start | bytes 24584 | tf_op jit(solution)/shard_map/ppermute | solution.py:303
  21.1 1.3 %collective-permute-start.8 = (f32[16,128]{1,0:T(8,128)S(1)}, f32[16,128]{1,0:T(8,128)S(1)}, u32[]{:S(2)}, u32[]{:S(2)}) collective-permute-start(f32[16,128]{1,0:T(8,128)S(1)} %get-tuple-element.44.rest_0_), channel_id=1, source_target_pairs={{0,1},{1,2},{2,3},{3,0},{4,5},{5,6},{6,7},{7,4},{8,9},{9,10},{10,1... | collective-permute-start | bytes 24584 | tf_op jit(solution)/shard_map/ppermute | solution.py:303
  22.4 2.0 %collective-permute-start.9 = (f32[16,128]{1,0:T(8,128)S(1)}, f32[16,128]{1,0:T(8,128)S(1)}, u32[]{:S(2)}, u32[]{:S(2)}) collective-permute-start(f32[16,128]{1,0:T(8,128)S(1)} %get-tuple-element.44.rest_0_), channel_id=1, source_target_pairs={{0,3},{1,0},{2,1},{3,2},{4,7},{5,4},{6,5},{7,6},{8,11},{9,8},{10,9... | collective-permute-start | bytes 24584 | tf_op jit(solution)/shard_map/ppermute | solution.py:303
  24.4 1.0 %collective-permute-done.8.rest_2_ = f32[16,128]{1,0:T(8,128)S(1)} collective-permute-done((f32[16,128]{1,0:T(8,128)S(1)}, f32[16,128]{1,0:T(8,128)S(1)}, u32[]{:S(2)}, u32[]{:S(2)}) %collective-permute-start.8) | collective-permute-done | bytes 8224 | tf_op jit(solution)/shard_map/ppermute | solution.py:303
  25.4 0.4 send.1
  25.8 2.3 %collective-permute-start.10 = (bf16[2,8,4096]{2,1,0:T(8,128)(2,1)S(1)}, bf16[2,8,4096]{2,1,0:T(8,128)(2,1)S(1)}, u32[]{:S(2)}, u32[]{:S(2)}) collective-permute-start(bf16[2,8,4096]{2,1,0:T(8,128)(2,1)S(1)} %get-tuple-element.49), channel_id=1, source_target_pairs={{0,24},{4,28},{8,16},{12,20},{16,8},{20,12},{24,0},{28,4},{1,25},{... | collective-permute-start | bytes 393224 | tf_op jit(solution)/shard_map/ppermute | solution.py:269
  28.1 0.2 collective-permute-start.11
  28.3 0.3 collective-permute-start.12
  28.5 3.5 %collective-permute-start.13 = (bf16[2,8,4096]{2,1,0:T(8,128)(2,1)S(1)}, bf16[2,8,4096]{2,1,0:T(8,128)(2,1)S(1)}, u32[]{:S(2)}, u32[]{:S(2)}) collective-permute-start(bf16[2,8,4096]{2,1,0:T(8,128)(2,1)S(1)} %get-tuple-element.52), channel_id=1, source_target_pairs={{0,12},{4,8},{8,4},{12,0},{16,28},{20,24},{24,20},{28,16},{1,13},{... | collective-permute-start | bytes 393224 | tf_op jit(solution)/shard_map/ppermute | solution.py:269
  32.0 0.0 collective-permute-start.14
  32.1 4.4 %collective-permute-start.15 = (bf16[2,8,4096]{2,1,0:T(8,128)(2,1)S(1)}, bf16[2,8,4096]{2,1,0:T(8,128)(2,1)S(1)}, u32[]{:S(2)}, u32[]{:S(2)}) collective-permute-start(bf16[2,8,4096]{2,1,0:T(8,128)(2,1)S(1)} %get-tuple-element.54), channel_id=1, source_target_pairs={{0,28},{4,24},{8,20},{12,16},{16,12},{20,8},{24,4},{28,0},{1,29},{... | collective-permute-start | bytes 393224 | tf_op jit(solution)/shard_map/ppermute | solution.py:269
  36.5 2.5 %store.1 = (f32[16,8,4096]{2,1,0:T(8,128)}, f32[16,8,4096]{2,1,0:T(8,128)}) custom-call(f32[16,8,128]{2,1,0:T(8,128)S(1)} %get-tuple-element.45.scale_ref, f32[16,8,4096]{2,1,0:T(8,128)S(1)} %get-tuple-element.42.acc_ref, f32[16,8,4096]{2,1,0:T(8,128)S(1)} %get-tuple-element.43.base_ref, f32[16,8,4096]{2,1,0:T(8,128)S(1)} %copy-done), custom_call_target="tpu_custom_call" | custom-call | flops 1000000 | bytes 12582912 | tf_op jit(solution)/shard_map/store/pallas_call | solution.py:315
  39.0 2.2 %collective-permute-done.15.rest_5_ = bf16[2,8,4096]{2,1,0:T(8,128)(2,1)S(1)} collective-permute-done((bf16[2,8,4096]{2,1,0:T(8,128)(2,1)S(1)}, bf16[2,8,4096]{2,1,0:T(8,128)(2,1)S(1)}, u32[]{:S(2)}, u32[]{:S(2)}) %collective-permute-start.15) | collective-permute-done | bytes 131104 | tf_op jit(solution)/shard_map/ppermute | solution.py:269
  41.2 1.1 %unpack.1 = bf16[1,16,8,4096]{3,2,1,0:T(8,128)(2,1)} custom-call(s32[16]{0:T(128)S(4)} %get-tuple-element.48.places_ref, bf16[2,8,4096]{2,1,0:T(8,128)(2,1)S(1)} %collective-permute-done.10.rest_0_, bf16[2,8,4096]{2,1,0:T(8,128)(2,1)S(1)} %collective-permute-done.11.rest_1_, bf16[2,8,4096]{2,1,0:T(8,128)(2,1)S(1)} %collective-permute-done.12.rest_2_, ...), custom_call_target="tpu_custom_call" | custom-call | tf_op jit(solution)/shard_map/unpack/pallas_call | solution.py:325
  (18 shorter events, 0.1 us)
Async XLA Ops:
  2.8 6.3 %collective-permute-start = (bf16[2,8,4096]{2,1,0:T(8,128)(2,1)S(1)}, bf16[2,8,4096]{2,1,0:T(8,128)(2,1)S(1)}, u32[]{:S(2)}, u32[]{:S(2)}) collective-permute-start(bf16[2,8,4096]{2,1,0:T(8,128)(2,1)S(1)} %get-tuple-element.35), channel_id=1, source_target_pairs={{0,24},{4,28},{8,16},{12,20},{16,8},{20,12},{24,0},{28,4},{1,25},{... | collective-permute-start | bytes 393224 | tf_op jit(solution)/shard_map/ppermute | solution.py:269
  5.9 7.8 %collective-permute-start.1 = (bf16[2,8,4096]{2,1,0:T(8,128)(2,1)S(1)}, bf16[2,8,4096]{2,1,0:T(8,128)(2,1)S(1)}, u32[]{:S(2)}, u32[]{:S(2)}) collective-permute-start(bf16[2,8,4096]{2,1,0:T(8,128)(2,1)S(1)} %get-tuple-element.36), channel_id=1, source_target_pairs={{0,16},{4,20},{8,24},{12,28},{16,0},{20,4},{24,8},{28,12},{1,17},{... | collective-permute-start | bytes 393224 | tf_op jit(solution)/shard_map/ppermute | solution.py:269
  6.1 10.8 %collective-permute-start.2 = (bf16[2,8,4096]{2,1,0:T(8,128)(2,1)S(1)}, bf16[2,8,4096]{2,1,0:T(8,128)(2,1)S(1)}, u32[]{:S(2)}, u32[]{:S(2)}) collective-permute-start(bf16[2,8,4096]{2,1,0:T(8,128)(2,1)S(1)} %get-tuple-element.37), channel_id=1, source_target_pairs={{0,8},{4,12},{8,0},{12,4},{16,24},{20,28},{24,16},{28,20},{1,9},{5... | collective-permute-start | bytes 393224 | tf_op jit(solution)/shard_map/ppermute | solution.py:269
  6.3 10.6 %collective-permute-start.3 = (bf16[2,8,4096]{2,1,0:T(8,128)(2,1)S(1)}, bf16[2,8,4096]{2,1,0:T(8,128)(2,1)S(1)}, u32[]{:S(2)}, u32[]{:S(2)}) collective-permute-start(bf16[2,8,4096]{2,1,0:T(8,128)(2,1)S(1)} %get-tuple-element.38), channel_id=1, source_target_pairs={{0,12},{4,8},{8,4},{12,0},{16,28},{20,24},{24,20},{28,16},{1,13},{... | collective-permute-start | bytes 393224 | tf_op jit(solution)/shard_map/ppermute | solution.py:269
  9.0 7.9 %collective-permute-start.4 = (bf16[2,8,4096]{2,1,0:T(8,128)(2,1)S(1)}, bf16[2,8,4096]{2,1,0:T(8,128)(2,1)S(1)}, u32[]{:S(2)}, u32[]{:S(2)}) collective-permute-start(bf16[2,8,4096]{2,1,0:T(8,128)(2,1)S(1)} %get-tuple-element.39), channel_id=1, source_target_pairs={{0,20},{4,16},{8,28},{12,24},{16,4},{20,0},{24,12},{28,8},{1,21},{... | collective-permute-start | bytes 393224 | tf_op jit(solution)/shard_map/ppermute | solution.py:269
  9.1 9.1 %collective-permute-start.5 = (bf16[2,8,4096]{2,1,0:T(8,128)(2,1)S(1)}, bf16[2,8,4096]{2,1,0:T(8,128)(2,1)S(1)}, u32[]{:S(2)}, u32[]{:S(2)}) collective-permute-start(bf16[2,8,4096]{2,1,0:T(8,128)(2,1)S(1)} %get-tuple-element.40), channel_id=1, source_target_pairs={{0,28},{4,24},{8,20},{12,16},{16,12},{20,8},{24,4},{28,0},{1,29},{... | collective-permute-start | bytes 393224 | tf_op jit(solution)/shard_map/ppermute | solution.py:269
  13.8 4.4 %collective-permute-start.6 = (bf16[2,8,4096]{2,1,0:T(8,128)(2,1)S(1)}, bf16[2,8,4096]{2,1,0:T(8,128)(2,1)S(1)}, u32[]{:S(2)}, u32[]{:S(2)}) collective-permute-start(bf16[2,8,4096]{2,1,0:T(8,128)(2,1)S(1)} %get-tuple-element.41), channel_id=1, source_target_pairs={{0,4},{4,0},{8,12},{12,8},{16,20},{20,16},{24,28},{28,24},{1,5},{5... | collective-permute-start | bytes 393224 | tf_op jit(solution)/shard_map/ppermute | solution.py:269
  18.6 5.8 %collective-permute-start.7 = (f32[16,128]{1,0:T(8,128)S(1)}, f32[16,128]{1,0:T(8,128)S(1)}, u32[]{:S(2)}, u32[]{:S(2)}) collective-permute-start(f32[16,128]{1,0:T(8,128)S(1)} %get-tuple-element.44.rest_0_), channel_id=1, source_target_pairs={{0,2},{1,3},{2,0},{3,1},{4,6},{5,7},{6,4},{7,5},{8,10},{9,11},{10,... | collective-permute-start | bytes 24584 | tf_op jit(solution)/shard_map/ppermute | solution.py:303
  21.1 4.3 %collective-permute-start.8 = (f32[16,128]{1,0:T(8,128)S(1)}, f32[16,128]{1,0:T(8,128)S(1)}, u32[]{:S(2)}, u32[]{:S(2)}) collective-permute-start(f32[16,128]{1,0:T(8,128)S(1)} %get-tuple-element.44.rest_0_), channel_id=1, source_target_pairs={{0,1},{1,2},{2,3},{3,0},{4,5},{5,6},{6,7},{7,4},{8,9},{9,10},{10,1... | collective-permute-start | bytes 24584 | tf_op jit(solution)/shard_map/ppermute | solution.py:303
  22.4 3.0 %collective-permute-start.9 = (f32[16,128]{1,0:T(8,128)S(1)}, f32[16,128]{1,0:T(8,128)S(1)}, u32[]{:S(2)}, u32[]{:S(2)}) collective-permute-start(f32[16,128]{1,0:T(8,128)S(1)} %get-tuple-element.44.rest_0_), channel_id=1, source_target_pairs={{0,3},{1,0},{2,1},{3,2},{4,7},{5,4},{6,5},{7,6},{8,11},{9,8},{10,9... | collective-permute-start | bytes 24584 | tf_op jit(solution)/shard_map/ppermute | solution.py:303
  25.4 11.0 %copy-start = (f32[16,8,4096]{2,1,0:T(8,128)S(1)}, f32[16,8,4096]{2,1,0:T(8,128)}, u32[]{:S(2)}) copy-start(f32[16,8,4096]{2,1,0:T(8,128)} %past_ref.1) | copy-start | bytes 6291460
  25.8 6.3 %collective-permute-start.10 = (bf16[2,8,4096]{2,1,0:T(8,128)(2,1)S(1)}, bf16[2,8,4096]{2,1,0:T(8,128)(2,1)S(1)}, u32[]{:S(2)}, u32[]{:S(2)}) collective-permute-start(bf16[2,8,4096]{2,1,0:T(8,128)(2,1)S(1)} %get-tuple-element.49), channel_id=1, source_target_pairs={{0,24},{4,28},{8,16},{12,20},{16,8},{20,12},{24,0},{28,4},{1,25},{... | collective-permute-start | bytes 393224 | tf_op jit(solution)/shard_map/ppermute | solution.py:269
  28.1 8.4 %collective-permute-start.11 = (bf16[2,8,4096]{2,1,0:T(8,128)(2,1)S(1)}, bf16[2,8,4096]{2,1,0:T(8,128)(2,1)S(1)}, u32[]{:S(2)}, u32[]{:S(2)}) collective-permute-start(bf16[2,8,4096]{2,1,0:T(8,128)(2,1)S(1)} %get-tuple-element.50), channel_id=1, source_target_pairs={{0,16},{4,20},{8,24},{12,28},{16,0},{20,4},{24,8},{28,12},{1,17},{... | collective-permute-start | bytes 393224 | tf_op jit(solution)/shard_map/ppermute | solution.py:269
  28.3 10.7 %collective-permute-start.12 = (bf16[2,8,4096]{2,1,0:T(8,128)(2,1)S(1)}, bf16[2,8,4096]{2,1,0:T(8,128)(2,1)S(1)}, u32[]{:S(2)}, u32[]{:S(2)}) collective-permute-start(bf16[2,8,4096]{2,1,0:T(8,128)(2,1)S(1)} %get-tuple-element.51), channel_id=1, source_target_pairs={{0,8},{4,12},{8,0},{12,4},{16,24},{20,28},{24,16},{28,20},{1,9},{5... | collective-permute-start | bytes 393224 | tf_op jit(solution)/shard_map/ppermute | solution.py:269
  28.5 10.5 %collective-permute-start.13 = (bf16[2,8,4096]{2,1,0:T(8,128)(2,1)S(1)}, bf16[2,8,4096]{2,1,0:T(8,128)(2,1)S(1)}, u32[]{:S(2)}, u32[]{:S(2)}) collective-permute-start(bf16[2,8,4096]{2,1,0:T(8,128)(2,1)S(1)} %get-tuple-element.52), channel_id=1, source_target_pairs={{0,12},{4,8},{8,4},{12,0},{16,28},{20,24},{24,20},{28,16},{1,13},{... | collective-permute-start | bytes 393224 | tf_op jit(solution)/shard_map/ppermute | solution.py:269
  32.0 7.0 %collective-permute-start.14 = (bf16[2,8,4096]{2,1,0:T(8,128)(2,1)S(1)}, bf16[2,8,4096]{2,1,0:T(8,128)(2,1)S(1)}, u32[]{:S(2)}, u32[]{:S(2)}) collective-permute-start(bf16[2,8,4096]{2,1,0:T(8,128)(2,1)S(1)} %get-tuple-element.53), channel_id=1, source_target_pairs={{0,20},{4,16},{8,28},{12,24},{16,4},{20,0},{24,12},{28,8},{1,21},{... | collective-permute-start | bytes 393224 | tf_op jit(solution)/shard_map/ppermute | solution.py:269
  32.1 9.1 %collective-permute-start.15 = (bf16[2,8,4096]{2,1,0:T(8,128)(2,1)S(1)}, bf16[2,8,4096]{2,1,0:T(8,128)(2,1)S(1)}, u32[]{:S(2)}, u32[]{:S(2)}) collective-permute-start(bf16[2,8,4096]{2,1,0:T(8,128)(2,1)S(1)} %get-tuple-element.54), channel_id=1, source_target_pairs={{0,28},{4,24},{8,20},{12,16},{16,12},{20,8},{24,4},{28,0},{1,29},{... | collective-permute-start | bytes 393224 | tf_op jit(solution)/shard_map/ppermute | solution.py:269
  36.4 4.8 %collective-permute-start.16 = (bf16[2,8,4096]{2,1,0:T(8,128)(2,1)S(1)}, bf16[2,8,4096]{2,1,0:T(8,128)(2,1)S(1)}, u32[]{:S(2)}, u32[]{:S(2)}) collective-permute-start(bf16[2,8,4096]{2,1,0:T(8,128)(2,1)S(1)} %get-tuple-element.55), channel_id=1, source_target_pairs={{0,4},{4,0},{8,12},{12,8},{16,20},{20,16},{24,28},{28,24},{1,5},{5... | collective-permute-start | bytes 393224 | tf_op jit(solution)/shard_map/ppermute | solution.py:269

commit v8 on v7

--- a/solution.py
+++ b/solution.py
@@ -35,30 +35,33 @@
     return [pl.ds(at, step) for at in range(0, width, step)]
 
 
-def pack_kernel(owned, order, ids_ref, local_ref, places_ref, *rest):
-    pieces, (seen, sems) = rest[:-2], rest[-2:]
-    me = lax.axis_index("path").astype(jnp.int32)
-    paths = len(order)
+def pack_kernel(owned, order, ids_hbm, local_hbm, places_ref, *rest):
+    pieces, (ids_ref, local_ref, seen, sems) = rest[:-4], rest[-4:]
+    me = lax.axis_index("path").astype(jnp.int32)
+    paths, held = ids_ref.shape
+    part = held // PARTS
+    ids_copy = pltpu.make_async_copy(ids_hbm, ids_ref, sems.at[PARTS])
+    ids_copy.start()
+    copies = []
+    for i in range(PARTS):
+        at = pl.ds(i * part, part)
+        copies.append(pltpu.make_async_copy(local_hbm.at[at], local_ref.at[at], sems.at[i]))
+        copies[-1].start()
     for i in range(paths):
         seen[i] = jnp.int32(0)
     for i in range(paths * CAP):
         places_ref[i] = jnp.int32(-1)
-    for k in range(ids_ref.shape[1]):
+    ids_copy.wait()
+    for k in range(held):
         group = lax.div(ids_ref[me, k], jnp.int32(owned))
         rank = seen[group]
         seen[group] = rank + 1
         places_ref[group * CAP + rank] = jnp.int32(k)
-    copies = []
-    for d, piece in zip(order, pieces, strict=True):
-        for r in range(CAP):
-            k = jnp.maximum(places_ref[(me ^ d) * CAP + r], 0)
-            copy = pltpu.make_async_copy(
-                local_ref.at[k], piece.at[r], sems.at[d * CAP + r]
-            )
-            copy.start()
-            copies.append(copy)
     for copy in copies:
         copy.wait()
+    for d, piece in zip(order, pieces, strict=True):
+        for r in range(CAP):
+            piece[r] = local_ref[jnp.maximum(places_ref[(me ^ d) * CAP + r], 0)]
 
 
 def find_slots(me, owned, ids_ref, counts_ref, module_ref, weight_ref, total_ref):
@@ -261,7 +264,7 @@
         pltpu.SemaphoreType.DMA((2, PARTS)),
     ]
     limits = pltpu.CompilerParams(vmem_limit_bytes=24 * 1024 * 1024)
-    far = sorted(range(2, paths, 2), key=lambda d: (-d.bit_count(), -d))
+    far = sorted(range(2, paths, 2), key=lambda d: (-d.bit_count(), d))
     order = far + [d + 1 for d in far[::-1]] + [1]
 
     def exchange(pieces):
@@ -273,9 +276,15 @@
     places, *packed = pl.pallas_call(
         functools.partial(pack_kernel, owned, [*order, 0]),
         out_shape=[pltpu.SMEM((slots,), jnp.int32)] + [piece] * paths,
-        in_specs=[SMEM, ANY],
+        in_specs=[ANY] * 2,
         out_specs=[SMEM] + [VMEM] * paths,
-        scratch_shapes=[pltpu.SMEM((paths,), jnp.int32), pltpu.SemaphoreType.DMA((slots,))],
+        scratch_shapes=[
+            pltpu.SMEM(module_ids.shape, jnp.int32),
+            pltpu.VMEM((held, rows, width), jnp.bfloat16),
+            pltpu.SMEM((paths,), jnp.int32),
+            pltpu.SemaphoreType.DMA((PARTS + 1,)),
+        ],
+        compiler_params=limits,
         name="pack",
     )(module_ids, *in_hbm(path_params.reshape(held, rows, width)))
 

time: 42.6 us -> 41.4 us (0.972)
  waiting for transfers between devices: 4.54 us -> 3.25 us
  Pallas kernels: 9.76 us -> 8.88 us
  starting transfers between devices: 27.3 us -> 28 us
    ppermute x14, waiting for transfers between devices: 3.51 us -> 2.21 us  [exchange(): lax.ppermute(x, 'path', [(i, i ^ d) for i in range(paths)])]
    pallas_call x1, Pallas kernels: 2.21 us -> 1.31 us  [on_device(): pl.pallas_call(functools.partial(pack_kernel, owned, [*order, 0]), out_sh...]
    ppermute x14, starting transfers between devices: 21.5 us -> 22.1 us  [exchange(): lax.ppermute(x, 'path', [(i, i ^ d) for i in range(paths)])]
  transfers between devices with their start and end apart: 17 -> 17, of which waited for: 3 -> 3; matrix products, arithmetic and copies ran while one was open for 0% -> 0% of each run, Pallas kernels for 13% -> 14%
where the time goes in v8:
time: 41.4 us; the launch traced here: 40.8 us
  starting transfers between devices  28 us (68%)
  Pallas kernels  8.88 us (21%)
  waiting for transfers between devices  3.25 us (8%)
  between operations  0.72 us (2%)
    ppermute x14, starting transfers between devices, exchange(): lax.ppermute(x, 'path', [(i, i ^ d) for i in range(paths)])  22.1 us
    ppermute x3, starting transfers between devices, on_device(): lax.ppermute(squares, 'shard', [(i, (i + d) % shards) for i in range(shar...  5.83 us
    pallas_call x1, Pallas kernels, on_device(): pl.pallas_call(early_kernel, out_shape=tables + [held_module] * 2, in_spe...  3.12 us
    pallas_call x1, Pallas kernels, on_device(): pl.pallas_call(store_kernel, out_shape=[module] * 2, in_specs=[VMEM] * 4,...  2.52 us
    ppermute x14, waiting for transfers between devices, exchange(): lax.ppermute(x, 'path', [(i, i ^ d) for i in range(paths)])  2.21 us
    pallas_call x1, Pallas kernels, on_device(): pl.pallas_call(functools.partial(pack_kernel, owned, [*order, 0]), out_sh...  1.31 us
    pallas_call x1, Pallas kernels, on_device(): pl.pallas_call(functools.partial(unpack_kernel, [*order, 0]), out_shape=j...  1.11 us
    ppermute x3, waiting for transfers between devices, on_device(): lax.ppermute(squares, 'shard', [(i, (i + d) % shards) for i in range(shar...  1.04 us
  transfers between devices with their start and end apart: 17, of which 3 were waited for; matrix products, arithmetic and copies ran while one was open for 0% of the time, Pallas kernels for 14%

profile of v8, /device:TPU:1, one launch (start us, length us, event | category | flops | bytes accessed | tf_op | source)
XLA Modules:
  0.0 40.8 jit_solution(14652546633336819708)
XLA Ops:
  0.6 1.3 %pack.1 = (s32[16]{0:T(128)S(4)}, bf16[2,8,4096]{2,1,0:T(8,128)(2,1)S(1)}, bf16[2,8,4096]{2,1,0:T(8,128)(2,1)S(1)}, bf16[2,8,4096]{2,1,0:T(8,128)(2,1)S(1)}, bf1...) custom-call(s32[8,16]{1,0:T(8,128)} %ids_ref.1, ...), custom_call_target="tpu_custom_call" | custom-call | tf_op jit(solution)/shard_map/pack/pallas_call | solution.py:276
  1.9 3.1 %collective-permute-start = (bf16[2,8,4096]{2,1,0:T(8,128)(2,1)S(1)}, bf16[2,8,4096]{2,1,0:T(8,128)(2,1)S(1)}, u32[]{:S(2)}, u32[]{:S(2)}) collective-permute-start(bf16[2,8,4096]{2,1,0:T(8,128)(2,1)S(1)} %get-tuple-element.35), channel_id=1, source_target_pairs={{0,24},{4,28},{8,16},{12,20},{16,8},{20,12},{24,0},{28,4},{1,25},{... | collective-permute-start | bytes 393224 | tf_op jit(solution)/shard_map/ppermute | solution.py:272
  5.0 0.3 collective-permute-start.1
  5.3 0.1 collective-permute-start.2
  5.4 2.8 %collective-permute-start.3 = (bf16[2,8,4096]{2,1,0:T(8,128)(2,1)S(1)}, bf16[2,8,4096]{2,1,0:T(8,128)(2,1)S(1)}, u32[]{:S(2)}, u32[]{:S(2)}) collective-permute-start(bf16[2,8,4096]{2,1,0:T(8,128)(2,1)S(1)} %get-tuple-element.38), channel_id=1, source_target_pairs={{0,20},{4,16},{8,28},{12,24},{16,4},{20,0},{24,12},{28,8},{1,21},{... | collective-permute-start | bytes 393224 | tf_op jit(solution)/shard_map/ppermute | solution.py:272
  8.1 0.1 collective-permute-start.4
  8.2 4.6 %collective-permute-start.5 = (bf16[2,8,4096]{2,1,0:T(8,128)(2,1)S(1)}, bf16[2,8,4096]{2,1,0:T(8,128)(2,1)S(1)}, u32[]{:S(2)}, u32[]{:S(2)}) collective-permute-start(bf16[2,8,4096]{2,1,0:T(8,128)(2,1)S(1)} %get-tuple-element.40), channel_id=1, source_target_pairs={{0,28},{4,24},{8,20},{12,16},{16,12},{20,8},{24,4},{28,0},{1,29},{... | collective-permute-start | bytes 393224 | tf_op jit(solution)/shard_map/ppermute | solution.py:272
  12.9 0.8 %collective-permute-start.6 = (bf16[2,8,4096]{2,1,0:T(8,128)(2,1)S(1)}, bf16[2,8,4096]{2,1,0:T(8,128)(2,1)S(1)}, u32[]{:S(2)}, u32[]{:S(2)}) collective-permute-start(bf16[2,8,4096]{2,1,0:T(8,128)(2,1)S(1)} %get-tuple-element.41), channel_id=1, source_target_pairs={{0,4},{4,0},{8,12},{12,8},{16,20},{20,16},{24,28},{28,24},{1,5},{5... | collective-permute-start | bytes 393224 | tf_op jit(solution)/shard_map/ppermute | solution.py:272
  13.7 3.1 %early.1 = (s32[24]{0:T(128)S(4)}, f32[24]{0:T(128)S(4)}, f32[16]{0:T(128)S(4)}, f32[16,8,4096]{2,1,0:T(8,128)S(1)}, f32[16,8,4096]{2,1,0:T(8,128)S(1)}) custom-call(s32[8,16]{1,0:T(8,128)} %ids_ref.1, s32[8,16]{1,0:T(8,128)} %counts_ref.1, bf16[2,8,4096]{2,1,0:T(8,128)(2,1)S(1)} %get-tuple-element.30.own_ref, f32[16,8,4096]{2,1,0:T(8,128)} %params_hbm.1, ...), custom_call_target="tpu_custom_call" | custom-call | flops 1000000 | bytes 12582912 | tf_op jit(solution)/shard_map/early/pallas_call | solution.py:292
  16.8 0.4 collective-permute-done.5.rest_5_
  17.2 0.5 %combine.1 = (f32[16,8,4096]{2,1,0:T(8,128)S(1)}, f32[16,128]{1,0:T(8,128)S(1)}) custom-call(s32[24]{0:T(128)S(4)} %get-tuple-element.31.module_ref, f32[24]{0:T(128)S(4)} %get-tuple-element.33.weight_ref, f32[16]{0:T(128)S(4)} %get-tuple-element.32.total_ref, f32[16,8,4096]{2,1,0:T(8,128)S(1)} %get-tuple-element.34.acc_in, ...), custom_call_target="tpu_custom_call", output_to_operand_aliasing={{0}: (3, {})} | custom-call | tf_op jit(solution)/shard_map/combine/pallas_call | solution.py:302
  17.7 2.6 %collective-permute-start.7 = (f32[16,128]{1,0:T(8,128)S(1)}, f32[16,128]{1,0:T(8,128)S(1)}, u32[]{:S(2)}, u32[]{:S(2)}) collective-permute-start(f32[16,128]{1,0:T(8,128)S(1)} %get-tuple-element.44.rest_0_), channel_id=1, source_target_pairs={{0,2},{1,3},{2,0},{3,1},{4,6},{5,7},{6,4},{7,5},{8,10},{9,11},{10,... | collective-permute-start | bytes 24584 | tf_op jit(solution)/shard_map/ppermute | solution.py:312
  20.2 1.3 %collective-permute-start.8 = (f32[16,128]{1,0:T(8,128)S(1)}, f32[16,128]{1,0:T(8,128)S(1)}, u32[]{:S(2)}, u32[]{:S(2)}) collective-permute-start(f32[16,128]{1,0:T(8,128)S(1)} %get-tuple-element.44.rest_0_), channel_id=1, source_target_pairs={{0,1},{1,2},{2,3},{3,0},{4,5},{5,6},{6,7},{7,4},{8,9},{9,10},{10,1... | collective-permute-start | bytes 24584 | tf_op jit(solution)/shard_map/ppermute | solution.py:312
  21.5 2.0 %collective-permute-start.9 = (f32[16,128]{1,0:T(8,128)S(1)}, f32[16,128]{1,0:T(8,128)S(1)}, u32[]{:S(2)}, u32[]{:S(2)}) collective-permute-start(f32[16,128]{1,0:T(8,128)S(1)} %get-tuple-element.44.rest_0_), channel_id=1, source_target_pairs={{0,3},{1,0},{2,1},{3,2},{4,7},{5,4},{6,5},{7,6},{8,11},{9,8},{10,9... | collective-permute-start | bytes 24584 | tf_op jit(solution)/shard_map/ppermute | solution.py:312
  23.5 1.0 %collective-permute-done.8.rest_2_ = f32[16,128]{1,0:T(8,128)S(1)} collective-permute-done((f32[16,128]{1,0:T(8,128)S(1)}, f32[16,128]{1,0:T(8,128)S(1)}, u32[]{:S(2)}, u32[]{:S(2)}) %collective-permute-start.8) | collective-permute-done | bytes 8224 | tf_op jit(solution)/shard_map/ppermute | solution.py:312
  24.5 0.4 send.1
  24.9 2.2 %collective-permute-start.10 = (bf16[2,8,4096]{2,1,0:T(8,128)(2,1)S(1)}, bf16[2,8,4096]{2,1,0:T(8,128)(2,1)S(1)}, u32[]{:S(2)}, u32[]{:S(2)}) collective-permute-start(bf16[2,8,4096]{2,1,0:T(8,128)(2,1)S(1)} %get-tuple-element.49), channel_id=1, source_target_pairs={{0,24},{4,28},{8,16},{12,20},{16,8},{20,12},{24,0},{28,4},{1,25},{... | collective-permute-start | bytes 393224 | tf_op jit(solution)/shard_map/ppermute | solution.py:272
  27.1 0.3 collective-permute-start.11
  27.4 0.2 collective-permute-start.12
  27.6 3.6 %collective-permute-start.13 = (bf16[2,8,4096]{2,1,0:T(8,128)(2,1)S(1)}, bf16[2,8,4096]{2,1,0:T(8,128)(2,1)S(1)}, u32[]{:S(2)}, u32[]{:S(2)}) collective-permute-start(bf16[2,8,4096]{2,1,0:T(8,128)(2,1)S(1)} %get-tuple-element.52), channel_id=1, source_target_pairs={{0,20},{4,16},{8,28},{12,24},{16,4},{20,0},{24,12},{28,8},{1,21},{... | collective-permute-start | bytes 393224 | tf_op jit(solution)/shard_map/ppermute | solution.py:272
  31.2 4.2 %collective-permute-start.15 = (bf16[2,8,4096]{2,1,0:T(8,128)(2,1)S(1)}, bf16[2,8,4096]{2,1,0:T(8,128)(2,1)S(1)}, u32[]{:S(2)}, u32[]{:S(2)}) collective-permute-start(bf16[2,8,4096]{2,1,0:T(8,128)(2,1)S(1)} %get-tuple-element.54), channel_id=1, source_target_pairs={{0,28},{4,24},{8,20},{12,16},{16,12},{20,8},{24,4},{28,0},{1,29},{... | collective-permute-start | bytes 393224 | tf_op jit(solution)/shard_map/ppermute | solution.py:272
  35.3 2.5 %store.1 = (f32[16,8,4096]{2,1,0:T(8,128)}, f32[16,8,4096]{2,1,0:T(8,128)}) custom-call(f32[16,8,128]{2,1,0:T(8,128)S(1)} %get-tuple-element.45.scale_ref, f32[16,8,4096]{2,1,0:T(8,128)S(1)} %get-tuple-element.42.acc_ref, f32[16,8,4096]{2,1,0:T(8,128)S(1)} %get-tuple-element.43.base_ref, f32[16,8,4096]{2,1,0:T(8,128)S(1)} %copy-done), custom_call_target="tpu_custom_call" | custom-call | flops 1000000 | bytes 12582912 | tf_op jit(solution)/shard_map/store/pallas_call | solution.py:324
  37.9 1.8 %collective-permute-done.13.rest_3_ = bf16[2,8,4096]{2,1,0:T(8,128)(2,1)S(1)} collective-permute-done((bf16[2,8,4096]{2,1,0:T(8,128)(2,1)S(1)}, bf16[2,8,4096]{2,1,0:T(8,128)(2,1)S(1)}, u32[]{:S(2)}, u32[]{:S(2)}) %collective-permute-start.13) | collective-permute-done | bytes 131104 | tf_op jit(solution)/shard_map/ppermute | solution.py:272
  39.7 1.1 %unpack.1 = bf16[1,16,8,4096]{3,2,1,0:T(8,128)(2,1)} custom-call(s32[16]{0:T(128)S(4)} %get-tuple-element.48.places_ref, bf16[2,8,4096]{2,1,0:T(8,128)(2,1)S(1)} %collective-permute-done.10.rest_0_, bf16[2,8,4096]{2,1,0:T(8,128)(2,1)S(1)} %collective-permute-done.11.rest_1_, bf16[2,8,4096]{2,1,0:T(8,128)(2,1)S(1)} %collective-permute-done.12.rest_2_, ...), custom_call_target="tpu_custom_call" | custom-call | tf_op jit(solution)/shard_map/unpack/pallas_call | solution.py:334
  (18 shorter events, 0.1 us)
Async XLA Ops:
  1.9 6.3 %collective-permute-start = (bf16[2,8,4096]{2,1,0:T(8,128)(2,1)S(1)}, bf16[2,8,4096]{2,1,0:T(8,128)(2,1)S(1)}, u32[]{:S(2)}, u32[]{:S(2)}) collective-permute-start(bf16[2,8,4096]{2,1,0:T(8,128)(2,1)S(1)} %get-tuple-element.35), channel_id=1, source_target_pairs={{0,24},{4,28},{8,16},{12,20},{16,8},{20,12},{24,0},{28,4},{1,25},{... | collective-permute-start | bytes 393224 | tf_op jit(solution)/shard_map/ppermute | solution.py:272
  5.0 7.8 %collective-permute-start.1 = (bf16[2,8,4096]{2,1,0:T(8,128)(2,1)S(1)}, bf16[2,8,4096]{2,1,0:T(8,128)(2,1)S(1)}, u32[]{:S(2)}, u32[]{:S(2)}) collective-permute-start(bf16[2,8,4096]{2,1,0:T(8,128)(2,1)S(1)} %get-tuple-element.36), channel_id=1, source_target_pairs={{0,8},{4,12},{8,0},{12,4},{16,24},{20,28},{24,16},{28,20},{1,9},{5... | collective-permute-start | bytes 393224 | tf_op jit(solution)/shard_map/ppermute | solution.py:272
  5.3 11.5 %collective-permute-start.2 = (bf16[2,8,4096]{2,1,0:T(8,128)(2,1)S(1)}, bf16[2,8,4096]{2,1,0:T(8,128)(2,1)S(1)}, u32[]{:S(2)}, u32[]{:S(2)}) collective-permute-start(bf16[2,8,4096]{2,1,0:T(8,128)(2,1)S(1)} %get-tuple-element.37), channel_id=1, source_target_pairs={{0,16},{4,20},{8,24},{12,28},{16,0},{20,4},{24,8},{28,12},{1,17},{... | collective-permute-start | bytes 393224 | tf_op jit(solution)/shard_map/ppermute | solution.py:272
  5.4 11.4 %collective-permute-start.3 = (bf16[2,8,4096]{2,1,0:T(8,128)(2,1)S(1)}, bf16[2,8,4096]{2,1,0:T(8,128)(2,1)S(1)}, u32[]{:S(2)}, u32[]{:S(2)}) collective-permute-start(bf16[2,8,4096]{2,1,0:T(8,128)(2,1)S(1)} %get-tuple-element.38), channel_id=1, source_target_pairs={{0,20},{4,16},{8,28},{12,24},{16,4},{20,0},{24,12},{28,8},{1,21},{... | collective-permute-start | bytes 393224 | tf_op jit(solution)/shard_map/ppermute | solution.py:272
  8.1 8.7 %collective-permute-start.4 = (bf16[2,8,4096]{2,1,0:T(8,128)(2,1)S(1)}, bf16[2,8,4096]{2,1,0:T(8,128)(2,1)S(1)}, u32[]{:S(2)}, u32[]{:S(2)}) collective-permute-start(bf16[2,8,4096]{2,1,0:T(8,128)(2,1)S(1)} %get-tuple-element.39), channel_id=1, source_target_pairs={{0,12},{4,8},{8,4},{12,0},{16,28},{20,24},{24,20},{28,16},{1,13},{... | collective-permute-start | bytes 393224 | tf_op jit(solution)/shard_map/ppermute | solution.py:272
  8.2 9.0 %collective-permute-start.5 = (bf16[2,8,4096]{2,1,0:T(8,128)(2,1)S(1)}, bf16[2,8,4096]{2,1,0:T(8,128)(2,1)S(1)}, u32[]{:S(2)}, u32[]{:S(2)}) collective-permute-start(bf16[2,8,4096]{2,1,0:T(8,128)(2,1)S(1)} %get-tuple-element.40), channel_id=1, source_target_pairs={{0,28},{4,24},{8,20},{12,16},{16,12},{20,8},{24,4},{28,0},{1,29},{... | collective-permute-start | bytes 393224 | tf_op jit(solution)/shard_map/ppermute | solution.py:272
  12.9 4.3 %collective-permute-start.6 = (bf16[2,8,4096]{2,1,0:T(8,128)(2,1)S(1)}, bf16[2,8,4096]{2,1,0:T(8,128)(2,1)S(1)}, u32[]{:S(2)}, u32[]{:S(2)}) collective-permute-start(bf16[2,8,4096]{2,1,0:T(8,128)(2,1)S(1)} %get-tuple-element.41), channel_id=1, source_target_pairs={{0,4},{4,0},{8,12},{12,8},{16,20},{20,16},{24,28},{28,24},{1,5},{5... | collective-permute-start | bytes 393224 | tf_op jit(solution)/shard_map/ppermute | solution.py:272
  17.7 5.8 %collective-permute-start.7 = (f32[16,128]{1,0:T(8,128)S(1)}, f32[16,128]{1,0:T(8,128)S(1)}, u32[]{:S(2)}, u32[]{:S(2)}) collective-permute-start(f32[16,128]{1,0:T(8,128)S(1)} %get-tuple-element.44.rest_0_), channel_id=1, source_target_pairs={{0,2},{1,3},{2,0},{3,1},{4,6},{5,7},{6,4},{7,5},{8,10},{9,11},{10,... | collective-permute-start | bytes 24584 | tf_op jit(solution)/shard_map/ppermute | solution.py:312
  20.2 4.3 %collective-permute-start.8 = (f32[16,128]{1,0:T(8,128)S(1)}, f32[16,128]{1,0:T(8,128)S(1)}, u32[]{:S(2)}, u32[]{:S(2)}) collective-permute-start(f32[16,128]{1,0:T(8,128)S(1)} %get-tuple-element.44.rest_0_), channel_id=1, source_target_pairs={{0,1},{1,2},{2,3},{3,0},{4,5},{5,6},{6,7},{7,4},{8,9},{9,10},{10,1... | collective-permute-start | bytes 24584 | tf_op jit(solution)/shard_map/ppermute | solution.py:312
  21.5 3.0 %collective-permute-start.9 = (f32[16,128]{1,0:T(8,128)S(1)}, f32[16,128]{1,0:T(8,128)S(1)}, u32[]{:S(2)}, u32[]{:S(2)}) collective-permute-start(f32[16,128]{1,0:T(8,128)S(1)} %get-tuple-element.44.rest_0_), channel_id=1, source_target_pairs={{0,3},{1,0},{2,1},{3,2},{4,7},{5,4},{6,5},{7,6},{8,11},{9,8},{10,9... | collective-permute-start | bytes 24584 | tf_op jit(solution)/shard_map/ppermute | solution.py:312
  24.5 10.8 %copy-start = (f32[16,8,4096]{2,1,0:T(8,128)S(1)}, f32[16,8,4096]{2,1,0:T(8,128)}, u32[]{:S(2)}) copy-start(f32[16,8,4096]{2,1,0:T(8,128)} %past_ref.1) | copy-start | bytes 6291460
  24.9 6.3 %collective-permute-start.10 = (bf16[2,8,4096]{2,1,0:T(8,128)(2,1)S(1)}, bf16[2,8,4096]{2,1,0:T(8,128)(2,1)S(1)}, u32[]{:S(2)}, u32[]{:S(2)}) collective-permute-start(bf16[2,8,4096]{2,1,0:T(8,128)(2,1)S(1)} %get-tuple-element.49), channel_id=1, source_target_pairs={{0,24},{4,28},{8,16},{12,20},{16,8},{20,12},{24,0},{28,4},{1,25},{... | collective-permute-start | bytes 393224 | tf_op jit(solution)/shard_map/ppermute | solution.py:272
  27.1 8.2 %collective-permute-start.11 = (bf16[2,8,4096]{2,1,0:T(8,128)(2,1)S(1)}, bf16[2,8,4096]{2,1,0:T(8,128)(2,1)S(1)}, u32[]{:S(2)}, u32[]{:S(2)}) collective-permute-start(bf16[2,8,4096]{2,1,0:T(8,128)(2,1)S(1)} %get-tuple-element.50), channel_id=1, source_target_pairs={{0,8},{4,12},{8,0},{12,4},{16,24},{20,28},{24,16},{28,20},{1,9},{5... | collective-permute-start | bytes 393224 | tf_op jit(solution)/shard_map/ppermute | solution.py:272
  27.4 10.5 %collective-permute-start.12 = (bf16[2,8,4096]{2,1,0:T(8,128)(2,1)S(1)}, bf16[2,8,4096]{2,1,0:T(8,128)(2,1)S(1)}, u32[]{:S(2)}, u32[]{:S(2)}) collective-permute-start(bf16[2,8,4096]{2,1,0:T(8,128)(2,1)S(1)} %get-tuple-element.51), channel_id=1, source_target_pairs={{0,16},{4,20},{8,24},{12,28},{16,0},{20,4},{24,8},{28,12},{1,17},{... | collective-permute-start | bytes 393224 | tf_op jit(solution)/shard_map/ppermute | solution.py:272
  27.6 12.1 %collective-permute-start.13 = (bf16[2,8,4096]{2,1,0:T(8,128)(2,1)S(1)}, bf16[2,8,4096]{2,1,0:T(8,128)(2,1)S(1)}, u32[]{:S(2)}, u32[]{:S(2)}) collective-permute-start(bf16[2,8,4096]{2,1,0:T(8,128)(2,1)S(1)} %get-tuple-element.52), channel_id=1, source_target_pairs={{0,20},{4,16},{8,28},{12,24},{16,4},{20,0},{24,12},{28,8},{1,21},{... | collective-permute-start | bytes 393224 | tf_op jit(solution)/shard_map/ppermute | solution.py:272
  31.2 8.5 %collective-permute-start.14 = (bf16[2,8,4096]{2,1,0:T(8,128)(2,1)S(1)}, bf16[2,8,4096]{2,1,0:T(8,128)(2,1)S(1)}, u32[]{:S(2)}, u32[]{:S(2)}) collective-permute-start(bf16[2,8,4096]{2,1,0:T(8,128)(2,1)S(1)} %get-tuple-element.53), channel_id=1, source_target_pairs={{0,12},{4,8},{8,4},{12,0},{16,28},{20,24},{24,20},{28,16},{1,13},{... | collective-permute-start | bytes 393224 | tf_op jit(solution)/shard_map/ppermute | solution.py:272
  31.2 8.5 %collective-permute-start.15 = (bf16[2,8,4096]{2,1,0:T(8,128)(2,1)S(1)}, bf16[2,8,4096]{2,1,0:T(8,128)(2,1)S(1)}, u32[]{:S(2)}, u32[]{:S(2)}) collective-permute-start(bf16[2,8,4096]{2,1,0:T(8,128)(2,1)S(1)} %get-tuple-element.54), channel_id=1, source_target_pairs={{0,28},{4,24},{8,20},{12,16},{16,12},{20,8},{24,4},{28,0},{1,29},{... | collective-permute-start | bytes 393224 | tf_op jit(solution)/shard_map/ppermute | solution.py:272
  35.3 4.4 %collective-permute-start.16 = (bf16[2,8,4096]{2,1,0:T(8,128)(2,1)S(1)}, bf16[2,8,4096]{2,1,0:T(8,128)(2,1)S(1)}, u32[]{:S(2)}, u32[]{:S(2)}) collective-permute-start(bf16[2,8,4096]{2,1,0:T(8,128)(2,1)S(1)} %get-tuple-element.55), channel_id=1, source_target_pairs={{0,4},{4,0},{8,12},{12,8},{16,20},{20,16},{24,28},{28,24},{1,5},{5... | collective-permute-start | bytes 393224 | tf_op jit(solution)/shard_map/ppermute | solution.py:272

commit v9 on v8

--- a/solution.py
+++ b/solution.py
@@ -146,18 +146,26 @@
     )
 
 
+def diagonal(owned):
+    row = lax.broadcasted_iota(jnp.int32, (owned, 128), 0)
+    return row == lax.broadcasted_iota(jnp.int32, (owned, 128), 1)
+
+
 def combine_kernel(order, module_ref, weight_ref, total_ref, acc_in, *rest):
     pieces, (acc_ref, squares_ref) = rest[:-2], rest[-2:]
     me = lax.axis_index("path").astype(jnp.int32)
     subtract(me, pieces, order, module_ref, weight_ref, acc_ref)
     owned, rows, width = acc_ref.shape
+    sums = []
     for m in range(owned):
         inverse = 1.0 / jnp.maximum(jnp.full((rows, 128), total_ref[m], jnp.float32), 1.0)
         added = jnp.zeros((rows, 128), jnp.float32)
         for at in range(0, width, 128):
             raw = acc_ref[m, :, pl.ds(at, 128)] * inverse
             added = added + raw * raw
-        squares_ref[pl.ds(m, 1), :] = jnp.sum(added, axis=0, keepdims=True)
+        sums.append(jnp.sum(added, axis=0, keepdims=True))
+    sums = jnp.sum(jnp.concatenate(sums, axis=0), axis=1, keepdims=True)
+    squares_ref[...] = jnp.sum(jnp.where(diagonal(owned), sums, 0.0), axis=0, keepdims=True)
 
 
 def scales(entries, total, squares):
@@ -177,6 +185,7 @@
     total = jnp.concatenate(
         [jnp.full((1, 128), total_ref[m], jnp.float32) for m in range(owned)], axis=0
     )
+    summed = jnp.where(diagonal(owned), summed, 0.0)
     scale = scales(rows * width * shards, total, summed)
     for m in range(owned):
         scale_ref[m] = jnp.broadcast_to(scale[m : m + 1, :], (rows, 128))
@@ -265,7 +274,7 @@
     ]
     limits = pltpu.CompilerParams(vmem_limit_bytes=24 * 1024 * 1024)
     far = sorted(range(2, paths, 2), key=lambda d: (-d.bit_count(), d))
-    order = far + [d + 1 for d in far[::-1]] + [1]
+    order = far + [d + 1 for d in far[-1:] + far[:-1]] + [1]
 
     def exchange(pieces):
         return [
@@ -301,7 +310,7 @@
     )(module_ids, counts, *in_vmem(packed[-1]), *in_hbm(global_params, momentum))
     acc, squares = pl.pallas_call(
         functools.partial(combine_kernel, order),
-        out_shape=[held_module, jax.ShapeDtypeStruct((owned, 128), jnp.float32)],
+        out_shape=[held_module, jax.ShapeDtypeStruct((1, 128), jnp.float32)],
         in_specs=[SMEM] * 3 + [VMEM] * paths,
         out_specs=[VMEM] * 2,
         input_output_aliases={3: 0},

time: 41.4 us -> 41.2 us (level)
  starting transfers between devices: 28 us -> 27.3 us
  waiting for transfers between devices: 3.25 us -> 3.72 us
    ppermute x14, waiting for transfers between devices: 2.21 us -> 2.79 us  [exchange(): lax.ppermute(x, 'path', [(i, i ^ d) for i in range(paths)])]
  transfers between devices with their start and end apart: 17 -> 17, of which waited for: 3 -> 4; matrix products, arithmetic and copies ran while one was open for 0% -> 0% of each run, Pallas kernels for 14% -> 14%
where the time goes in v9:
time: 41.2 us; the launch traced here: 40.7 us
  starting transfers between devices  27.3 us (66%)
  Pallas kernels  8.96 us (22%)
  waiting for transfers between devices  3.72 us (9%)
  between operations  0.7 us (2%)
    ppermute x14, starting transfers between devices, exchange(): lax.ppermute(x, 'path', [(i, i ^ d) for i in range(paths)])  21.7 us
    ppermute x3, starting transfers between devices, on_device(): lax.ppermute(squares, 'shard', [(i, (i + d) % shards) for i in range(shar...  5.59 us
    pallas_call x1, Pallas kernels, on_device(): pl.pallas_call(early_kernel, out_shape=tables + [held_module] * 2, in_spe...  3.12 us
    ppermute x14, waiting for transfers between devices, exchange(): lax.ppermute(x, 'path', [(i, i ^ d) for i in range(paths)])  2.79 us
    pallas_call x1, Pallas kernels, on_device(): pl.pallas_call(store_kernel, out_shape=[module] * 2, in_specs=[VMEM] * 4,...  2.52 us
    pallas_call x1, Pallas kernels, on_device(): pl.pallas_call(functools.partial(pack_kernel, owned, [*order, 0]), out_sh...  1.31 us
    pallas_call x1, Pallas kernels, on_device(): pl.pallas_call(functools.partial(unpack_kernel, [*order, 0]), out_shape=j...  1.11 us
    ppermute x3, waiting for transfers between devices, on_device(): lax.ppermute(squares, 'shard', [(i, (i + d) % shards) for i in range(shar...  0.93 us
  transfers between devices with their start and end apart: 17, of which 4 were waited for; matrix products, arithmetic and copies ran while one was open for 0% of the time, Pallas kernels for 14%

profile of v9, /device:TPU:1, one launch (start us, length us, event | category | flops | bytes accessed | tf_op | source)
XLA Modules:
  0.0 40.7 jit_solution(6012664351417049986)
XLA Ops:
  0.6 1.3 %pack.1 = (s32[16]{0:T(128)S(4)}, bf16[2,8,4096]{2,1,0:T(8,128)(2,1)S(1)}, bf16[2,8,4096]{2,1,0:T(8,128)(2,1)S(1)}, bf16[2,8,4096]{2,1,0:T(8,128)(2,1)S(1)}, bf1...) custom-call(s32[8,16]{1,0:T(8,128)} %ids_ref.1, ...), custom_call_target="tpu_custom_call" | custom-call | tf_op jit(solution)/shard_map/pack/pallas_call | solution.py:285
  1.9 3.1 %collective-permute-start = (bf16[2,8,4096]{2,1,0:T(8,128)(2,1)S(1)}, bf16[2,8,4096]{2,1,0:T(8,128)(2,1)S(1)}, u32[]{:S(2)}, u32[]{:S(2)}) collective-permute-start(bf16[2,8,4096]{2,1,0:T(8,128)(2,1)S(1)} %get-tuple-element.35), channel_id=1, source_target_pairs={{0,24},{4,28},{8,16},{12,20},{16,8},{20,12},{24,0},{28,4},{1,25},{... | collective-permute-start | bytes 393224 | tf_op jit(solution)/shard_map/ppermute | solution.py:281
  5.0 0.3 collective-permute-start.1
  5.4 2.8 %collective-permute-start.3 = (bf16[2,8,4096]{2,1,0:T(8,128)(2,1)S(1)}, bf16[2,8,4096]{2,1,0:T(8,128)(2,1)S(1)}, u32[]{:S(2)}, u32[]{:S(2)}) collective-permute-start(bf16[2,8,4096]{2,1,0:T(8,128)(2,1)S(1)} %get-tuple-element.38), channel_id=1, source_target_pairs={{0,20},{4,16},{8,28},{12,24},{16,4},{20,0},{24,12},{28,8},{1,21},{... | collective-permute-start | bytes 393224 | tf_op jit(solution)/shard_map/ppermute | solution.py:281
  8.1 0.9 %collective-permute-start.4 = (bf16[2,8,4096]{2,1,0:T(8,128)(2,1)S(1)}, bf16[2,8,4096]{2,1,0:T(8,128)(2,1)S(1)}, u32[]{:S(2)}, u32[]{:S(2)}) collective-permute-start(bf16[2,8,4096]{2,1,0:T(8,128)(2,1)S(1)} %get-tuple-element.39), channel_id=1, source_target_pairs={{0,28},{4,24},{8,20},{12,16},{16,12},{20,8},{24,4},{28,0},{1,29},{... | collective-permute-start | bytes 393224 | tf_op jit(solution)/shard_map/ppermute | solution.py:281
  9.1 2.8 %collective-permute-start.5 = (bf16[2,8,4096]{2,1,0:T(8,128)(2,1)S(1)}, bf16[2,8,4096]{2,1,0:T(8,128)(2,1)S(1)}, u32[]{:S(2)}, u32[]{:S(2)}) collective-permute-start(bf16[2,8,4096]{2,1,0:T(8,128)(2,1)S(1)} %get-tuple-element.40), channel_id=1, source_target_pairs={{0,12},{4,8},{8,4},{12,0},{16,28},{20,24},{24,20},{28,16},{1,13},{... | collective-permute-start | bytes 393224 | tf_op jit(solution)/shard_map/ppermute | solution.py:281
  11.9 1.8 %collective-permute-start.6 = (bf16[2,8,4096]{2,1,0:T(8,128)(2,1)S(1)}, bf16[2,8,4096]{2,1,0:T(8,128)(2,1)S(1)}, u32[]{:S(2)}, u32[]{:S(2)}) collective-permute-start(bf16[2,8,4096]{2,1,0:T(8,128)(2,1)S(1)} %get-tuple-element.41), channel_id=1, source_target_pairs={{0,4},{4,0},{8,12},{12,8},{16,20},{20,16},{24,28},{28,24},{1,5},{5... | collective-permute-start | bytes 393224 | tf_op jit(solution)/shard_map/ppermute | solution.py:281
  13.7 3.1 %early.1 = (s32[24]{0:T(128)S(4)}, f32[24]{0:T(128)S(4)}, f32[16]{0:T(128)S(4)}, f32[16,8,4096]{2,1,0:T(8,128)S(1)}, f32[16,8,4096]{2,1,0:T(8,128)S(1)}) custom-call(s32[8,16]{1,0:T(8,128)} %ids_ref.1, s32[8,16]{1,0:T(8,128)} %counts_ref.1, bf16[2,8,4096]{2,1,0:T(8,128)(2,1)S(1)} %get-tuple-element.30.own_ref, f32[16,8,4096]{2,1,0:T(8,128)} %params_hbm.1, ...), custom_call_target="tpu_custom_call" | custom-call | flops 1000000 | bytes 12582912 | tf_op jit(solution)/shard_map/early/pallas_call | solution.py:301
  16.8 0.4 collective-permute-done.3.rest_3_
  17.4 0.5 %combine.1 = (f32[16,8,4096]{2,1,0:T(8,128)S(1)}, f32[1,128]{1,0:T(1,128)S(1)}) custom-call(s32[24]{0:T(128)S(4)} %get-tuple-element.31.module_ref, f32[24]{0:T(128)S(4)} %get-tuple-element.33.weight_ref, f32[16]{0:T(128)S(4)} %get-tuple-element.32.total_ref, f32[16,8,4096]{2,1,0:T(8,128)S(1)} %get-tuple-element.34.acc_in, ...), custom_call_target="tpu_custom_call", output_to_operand_aliasing={{0}: (3, {})} | custom-call | tf_op jit(solution)/shard_map/combine/pallas_call | solution.py:311
  18.0 2.3 %collective-permute-start.7 = (f32[1,128]{1,0:T(1,128)S(1)}, f32[1,128]{1,0:T(1,128)S(1)}, u32[]{:S(2)}, u32[]{:S(2)}) collective-permute-start(f32[1,128]{1,0:T(1,128)S(1)} %get-tuple-element.44.rest_0_), channel_id=1, source_target_pairs={{0,2},{1,3},{2,0},{3,1},{4,6},{5,7},{6,4},{7,5},{8,10},{9,11},{10,... | collective-permute-start | bytes 1544 | tf_op jit(solution)/shard_map/ppermute | solution.py:321
  20.3 1.3 %collective-permute-start.8 = (f32[1,128]{1,0:T(1,128)S(1)}, f32[1,128]{1,0:T(1,128)S(1)}, u32[]{:S(2)}, u32[]{:S(2)}) collective-permute-start(f32[1,128]{1,0:T(1,128)S(1)} %get-tuple-element.44.rest_0_), channel_id=1, source_target_pairs={{0,1},{1,2},{2,3},{3,0},{4,5},{5,6},{6,7},{7,4},{8,9},{9,10},{10,1... | collective-permute-start | bytes 1544 | tf_op jit(solution)/shard_map/ppermute | solution.py:321
  21.6 2.0 %collective-permute-start.9 = (f32[1,128]{1,0:T(1,128)S(1)}, f32[1,128]{1,0:T(1,128)S(1)}, u32[]{:S(2)}, u32[]{:S(2)}) collective-permute-start(f32[1,128]{1,0:T(1,128)S(1)} %get-tuple-element.44.rest_0_), channel_id=1, source_target_pairs={{0,3},{1,0},{2,1},{3,2},{4,7},{5,4},{6,5},{7,6},{8,11},{9,8},{10,9... | collective-permute-start | bytes 1544 | tf_op jit(solution)/shard_map/ppermute | solution.py:321
  23.6 0.9 %collective-permute-done.8.rest_2_ = f32[1,128]{1,0:T(1,128)S(1)} collective-permute-done((f32[1,128]{1,0:T(1,128)S(1)}, f32[1,128]{1,0:T(1,128)S(1)}, u32[]{:S(2)}, u32[]{:S(2)}) %collective-permute-start.8) | collective-permute-done | bytes 544 | tf_op jit(solution)/shard_map/ppermute | solution.py:321
  24.5 0.4 send.1
  24.9 2.2 %collective-permute-start.10 = (bf16[2,8,4096]{2,1,0:T(8,128)(2,1)S(1)}, bf16[2,8,4096]{2,1,0:T(8,128)(2,1)S(1)}, u32[]{:S(2)}, u32[]{:S(2)}) collective-permute-start(bf16[2,8,4096]{2,1,0:T(8,128)(2,1)S(1)} %get-tuple-element.49), channel_id=1, source_target_pairs={{0,24},{4,28},{8,16},{12,20},{16,8},{20,12},{24,0},{28,4},{1,25},{... | collective-permute-start | bytes 393224 | tf_op jit(solution)/shard_map/ppermute | solution.py:281
  27.3 0.3 collective-permute-start.12
  27.6 3.8 %collective-permute-start.13 = (bf16[2,8,4096]{2,1,0:T(8,128)(2,1)S(1)}, bf16[2,8,4096]{2,1,0:T(8,128)(2,1)S(1)}, u32[]{:S(2)}, u32[]{:S(2)}) collective-permute-start(bf16[2,8,4096]{2,1,0:T(8,128)(2,1)S(1)} %get-tuple-element.52), channel_id=1, source_target_pairs={{0,20},{4,16},{8,28},{12,24},{16,4},{20,0},{24,12},{28,8},{1,21},{... | collective-permute-start | bytes 393224 | tf_op jit(solution)/shard_map/ppermute | solution.py:281
  31.3 0.9 %collective-permute-start.14 = (bf16[2,8,4096]{2,1,0:T(8,128)(2,1)S(1)}, bf16[2,8,4096]{2,1,0:T(8,128)(2,1)S(1)}, u32[]{:S(2)}, u32[]{:S(2)}) collective-permute-start(bf16[2,8,4096]{2,1,0:T(8,128)(2,1)S(1)} %get-tuple-element.53), channel_id=1, source_target_pairs={{0,28},{4,24},{8,20},{12,16},{16,12},{20,8},{24,4},{28,0},{1,29},{... | collective-permute-start | bytes 393224 | tf_op jit(solution)/shard_map/ppermute | solution.py:281
  32.3 2.1 %collective-permute-start.15 = (bf16[2,8,4096]{2,1,0:T(8,128)(2,1)S(1)}, bf16[2,8,4096]{2,1,0:T(8,128)(2,1)S(1)}, u32[]{:S(2)}, u32[]{:S(2)}) collective-permute-start(bf16[2,8,4096]{2,1,0:T(8,128)(2,1)S(1)} %get-tuple-element.54), channel_id=1, source_target_pairs={{0,12},{4,8},{8,4},{12,0},{16,28},{20,24},{24,20},{28,16},{1,13},{... | collective-permute-start | bytes 393224 | tf_op jit(solution)/shard_map/ppermute | solution.py:281
  34.4 0.5 %collective-permute-start.16 = (bf16[2,8,4096]{2,1,0:T(8,128)(2,1)S(1)}, bf16[2,8,4096]{2,1,0:T(8,128)(2,1)S(1)}, u32[]{:S(2)}, u32[]{:S(2)}) collective-permute-start(bf16[2,8,4096]{2,1,0:T(8,128)(2,1)S(1)} %get-tuple-element.55), channel_id=1, source_target_pairs={{0,4},{4,0},{8,12},{12,8},{16,20},{20,16},{24,28},{28,24},{1,5},{5... | collective-permute-start | bytes 393224 | tf_op jit(solution)/shard_map/ppermute | solution.py:281
  34.9 2.5 %store.1 = (f32[16,8,4096]{2,1,0:T(8,128)}, f32[16,8,4096]{2,1,0:T(8,128)}) custom-call(f32[16,8,128]{2,1,0:T(8,128)S(1)} %get-tuple-element.45.scale_ref, f32[16,8,4096]{2,1,0:T(8,128)S(1)} %get-tuple-element.42.acc_ref, f32[16,8,4096]{2,1,0:T(8,128)S(1)} %get-tuple-element.43.base_ref, f32[16,8,4096]{2,1,0:T(8,128)S(1)} %copy-done), custom_call_target="tpu_custom_call" | custom-call | flops 1000000 | bytes 12582912 | tf_op jit(solution)/shard_map/store/pallas_call | solution.py:333
  37.4 2.1 %collective-permute-done.13.rest_3_ = bf16[2,8,4096]{2,1,0:T(8,128)(2,1)S(1)} collective-permute-done((bf16[2,8,4096]{2,1,0:T(8,128)(2,1)S(1)}, bf16[2,8,4096]{2,1,0:T(8,128)(2,1)S(1)}, u32[]{:S(2)}, u32[]{:S(2)}) %collective-permute-start.13) | collective-permute-done | bytes 131104 | tf_op jit(solution)/shard_map/ppermute | solution.py:281
  39.6 1.1 %unpack.1 = bf16[1,16,8,4096]{3,2,1,0:T(8,128)(2,1)} custom-call(s32[16]{0:T(128)S(4)} %get-tuple-element.48.places_ref, bf16[2,8,4096]{2,1,0:T(8,128)(2,1)S(1)} %collective-permute-done.10.rest_0_, bf16[2,8,4096]{2,1,0:T(8,128)(2,1)S(1)} %collective-permute-done.11.rest_1_, bf16[2,8,4096]{2,1,0:T(8,128)(2,1)S(1)} %collective-permute-done.12.rest_2_, ...), custom_call_target="tpu_custom_call" | custom-call | tf_op jit(solution)/shard_map/unpack/pallas_call | solution.py:343
  (18 shorter events, 0.6 us)
Async XLA Ops:
  1.9 7.1 %collective-permute-start = (bf16[2,8,4096]{2,1,0:T(8,128)(2,1)S(1)}, bf16[2,8,4096]{2,1,0:T(8,128)(2,1)S(1)}, u32[]{:S(2)}, u32[]{:S(2)}) collective-permute-start(bf16[2,8,4096]{2,1,0:T(8,128)(2,1)S(1)} %get-tuple-element.35), channel_id=1, source_target_pairs={{0,24},{4,28},{8,16},{12,20},{16,8},{20,12},{24,0},{28,4},{1,25},{... | collective-permute-start | bytes 393224 | tf_op jit(solution)/shard_map/ppermute | solution.py:281
  5.0 6.9 %collective-permute-start.1 = (bf16[2,8,4096]{2,1,0:T(8,128)(2,1)S(1)}, bf16[2,8,4096]{2,1,0:T(8,128)(2,1)S(1)}, u32[]{:S(2)}, u32[]{:S(2)}) collective-permute-start(bf16[2,8,4096]{2,1,0:T(8,128)(2,1)S(1)} %get-tuple-element.36), channel_id=1, source_target_pairs={{0,8},{4,12},{8,0},{12,4},{16,24},{20,28},{24,16},{28,20},{1,9},{5... | collective-permute-start | bytes 393224 | tf_op jit(solution)/shard_map/ppermute | solution.py:281
  5.3 11.5 %collective-permute-start.2 = (bf16[2,8,4096]{2,1,0:T(8,128)(2,1)S(1)}, bf16[2,8,4096]{2,1,0:T(8,128)(2,1)S(1)}, u32[]{:S(2)}, u32[]{:S(2)}) collective-permute-start(bf16[2,8,4096]{2,1,0:T(8,128)(2,1)S(1)} %get-tuple-element.37), channel_id=1, source_target_pairs={{0,16},{4,20},{8,24},{12,28},{16,0},{20,4},{24,8},{28,12},{1,17},{... | collective-permute-start | bytes 393224 | tf_op jit(solution)/shard_map/ppermute | solution.py:281
  5.4 11.8 %collective-permute-start.3 = (bf16[2,8,4096]{2,1,0:T(8,128)(2,1)S(1)}, bf16[2,8,4096]{2,1,0:T(8,128)(2,1)S(1)}, u32[]{:S(2)}, u32[]{:S(2)}) collective-permute-start(bf16[2,8,4096]{2,1,0:T(8,128)(2,1)S(1)} %get-tuple-element.38), channel_id=1, source_target_pairs={{0,20},{4,16},{8,28},{12,24},{16,4},{20,0},{24,12},{28,8},{1,21},{... | collective-permute-start | bytes 393224 | tf_op jit(solution)/shard_map/ppermute | solution.py:281
  8.1 9.1 %collective-permute-start.4 = (bf16[2,8,4096]{2,1,0:T(8,128)(2,1)S(1)}, bf16[2,8,4096]{2,1,0:T(8,128)(2,1)S(1)}, u32[]{:S(2)}, u32[]{:S(2)}) collective-permute-start(bf16[2,8,4096]{2,1,0:T(8,128)(2,1)S(1)} %get-tuple-element.39), channel_id=1, source_target_pairs={{0,28},{4,24},{8,20},{12,16},{16,12},{20,8},{24,4},{28,0},{1,29},{... | collective-permute-start | bytes 393224 | tf_op jit(solution)/shard_map/ppermute | solution.py:281
  9.1 8.4 %collective-permute-start.5 = (bf16[2,8,4096]{2,1,0:T(8,128)(2,1)S(1)}, bf16[2,8,4096]{2,1,0:T(8,128)(2,1)S(1)}, u32[]{:S(2)}, u32[]{:S(2)}) collective-permute-start(bf16[2,8,4096]{2,1,0:T(8,128)(2,1)S(1)} %get-tuple-element.40), channel_id=1, source_target_pairs={{0,12},{4,8},{8,4},{12,0},{16,28},{20,24},{24,20},{28,16},{1,13},{... | collective-permute-start | bytes 393224 | tf_op jit(solution)/shard_map/ppermute | solution.py:281
  11.9 5.6 %collective-permute-start.6 = (bf16[2,8,4096]{2,1,0:T(8,128)(2,1)S(1)}, bf16[2,8,4096]{2,1,0:T(8,128)(2,1)S(1)}, u32[]{:S(2)}, u32[]{:S(2)}) collective-permute-start(bf16[2,8,4096]{2,1,0:T(8,128)(2,1)S(1)} %get-tuple-element.41), channel_id=1, source_target_pairs={{0,4},{4,0},{8,12},{12,8},{16,20},{20,16},{24,28},{28,24},{1,5},{5... | collective-permute-start | bytes 393224 | tf_op jit(solution)/shard_map/ppermute | solution.py:281
  18.0 5.6 %collective-permute-start.7 = (f32[1,128]{1,0:T(1,128)S(1)}, f32[1,128]{1,0:T(1,128)S(1)}, u32[]{:S(2)}, u32[]{:S(2)}) collective-permute-start(f32[1,128]{1,0:T(1,128)S(1)} %get-tuple-element.44.rest_0_), channel_id=1, source_target_pairs={{0,2},{1,3},{2,0},{3,1},{4,6},{5,7},{6,4},{7,5},{8,10},{9,11},{10,... | collective-permute-start | bytes 1544 | tf_op jit(solution)/shard_map/ppermute | solution.py:321
  20.3 4.2 %collective-permute-start.8 = (f32[1,128]{1,0:T(1,128)S(1)}, f32[1,128]{1,0:T(1,128)S(1)}, u32[]{:S(2)}, u32[]{:S(2)}) collective-permute-start(f32[1,128]{1,0:T(1,128)S(1)} %get-tuple-element.44.rest_0_), channel_id=1, source_target_pairs={{0,1},{1,2},{2,3},{3,0},{4,5},{5,6},{6,7},{7,4},{8,9},{9,10},{10,1... | collective-permute-start | bytes 1544 | tf_op jit(solution)/shard_map/ppermute | solution.py:321
  21.6 2.9 %collective-permute-start.9 = (f32[1,128]{1,0:T(1,128)S(1)}, f32[1,128]{1,0:T(1,128)S(1)}, u32[]{:S(2)}, u32[]{:S(2)}) collective-permute-start(f32[1,128]{1,0:T(1,128)S(1)} %get-tuple-element.44.rest_0_), channel_id=1, source_target_pairs={{0,3},{1,0},{2,1},{3,2},{4,7},{5,4},{6,5},{7,6},{8,11},{9,8},{10,9... | collective-permute-start | bytes 1544 | tf_op jit(solution)/shard_map/ppermute | solution.py:321
  24.5 10.4 %copy-start = (f32[16,8,4096]{2,1,0:T(8,128)S(1)}, f32[16,8,4096]{2,1,0:T(8,128)}, u32[]{:S(2)}) copy-start(f32[16,8,4096]{2,1,0:T(8,128)} %past_ref.1) | copy-start | bytes 6291460
  24.9 7.4 %collective-permute-start.10 = (bf16[2,8,4096]{2,1,0:T(8,128)(2,1)S(1)}, bf16[2,8,4096]{2,1,0:T(8,128)(2,1)S(1)}, u32[]{:S(2)}, u32[]{:S(2)}) collective-permute-start(bf16[2,8,4096]{2,1,0:T(8,128)(2,1)S(1)} %get-tuple-element.49), channel_id=1, source_target_pairs={{0,24},{4,28},{8,16},{12,20},{16,8},{20,12},{24,0},{28,4},{1,25},{... | collective-permute-start | bytes 393224 | tf_op jit(solution)/shard_map/ppermute | solution.py:281
  27.1 7.3 %collective-permute-start.11 = (bf16[2,8,4096]{2,1,0:T(8,128)(2,1)S(1)}, bf16[2,8,4096]{2,1,0:T(8,128)(2,1)S(1)}, u32[]{:S(2)}, u32[]{:S(2)}) collective-permute-start(bf16[2,8,4096]{2,1,0:T(8,128)(2,1)S(1)} %get-tuple-element.50), channel_id=1, source_target_pairs={{0,8},{4,12},{8,0},{12,4},{16,24},{20,28},{24,16},{28,20},{1,9},{5... | collective-permute-start | bytes 393224 | tf_op jit(solution)/shard_map/ppermute | solution.py:281
  27.3 10.1 %collective-permute-start.12 = (bf16[2,8,4096]{2,1,0:T(8,128)(2,1)S(1)}, bf16[2,8,4096]{2,1,0:T(8,128)(2,1)S(1)}, u32[]{:S(2)}, u32[]{:S(2)}) collective-permute-start(bf16[2,8,4096]{2,1,0:T(8,128)(2,1)S(1)} %get-tuple-element.51), channel_id=1, source_target_pairs={{0,16},{4,20},{8,24},{12,28},{16,0},{20,4},{24,8},{28,12},{1,17},{... | collective-permute-start | bytes 393224 | tf_op jit(solution)/shard_map/ppermute | solution.py:281
  27.6 12.0 %collective-permute-start.13 = (bf16[2,8,4096]{2,1,0:T(8,128)(2,1)S(1)}, bf16[2,8,4096]{2,1,0:T(8,128)(2,1)S(1)}, u32[]{:S(2)}, u32[]{:S(2)}) collective-permute-start(bf16[2,8,4096]{2,1,0:T(8,128)(2,1)S(1)} %get-tuple-element.52), channel_id=1, source_target_pairs={{0,20},{4,16},{8,28},{12,24},{16,4},{20,0},{24,12},{28,8},{1,21},{... | collective-permute-start | bytes 393224 | tf_op jit(solution)/shard_map/ppermute | solution.py:281
  31.3 8.2 %collective-permute-start.14 = (bf16[2,8,4096]{2,1,0:T(8,128)(2,1)S(1)}, bf16[2,8,4096]{2,1,0:T(8,128)(2,1)S(1)}, u32[]{:S(2)}, u32[]{:S(2)}) collective-permute-start(bf16[2,8,4096]{2,1,0:T(8,128)(2,1)S(1)} %get-tuple-element.53), channel_id=1, source_target_pairs={{0,28},{4,24},{8,20},{12,16},{16,12},{20,8},{24,4},{28,0},{1,29},{... | collective-permute-start | bytes 393224 | tf_op jit(solution)/shard_map/ppermute | solution.py:281
  32.3 7.3 %collective-permute-start.15 = (bf16[2,8,4096]{2,1,0:T(8,128)(2,1)S(1)}, bf16[2,8,4096]{2,1,0:T(8,128)(2,1)S(1)}, u32[]{:S(2)}, u32[]{:S(2)}) collective-permute-start(bf16[2,8,4096]{2,1,0:T(8,128)(2,1)S(1)} %get-tuple-element.54), channel_id=1, source_target_pairs={{0,12},{4,8},{8,4},{12,0},{16,28},{20,24},{24,20},{28,16},{1,13},{... | collective-permute-start | bytes 393224 | tf_op jit(solution)/shard_map/ppermute | solution.py:281
  34.4 5.2 %collective-permute-start.16 = (bf16[2,8,4096]{2,1,0:T(8,128)(2,1)S(1)}, bf16[2,8,4096]{2,1,0:T(8,128)(2,1)S(1)}, u32[]{:S(2)}, u32[]{:S(2)}) collective-permute-start(bf16[2,8,4096]{2,1,0:T(8,128)(2,1)S(1)} %get-tuple-element.55), channel_id=1, source_target_pairs={{0,4},{4,0},{8,12},{12,8},{16,20},{20,16},{24,28},{28,24},{1,5},{5... | collective-permute-start | bytes 393224 | tf_op jit(solution)/shard_map/ppermute | solution.py:281

commit v10 on v9

--- a/solution.py
+++ b/solution.py
@@ -10,6 +10,7 @@
 CAP = 2
 CHUNK = 1024
 PARTS = 4
+SOON = 2
 outer_momentum = 0.9
 outer_rate = 0.7
 
@@ -39,14 +40,15 @@
     pieces, (ids_ref, local_ref, seen, sems) = rest[:-4], rest[-4:]
     me = lax.axis_index("path").astype(jnp.int32)
     paths, held = ids_ref.shape
-    part = held // PARTS
-    ids_copy = pltpu.make_async_copy(ids_hbm, ids_ref, sems.at[PARTS])
+    parts = chunks(local_ref.shape[2])
+    ids_copy = pltpu.make_async_copy(ids_hbm, ids_ref, sems.at[len(parts)])
     ids_copy.start()
-    copies = []
-    for i in range(PARTS):
-        at = pl.ds(i * part, part)
-        copies.append(pltpu.make_async_copy(local_hbm.at[at], local_ref.at[at], sems.at[i]))
-        copies[-1].start()
+    copies = [
+        pltpu.make_async_copy(local_hbm.at[:, :, c], local_ref.at[:, :, c], sems.at[i])
+        for i, c in enumerate(parts)
+    ]
+    for copy in copies:
+        copy.start()
     for i in range(paths):
         seen[i] = jnp.int32(0)
     for i in range(paths * CAP):
@@ -57,11 +59,12 @@
         rank = seen[group]
         seen[group] = rank + 1
         places_ref[group * CAP + rank] = jnp.int32(k)
-    for copy in copies:
+    for c, copy in zip(parts, copies, strict=True):
         copy.wait()
-    for d, piece in zip(order, pieces, strict=True):
-        for r in range(CAP):
-            piece[r] = local_ref[jnp.maximum(places_ref[(me ^ d) * CAP + r], 0)]
+        for d, piece in zip(order, pieces, strict=True):
+            for r in range(CAP):
+                k = jnp.maximum(places_ref[(me ^ d) * CAP + r], 0)
+                piece[r, :, c] = local_ref[k, :, c]
 
 
 def find_slots(me, owned, ids_ref, counts_ref, module_ref, weight_ref, total_ref):
@@ -200,9 +203,11 @@
                 )
 
 
-def store_kernel(
-    scale_ref, acc_ref, base_ref, past_ref, updated_hbm, velocity_hbm, updated_ref, velocity_ref, sems
-):
+def store_kernel(distances, places_ref, scale_ref, acc_ref, base_ref, past_ref, *rest):
+    n = len(distances)
+    pieces, (updated_hbm, velocity_hbm, out_hbm) = rest[:n], rest[n : n + 3]
+    updated_ref, velocity_ref, sems, piece_sems = rest[n + 3 :]
+    placed(distances, pieces, places_ref, out_hbm, piece_sems, start)
     rate = outer_rate * (1.0 + outer_momentum)
     owned, _, width = acc_ref.shape
     part = owned // PARTS
@@ -232,25 +237,32 @@
     for i in range(PARTS):
         for copy in copies(i):
             copy.wait()
-
-
-def unpack_kernel(order, places_ref, *rest):
-    pieces, (out_ref, sems) = rest[:-2], rest[-2:]
-    me = lax.axis_index("path").astype(jnp.int32)
-    for wait in (False, True):
-        for d, piece in zip(order, pieces, strict=True):
-            for r in range(CAP):
-                k = places_ref[(me ^ d) * CAP + r]
-
-                @pl.when(k >= 0)
-                def _():
-                    copy = pltpu.make_async_copy(
-                        piece.at[r], out_ref.at[0, k], sems.at[d * CAP + r]
-                    )
-                    if wait:
-                        copy.wait()
-                    else:
-                        copy.start()
+    placed(distances, pieces, places_ref, out_hbm, piece_sems, wait)
+
+
+def placed(distances, pieces, places_ref, out_ref, sems, act):
+    me = lax.axis_index("path").astype(jnp.int32)
+    for n, (d, piece) in enumerate(zip(distances, pieces, strict=True)):
+        for r in range(CAP):
+            k = places_ref[(me ^ d) * CAP + r]
+
+            @pl.when(k >= 0)
+            def _():
+                act(pltpu.make_async_copy(piece.at[r], out_ref.at[0, k], sems.at[n * CAP + r]))
+
+
+def start(copy):
+    copy.start()
+
+
+def wait(copy):
+    copy.wait()
+
+
+def unpack_kernel(distances, places_ref, *rest):
+    pieces, (out_ref, sems) = rest[: len(distances)], rest[-2:]
+    placed(distances, pieces, places_ref, out_ref, sems, start)
+    placed(distances, pieces, places_ref, out_ref, sems, wait)
 
 
 def on_device(path_params, global_params, momentum, module_ids, token_counts):
@@ -274,16 +286,17 @@
     ]
     limits = pltpu.CompilerParams(vmem_limit_bytes=24 * 1024 * 1024)
     far = sorted(range(2, paths, 2), key=lambda d: (-d.bit_count(), d))
-    order = far + [d + 1 for d in far[-1:] + far[:-1]] + [1]
-
-    def exchange(pieces):
+    there = far + [d + 1 for d in far[::-1]] + [1]
+    back = far + [d + 1 for d in far[-1:] + far[:-1]] + [1]
+
+    def exchange(order, pieces):
         return [
             lax.ppermute(x, "path", [(i, i ^ d) for i in range(paths)])
             for d, x in zip(order, pieces)
         ]
 
     places, *packed = pl.pallas_call(
-        functools.partial(pack_kernel, owned, [*order, 0]),
+        functools.partial(pack_kernel, owned, [*there, 0]),
         out_shape=[pltpu.SMEM((slots,), jnp.int32)] + [piece] * paths,
         in_specs=[ANY] * 2,
         out_specs=[SMEM] + [VMEM] * paths,
@@ -291,13 +304,13 @@
             pltpu.SMEM(module_ids.shape, jnp.int32),
             pltpu.VMEM((held, rows, width), jnp.bfloat16),
             pltpu.SMEM((paths,), jnp.int32),
-            pltpu.SemaphoreType.DMA((PARTS + 1,)),
+            pltpu.SemaphoreType.DMA((len(chunks(width)) + 1,)),
         ],
         compiler_params=limits,
         name="pack",
     )(module_ids, *in_hbm(path_params.reshape(held, rows, width)))
 
-    arrived = exchange(packed)
+    arrived = exchange(there, packed)
     table, weights, total, acc, base = pl.pallas_call(
         early_kernel,
         out_shape=tables + [held_module] * 2,
@@ -309,7 +322,7 @@
         name="early",
     )(module_ids, counts, *in_vmem(packed[-1]), *in_hbm(global_params, momentum))
     acc, squares = pl.pallas_call(
-        functools.partial(combine_kernel, order),
+        functools.partial(combine_kernel, there),
         out_shape=[held_module, jax.ShapeDtypeStruct((1, 128), jnp.float32)],
         in_specs=[SMEM] * 3 + [VMEM] * paths,
         out_specs=[VMEM] * 2,
@@ -319,35 +332,41 @@
     )(*in_smem(table, weights, total), *in_vmem(acc, *arrived))
     parts = [squares] + [
         lax.ppermute(squares, "shard", [(i, (i + d) % shards) for i in range(shards)])
-        for d in sorted(range(1, shards), key=lambda d: (d != 2, d))
+        for d in sorted(range(1, shards), key=lambda d: (d == 2, -d))
     ]
     scale, *outgoing = pl.pallas_call(
-        functools.partial(send_kernel, [*order, 0], shards),
+        functools.partial(send_kernel, [*back, 0], shards),
         out_shape=[jax.ShapeDtypeStruct((owned, rows, 128), jnp.float32)] + [piece] * paths,
         in_specs=[SMEM] * 2 + [VMEM] * (2 + shards),
         out_specs=[VMEM] * (1 + paths),
         compiler_params=limits,
         name="send",
     )(*in_smem(table, total), *in_vmem(acc, base), *parts)
-    returned = [*exchange(outgoing), outgoing[-1]]
-    updated, velocity = pl.pallas_call(
-        store_kernel,
-        out_shape=[module] * 2,
-        in_specs=[VMEM] * 4,
-        out_specs=[ANY] * 2,
-        scratch_shapes=room,
+    returned = {0: outgoing[-1], **dict(zip(back, exchange(back, outgoing)))}
+    soon, last = [0, *back[:SOON]], back[SOON:]
+    whole = jax.ShapeDtypeStruct(path_params.shape, path_params.dtype)
+    updated, velocity, path_out = pl.pallas_call(
+        functools.partial(store_kernel, soon),
+        out_shape=[module] * 2 + [whole],
+        in_specs=[SMEM] + [VMEM] * (4 + len(soon)),
+        out_specs=[ANY] * 3,
+        scratch_shapes=room + [pltpu.SemaphoreType.DMA((len(soon) * CAP,))],
         compiler_params=limits,
         cost_estimate=pl.CostEstimate(flops=10**6, bytes_accessed=12 * 2**20, transcendentals=0),
         name="store",
-    )(scale, *in_vmem(acc, base), momentum)
+    )(
+        *in_smem(places), scale, *in_vmem(acc, base), momentum,
+        *in_vmem(*[returned[d] for d in soon]),
+    )
     path_out = pl.pallas_call(
-        functools.partial(unpack_kernel, [*order, 0]),
-        out_shape=jax.ShapeDtypeStruct(path_params.shape, path_params.dtype),
-        in_specs=[SMEM] + [VMEM] * paths,
+        functools.partial(unpack_kernel, last),
+        out_shape=whole,
+        in_specs=[SMEM] + [VMEM] * len(last) + [ANY],
         out_specs=ANY,
-        scratch_shapes=[pltpu.SemaphoreType.DMA((slots,))],
+        input_output_aliases={1 + len(last): 0},
+        scratch_shapes=[pltpu.SemaphoreType.DMA((len(last) * CAP,))],
         name="unpack",
-    )(*in_smem(places), *in_vmem(*returned))
+    )(*in_smem(places), *in_vmem(*[returned[d] for d in last]), path_out)
     return updated, velocity, path_out
 
 

time: 41.2 us -> 40.7 us (0.988)
  waiting for transfers between devices: 3.72 us -> 3.17 us
    ppermute x14, waiting for transfers between devices: 2.79 us -> 2.24 us  [exchange(): lax.ppermute(x, 'path', [(i, i ^ d) for i in range(paths)])]
  transfers between devices with their start and end apart: 17 -> 17, of which waited for: 4 -> 3; matrix products, arithmetic and copies ran while one was open for 0% -> 0% of each run, Pallas kernels for 14% -> 14%
where the time goes in v10:
time: 40.7 us; the launch traced here: 40.4 us
  starting transfers between devices  27.7 us (68%)
  Pallas kernels  8.8 us (22%)
  waiting for transfers between devices  3.17 us (8%)
  between operations  0.71 us (2%)
    ppermute x14, starting transfers between devices, exchange(): lax.ppermute(x, 'path', [(i, i ^ d) for i in range(paths)])  22 us
    ppermute x3, starting transfers between devices, on_device(): lax.ppermute(squares, 'shard', [(i, (i + d) % shards) for i in range(shar...  5.77 us
    pallas_call x1, Pallas kernels, on_device(): pl.pallas_call(early_kernel, out_shape=tables + [held_module] * 2, in_spe...  3.12 us
    pallas_call x1, Pallas kernels, on_device(): pl.pallas_call(functools.partial(store_kernel, soon), out_shape=[module]...  2.59 us
    ppermute x14, waiting for transfers between devices, exchange(): lax.ppermute(x, 'path', [(i, i ^ d) for i in range(paths)])  2.24 us
    pallas_call x1, Pallas kernels, on_device(): pl.pallas_call(functools.partial(pack_kernel, owned, [*there, 0]), out_sh...  1.26 us
    pallas_call x1, Pallas kernels, on_device(): pl.pallas_call(functools.partial(unpack_kernel, last), out_shape=whole, i...  0.93 us
    ppermute x3, waiting for transfers between devices, on_device(): lax.ppermute(squares, 'shard', [(i, (i + d) % shards) for i in range(shar...  0.93 us
  transfers between devices with their start and end apart: 17, of which 3 were waited for; matrix products, arithmetic and copies ran while one was open for 0% of the time, Pallas kernels for 14%

profile of v10, /device:TPU:1, one launch (start us, length us, event | category | flops | bytes accessed | tf_op | source)
XLA Modules:
  0.0 40.4 jit_solution(5004542447836501445)
XLA Ops:
  0.6 1.3 %pack.1 = (s32[16]{0:T(128)S(4)}, bf16[2,8,4096]{2,1,0:T(8,128)(2,1)S(1)}, bf16[2,8,4096]{2,1,0:T(8,128)(2,1)S(1)}, bf16[2,8,4096]{2,1,0:T(8,128)(2,1)S(1)}, bf1...) custom-call(s32[8,16]{1,0:T(8,128)} %ids_ref.1, ...), custom_call_target="tpu_custom_call" | custom-call | tf_op jit(solution)/shard_map/pack/pallas_call | solution.py:298
  1.9 3.1 %collective-permute-start = (bf16[2,8,4096]{2,1,0:T(8,128)(2,1)S(1)}, bf16[2,8,4096]{2,1,0:T(8,128)(2,1)S(1)}, u32[]{:S(2)}, u32[]{:S(2)}) collective-permute-start(bf16[2,8,4096]{2,1,0:T(8,128)(2,1)S(1)} %get-tuple-element.37), channel_id=1, source_target_pairs={{0,24},{4,28},{8,16},{12,20},{16,8},{20,12},{24,0},{28,4},{1,25},{... | collective-permute-start | bytes 393224 | tf_op jit(solution)/shard_map/ppermute | solution.py:294
  5.0 0.3 collective-permute-start.1
  5.3 2.8 %collective-permute-start.3 = (bf16[2,8,4096]{2,1,0:T(8,128)(2,1)S(1)}, bf16[2,8,4096]{2,1,0:T(8,128)(2,1)S(1)}, u32[]{:S(2)}, u32[]{:S(2)}) collective-permute-start(bf16[2,8,4096]{2,1,0:T(8,128)(2,1)S(1)} %get-tuple-element.40), channel_id=1, source_target_pairs={{0,20},{4,16},{8,28},{12,24},{16,4},{20,0},{24,12},{28,8},{1,21},{... | collective-permute-start | bytes 393224 | tf_op jit(solution)/shard_map/ppermute | solution.py:294
  8.2 4.6 %collective-permute-start.5 = (bf16[2,8,4096]{2,1,0:T(8,128)(2,1)S(1)}, bf16[2,8,4096]{2,1,0:T(8,128)(2,1)S(1)}, u32[]{:S(2)}, u32[]{:S(2)}) collective-permute-start(bf16[2,8,4096]{2,1,0:T(8,128)(2,1)S(1)} %get-tuple-element.42), channel_id=1, source_target_pairs={{0,28},{4,24},{8,20},{12,16},{16,12},{20,8},{24,4},{28,0},{1,29},{... | collective-permute-start | bytes 393224 | tf_op jit(solution)/shard_map/ppermute | solution.py:294
  12.8 0.8 %collective-permute-start.6 = (bf16[2,8,4096]{2,1,0:T(8,128)(2,1)S(1)}, bf16[2,8,4096]{2,1,0:T(8,128)(2,1)S(1)}, u32[]{:S(2)}, u32[]{:S(2)}) collective-permute-start(bf16[2,8,4096]{2,1,0:T(8,128)(2,1)S(1)} %get-tuple-element.43), channel_id=1, source_target_pairs={{0,4},{4,0},{8,12},{12,8},{16,20},{20,16},{24,28},{28,24},{1,5},{5... | collective-permute-start | bytes 393224 | tf_op jit(solution)/shard_map/ppermute | solution.py:294
  13.6 3.1 %early.1 = (s32[24]{0:T(128)S(4)}, f32[24]{0:T(128)S(4)}, f32[16]{0:T(128)S(4)}, f32[16,8,4096]{2,1,0:T(8,128)S(1)}, f32[16,8,4096]{2,1,0:T(8,128)S(1)}) custom-call(s32[8,16]{1,0:T(8,128)} %ids_ref.1, s32[8,16]{1,0:T(8,128)} %counts_ref.1, bf16[2,8,4096]{2,1,0:T(8,128)(2,1)S(1)} %get-tuple-element.32.own_ref, f32[16,8,4096]{2,1,0:T(8,128)} %params_hbm.1, ...), custom_call_target="tpu_custom_call" | custom-call | flops 1000000 | bytes 12582912 | tf_op jit(solution)/shard_map/early/pallas_call | solution.py:314
  16.8 0.4 collective-permute-done.5.rest_5_
  17.2 0.5 %combine.1 = (f32[16,8,4096]{2,1,0:T(8,128)S(1)}, f32[1,128]{1,0:T(1,128)S(1)}) custom-call(s32[24]{0:T(128)S(4)} %get-tuple-element.33.module_ref, f32[24]{0:T(128)S(4)} %get-tuple-element.35.weight_ref, f32[16]{0:T(128)S(4)} %get-tuple-element.34.total_ref, f32[16,8,4096]{2,1,0:T(8,128)S(1)} %get-tuple-element.36.acc_in, ...), custom_call_target="tpu_custom_call", output_to_operand_aliasing={{0}: (3, {})} | custom-call | tf_op jit(solution)/shard_map/combine/pallas_call | solution.py:324
  17.7 2.5 %collective-permute-start.9 = (f32[1,128]{1,0:T(1,128)S(1)}, f32[1,128]{1,0:T(1,128)S(1)}, u32[]{:S(2)}, u32[]{:S(2)}) collective-permute-start(f32[1,128]{1,0:T(1,128)S(1)} %get-tuple-element.46.rest_0_), channel_id=1, source_target_pairs={{0,2},{1,3},{2,0},{3,1},{4,6},{5,7},{6,4},{7,5},{8,10},{9,11},{10,... | collective-permute-start | bytes 1544 | tf_op jit(solution)/shard_map/ppermute | solution.py:334
  20.2 1.3 %collective-permute-start.8 = (f32[1,128]{1,0:T(1,128)S(1)}, f32[1,128]{1,0:T(1,128)S(1)}, u32[]{:S(2)}, u32[]{:S(2)}) collective-permute-start(f32[1,128]{1,0:T(1,128)S(1)} %get-tuple-element.46.rest_0_), channel_id=1, source_target_pairs={{0,1},{1,2},{2,3},{3,0},{4,5},{5,6},{6,7},{7,4},{8,9},{9,10},{10,1... | collective-permute-start | bytes 1544 | tf_op jit(solution)/shard_map/ppermute | solution.py:334
  21.5 2.0 %collective-permute-start.7 = (f32[1,128]{1,0:T(1,128)S(1)}, f32[1,128]{1,0:T(1,128)S(1)}, u32[]{:S(2)}, u32[]{:S(2)}) collective-permute-start(f32[1,128]{1,0:T(1,128)S(1)} %get-tuple-element.46.rest_0_), channel_id=1, source_target_pairs={{0,3},{1,0},{2,1},{3,2},{4,7},{5,4},{6,5},{7,6},{8,11},{9,8},{10,9... | collective-permute-start | bytes 1544 | tf_op jit(solution)/shard_map/ppermute | solution.py:334
  23.5 0.9 %collective-permute-done.8.rest_2_ = f32[1,128]{1,0:T(1,128)S(1)} collective-permute-done((f32[1,128]{1,0:T(1,128)S(1)}, f32[1,128]{1,0:T(1,128)S(1)}, u32[]{:S(2)}, u32[]{:S(2)}) %collective-permute-start.8) | collective-permute-done | bytes 544 | tf_op jit(solution)/shard_map/ppermute | solution.py:334
  24.4 0.4 send.1
  24.8 2.2 %collective-permute-start.10 = (bf16[2,8,4096]{2,1,0:T(8,128)(2,1)S(1)}, bf16[2,8,4096]{2,1,0:T(8,128)(2,1)S(1)}, u32[]{:S(2)}, u32[]{:S(2)}) collective-permute-start(bf16[2,8,4096]{2,1,0:T(8,128)(2,1)S(1)} %get-tuple-element.49), channel_id=1, source_target_pairs={{0,24},{4,28},{8,16},{12,20},{16,8},{20,12},{24,0},{28,4},{1,25},{... | collective-permute-start | bytes 393224 | tf_op jit(solution)/shard_map/ppermute | solution.py:294
  27.0 0.3 collective-permute-start.11
  27.2 0.2 collective-permute-start.12
  27.5 3.6 %collective-permute-start.13 = (bf16[2,8,4096]{2,1,0:T(8,128)(2,1)S(1)}, bf16[2,8,4096]{2,1,0:T(8,128)(2,1)S(1)}, u32[]{:S(2)}, u32[]{:S(2)}) collective-permute-start(bf16[2,8,4096]{2,1,0:T(8,128)(2,1)S(1)} %get-tuple-element.54), channel_id=1, source_target_pairs={{0,20},{4,16},{8,28},{12,24},{16,4},{20,0},{24,12},{28,8},{1,21},{... | collective-permute-start | bytes 393224 | tf_op jit(solution)/shard_map/ppermute | solution.py:294
  31.0 0.9 %collective-permute-start.14 = (bf16[2,8,4096]{2,1,0:T(8,128)(2,1)S(1)}, bf16[2,8,4096]{2,1,0:T(8,128)(2,1)S(1)}, u32[]{:S(2)}, u32[]{:S(2)}) collective-permute-start(bf16[2,8,4096]{2,1,0:T(8,128)(2,1)S(1)} %get-tuple-element.55), channel_id=1, source_target_pairs={{0,28},{4,24},{8,20},{12,16},{16,12},{20,8},{24,4},{28,0},{1,29},{... | collective-permute-start | bytes 393224 | tf_op jit(solution)/shard_map/ppermute | solution.py:294
  32.0 2.3 %collective-permute-start.15 = (bf16[2,8,4096]{2,1,0:T(8,128)(2,1)S(1)}, bf16[2,8,4096]{2,1,0:T(8,128)(2,1)S(1)}, u32[]{:S(2)}, u32[]{:S(2)}) collective-permute-start(bf16[2,8,4096]{2,1,0:T(8,128)(2,1)S(1)} %get-tuple-element.56), channel_id=1, source_target_pairs={{0,12},{4,8},{8,4},{12,0},{16,28},{20,24},{24,20},{28,16},{1,13},{... | collective-permute-start | bytes 393224 | tf_op jit(solution)/shard_map/ppermute | solution.py:294
  34.2 0.8 %collective-permute-start.16 = (bf16[2,8,4096]{2,1,0:T(8,128)(2,1)S(1)}, bf16[2,8,4096]{2,1,0:T(8,128)(2,1)S(1)}, u32[]{:S(2)}, u32[]{:S(2)}) collective-permute-start(bf16[2,8,4096]{2,1,0:T(8,128)(2,1)S(1)} %get-tuple-element.57), channel_id=1, source_target_pairs={{0,4},{4,0},{8,12},{12,8},{16,20},{20,16},{24,28},{28,24},{1,5},{5... | collective-permute-start | bytes 393224 | tf_op jit(solution)/shard_map/ppermute | solution.py:294
  35.0 2.6 %store.1 = (f32[16,8,4096]{2,1,0:T(8,128)}, f32[16,8,4096]{2,1,0:T(8,128)}, bf16[1,16,8,4096]{3,2,1,0:T(8,128)(2,1)}) custom-call(s32[16]{0:T(128)S(4)} %get-tuple-element.31.places_ref, f32[16,8,128]{2,1,0:T(8,128)S(1)} %get-tuple-element.47.scale_ref, f32[16,8,4096]{2,1,0:T(8,128)S(1)} %get-tuple-element.44.acc_ref, ...), custom_call_target="tpu_custom_call" | custom-call | flops 1000000 | bytes 12582912 | tf_op jit(solution)/shard_map/store/pallas_call | solution.py:348
  37.7 1.8 %collective-permute-done.13.rest_1_ = bf16[2,8,4096]{2,1,0:T(8,128)(2,1)S(1)} collective-permute-done((bf16[2,8,4096]{2,1,0:T(8,128)(2,1)S(1)}, bf16[2,8,4096]{2,1,0:T(8,128)(2,1)S(1)}, u32[]{:S(2)}, u32[]{:S(2)}) %collective-permute-start.13) | collective-permute-done | bytes 131104 | tf_op jit(solution)/shard_map/ppermute | solution.py:294
  39.5 0.9 %unpack.1 = bf16[1,16,8,4096]{3,2,1,0:T(8,128)(2,1)} custom-call(s32[16]{0:T(128)S(4)} %get-tuple-element.31.places_ref, bf16[2,8,4096]{2,1,0:T(8,128)(2,1)S(1)} %collective-permute-done.12.rest_0_, bf16[2,8,4096]{2,1,0:T(8,128)(2,1)S(1)} %collective-permute-done.13.rest_1_, ...), custom_call_target="tpu_custom_call", output_to_operand_aliasing={{}: (6, {})} | custom-call | tf_op jit(solution)/shard_map/unpack/pallas_call | solution.py:361
  (18 shorter events, 0.2 us)
Async XLA Ops:
  1.9 6.3 %collective-permute-start = (bf16[2,8,4096]{2,1,0:T(8,128)(2,1)S(1)}, bf16[2,8,4096]{2,1,0:T(8,128)(2,1)S(1)}, u32[]{:S(2)}, u32[]{:S(2)}) collective-permute-start(bf16[2,8,4096]{2,1,0:T(8,128)(2,1)S(1)} %get-tuple-element.37), channel_id=1, source_target_pairs={{0,24},{4,28},{8,16},{12,20},{16,8},{20,12},{24,0},{28,4},{1,25},{... | collective-permute-start | bytes 393224 | tf_op jit(solution)/shard_map/ppermute | solution.py:294
  5.0 7.8 %collective-permute-start.1 = (bf16[2,8,4096]{2,1,0:T(8,128)(2,1)S(1)}, bf16[2,8,4096]{2,1,0:T(8,128)(2,1)S(1)}, u32[]{:S(2)}, u32[]{:S(2)}) collective-permute-start(bf16[2,8,4096]{2,1,0:T(8,128)(2,1)S(1)} %get-tuple-element.38), channel_id=1, source_target_pairs={{0,8},{4,12},{8,0},{12,4},{16,24},{20,28},{24,16},{28,20},{1,9},{5... | collective-permute-start | bytes 393224 | tf_op jit(solution)/shard_map/ppermute | solution.py:294
  5.2 11.5 %collective-permute-start.2 = (bf16[2,8,4096]{2,1,0:T(8,128)(2,1)S(1)}, bf16[2,8,4096]{2,1,0:T(8,128)(2,1)S(1)}, u32[]{:S(2)}, u32[]{:S(2)}) collective-permute-start(bf16[2,8,4096]{2,1,0:T(8,128)(2,1)S(1)} %get-tuple-element.39), channel_id=1, source_target_pairs={{0,16},{4,20},{8,24},{12,28},{16,0},{20,4},{24,8},{28,12},{1,17},{... | collective-permute-start | bytes 393224 | tf_op jit(solution)/shard_map/ppermute | solution.py:294
  5.3 11.4 %collective-permute-start.3 = (bf16[2,8,4096]{2,1,0:T(8,128)(2,1)S(1)}, bf16[2,8,4096]{2,1,0:T(8,128)(2,1)S(1)}, u32[]{:S(2)}, u32[]{:S(2)}) collective-permute-start(bf16[2,8,4096]{2,1,0:T(8,128)(2,1)S(1)} %get-tuple-element.40), channel_id=1, source_target_pairs={{0,20},{4,16},{8,28},{12,24},{16,4},{20,0},{24,12},{28,8},{1,21},{... | collective-permute-start | bytes 393224 | tf_op jit(solution)/shard_map/ppermute | solution.py:294
  8.1 8.7 %collective-permute-start.4 = (bf16[2,8,4096]{2,1,0:T(8,128)(2,1)S(1)}, bf16[2,8,4096]{2,1,0:T(8,128)(2,1)S(1)}, u32[]{:S(2)}, u32[]{:S(2)}) collective-permute-start(bf16[2,8,4096]{2,1,0:T(8,128)(2,1)S(1)} %get-tuple-element.41), channel_id=1, source_target_pairs={{0,12},{4,8},{8,4},{12,0},{16,28},{20,24},{24,20},{28,16},{1,13},{... | collective-permute-start | bytes 393224 | tf_op jit(solution)/shard_map/ppermute | solution.py:294
  8.2 9.0 %collective-permute-start.5 = (bf16[2,8,4096]{2,1,0:T(8,128)(2,1)S(1)}, bf16[2,8,4096]{2,1,0:T(8,128)(2,1)S(1)}, u32[]{:S(2)}, u32[]{:S(2)}) collective-permute-start(bf16[2,8,4096]{2,1,0:T(8,128)(2,1)S(1)} %get-tuple-element.42), channel_id=1, source_target_pairs={{0,28},{4,24},{8,20},{12,16},{16,12},{20,8},{24,4},{28,0},{1,29},{... | collective-permute-start | bytes 393224 | tf_op jit(solution)/shard_map/ppermute | solution.py:294
  12.8 4.3 %collective-permute-start.6 = (bf16[2,8,4096]{2,1,0:T(8,128)(2,1)S(1)}, bf16[2,8,4096]{2,1,0:T(8,128)(2,1)S(1)}, u32[]{:S(2)}, u32[]{:S(2)}) collective-permute-start(bf16[2,8,4096]{2,1,0:T(8,128)(2,1)S(1)} %get-tuple-element.43), channel_id=1, source_target_pairs={{0,4},{4,0},{8,12},{12,8},{16,20},{20,16},{24,28},{28,24},{1,5},{5... | collective-permute-start | bytes 393224 | tf_op jit(solution)/shard_map/ppermute | solution.py:294
  17.7 5.8 %collective-permute-start.9 = (f32[1,128]{1,0:T(1,128)S(1)}, f32[1,128]{1,0:T(1,128)S(1)}, u32[]{:S(2)}, u32[]{:S(2)}) collective-permute-start(f32[1,128]{1,0:T(1,128)S(1)} %get-tuple-element.46.rest_0_), channel_id=1, source_target_pairs={{0,2},{1,3},{2,0},{3,1},{4,6},{5,7},{6,4},{7,5},{8,10},{9,11},{10,... | collective-permute-start | bytes 1544 | tf_op jit(solution)/shard_map/ppermute | solution.py:334
  20.2 4.2 %collective-permute-start.8 = (f32[1,128]{1,0:T(1,128)S(1)}, f32[1,128]{1,0:T(1,128)S(1)}, u32[]{:S(2)}, u32[]{:S(2)}) collective-permute-start(f32[1,128]{1,0:T(1,128)S(1)} %get-tuple-element.46.rest_0_), channel_id=1, source_target_pairs={{0,1},{1,2},{2,3},{3,0},{4,5},{5,6},{6,7},{7,4},{8,9},{9,10},{10,1... | collective-permute-start | bytes 1544 | tf_op jit(solution)/shard_map/ppermute | solution.py:334
  21.5 2.9 %collective-permute-start.7 = (f32[1,128]{1,0:T(1,128)S(1)}, f32[1,128]{1,0:T(1,128)S(1)}, u32[]{:S(2)}, u32[]{:S(2)}) collective-permute-start(f32[1,128]{1,0:T(1,128)S(1)} %get-tuple-element.46.rest_0_), channel_id=1, source_target_pairs={{0,3},{1,0},{2,1},{3,2},{4,7},{5,4},{6,5},{7,6},{8,11},{9,8},{10,9... | collective-permute-start | bytes 1544 | tf_op jit(solution)/shard_map/ppermute | solution.py:334
  24.4 10.7 %copy-start = (f32[16,8,4096]{2,1,0:T(8,128)S(1)}, f32[16,8,4096]{2,1,0:T(8,128)}, u32[]{:S(2)}) copy-start(f32[16,8,4096]{2,1,0:T(8,128)} %past_ref.1) | copy-start | bytes 6291460
  24.8 7.2 %collective-permute-start.10 = (bf16[2,8,4096]{2,1,0:T(8,128)(2,1)S(1)}, bf16[2,8,4096]{2,1,0:T(8,128)(2,1)S(1)}, u32[]{:S(2)}, u32[]{:S(2)}) collective-permute-start(bf16[2,8,4096]{2,1,0:T(8,128)(2,1)S(1)} %get-tuple-element.49), channel_id=1, source_target_pairs={{0,24},{4,28},{8,16},{12,20},{16,8},{20,12},{24,0},{28,4},{1,25},{... | collective-permute-start | bytes 393224 | tf_op jit(solution)/shard_map/ppermute | solution.py:294
  27.0 7.3 %collective-permute-start.11 = (bf16[2,8,4096]{2,1,0:T(8,128)(2,1)S(1)}, bf16[2,8,4096]{2,1,0:T(8,128)(2,1)S(1)}, u32[]{:S(2)}, u32[]{:S(2)}) collective-permute-start(bf16[2,8,4096]{2,1,0:T(8,128)(2,1)S(1)} %get-tuple-element.50), channel_id=1, source_target_pairs={{0,8},{4,12},{8,0},{12,4},{16,24},{20,28},{24,16},{28,20},{1,9},{5... | collective-permute-start | bytes 393224 | tf_op jit(solution)/shard_map/ppermute | solution.py:294
  27.2 10.4 %collective-permute-start.12 = (bf16[2,8,4096]{2,1,0:T(8,128)(2,1)S(1)}, bf16[2,8,4096]{2,1,0:T(8,128)(2,1)S(1)}, u32[]{:S(2)}, u32[]{:S(2)}) collective-permute-start(bf16[2,8,4096]{2,1,0:T(8,128)(2,1)S(1)} %get-tuple-element.53), channel_id=1, source_target_pairs={{0,16},{4,20},{8,24},{12,28},{16,0},{20,4},{24,8},{28,12},{1,17},{... | collective-permute-start | bytes 393224 | tf_op jit(solution)/shard_map/ppermute | solution.py:294
  27.5 12.0 %collective-permute-start.13 = (bf16[2,8,4096]{2,1,0:T(8,128)(2,1)S(1)}, bf16[2,8,4096]{2,1,0:T(8,128)(2,1)S(1)}, u32[]{:S(2)}, u32[]{:S(2)}) collective-permute-start(bf16[2,8,4096]{2,1,0:T(8,128)(2,1)S(1)} %get-tuple-element.54), channel_id=1, source_target_pairs={{0,20},{4,16},{8,28},{12,24},{16,4},{20,0},{24,12},{28,8},{1,21},{... | collective-permute-start | bytes 393224 | tf_op jit(solution)/shard_map/ppermute | solution.py:294
  31.0 8.5 %collective-permute-start.14 = (bf16[2,8,4096]{2,1,0:T(8,128)(2,1)S(1)}, bf16[2,8,4096]{2,1,0:T(8,128)(2,1)S(1)}, u32[]{:S(2)}, u32[]{:S(2)}) collective-permute-start(bf16[2,8,4096]{2,1,0:T(8,128)(2,1)S(1)} %get-tuple-element.55), channel_id=1, source_target_pairs={{0,28},{4,24},{8,20},{12,16},{16,12},{20,8},{24,4},{28,0},{1,29},{... | collective-permute-start | bytes 393224 | tf_op jit(solution)/shard_map/ppermute | solution.py:294
  32.0 7.5 %collective-permute-start.15 = (bf16[2,8,4096]{2,1,0:T(8,128)(2,1)S(1)}, bf16[2,8,4096]{2,1,0:T(8,128)(2,1)S(1)}, u32[]{:S(2)}, u32[]{:S(2)}) collective-permute-start(bf16[2,8,4096]{2,1,0:T(8,128)(2,1)S(1)} %get-tuple-element.56), channel_id=1, source_target_pairs={{0,12},{4,8},{8,4},{12,0},{16,28},{20,24},{24,20},{28,16},{1,13},{... | collective-permute-start | bytes 393224 | tf_op jit(solution)/shard_map/ppermute | solution.py:294
  34.2 5.3 %collective-permute-start.16 = (bf16[2,8,4096]{2,1,0:T(8,128)(2,1)S(1)}, bf16[2,8,4096]{2,1,0:T(8,128)(2,1)S(1)}, u32[]{:S(2)}, u32[]{:S(2)}) collective-permute-start(bf16[2,8,4096]{2,1,0:T(8,128)(2,1)S(1)} %get-tuple-element.57), channel_id=1, source_target_pairs={{0,4},{4,0},{8,12},{12,8},{16,20},{20,16},{24,28},{28,24},{1,5},{5... | collective-permute-start | bytes 393224 | tf_op jit(solution)/shard_map/ppermute | solution.py:294

commit v11 on v10

--- a/solution.py
+++ b/solution.py
@@ -1,4 +1,5 @@
 import functools
+import math
 
 import jax
 import jax.numpy as jnp
@@ -108,7 +109,8 @@
 
 def prepare(me, own_ref, params_hbm, past_hbm, tables, acc_ref, base_ref, params_ref, past_ref, sems, find):
     owned, _, width = acc_ref.shape
-    part = owned // PARTS
+    parts = math.gcd(owned, PARTS)
+    part = owned // parts
 
     def copies(i):
         at = pl.ds(i * part, part)
@@ -117,12 +119,12 @@
             for n, (hbm, ref) in enumerate(((params_hbm, params_ref), (past_hbm, past_ref)))
         ]
 
-    for i in range(PARTS):
+    for i in range(parts):
         for copy in copies(i):
             copy.start()
     find()
     module_ref, weight_ref, total_ref = tables
-    for i in range(PARTS):
+    for i in range(parts):
         for copy in copies(i):
             copy.wait()
 
@@ -161,12 +163,12 @@
     owned, rows, width = acc_ref.shape
     sums = []
     for m in range(owned):
-        inverse = 1.0 / jnp.maximum(jnp.full((rows, 128), total_ref[m], jnp.float32), 1.0)
+        inverse = 1.0 / jnp.maximum(jnp.full((1, 128), total_ref[m], jnp.float32), 1.0)
         added = jnp.zeros((rows, 128), jnp.float32)
         for at in range(0, width, 128):
-            raw = acc_ref[m, :, pl.ds(at, 128)] * inverse
-            added = added + raw * raw
-        sums.append(jnp.sum(added, axis=0, keepdims=True))
+            acc = acc_ref[m, :, pl.ds(at, 128)]
+            added = added + acc * acc
+        sums.append(jnp.sum(added, axis=0, keepdims=True) * (inverse * inverse))
     sums = jnp.sum(jnp.concatenate(sums, axis=0), axis=1, keepdims=True)
     squares_ref[...] = jnp.sum(jnp.where(diagonal(owned), sums, 0.0), axis=0, keepdims=True)
 
@@ -210,7 +212,8 @@
     placed(distances, pieces, places_ref, out_hbm, piece_sems, start)
     rate = outer_rate * (1.0 + outer_momentum)
     owned, _, width = acc_ref.shape
-    part = owned // PARTS
+    parts = math.gcd(owned, PARTS)
+    part = owned // parts
 
     def copies(i):
         at = pl.ds(i * part, part)
@@ -221,7 +224,7 @@
             )
         ]
 
-    for i in range(PARTS):
+    for i in range(parts):
 
         def fill(m, _):
             scale = scale_ref[m][:, :1]
@@ -234,7 +237,7 @@
         lax.fori_loop(i * part, (i + 1) * part, fill, 0)
         for copy in copies(i):
             copy.start()
-    for i in range(PARTS):
+    for i in range(parts):
         for copy in copies(i):
             copy.wait()
     placed(distances, pieces, places_ref, out_hbm, piece_sems, wait)

time: 40.7 us -> 40.6 us (level)
  no operation moved by 1% of the time
where the time goes in v11:
time: 40.6 us; the launch traced here: 40.4 us
  starting transfers between devices  27.7 us (68%)
  Pallas kernels  8.72 us (21%)
  waiting for transfers between devices  3.17 us (8%)
  between operations  0.71 us (2%)
    ppermute x14, starting transfers between devices, exchange(): lax.ppermute(x, 'path', [(i, i ^ d) for i in range(paths)])  22 us
    ppermute x3, starting transfers between devices, on_device(): lax.ppermute(squares, 'shard', [(i, (i + d) % shards) for i in range(shar...  5.77 us
    pallas_call x1, Pallas kernels, on_device(): pl.pallas_call(early_kernel, out_shape=tables + [held_module] * 2, in_spe...  3.12 us
    pallas_call x1, Pallas kernels, on_device(): pl.pallas_call(functools.partial(store_kernel, soon), out_shape=[module]...  2.59 us
    ppermute x14, waiting for transfers between devices, exchange(): lax.ppermute(x, 'path', [(i, i ^ d) for i in range(paths)])  2.24 us
    pallas_call x1, Pallas kernels, on_device(): pl.pallas_call(functools.partial(pack_kernel, owned, [*there, 0]), out_sh...  1.26 us
    pallas_call x1, Pallas kernels, on_device(): pl.pallas_call(functools.partial(unpack_kernel, last), out_shape=whole, i...  0.93 us
    ppermute x3, waiting for transfers between devices, on_device(): lax.ppermute(squares, 'shard', [(i, (i + d) % shards) for i in range(shar...  0.93 us
  transfers between devices with their start and end apart: 17, of which 3 were waited for; matrix products, arithmetic and copies ran while one was open for 0% of the time, Pallas kernels for 14%

profile of v11, /device:TPU:1, one launch (start us, length us, event | category | flops | bytes accessed | tf_op | source)
XLA Modules:
  0.0 40.4 jit_solution(17476810815335249303)
XLA Ops:
  0.6 1.3 %pack.1 = (s32[16]{0:T(128)S(4)}, bf16[2,8,4096]{2,1,0:T(8,128)(2,1)S(1)}, bf16[2,8,4096]{2,1,0:T(8,128)(2,1)S(1)}, bf16[2,8,4096]{2,1,0:T(8,128)(2,1)S(1)}, bf1...) custom-call(s32[8,16]{1,0:T(8,128)} %ids_ref.1, ...), custom_call_target="tpu_custom_call" | custom-call | tf_op jit(solution)/shard_map/pack/pallas_call | solution.py:301
  1.9 3.1 %collective-permute-start = (bf16[2,8,4096]{2,1,0:T(8,128)(2,1)S(1)}, bf16[2,8,4096]{2,1,0:T(8,128)(2,1)S(1)}, u32[]{:S(2)}, u32[]{:S(2)}) collective-permute-start(bf16[2,8,4096]{2,1,0:T(8,128)(2,1)S(1)} %get-tuple-element.37), channel_id=1, source_target_pairs={{0,24},{4,28},{8,16},{12,20},{16,8},{20,12},{24,0},{28,4},{1,25},{... | collective-permute-start | bytes 393224 | tf_op jit(solution)/shard_map/ppermute | solution.py:297
  5.0 0.3 collective-permute-start.1
  5.3 2.8 %collective-permute-start.3 = (bf16[2,8,4096]{2,1,0:T(8,128)(2,1)S(1)}, bf16[2,8,4096]{2,1,0:T(8,128)(2,1)S(1)}, u32[]{:S(2)}, u32[]{:S(2)}) collective-permute-start(bf16[2,8,4096]{2,1,0:T(8,128)(2,1)S(1)} %get-tuple-element.40), channel_id=1, source_target_pairs={{0,20},{4,16},{8,28},{12,24},{16,4},{20,0},{24,12},{28,8},{1,21},{... | collective-permute-start | bytes 393224 | tf_op jit(solution)/shard_map/ppermute | solution.py:297
  8.2 4.6 %collective-permute-start.5 = (bf16[2,8,4096]{2,1,0:T(8,128)(2,1)S(1)}, bf16[2,8,4096]{2,1,0:T(8,128)(2,1)S(1)}, u32[]{:S(2)}, u32[]{:S(2)}) collective-permute-start(bf16[2,8,4096]{2,1,0:T(8,128)(2,1)S(1)} %get-tuple-element.42), channel_id=1, source_target_pairs={{0,28},{4,24},{8,20},{12,16},{16,12},{20,8},{24,4},{28,0},{1,29},{... | collective-permute-start | bytes 393224 | tf_op jit(solution)/shard_map/ppermute | solution.py:297
  12.8 0.8 %collective-permute-start.6 = (bf16[2,8,4096]{2,1,0:T(8,128)(2,1)S(1)}, bf16[2,8,4096]{2,1,0:T(8,128)(2,1)S(1)}, u32[]{:S(2)}, u32[]{:S(2)}) collective-permute-start(bf16[2,8,4096]{2,1,0:T(8,128)(2,1)S(1)} %get-tuple-element.43), channel_id=1, source_target_pairs={{0,4},{4,0},{8,12},{12,8},{16,20},{20,16},{24,28},{28,24},{1,5},{5... | collective-permute-start | bytes 393224 | tf_op jit(solution)/shard_map/ppermute | solution.py:297
  13.6 3.1 %early.1 = (s32[24]{0:T(128)S(4)}, f32[24]{0:T(128)S(4)}, f32[16]{0:T(128)S(4)}, f32[16,8,4096]{2,1,0:T(8,128)S(1)}, f32[16,8,4096]{2,1,0:T(8,128)S(1)}) custom-call(s32[8,16]{1,0:T(8,128)} %ids_ref.1, s32[8,16]{1,0:T(8,128)} %counts_ref.1, bf16[2,8,4096]{2,1,0:T(8,128)(2,1)S(1)} %get-tuple-element.32.own_ref, f32[16,8,4096]{2,1,0:T(8,128)} %params_hbm.1, ...), custom_call_target="tpu_custom_call" | custom-call | flops 1000000 | bytes 12582912 | tf_op jit(solution)/shard_map/early/pallas_call | solution.py:317
  16.8 0.4 collective-permute-done.5.rest_5_
  17.2 0.5 %combine.1 = (f32[16,8,4096]{2,1,0:T(8,128)S(1)}, f32[1,128]{1,0:T(1,128)S(1)}) custom-call(s32[24]{0:T(128)S(4)} %get-tuple-element.33.module_ref, f32[24]{0:T(128)S(4)} %get-tuple-element.35.weight_ref, f32[16]{0:T(128)S(4)} %get-tuple-element.34.total_ref, f32[16,8,4096]{2,1,0:T(8,128)S(1)} %get-tuple-element.36.acc_in, ...), custom_call_target="tpu_custom_call", output_to_operand_aliasing={{0}: (3, {})} | custom-call | tf_op jit(solution)/shard_map/combine/pallas_call | solution.py:327
  17.6 2.5 %collective-permute-start.9 = (f32[1,128]{1,0:T(1,128)S(1)}, f32[1,128]{1,0:T(1,128)S(1)}, u32[]{:S(2)}, u32[]{:S(2)}) collective-permute-start(f32[1,128]{1,0:T(1,128)S(1)} %get-tuple-element.46.rest_0_), channel_id=1, source_target_pairs={{0,2},{1,3},{2,0},{3,1},{4,6},{5,7},{6,4},{7,5},{8,10},{9,11},{10,... | collective-permute-start | bytes 1544 | tf_op jit(solution)/shard_map/ppermute | solution.py:337
  20.1 1.3 %collective-permute-start.8 = (f32[1,128]{1,0:T(1,128)S(1)}, f32[1,128]{1,0:T(1,128)S(1)}, u32[]{:S(2)}, u32[]{:S(2)}) collective-permute-start(f32[1,128]{1,0:T(1,128)S(1)} %get-tuple-element.46.rest_0_), channel_id=1, source_target_pairs={{0,1},{1,2},{2,3},{3,0},{4,5},{5,6},{6,7},{7,4},{8,9},{9,10},{10,1... | collective-permute-start | bytes 1544 | tf_op jit(solution)/shard_map/ppermute | solution.py:337
  21.4 2.0 %collective-permute-start.7 = (f32[1,128]{1,0:T(1,128)S(1)}, f32[1,128]{1,0:T(1,128)S(1)}, u32[]{:S(2)}, u32[]{:S(2)}) collective-permute-start(f32[1,128]{1,0:T(1,128)S(1)} %get-tuple-element.46.rest_0_), channel_id=1, source_target_pairs={{0,3},{1,0},{2,1},{3,2},{4,7},{5,4},{6,5},{7,6},{8,11},{9,8},{10,9... | collective-permute-start | bytes 1544 | tf_op jit(solution)/shard_map/ppermute | solution.py:337
  23.4 0.9 %collective-permute-done.8.rest_2_ = f32[1,128]{1,0:T(1,128)S(1)} collective-permute-done((f32[1,128]{1,0:T(1,128)S(1)}, f32[1,128]{1,0:T(1,128)S(1)}, u32[]{:S(2)}, u32[]{:S(2)}) %collective-permute-start.8) | collective-permute-done | bytes 544 | tf_op jit(solution)/shard_map/ppermute | solution.py:337
  24.3 0.4 send.1
  24.7 2.2 %collective-permute-start.10 = (bf16[2,8,4096]{2,1,0:T(8,128)(2,1)S(1)}, bf16[2,8,4096]{2,1,0:T(8,128)(2,1)S(1)}, u32[]{:S(2)}, u32[]{:S(2)}) collective-permute-start(bf16[2,8,4096]{2,1,0:T(8,128)(2,1)S(1)} %get-tuple-element.49), channel_id=1, source_target_pairs={{0,24},{4,28},{8,16},{12,20},{16,8},{20,12},{24,0},{28,4},{1,25},{... | collective-permute-start | bytes 393224 | tf_op jit(solution)/shard_map/ppermute | solution.py:297
  26.9 0.3 collective-permute-start.11
  27.2 0.2 collective-permute-start.12
  27.4 3.6 %collective-permute-start.13 = (bf16[2,8,4096]{2,1,0:T(8,128)(2,1)S(1)}, bf16[2,8,4096]{2,1,0:T(8,128)(2,1)S(1)}, u32[]{:S(2)}, u32[]{:S(2)}) collective-permute-start(bf16[2,8,4096]{2,1,0:T(8,128)(2,1)S(1)} %get-tuple-element.54), channel_id=1, source_target_pairs={{0,20},{4,16},{8,28},{12,24},{16,4},{20,0},{24,12},{28,8},{1,21},{... | collective-permute-start | bytes 393224 | tf_op jit(solution)/shard_map/ppermute | solution.py:297
  31.0 0.9 %collective-permute-start.14 = (bf16[2,8,4096]{2,1,0:T(8,128)(2,1)S(1)}, bf16[2,8,4096]{2,1,0:T(8,128)(2,1)S(1)}, u32[]{:S(2)}, u32[]{:S(2)}) collective-permute-start(bf16[2,8,4096]{2,1,0:T(8,128)(2,1)S(1)} %get-tuple-element.55), channel_id=1, source_target_pairs={{0,28},{4,24},{8,20},{12,16},{16,12},{20,8},{24,4},{28,0},{1,29},{... | collective-permute-start | bytes 393224 | tf_op jit(solution)/shard_map/ppermute | solution.py:297
  31.9 2.3 %collective-permute-start.15 = (bf16[2,8,4096]{2,1,0:T(8,128)(2,1)S(1)}, bf16[2,8,4096]{2,1,0:T(8,128)(2,1)S(1)}, u32[]{:S(2)}, u32[]{:S(2)}) collective-permute-start(bf16[2,8,4096]{2,1,0:T(8,128)(2,1)S(1)} %get-tuple-element.56), channel_id=1, source_target_pairs={{0,12},{4,8},{8,4},{12,0},{16,28},{20,24},{24,20},{28,16},{1,13},{... | collective-permute-start | bytes 393224 | tf_op jit(solution)/shard_map/ppermute | solution.py:297
  34.2 0.8 %collective-permute-start.16 = (bf16[2,8,4096]{2,1,0:T(8,128)(2,1)S(1)}, bf16[2,8,4096]{2,1,0:T(8,128)(2,1)S(1)}, u32[]{:S(2)}, u32[]{:S(2)}) collective-permute-start(bf16[2,8,4096]{2,1,0:T(8,128)(2,1)S(1)} %get-tuple-element.57), channel_id=1, source_target_pairs={{0,4},{4,0},{8,12},{12,8},{16,20},{20,16},{24,28},{28,24},{1,5},{5... | collective-permute-start | bytes 393224 | tf_op jit(solution)/shard_map/ppermute | solution.py:297
  35.0 2.6 %store.1 = (f32[16,8,4096]{2,1,0:T(8,128)}, f32[16,8,4096]{2,1,0:T(8,128)}, bf16[1,16,8,4096]{3,2,1,0:T(8,128)(2,1)}) custom-call(s32[16]{0:T(128)S(4)} %get-tuple-element.31.places_ref, f32[16,8,128]{2,1,0:T(8,128)S(1)} %get-tuple-element.47.scale_ref, f32[16,8,4096]{2,1,0:T(8,128)S(1)} %get-tuple-element.44.acc_ref, ...), custom_call_target="tpu_custom_call" | custom-call | flops 1000000 | bytes 12582912 | tf_op jit(solution)/shard_map/store/pallas_call | solution.py:351
  37.6 1.8 %collective-permute-done.13.rest_1_ = bf16[2,8,4096]{2,1,0:T(8,128)(2,1)S(1)} collective-permute-done((bf16[2,8,4096]{2,1,0:T(8,128)(2,1)S(1)}, bf16[2,8,4096]{2,1,0:T(8,128)(2,1)S(1)}, u32[]{:S(2)}, u32[]{:S(2)}) %collective-permute-start.13) | collective-permute-done | bytes 131104 | tf_op jit(solution)/shard_map/ppermute | solution.py:297
  39.4 0.9 %unpack.1 = bf16[1,16,8,4096]{3,2,1,0:T(8,128)(2,1)} custom-call(s32[16]{0:T(128)S(4)} %get-tuple-element.31.places_ref, bf16[2,8,4096]{2,1,0:T(8,128)(2,1)S(1)} %collective-permute-done.12.rest_0_, bf16[2,8,4096]{2,1,0:T(8,128)(2,1)S(1)} %collective-permute-done.13.rest_1_, ...), custom_call_target="tpu_custom_call", output_to_operand_aliasing={{}: (6, {})} | custom-call | tf_op jit(solution)/shard_map/unpack/pallas_call | solution.py:364
  (18 shorter events, 0.2 us)
Async XLA Ops:
  1.9 6.3 %collective-permute-start = (bf16[2,8,4096]{2,1,0:T(8,128)(2,1)S(1)}, bf16[2,8,4096]{2,1,0:T(8,128)(2,1)S(1)}, u32[]{:S(2)}, u32[]{:S(2)}) collective-permute-start(bf16[2,8,4096]{2,1,0:T(8,128)(2,1)S(1)} %get-tuple-element.37), channel_id=1, source_target_pairs={{0,24},{4,28},{8,16},{12,20},{16,8},{20,12},{24,0},{28,4},{1,25},{... | collective-permute-start | bytes 393224 | tf_op jit(solution)/shard_map/ppermute | solution.py:297
  5.0 7.8 %collective-permute-start.1 = (bf16[2,8,4096]{2,1,0:T(8,128)(2,1)S(1)}, bf16[2,8,4096]{2,1,0:T(8,128)(2,1)S(1)}, u32[]{:S(2)}, u32[]{:S(2)}) collective-permute-start(bf16[2,8,4096]{2,1,0:T(8,128)(2,1)S(1)} %get-tuple-element.38), channel_id=1, source_target_pairs={{0,8},{4,12},{8,0},{12,4},{16,24},{20,28},{24,16},{28,20},{1,9},{5... | collective-permute-start | bytes 393224 | tf_op jit(solution)/shard_map/ppermute | solution.py:297
  5.2 11.5 %collective-permute-start.2 = (bf16[2,8,4096]{2,1,0:T(8,128)(2,1)S(1)}, bf16[2,8,4096]{2,1,0:T(8,128)(2,1)S(1)}, u32[]{:S(2)}, u32[]{:S(2)}) collective-permute-start(bf16[2,8,4096]{2,1,0:T(8,128)(2,1)S(1)} %get-tuple-element.39), channel_id=1, source_target_pairs={{0,16},{4,20},{8,24},{12,28},{16,0},{20,4},{24,8},{28,12},{1,17},{... | collective-permute-start | bytes 393224 | tf_op jit(solution)/shard_map/ppermute | solution.py:297
  5.3 11.4 %collective-permute-start.3 = (bf16[2,8,4096]{2,1,0:T(8,128)(2,1)S(1)}, bf16[2,8,4096]{2,1,0:T(8,128)(2,1)S(1)}, u32[]{:S(2)}, u32[]{:S(2)}) collective-permute-start(bf16[2,8,4096]{2,1,0:T(8,128)(2,1)S(1)} %get-tuple-element.40), channel_id=1, source_target_pairs={{0,20},{4,16},{8,28},{12,24},{16,4},{20,0},{24,12},{28,8},{1,21},{... | collective-permute-start | bytes 393224 | tf_op jit(solution)/shard_map/ppermute | solution.py:297
  8.1 8.7 %collective-permute-start.4 = (bf16[2,8,4096]{2,1,0:T(8,128)(2,1)S(1)}, bf16[2,8,4096]{2,1,0:T(8,128)(2,1)S(1)}, u32[]{:S(2)}, u32[]{:S(2)}) collective-permute-start(bf16[2,8,4096]{2,1,0:T(8,128)(2,1)S(1)} %get-tuple-element.41), channel_id=1, source_target_pairs={{0,12},{4,8},{8,4},{12,0},{16,28},{20,24},{24,20},{28,16},{1,13},{... | collective-permute-start | bytes 393224 | tf_op jit(solution)/shard_map/ppermute | solution.py:297
  8.2 9.0 %collective-permute-start.5 = (bf16[2,8,4096]{2,1,0:T(8,128)(2,1)S(1)}, bf16[2,8,4096]{2,1,0:T(8,128)(2,1)S(1)}, u32[]{:S(2)}, u32[]{:S(2)}) collective-permute-start(bf16[2,8,4096]{2,1,0:T(8,128)(2,1)S(1)} %get-tuple-element.42), channel_id=1, source_target_pairs={{0,28},{4,24},{8,20},{12,16},{16,12},{20,8},{24,4},{28,0},{1,29},{... | collective-permute-start | bytes 393224 | tf_op jit(solution)/shard_map/ppermute | solution.py:297
  12.8 4.3 %collective-permute-start.6 = (bf16[2,8,4096]{2,1,0:T(8,128)(2,1)S(1)}, bf16[2,8,4096]{2,1,0:T(8,128)(2,1)S(1)}, u32[]{:S(2)}, u32[]{:S(2)}) collective-permute-start(bf16[2,8,4096]{2,1,0:T(8,128)(2,1)S(1)} %get-tuple-element.43), channel_id=1, source_target_pairs={{0,4},{4,0},{8,12},{12,8},{16,20},{20,16},{24,28},{28,24},{1,5},{5... | collective-permute-start | bytes 393224 | tf_op jit(solution)/shard_map/ppermute | solution.py:297
  17.6 5.8 %collective-permute-start.9 = (f32[1,128]{1,0:T(1,128)S(1)}, f32[1,128]{1,0:T(1,128)S(1)}, u32[]{:S(2)}, u32[]{:S(2)}) collective-permute-start(f32[1,128]{1,0:T(1,128)S(1)} %get-tuple-element.46.rest_0_), channel_id=1, source_target_pairs={{0,2},{1,3},{2,0},{3,1},{4,6},{5,7},{6,4},{7,5},{8,10},{9,11},{10,... | collective-permute-start | bytes 1544 | tf_op jit(solution)/shard_map/ppermute | solution.py:337
  20.1 4.2 %collective-permute-start.8 = (f32[1,128]{1,0:T(1,128)S(1)}, f32[1,128]{1,0:T(1,128)S(1)}, u32[]{:S(2)}, u32[]{:S(2)}) collective-permute-start(f32[1,128]{1,0:T(1,128)S(1)} %get-tuple-element.46.rest_0_), channel_id=1, source_target_pairs={{0,1},{1,2},{2,3},{3,0},{4,5},{5,6},{6,7},{7,4},{8,9},{9,10},{10,1... | collective-permute-start | bytes 1544 | tf_op jit(solution)/shard_map/ppermute | solution.py:337
  21.4 2.9 %collective-permute-start.7 = (f32[1,128]{1,0:T(1,128)S(1)}, f32[1,128]{1,0:T(1,128)S(1)}, u32[]{:S(2)}, u32[]{:S(2)}) collective-permute-start(f32[1,128]{1,0:T(1,128)S(1)} %get-tuple-element.46.rest_0_), channel_id=1, source_target_pairs={{0,3},{1,0},{2,1},{3,2},{4,7},{5,4},{6,5},{7,6},{8,11},{9,8},{10,9... | collective-permute-start | bytes 1544 | tf_op jit(solution)/shard_map/ppermute | solution.py:337
  24.3 10.7 %copy-start = (f32[16,8,4096]{2,1,0:T(8,128)S(1)}, f32[16,8,4096]{2,1,0:T(8,128)}, u32[]{:S(2)}) copy-start(f32[16,8,4096]{2,1,0:T(8,128)} %past_ref.1) | copy-start | bytes 6291460
  24.7 7.2 %collective-permute-start.10 = (bf16[2,8,4096]{2,1,0:T(8,128)(2,1)S(1)}, bf16[2,8,4096]{2,1,0:T(8,128)(2,1)S(1)}, u32[]{:S(2)}, u32[]{:S(2)}) collective-permute-start(bf16[2,8,4096]{2,1,0:T(8,128)(2,1)S(1)} %get-tuple-element.49), channel_id=1, source_target_pairs={{0,24},{4,28},{8,16},{12,20},{16,8},{20,12},{24,0},{28,4},{1,25},{... | collective-permute-start | bytes 393224 | tf_op jit(solution)/shard_map/ppermute | solution.py:297
  26.9 7.3 %collective-permute-start.11 = (bf16[2,8,4096]{2,1,0:T(8,128)(2,1)S(1)}, bf16[2,8,4096]{2,1,0:T(8,128)(2,1)S(1)}, u32[]{:S(2)}, u32[]{:S(2)}) collective-permute-start(bf16[2,8,4096]{2,1,0:T(8,128)(2,1)S(1)} %get-tuple-element.50), channel_id=1, source_target_pairs={{0,8},{4,12},{8,0},{12,4},{16,24},{20,28},{24,16},{28,20},{1,9},{5... | collective-permute-start | bytes 393224 | tf_op jit(solution)/shard_map/ppermute | solution.py:297
  27.2 10.4 %collective-permute-start.12 = (bf16[2,8,4096]{2,1,0:T(8,128)(2,1)S(1)}, bf16[2,8,4096]{2,1,0:T(8,128)(2,1)S(1)}, u32[]{:S(2)}, u32[]{:S(2)}) collective-permute-start(bf16[2,8,4096]{2,1,0:T(8,128)(2,1)S(1)} %get-tuple-element.53), channel_id=1, source_target_pairs={{0,16},{4,20},{8,24},{12,28},{16,0},{20,4},{24,8},{28,12},{1,17},{... | collective-permute-start | bytes 393224 | tf_op jit(solution)/shard_map/ppermute | solution.py:297
  27.4 12.0 %collective-permute-start.13 = (bf16[2,8,4096]{2,1,0:T(8,128)(2,1)S(1)}, bf16[2,8,4096]{2,1,0:T(8,128)(2,1)S(1)}, u32[]{:S(2)}, u32[]{:S(2)}) collective-permute-start(bf16[2,8,4096]{2,1,0:T(8,128)(2,1)S(1)} %get-tuple-element.54), channel_id=1, source_target_pairs={{0,20},{4,16},{8,28},{12,24},{16,4},{20,0},{24,12},{28,8},{1,21},{... | collective-permute-start | bytes 393224 | tf_op jit(solution)/shard_map/ppermute | solution.py:297
  31.0 8.5 %collective-permute-start.14 = (bf16[2,8,4096]{2,1,0:T(8,128)(2,1)S(1)}, bf16[2,8,4096]{2,1,0:T(8,128)(2,1)S(1)}, u32[]{:S(2)}, u32[]{:S(2)}) collective-permute-start(bf16[2,8,4096]{2,1,0:T(8,128)(2,1)S(1)} %get-tuple-element.55), channel_id=1, source_target_pairs={{0,28},{4,24},{8,20},{12,16},{16,12},{20,8},{24,4},{28,0},{1,29},{... | collective-permute-start | bytes 393224 | tf_op jit(solution)/shard_map/ppermute | solution.py:297
  31.9 7.5 %collective-permute-start.15 = (bf16[2,8,4096]{2,1,0:T(8,128)(2,1)S(1)}, bf16[2,8,4096]{2,1,0:T(8,128)(2,1)S(1)}, u32[]{:S(2)}, u32[]{:S(2)}) collective-permute-start(bf16[2,8,4096]{2,1,0:T(8,128)(2,1)S(1)} %get-tuple-element.56), channel_id=1, source_target_pairs={{0,12},{4,8},{8,4},{12,0},{16,28},{20,24},{24,20},{28,16},{1,13},{... | collective-permute-start | bytes 393224 | tf_op jit(solution)/shard_map/ppermute | solution.py:297
  34.2 5.3 %collective-permute-start.16 = (bf16[2,8,4096]{2,1,0:T(8,128)(2,1)S(1)}, bf16[2,8,4096]{2,1,0:T(8,128)(2,1)S(1)}, u32[]{:S(2)}, u32[]{:S(2)}) collective-permute-start(bf16[2,8,4096]{2,1,0:T(8,128)(2,1)S(1)} %get-tuple-element.57), channel_id=1, source_target_pairs={{0,4},{4,0},{8,12},{12,8},{16,20},{20,16},{24,28},{28,24},{1,5},{5... | collective-permute-start | bytes 393224 | tf_op jit(solution)/shard_map/ppermute | solution.py:297

commit v12 on v11

--- a/solution.py
+++ b/solution.py
@@ -12,6 +12,7 @@
 CHUNK = 1024
 PARTS = 4
 SOON = 2
+AHEAD = 3
 outer_momentum = 0.9
 outer_rate = 0.7
 
@@ -298,21 +299,26 @@
             for d, x in zip(order, pieces)
         ]
 
-    places, *packed = pl.pallas_call(
-        functools.partial(pack_kernel, owned, [*there, 0]),
-        out_shape=[pltpu.SMEM((slots,), jnp.int32)] + [piece] * paths,
-        in_specs=[ANY] * 2,
-        out_specs=[SMEM] + [VMEM] * paths,
-        scratch_shapes=[
-            pltpu.SMEM(module_ids.shape, jnp.int32),
-            pltpu.VMEM((held, rows, width), jnp.bfloat16),
-            pltpu.SMEM((paths,), jnp.int32),
-            pltpu.SemaphoreType.DMA((len(chunks(width)) + 1,)),
-        ],
-        compiler_params=limits,
-        name="pack",
-    )(module_ids, *in_hbm(path_params.reshape(held, rows, width)))
-
+    (local,) = in_hbm(path_params.reshape(held, rows, width))
+
+    def pack(distances):
+        return pl.pallas_call(
+            functools.partial(pack_kernel, owned, distances),
+            out_shape=[pltpu.SMEM((slots,), jnp.int32)] + [piece] * len(distances),
+            in_specs=[ANY] * 2,
+            out_specs=[SMEM] + [VMEM] * len(distances),
+            scratch_shapes=[
+                pltpu.SMEM(module_ids.shape, jnp.int32),
+                pltpu.VMEM((held, rows, width), jnp.bfloat16),
+                pltpu.SMEM((paths,), jnp.int32),
+                pltpu.SemaphoreType.DMA((len(chunks(width)) + 1,)),
+            ],
+            compiler_params=limits,
+            name="pack",
+        )(module_ids, local)
+
+    places, *packed = pack(there[:AHEAD])
+    packed += pack([*there[AHEAD:], 0])[1:]
     arrived = exchange(there, packed)
     table, weights, total, acc, base = pl.pallas_call(
         early_kernel,
@@ -337,14 +343,18 @@
         lax.ppermute(squares, "shard", [(i, (i + d) % shards) for i in range(shards)])
         for d in sorted(range(1, shards), key=lambda d: (d == 2, -d))
     ]
-    scale, *outgoing = pl.pallas_call(
-        functools.partial(send_kernel, [*back, 0], shards),
-        out_shape=[jax.ShapeDtypeStruct((owned, rows, 128), jnp.float32)] + [piece] * paths,
-        in_specs=[SMEM] * 2 + [VMEM] * (2 + shards),
-        out_specs=[VMEM] * (1 + paths),
-        compiler_params=limits,
-        name="send",
-    )(*in_smem(table, total), *in_vmem(acc, base), *parts)
+    def send(distances):
+        return pl.pallas_call(
+            functools.partial(send_kernel, distances, shards),
+            out_shape=[jax.ShapeDtypeStruct((owned, rows, 128), jnp.float32)]
+            + [piece] * len(distances),
+            in_specs=[SMEM] * 2 + [VMEM] * (2 + shards),
+            out_specs=[VMEM] * (1 + len(distances)),
+            compiler_params=limits,
+            name="send",
+        )(*in_smem(table, total), *in_vmem(acc, base), *parts)
+
+    scale, *outgoing = send([*back, 0])
     returned = {0: outgoing[-1], **dict(zip(back, exchange(back, outgoing)))}
     soon, last = [0, *back[:SOON]], back[SOON:]
     whole = jax.ShapeDtypeStruct(path_params.shape, path_params.dtype)

time: 40.6 us -> 40.7 us (level)
  starting transfers between devices: 27.7 us -> 25.5 us
  Pallas kernels: 8.72 us -> 9.96 us
  waiting for transfers between devices: 3.17 us -> 4.17 us
    ppermute x14, starting transfers between devices: 22 us -> 20 us  [exchange(): lax.ppermute(x, 'path', [(i, i ^ d) for i in range(paths)])]
    pallas_call x2 -> x3, Pallas kernels: 1.63 us -> 2.85 us  [the longest x2 2.49 us: pack(): pl.pallas_call(functools.partial(pack_kernel, owned, distances), out_shap...]
    ppermute x14, waiting for transfers between devices: 2.24 us -> 3.24 us  [exchange(): lax.ppermute(x, 'path', [(i, i ^ d) for i in range(paths)])]
  transfers between devices with their start and end apart: 17 -> 17, of which waited for: 3 -> 3; matrix products, arithmetic and copies ran while one was open for 0% -> 0% of each run, Pallas kernels for 14% -> 17%
where the time goes in v12:
time: 40.7 us; the launch traced here: 40.4 us
  starting transfers between devices  25.5 us (63%)
  Pallas kernels  9.96 us (24%)
  waiting for transfers between devices  4.17 us (10%)
  between operations  0.72 us (2%)
    ppermute x14, starting transfers between devices, exchange(): lax.ppermute(x, 'path', [(i, i ^ d) for i in range(paths)])  20 us
    ppermute x3, starting transfers between devices, on_device(): lax.ppermute(squares, 'shard', [(i, (i + d) % shards) for i in range(shar...  5.57 us
    ppermute x14, waiting for transfers between devices, exchange(): lax.ppermute(x, 'path', [(i, i ^ d) for i in range(paths)])  3.24 us
    pallas_call x1, Pallas kernels, on_device(): pl.pallas_call(early_kernel, out_shape=tables + [held_module] * 2, in_spe...  3.13 us
    pallas_call x1, Pallas kernels, on_device(): pl.pallas_call(functools.partial(store_kernel, soon), out_shape=[module]...  2.59 us
    pallas_call x2, Pallas kernels, pack(): pl.pallas_call(functools.partial(pack_kernel, owned, distances), out_shap...  2.49 us
    pallas_call x1, Pallas kernels, on_device(): pl.pallas_call(functools.partial(unpack_kernel, last), out_shape=whole, i...  0.93 us
    ppermute x3, waiting for transfers between devices, on_device(): lax.ppermute(squares, 'shard', [(i, (i + d) % shards) for i in range(shar...  0.93 us
  transfers between devices with their start and end apart: 17, of which 3 were waited for; matrix products, arithmetic and copies ran while one was open for 0% of the time, Pallas kernels for 17%

profile of v12, /device:TPU:1, one launch (start us, length us, event | category | flops | bytes accessed | tf_op | source)
XLA Modules:
  0.0 40.4 jit_solution(2294436173908509210)
XLA Ops:
  0.6 1.2 %pack.2 = (s32[16]{0:T(128)S(4)}, bf16[2,8,4096]{2,1,0:T(8,128)(2,1)S(1)}, bf16[2,8,4096]{2,1,0:T(8,128)(2,1)S(1)}, bf16[2,8,4096]{2,1,0:T(8,128)(2,1)S(1)}) custom-call(s32[8,16]{1,0:T(8,128)} %ids_ref.1, bf16[16,8,4096]{2,1,0:T(8,128)(2,1)} %bitcast.1), custom_call_target="tpu_custom_call" | custom-call | tf_op jit(solution)/shard_map/pack/pallas_call | solution.py:305
  1.9 3.1 %collective-permute-start = (bf16[2,8,4096]{2,1,0:T(8,128)(2,1)S(1)}, bf16[2,8,4096]{2,1,0:T(8,128)(2,1)S(1)}, u32[]{:S(2)}, u32[]{:S(2)}) collective-permute-start(bf16[2,8,4096]{2,1,0:T(8,128)(2,1)S(1)} %get-tuple-element.37), channel_id=1, source_target_pairs={{0,24},{4,28},{8,16},{12,20},{16,8},{20,12},{24,0},{28,4},{1,25},{... | collective-permute-start | bytes 393224 | tf_op jit(solution)/shard_map/ppermute | solution.py:298
  4.9 0.3 collective-permute-start.1
  5.3 1.2 %pack.3 = (s32[16]{0:T(128)S(4)}, bf16[2,8,4096]{2,1,0:T(8,128)(2,1)S(1)}, bf16[2,8,4096]{2,1,0:T(8,128)(2,1)S(1)}, bf16[2,8,4096]{2,1,0:T(8,128)(2,1)S(1)}, bf1...) custom-call(s32[8,16]{1,0:T(8,128)} %ids_ref.1, bf16[16,8,4096]{2,1,0:T(8,128)(2,1)} %bitcast.2), custom_call_target="tpu_custom_call" | custom-call | tf_op jit(solution)/shard_map/pack/pallas_call | solution.py:305
  6.6 2.8 %collective-permute-start.3 = (bf16[2,8,4096]{2,1,0:T(8,128)(2,1)S(1)}, bf16[2,8,4096]{2,1,0:T(8,128)(2,1)S(1)}, u32[]{:S(2)}, u32[]{:S(2)}) collective-permute-start(bf16[2,8,4096]{2,1,0:T(8,128)(2,1)S(1)} %get-tuple-element.40), channel_id=1, source_target_pairs={{0,20},{4,16},{8,28},{12,24},{16,4},{20,0},{24,12},{28,8},{1,21},{... | collective-permute-start | bytes 393224 | tf_op jit(solution)/shard_map/ppermute | solution.py:298
  9.5 3.3 %collective-permute-start.5 = (bf16[2,8,4096]{2,1,0:T(8,128)(2,1)S(1)}, bf16[2,8,4096]{2,1,0:T(8,128)(2,1)S(1)}, u32[]{:S(2)}, u32[]{:S(2)}) collective-permute-start(bf16[2,8,4096]{2,1,0:T(8,128)(2,1)S(1)} %get-tuple-element.42), channel_id=1, source_target_pairs={{0,28},{4,24},{8,20},{12,16},{16,12},{20,8},{24,4},{28,0},{1,29},{... | collective-permute-start | bytes 393224 | tf_op jit(solution)/shard_map/ppermute | solution.py:298
  12.8 3.1 %early.1 = (s32[24]{0:T(128)S(4)}, f32[24]{0:T(128)S(4)}, f32[16]{0:T(128)S(4)}, f32[16,8,4096]{2,1,0:T(8,128)S(1)}, f32[16,8,4096]{2,1,0:T(8,128)S(1)}) custom-call(s32[8,16]{1,0:T(8,128)} %ids_ref.1, s32[8,16]{1,0:T(8,128)} %counts_ref.1, bf16[2,8,4096]{2,1,0:T(8,128)(2,1)S(1)} %get-tuple-element.32.own_ref, f32[16,8,4096]{2,1,0:T(8,128)} %params_hbm.1, ...), custom_call_target="tpu_custom_call" | custom-call | flops 1000000 | bytes 12582912 | tf_op jit(solution)/shard_map/early/pallas_call | solution.py:323
  16.0 1.4 %collective-permute-done.5.rest_5_ = bf16[2,8,4096]{2,1,0:T(8,128)(2,1)S(1)} collective-permute-done((bf16[2,8,4096]{2,1,0:T(8,128)(2,1)S(1)}, bf16[2,8,4096]{2,1,0:T(8,128)(2,1)S(1)}, u32[]{:S(2)}, u32[]{:S(2)}) %collective-permute-start.5) | collective-permute-done | bytes 131104 | tf_op jit(solution)/shard_map/ppermute | solution.py:298
  17.4 0.5 %combine.1 = (f32[16,8,4096]{2,1,0:T(8,128)S(1)}, f32[1,128]{1,0:T(1,128)S(1)}) custom-call(s32[24]{0:T(128)S(4)} %get-tuple-element.33.module_ref, f32[24]{0:T(128)S(4)} %get-tuple-element.35.weight_ref, f32[16]{0:T(128)S(4)} %get-tuple-element.34.total_ref, f32[16,8,4096]{2,1,0:T(8,128)S(1)} %get-tuple-element.36.acc_in, ...), custom_call_target="tpu_custom_call", output_to_operand_aliasing={{0}: (3, {})} | custom-call | tf_op jit(solution)/shard_map/combine/pallas_call | solution.py:333
  17.8 2.3 %collective-permute-start.9 = (f32[1,128]{1,0:T(1,128)S(1)}, f32[1,128]{1,0:T(1,128)S(1)}, u32[]{:S(2)}, u32[]{:S(2)}) collective-permute-start(f32[1,128]{1,0:T(1,128)S(1)} %get-tuple-element.46.rest_0_), channel_id=1, source_target_pairs={{0,2},{1,3},{2,0},{3,1},{4,6},{5,7},{6,4},{7,5},{8,10},{9,11},{10,... | collective-permute-start | bytes 1544 | tf_op jit(solution)/shard_map/ppermute | solution.py:343
  20.1 1.3 %collective-permute-start.8 = (f32[1,128]{1,0:T(1,128)S(1)}, f32[1,128]{1,0:T(1,128)S(1)}, u32[]{:S(2)}, u32[]{:S(2)}) collective-permute-start(f32[1,128]{1,0:T(1,128)S(1)} %get-tuple-element.46.rest_0_), channel_id=1, source_target_pairs={{0,1},{1,2},{2,3},{3,0},{4,5},{5,6},{6,7},{7,4},{8,9},{9,10},{10,1... | collective-permute-start | bytes 1544 | tf_op jit(solution)/shard_map/ppermute | solution.py:343
  21.4 2.0 %collective-permute-start.7 = (f32[1,128]{1,0:T(1,128)S(1)}, f32[1,128]{1,0:T(1,128)S(1)}, u32[]{:S(2)}, u32[]{:S(2)}) collective-permute-start(f32[1,128]{1,0:T(1,128)S(1)} %get-tuple-element.46.rest_0_), channel_id=1, source_target_pairs={{0,3},{1,0},{2,1},{3,2},{4,7},{5,4},{6,5},{7,6},{8,11},{9,8},{10,9... | collective-permute-start | bytes 1544 | tf_op jit(solution)/shard_map/ppermute | solution.py:343
  23.4 0.9 %collective-permute-done.8.rest_2_ = f32[1,128]{1,0:T(1,128)S(1)} collective-permute-done((f32[1,128]{1,0:T(1,128)S(1)}, f32[1,128]{1,0:T(1,128)S(1)}, u32[]{:S(2)}, u32[]{:S(2)}) %collective-permute-start.8) | collective-permute-done | bytes 544 | tf_op jit(solution)/shard_map/ppermute | solution.py:343
  24.3 0.4 send.1
  24.7 2.2 %collective-permute-start.10 = (bf16[2,8,4096]{2,1,0:T(8,128)(2,1)S(1)}, bf16[2,8,4096]{2,1,0:T(8,128)(2,1)S(1)}, u32[]{:S(2)}, u32[]{:S(2)}) collective-permute-start(bf16[2,8,4096]{2,1,0:T(8,128)(2,1)S(1)} %get-tuple-element.49), channel_id=1, source_target_pairs={{0,24},{4,28},{8,16},{12,20},{16,8},{20,12},{24,0},{28,4},{1,25},{... | collective-permute-start | bytes 393224 | tf_op jit(solution)/shard_map/ppermute | solution.py:298
  26.9 0.3 collective-permute-start.11
  27.2 0.2 collective-permute-start.12
  27.4 3.5 %collective-permute-start.13 = (bf16[2,8,4096]{2,1,0:T(8,128)(2,1)S(1)}, bf16[2,8,4096]{2,1,0:T(8,128)(2,1)S(1)}, u32[]{:S(2)}, u32[]{:S(2)}) collective-permute-start(bf16[2,8,4096]{2,1,0:T(8,128)(2,1)S(1)} %get-tuple-element.54), channel_id=1, source_target_pairs={{0,20},{4,16},{8,28},{12,24},{16,4},{20,0},{24,12},{28,8},{1,21},{... | collective-permute-start | bytes 393224 | tf_op jit(solution)/shard_map/ppermute | solution.py:298
  30.9 1.0 %collective-permute-start.14 = (bf16[2,8,4096]{2,1,0:T(8,128)(2,1)S(1)}, bf16[2,8,4096]{2,1,0:T(8,128)(2,1)S(1)}, u32[]{:S(2)}, u32[]{:S(2)}) collective-permute-start(bf16[2,8,4096]{2,1,0:T(8,128)(2,1)S(1)} %get-tuple-element.55), channel_id=1, source_target_pairs={{0,28},{4,24},{8,20},{12,16},{16,12},{20,8},{24,4},{28,0},{1,29},{... | collective-permute-start | bytes 393224 | tf_op jit(solution)/shard_map/ppermute | solution.py:298
  31.9 2.3 %collective-permute-start.15 = (bf16[2,8,4096]{2,1,0:T(8,128)(2,1)S(1)}, bf16[2,8,4096]{2,1,0:T(8,128)(2,1)S(1)}, u32[]{:S(2)}, u32[]{:S(2)}) collective-permute-start(bf16[2,8,4096]{2,1,0:T(8,128)(2,1)S(1)} %get-tuple-element.56), channel_id=1, source_target_pairs={{0,12},{4,8},{8,4},{12,0},{16,28},{20,24},{24,20},{28,16},{1,13},{... | collective-permute-start | bytes 393224 | tf_op jit(solution)/shard_map/ppermute | solution.py:298
  34.2 0.9 %collective-permute-start.16 = (bf16[2,8,4096]{2,1,0:T(8,128)(2,1)S(1)}, bf16[2,8,4096]{2,1,0:T(8,128)(2,1)S(1)}, u32[]{:S(2)}, u32[]{:S(2)}) collective-permute-start(bf16[2,8,4096]{2,1,0:T(8,128)(2,1)S(1)} %get-tuple-element.57), channel_id=1, source_target_pairs={{0,4},{4,0},{8,12},{12,8},{16,20},{20,16},{24,28},{28,24},{1,5},{5... | collective-permute-start | bytes 393224 | tf_op jit(solution)/shard_map/ppermute | solution.py:298
  35.0 2.6 %store.1 = (f32[16,8,4096]{2,1,0:T(8,128)}, f32[16,8,4096]{2,1,0:T(8,128)}, bf16[1,16,8,4096]{3,2,1,0:T(8,128)(2,1)}) custom-call(s32[16]{0:T(128)S(4)} %get-tuple-element.31.places_ref, f32[16,8,128]{2,1,0:T(8,128)S(1)} %get-tuple-element.47.scale_ref, f32[16,8,4096]{2,1,0:T(8,128)S(1)} %get-tuple-element.44.acc_ref, ...), custom_call_target="tpu_custom_call" | custom-call | flops 1000000 | bytes 12582912 | tf_op jit(solution)/shard_map/store/pallas_call | solution.py:361
  37.6 1.8 %collective-permute-done.13.rest_1_ = bf16[2,8,4096]{2,1,0:T(8,128)(2,1)S(1)} collective-permute-done((bf16[2,8,4096]{2,1,0:T(8,128)(2,1)S(1)}, bf16[2,8,4096]{2,1,0:T(8,128)(2,1)S(1)}, u32[]{:S(2)}, u32[]{:S(2)}) %collective-permute-start.13) | collective-permute-done | bytes 131104 | tf_op jit(solution)/shard_map/ppermute | solution.py:298
  39.4 0.9 %unpack.1 = bf16[1,16,8,4096]{3,2,1,0:T(8,128)(2,1)} custom-call(s32[16]{0:T(128)S(4)} %get-tuple-element.31.places_ref, bf16[2,8,4096]{2,1,0:T(8,128)(2,1)S(1)} %collective-permute-done.12.rest_0_, bf16[2,8,4096]{2,1,0:T(8,128)(2,1)S(1)} %collective-permute-done.13.rest_1_, ...), custom_call_target="tpu_custom_call", output_to_operand_aliasing={{}: (6, {})} | custom-call | tf_op jit(solution)/shard_map/unpack/pallas_call | solution.py:374
  (19 shorter events, 0.2 us)
Async XLA Ops:
  1.9 7.6 %collective-permute-start = (bf16[2,8,4096]{2,1,0:T(8,128)(2,1)S(1)}, bf16[2,8,4096]{2,1,0:T(8,128)(2,1)S(1)}, u32[]{:S(2)}, u32[]{:S(2)}) collective-permute-start(bf16[2,8,4096]{2,1,0:T(8,128)(2,1)S(1)} %get-tuple-element.37), channel_id=1, source_target_pairs={{0,24},{4,28},{8,16},{12,20},{16,8},{20,12},{24,0},{28,4},{1,25},{... | collective-permute-start | bytes 393224 | tf_op jit(solution)/shard_map/ppermute | solution.py:298
  4.9 7.8 %collective-permute-start.1 = (bf16[2,8,4096]{2,1,0:T(8,128)(2,1)S(1)}, bf16[2,8,4096]{2,1,0:T(8,128)(2,1)S(1)}, u32[]{:S(2)}, u32[]{:S(2)}) collective-permute-start(bf16[2,8,4096]{2,1,0:T(8,128)(2,1)S(1)} %get-tuple-element.38), channel_id=1, source_target_pairs={{0,8},{4,12},{8,0},{12,4},{16,24},{20,28},{24,16},{28,20},{1,9},{5... | collective-permute-start | bytes 393224 | tf_op jit(solution)/shard_map/ppermute | solution.py:298
  5.2 10.7 %collective-permute-start.2 = (bf16[2,8,4096]{2,1,0:T(8,128)(2,1)S(1)}, bf16[2,8,4096]{2,1,0:T(8,128)(2,1)S(1)}, u32[]{:S(2)}, u32[]{:S(2)}) collective-permute-start(bf16[2,8,4096]{2,1,0:T(8,128)(2,1)S(1)} %get-tuple-element.39), channel_id=1, source_target_pairs={{0,16},{4,20},{8,24},{12,28},{16,0},{20,4},{24,8},{28,12},{1,17},{... | collective-permute-start | bytes 393224 | tf_op jit(solution)/shard_map/ppermute | solution.py:298
  6.6 9.4 %collective-permute-start.3 = (bf16[2,8,4096]{2,1,0:T(8,128)(2,1)S(1)}, bf16[2,8,4096]{2,1,0:T(8,128)(2,1)S(1)}, u32[]{:S(2)}, u32[]{:S(2)}) collective-permute-start(bf16[2,8,4096]{2,1,0:T(8,128)(2,1)S(1)} %get-tuple-element.40), channel_id=1, source_target_pairs={{0,20},{4,16},{8,28},{12,24},{16,4},{20,0},{24,12},{28,8},{1,21},{... | collective-permute-start | bytes 393224 | tf_op jit(solution)/shard_map/ppermute | solution.py:298
  9.4 6.6 %collective-permute-start.4 = (bf16[2,8,4096]{2,1,0:T(8,128)(2,1)S(1)}, bf16[2,8,4096]{2,1,0:T(8,128)(2,1)S(1)}, u32[]{:S(2)}, u32[]{:S(2)}) collective-permute-start(bf16[2,8,4096]{2,1,0:T(8,128)(2,1)S(1)} %get-tuple-element.41), channel_id=1, source_target_pairs={{0,12},{4,8},{8,4},{12,0},{16,28},{20,24},{24,20},{28,16},{1,13},{... | collective-permute-start | bytes 393224 | tf_op jit(solution)/shard_map/ppermute | solution.py:298
  9.5 7.9 %collective-permute-start.5 = (bf16[2,8,4096]{2,1,0:T(8,128)(2,1)S(1)}, bf16[2,8,4096]{2,1,0:T(8,128)(2,1)S(1)}, u32[]{:S(2)}, u32[]{:S(2)}) collective-permute-start(bf16[2,8,4096]{2,1,0:T(8,128)(2,1)S(1)} %get-tuple-element.42), channel_id=1, source_target_pairs={{0,28},{4,24},{8,20},{12,16},{16,12},{20,8},{24,4},{28,0},{1,29},{... | collective-permute-start | bytes 393224 | tf_op jit(solution)/shard_map/ppermute | solution.py:298
  12.8 4.6 %collective-permute-start.6 = (bf16[2,8,4096]{2,1,0:T(8,128)(2,1)S(1)}, bf16[2,8,4096]{2,1,0:T(8,128)(2,1)S(1)}, u32[]{:S(2)}, u32[]{:S(2)}) collective-permute-start(bf16[2,8,4096]{2,1,0:T(8,128)(2,1)S(1)} %get-tuple-element.43), channel_id=1, source_target_pairs={{0,4},{4,0},{8,12},{12,8},{16,20},{20,16},{24,28},{28,24},{1,5},{5... | collective-permute-start | bytes 393224 | tf_op jit(solution)/shard_map/ppermute | solution.py:298
  17.8 5.6 %collective-permute-start.9 = (f32[1,128]{1,0:T(1,128)S(1)}, f32[1,128]{1,0:T(1,128)S(1)}, u32[]{:S(2)}, u32[]{:S(2)}) collective-permute-start(f32[1,128]{1,0:T(1,128)S(1)} %get-tuple-element.46.rest_0_), channel_id=1, source_target_pairs={{0,2},{1,3},{2,0},{3,1},{4,6},{5,7},{6,4},{7,5},{8,10},{9,11},{10,... | collective-permute-start | bytes 1544 | tf_op jit(solution)/shard_map/ppermute | solution.py:343
  20.1 4.2 %collective-permute-start.8 = (f32[1,128]{1,0:T(1,128)S(1)}, f32[1,128]{1,0:T(1,128)S(1)}, u32[]{:S(2)}, u32[]{:S(2)}) collective-permute-start(f32[1,128]{1,0:T(1,128)S(1)} %get-tuple-element.46.rest_0_), channel_id=1, source_target_pairs={{0,1},{1,2},{2,3},{3,0},{4,5},{5,6},{6,7},{7,4},{8,9},{9,10},{10,1... | collective-permute-start | bytes 1544 | tf_op jit(solution)/shard_map/ppermute | solution.py:343
  21.4 2.9 %collective-permute-start.7 = (f32[1,128]{1,0:T(1,128)S(1)}, f32[1,128]{1,0:T(1,128)S(1)}, u32[]{:S(2)}, u32[]{:S(2)}) collective-permute-start(f32[1,128]{1,0:T(1,128)S(1)} %get-tuple-element.46.rest_0_), channel_id=1, source_target_pairs={{0,3},{1,0},{2,1},{3,2},{4,7},{5,4},{6,5},{7,6},{8,11},{9,8},{10,9... | collective-permute-start | bytes 1544 | tf_op jit(solution)/shard_map/ppermute | solution.py:343
  24.3 10.7 %copy-start = (f32[16,8,4096]{2,1,0:T(8,128)S(1)}, f32[16,8,4096]{2,1,0:T(8,128)}, u32[]{:S(2)}) copy-start(f32[16,8,4096]{2,1,0:T(8,128)} %past_ref.1) | copy-start | bytes 6291460
  24.7 7.2 %collective-permute-start.10 = (bf16[2,8,4096]{2,1,0:T(8,128)(2,1)S(1)}, bf16[2,8,4096]{2,1,0:T(8,128)(2,1)S(1)}, u32[]{:S(2)}, u32[]{:S(2)}) collective-permute-start(bf16[2,8,4096]{2,1,0:T(8,128)(2,1)S(1)} %get-tuple-element.49), channel_id=1, source_target_pairs={{0,24},{4,28},{8,16},{12,20},{16,8},{20,12},{24,0},{28,4},{1,25},{... | collective-permute-start | bytes 393224 | tf_op jit(solution)/shard_map/ppermute | solution.py:298
  26.9 7.3 %collective-permute-start.11 = (bf16[2,8,4096]{2,1,0:T(8,128)(2,1)S(1)}, bf16[2,8,4096]{2,1,0:T(8,128)(2,1)S(1)}, u32[]{:S(2)}, u32[]{:S(2)}) collective-permute-start(bf16[2,8,4096]{2,1,0:T(8,128)(2,1)S(1)} %get-tuple-element.50), channel_id=1, source_target_pairs={{0,8},{4,12},{8,0},{12,4},{16,24},{20,28},{24,16},{28,20},{1,9},{5... | collective-permute-start | bytes 393224 | tf_op jit(solution)/shard_map/ppermute | solution.py:298
  27.2 10.4 %collective-permute-start.12 = (bf16[2,8,4096]{2,1,0:T(8,128)(2,1)S(1)}, bf16[2,8,4096]{2,1,0:T(8,128)(2,1)S(1)}, u32[]{:S(2)}, u32[]{:S(2)}) collective-permute-start(bf16[2,8,4096]{2,1,0:T(8,128)(2,1)S(1)} %get-tuple-element.53), channel_id=1, source_target_pairs={{0,16},{4,20},{8,24},{12,28},{16,0},{20,4},{24,8},{28,12},{1,17},{... | collective-permute-start | bytes 393224 | tf_op jit(solution)/shard_map/ppermute | solution.py:298
  27.4 12.0 %collective-permute-start.13 = (bf16[2,8,4096]{2,1,0:T(8,128)(2,1)S(1)}, bf16[2,8,4096]{2,1,0:T(8,128)(2,1)S(1)}, u32[]{:S(2)}, u32[]{:S(2)}) collective-permute-start(bf16[2,8,4096]{2,1,0:T(8,128)(2,1)S(1)} %get-tuple-element.54), channel_id=1, source_target_pairs={{0,20},{4,16},{8,28},{12,24},{16,4},{20,0},{24,12},{28,8},{1,21},{... | collective-permute-start | bytes 393224 | tf_op jit(solution)/shard_map/ppermute | solution.py:298
  30.9 8.5 %collective-permute-start.14 = (bf16[2,8,4096]{2,1,0:T(8,128)(2,1)S(1)}, bf16[2,8,4096]{2,1,0:T(8,128)(2,1)S(1)}, u32[]{:S(2)}, u32[]{:S(2)}) collective-permute-start(bf16[2,8,4096]{2,1,0:T(8,128)(2,1)S(1)} %get-tuple-element.55), channel_id=1, source_target_pairs={{0,28},{4,24},{8,20},{12,16},{16,12},{20,8},{24,4},{28,0},{1,29},{... | collective-permute-start | bytes 393224 | tf_op jit(solution)/shard_map/ppermute | solution.py:298
  31.9 7.6 %collective-permute-start.15 = (bf16[2,8,4096]{2,1,0:T(8,128)(2,1)S(1)}, bf16[2,8,4096]{2,1,0:T(8,128)(2,1)S(1)}, u32[]{:S(2)}, u32[]{:S(2)}) collective-permute-start(bf16[2,8,4096]{2,1,0:T(8,128)(2,1)S(1)} %get-tuple-element.56), channel_id=1, source_target_pairs={{0,12},{4,8},{8,4},{12,0},{16,28},{20,24},{24,20},{28,16},{1,13},{... | collective-permute-start | bytes 393224 | tf_op jit(solution)/shard_map/ppermute | solution.py:298
  34.2 5.3 %collective-permute-start.16 = (bf16[2,8,4096]{2,1,0:T(8,128)(2,1)S(1)}, bf16[2,8,4096]{2,1,0:T(8,128)(2,1)S(1)}, u32[]{:S(2)}, u32[]{:S(2)}) collective-permute-start(bf16[2,8,4096]{2,1,0:T(8,128)(2,1)S(1)} %get-tuple-element.57), channel_id=1, source_target_pairs={{0,4},{4,0},{8,12},{12,8},{16,20},{20,16},{24,28},{28,24},{1,5},{5... | collective-permute-start | bytes 393224 | tf_op jit(solution)/shard_map/ppermute | solution.py:298

commit v13 on v11

--- a/solution.py
+++ b/solution.py
@@ -9,7 +9,7 @@
 from jax.sharding import PartitionSpec as P
 
 CAP = 2
-CHUNK = 1024
+CHUNK = 2048
 PARTS = 4
 SOON = 2
 outer_momentum = 0.9

time: 40.6 us -> 40.7 us (level)
  no operation moved by 1% of the time
where the time goes in v13:
time: 40.7 us; the launch traced here: 40.4 us
  starting transfers between devices  27.7 us (68%)
  Pallas kernels  8.8 us (22%)
  waiting for transfers between devices  3.11 us (8%)
  between operations  0.71 us (2%)
    ppermute x14, starting transfers between devices, exchange(): lax.ppermute(x, 'path', [(i, i ^ d) for i in range(paths)])  22 us
    ppermute x3, starting transfers between devices, on_device(): lax.ppermute(squares, 'shard', [(i, (i + d) % shards) for i in range(shar...  5.76 us
    pallas_call x1, Pallas kernels, on_device(): pl.pallas_call(early_kernel, out_shape=tables + [held_module] * 2, in_spe...  3.13 us
    pallas_call x1, Pallas kernels, on_device(): pl.pallas_call(functools.partial(store_kernel, soon), out_shape=[module]...  2.64 us
    ppermute x14, waiting for transfers between devices, exchange(): lax.ppermute(x, 'path', [(i, i ^ d) for i in range(paths)])  2.18 us
    pallas_call x1, Pallas kernels, on_device(): pl.pallas_call(functools.partial(pack_kernel, owned, [*there, 0]), out_sh...  1.27 us
    pallas_call x1, Pallas kernels, on_device(): pl.pallas_call(functools.partial(unpack_kernel, last), out_shape=whole, i...  0.93 us
    ppermute x3, waiting for transfers between devices, on_device(): lax.ppermute(squares, 'shard', [(i, (i + d) % shards) for i in range(shar...  0.93 us
  transfers between devices with their start and end apart: 17, of which 3 were waited for; matrix products, arithmetic and copies ran while one was open for 0% of the time, Pallas kernels for 14%

profile of v13, /device:TPU:1, one launch (start us, length us, event | category | flops | bytes accessed | tf_op | source)
XLA Modules:
  0.0 40.4 jit_solution(14460937235334391774)
XLA Ops:
  0.6 1.3 %pack.1 = (s32[16]{0:T(128)S(4)}, bf16[2,8,4096]{2,1,0:T(8,128)(2,1)S(1)}, bf16[2,8,4096]{2,1,0:T(8,128)(2,1)S(1)}, bf16[2,8,4096]{2,1,0:T(8,128)(2,1)S(1)}, bf1...) custom-call(s32[8,16]{1,0:T(8,128)} %ids_ref.1, ...), custom_call_target="tpu_custom_call" | custom-call | tf_op jit(solution)/shard_map/pack/pallas_call | solution.py:301
  1.9 3.1 %collective-permute-start = (bf16[2,8,4096]{2,1,0:T(8,128)(2,1)S(1)}, bf16[2,8,4096]{2,1,0:T(8,128)(2,1)S(1)}, u32[]{:S(2)}, u32[]{:S(2)}) collective-permute-start(bf16[2,8,4096]{2,1,0:T(8,128)(2,1)S(1)} %get-tuple-element.37), channel_id=1, source_target_pairs={{0,24},{4,28},{8,16},{12,20},{16,8},{20,12},{24,0},{28,4},{1,25},{... | collective-permute-start | bytes 393224 | tf_op jit(solution)/shard_map/ppermute | solution.py:297
  5.0 0.3 collective-permute-start.1
  5.3 2.8 %collective-permute-start.3 = (bf16[2,8,4096]{2,1,0:T(8,128)(2,1)S(1)}, bf16[2,8,4096]{2,1,0:T(8,128)(2,1)S(1)}, u32[]{:S(2)}, u32[]{:S(2)}) collective-permute-start(bf16[2,8,4096]{2,1,0:T(8,128)(2,1)S(1)} %get-tuple-element.40), channel_id=1, source_target_pairs={{0,20},{4,16},{8,28},{12,24},{16,4},{20,0},{24,12},{28,8},{1,21},{... | collective-permute-start | bytes 393224 | tf_op jit(solution)/shard_map/ppermute | solution.py:297
  8.2 4.6 %collective-permute-start.5 = (bf16[2,8,4096]{2,1,0:T(8,128)(2,1)S(1)}, bf16[2,8,4096]{2,1,0:T(8,128)(2,1)S(1)}, u32[]{:S(2)}, u32[]{:S(2)}) collective-permute-start(bf16[2,8,4096]{2,1,0:T(8,128)(2,1)S(1)} %get-tuple-element.42), channel_id=1, source_target_pairs={{0,28},{4,24},{8,20},{12,16},{16,12},{20,8},{24,4},{28,0},{1,29},{... | collective-permute-start | bytes 393224 | tf_op jit(solution)/shard_map/ppermute | solution.py:297
  12.8 0.8 %collective-permute-start.6 = (bf16[2,8,4096]{2,1,0:T(8,128)(2,1)S(1)}, bf16[2,8,4096]{2,1,0:T(8,128)(2,1)S(1)}, u32[]{:S(2)}, u32[]{:S(2)}) collective-permute-start(bf16[2,8,4096]{2,1,0:T(8,128)(2,1)S(1)} %get-tuple-element.43), channel_id=1, source_target_pairs={{0,4},{4,0},{8,12},{12,8},{16,20},{20,16},{24,28},{28,24},{1,5},{5... | collective-permute-start | bytes 393224 | tf_op jit(solution)/shard_map/ppermute | solution.py:297
  13.6 3.1 %early.1 = (s32[24]{0:T(128)S(4)}, f32[24]{0:T(128)S(4)}, f32[16]{0:T(128)S(4)}, f32[16,8,4096]{2,1,0:T(8,128)S(1)}, f32[16,8,4096]{2,1,0:T(8,128)S(1)}) custom-call(s32[8,16]{1,0:T(8,128)} %ids_ref.1, s32[8,16]{1,0:T(8,128)} %counts_ref.1, bf16[2,8,4096]{2,1,0:T(8,128)(2,1)S(1)} %get-tuple-element.32.own_ref, f32[16,8,4096]{2,1,0:T(8,128)} %params_hbm.1, ...), custom_call_target="tpu_custom_call" | custom-call | flops 1000000 | bytes 12582912 | tf_op jit(solution)/shard_map/early/pallas_call | solution.py:317
  16.8 0.4 collective-permute-done.5.rest_5_
  17.2 0.5 %combine.1 = (f32[16,8,4096]{2,1,0:T(8,128)S(1)}, f32[1,128]{1,0:T(1,128)S(1)}) custom-call(s32[24]{0:T(128)S(4)} %get-tuple-element.33.module_ref, f32[24]{0:T(128)S(4)} %get-tuple-element.35.weight_ref, f32[16]{0:T(128)S(4)} %get-tuple-element.34.total_ref, f32[16,8,4096]{2,1,0:T(8,128)S(1)} %get-tuple-element.36.acc_in, ...), custom_call_target="tpu_custom_call", output_to_operand_aliasing={{0}: (3, {})} | custom-call | tf_op jit(solution)/shard_map/combine/pallas_call | solution.py:327
  17.6 2.5 %collective-permute-start.9 = (f32[1,128]{1,0:T(1,128)S(1)}, f32[1,128]{1,0:T(1,128)S(1)}, u32[]{:S(2)}, u32[]{:S(2)}) collective-permute-start(f32[1,128]{1,0:T(1,128)S(1)} %get-tuple-element.46.rest_0_), channel_id=1, source_target_pairs={{0,2},{1,3},{2,0},{3,1},{4,6},{5,7},{6,4},{7,5},{8,10},{9,11},{10,... | collective-permute-start | bytes 1544 | tf_op jit(solution)/shard_map/ppermute | solution.py:337
  20.1 1.3 %collective-permute-start.8 = (f32[1,128]{1,0:T(1,128)S(1)}, f32[1,128]{1,0:T(1,128)S(1)}, u32[]{:S(2)}, u32[]{:S(2)}) collective-permute-start(f32[1,128]{1,0:T(1,128)S(1)} %get-tuple-element.46.rest_0_), channel_id=1, source_target_pairs={{0,1},{1,2},{2,3},{3,0},{4,5},{5,6},{6,7},{7,4},{8,9},{9,10},{10,1... | collective-permute-start | bytes 1544 | tf_op jit(solution)/shard_map/ppermute | solution.py:337
  21.4 2.0 %collective-permute-start.7 = (f32[1,128]{1,0:T(1,128)S(1)}, f32[1,128]{1,0:T(1,128)S(1)}, u32[]{:S(2)}, u32[]{:S(2)}) collective-permute-start(f32[1,128]{1,0:T(1,128)S(1)} %get-tuple-element.46.rest_0_), channel_id=1, source_target_pairs={{0,3},{1,0},{2,1},{3,2},{4,7},{5,4},{6,5},{7,6},{8,11},{9,8},{10,9... | collective-permute-start | bytes 1544 | tf_op jit(solution)/shard_map/ppermute | solution.py:337
  23.4 0.9 %collective-permute-done.8.rest_2_ = f32[1,128]{1,0:T(1,128)S(1)} collective-permute-done((f32[1,128]{1,0:T(1,128)S(1)}, f32[1,128]{1,0:T(1,128)S(1)}, u32[]{:S(2)}, u32[]{:S(2)}) %collective-permute-start.8) | collective-permute-done | bytes 544 | tf_op jit(solution)/shard_map/ppermute | solution.py:337
  24.3 0.4 send.1
  24.7 2.2 %collective-permute-start.10 = (bf16[2,8,4096]{2,1,0:T(8,128)(2,1)S(1)}, bf16[2,8,4096]{2,1,0:T(8,128)(2,1)S(1)}, u32[]{:S(2)}, u32[]{:S(2)}) collective-permute-start(bf16[2,8,4096]{2,1,0:T(8,128)(2,1)S(1)} %get-tuple-element.49), channel_id=1, source_target_pairs={{0,24},{4,28},{8,16},{12,20},{16,8},{20,12},{24,0},{28,4},{1,25},{... | collective-permute-start | bytes 393224 | tf_op jit(solution)/shard_map/ppermute | solution.py:297
  26.9 0.3 collective-permute-start.11
  27.2 0.2 collective-permute-start.12
  27.4 3.6 %collective-permute-start.13 = (bf16[2,8,4096]{2,1,0:T(8,128)(2,1)S(1)}, bf16[2,8,4096]{2,1,0:T(8,128)(2,1)S(1)}, u32[]{:S(2)}, u32[]{:S(2)}) collective-permute-start(bf16[2,8,4096]{2,1,0:T(8,128)(2,1)S(1)} %get-tuple-element.54), channel_id=1, source_target_pairs={{0,20},{4,16},{8,28},{12,24},{16,4},{20,0},{24,12},{28,8},{1,21},{... | collective-permute-start | bytes 393224 | tf_op jit(solution)/shard_map/ppermute | solution.py:297
  31.0 0.9 %collective-permute-start.14 = (bf16[2,8,4096]{2,1,0:T(8,128)(2,1)S(1)}, bf16[2,8,4096]{2,1,0:T(8,128)(2,1)S(1)}, u32[]{:S(2)}, u32[]{:S(2)}) collective-permute-start(bf16[2,8,4096]{2,1,0:T(8,128)(2,1)S(1)} %get-tuple-element.55), channel_id=1, source_target_pairs={{0,28},{4,24},{8,20},{12,16},{16,12},{20,8},{24,4},{28,0},{1,29},{... | collective-permute-start | bytes 393224 | tf_op jit(solution)/shard_map/ppermute | solution.py:297
  31.9 2.3 %collective-permute-start.15 = (bf16[2,8,4096]{2,1,0:T(8,128)(2,1)S(1)}, bf16[2,8,4096]{2,1,0:T(8,128)(2,1)S(1)}, u32[]{:S(2)}, u32[]{:S(2)}) collective-permute-start(bf16[2,8,4096]{2,1,0:T(8,128)(2,1)S(1)} %get-tuple-element.56), channel_id=1, source_target_pairs={{0,12},{4,8},{8,4},{12,0},{16,28},{20,24},{24,20},{28,16},{1,13},{... | collective-permute-start | bytes 393224 | tf_op jit(solution)/shard_map/ppermute | solution.py:297
  34.2 0.8 %collective-permute-start.16 = (bf16[2,8,4096]{2,1,0:T(8,128)(2,1)S(1)}, bf16[2,8,4096]{2,1,0:T(8,128)(2,1)S(1)}, u32[]{:S(2)}, u32[]{:S(2)}) collective-permute-start(bf16[2,8,4096]{2,1,0:T(8,128)(2,1)S(1)} %get-tuple-element.57), channel_id=1, source_target_pairs={{0,4},{4,0},{8,12},{12,8},{16,20},{20,16},{24,28},{28,24},{1,5},{5... | collective-permute-start | bytes 393224 | tf_op jit(solution)/shard_map/ppermute | solution.py:297
  35.0 2.6 %store.1 = (f32[16,8,4096]{2,1,0:T(8,128)}, f32[16,8,4096]{2,1,0:T(8,128)}, bf16[1,16,8,4096]{3,2,1,0:T(8,128)(2,1)}) custom-call(s32[16]{0:T(128)S(4)} %get-tuple-element.31.places_ref, f32[16,8,128]{2,1,0:T(8,128)S(1)} %get-tuple-element.47.scale_ref, f32[16,8,4096]{2,1,0:T(8,128)S(1)} %get-tuple-element.44.acc_ref, ...), custom_call_target="tpu_custom_call" | custom-call | flops 1000000 | bytes 12582912 | tf_op jit(solution)/shard_map/store/pallas_call | solution.py:351
  37.7 1.8 %collective-permute-done.13.rest_1_ = bf16[2,8,4096]{2,1,0:T(8,128)(2,1)S(1)} collective-permute-done((bf16[2,8,4096]{2,1,0:T(8,128)(2,1)S(1)}, bf16[2,8,4096]{2,1,0:T(8,128)(2,1)S(1)}, u32[]{:S(2)}, u32[]{:S(2)}) %collective-permute-start.13) | collective-permute-done | bytes 131104 | tf_op jit(solution)/shard_map/ppermute | solution.py:297
  39.4 0.9 %unpack.1 = bf16[1,16,8,4096]{3,2,1,0:T(8,128)(2,1)} custom-call(s32[16]{0:T(128)S(4)} %get-tuple-element.31.places_ref, bf16[2,8,4096]{2,1,0:T(8,128)(2,1)S(1)} %collective-permute-done.12.rest_0_, bf16[2,8,4096]{2,1,0:T(8,128)(2,1)S(1)} %collective-permute-done.13.rest_1_, ...), custom_call_target="tpu_custom_call", output_to_operand_aliasing={{}: (6, {})} | custom-call | tf_op jit(solution)/shard_map/unpack/pallas_call | solution.py:364
  (18 shorter events, 0.2 us)
Async XLA Ops:
  1.9 6.3 %collective-permute-start = (bf16[2,8,4096]{2,1,0:T(8,128)(2,1)S(1)}, bf16[2,8,4096]{2,1,0:T(8,128)(2,1)S(1)}, u32[]{:S(2)}, u32[]{:S(2)}) collective-permute-start(bf16[2,8,4096]{2,1,0:T(8,128)(2,1)S(1)} %get-tuple-element.37), channel_id=1, source_target_pairs={{0,24},{4,28},{8,16},{12,20},{16,8},{20,12},{24,0},{28,4},{1,25},{... | collective-permute-start | bytes 393224 | tf_op jit(solution)/shard_map/ppermute | solution.py:297
  5.0 7.8 %collective-permute-start.1 = (bf16[2,8,4096]{2,1,0:T(8,128)(2,1)S(1)}, bf16[2,8,4096]{2,1,0:T(8,128)(2,1)S(1)}, u32[]{:S(2)}, u32[]{:S(2)}) collective-permute-start(bf16[2,8,4096]{2,1,0:T(8,128)(2,1)S(1)} %get-tuple-element.38), channel_id=1, source_target_pairs={{0,8},{4,12},{8,0},{12,4},{16,24},{20,28},{24,16},{28,20},{1,9},{5... | collective-permute-start | bytes 393224 | tf_op jit(solution)/shard_map/ppermute | solution.py:297
  5.2 11.5 %collective-permute-start.2 = (bf16[2,8,4096]{2,1,0:T(8,128)(2,1)S(1)}, bf16[2,8,4096]{2,1,0:T(8,128)(2,1)S(1)}, u32[]{:S(2)}, u32[]{:S(2)}) collective-permute-start(bf16[2,8,4096]{2,1,0:T(8,128)(2,1)S(1)} %get-tuple-element.39), channel_id=1, source_target_pairs={{0,16},{4,20},{8,24},{12,28},{16,0},{20,4},{24,8},{28,12},{1,17},{... | collective-permute-start | bytes 393224 | tf_op jit(solution)/shard_map/ppermute | solution.py:297
  5.3 11.4 %collective-permute-start.3 = (bf16[2,8,4096]{2,1,0:T(8,128)(2,1)S(1)}, bf16[2,8,4096]{2,1,0:T(8,128)(2,1)S(1)}, u32[]{:S(2)}, u32[]{:S(2)}) collective-permute-start(bf16[2,8,4096]{2,1,0:T(8,128)(2,1)S(1)} %get-tuple-element.40), channel_id=1, source_target_pairs={{0,20},{4,16},{8,28},{12,24},{16,4},{20,0},{24,12},{28,8},{1,21},{... | collective-permute-start | bytes 393224 | tf_op jit(solution)/shard_map/ppermute | solution.py:297
  8.1 8.7 %collective-permute-start.4 = (bf16[2,8,4096]{2,1,0:T(8,128)(2,1)S(1)}, bf16[2,8,4096]{2,1,0:T(8,128)(2,1)S(1)}, u32[]{:S(2)}, u32[]{:S(2)}) collective-permute-start(bf16[2,8,4096]{2,1,0:T(8,128)(2,1)S(1)} %get-tuple-element.41), channel_id=1, source_target_pairs={{0,12},{4,8},{8,4},{12,0},{16,28},{20,24},{24,20},{28,16},{1,13},{... | collective-permute-start | bytes 393224 | tf_op jit(solution)/shard_map/ppermute | solution.py:297
  8.2 9.0 %collective-permute-start.5 = (bf16[2,8,4096]{2,1,0:T(8,128)(2,1)S(1)}, bf16[2,8,4096]{2,1,0:T(8,128)(2,1)S(1)}, u32[]{:S(2)}, u32[]{:S(2)}) collective-permute-start(bf16[2,8,4096]{2,1,0:T(8,128)(2,1)S(1)} %get-tuple-element.42), channel_id=1, source_target_pairs={{0,28},{4,24},{8,20},{12,16},{16,12},{20,8},{24,4},{28,0},{1,29},{... | collective-permute-start | bytes 393224 | tf_op jit(solution)/shard_map/ppermute | solution.py:297
  12.8 4.3 %collective-permute-start.6 = (bf16[2,8,4096]{2,1,0:T(8,128)(2,1)S(1)}, bf16[2,8,4096]{2,1,0:T(8,128)(2,1)S(1)}, u32[]{:S(2)}, u32[]{:S(2)}) collective-permute-start(bf16[2,8,4096]{2,1,0:T(8,128)(2,1)S(1)} %get-tuple-element.43), channel_id=1, source_target_pairs={{0,4},{4,0},{8,12},{12,8},{16,20},{20,16},{24,28},{28,24},{1,5},{5... | collective-permute-start | bytes 393224 | tf_op jit(solution)/shard_map/ppermute | solution.py:297
  17.6 5.8 %collective-permute-start.9 = (f32[1,128]{1,0:T(1,128)S(1)}, f32[1,128]{1,0:T(1,128)S(1)}, u32[]{:S(2)}, u32[]{:S(2)}) collective-permute-start(f32[1,128]{1,0:T(1,128)S(1)} %get-tuple-element.46.rest_0_), channel_id=1, source_target_pairs={{0,2},{1,3},{2,0},{3,1},{4,6},{5,7},{6,4},{7,5},{8,10},{9,11},{10,... | collective-permute-start | bytes 1544 | tf_op jit(solution)/shard_map/ppermute | solution.py:337
  20.1 4.2 %collective-permute-start.8 = (f32[1,128]{1,0:T(1,128)S(1)}, f32[1,128]{1,0:T(1,128)S(1)}, u32[]{:S(2)}, u32[]{:S(2)}) collective-permute-start(f32[1,128]{1,0:T(1,128)S(1)} %get-tuple-element.46.rest_0_), channel_id=1, source_target_pairs={{0,1},{1,2},{2,3},{3,0},{4,5},{5,6},{6,7},{7,4},{8,9},{9,10},{10,1... | collective-permute-start | bytes 1544 | tf_op jit(solution)/shard_map/ppermute | solution.py:337
  21.4 2.9 %collective-permute-start.7 = (f32[1,128]{1,0:T(1,128)S(1)}, f32[1,128]{1,0:T(1,128)S(1)}, u32[]{:S(2)}, u32[]{:S(2)}) collective-permute-start(f32[1,128]{1,0:T(1,128)S(1)} %get-tuple-element.46.rest_0_), channel_id=1, source_target_pairs={{0,3},{1,0},{2,1},{3,2},{4,7},{5,4},{6,5},{7,6},{8,11},{9,8},{10,9... | collective-permute-start | bytes 1544 | tf_op jit(solution)/shard_map/ppermute | solution.py:337
  24.3 10.7 %copy-start = (f32[16,8,4096]{2,1,0:T(8,128)S(1)}, f32[16,8,4096]{2,1,0:T(8,128)}, u32[]{:S(2)}) copy-start(f32[16,8,4096]{2,1,0:T(8,128)} %past_ref.1) | copy-start | bytes 6291460
  24.7 7.2 %collective-permute-start.10 = (bf16[2,8,4096]{2,1,0:T(8,128)(2,1)S(1)}, bf16[2,8,4096]{2,1,0:T(8,128)(2,1)S(1)}, u32[]{:S(2)}, u32[]{:S(2)}) collective-permute-start(bf16[2,8,4096]{2,1,0:T(8,128)(2,1)S(1)} %get-tuple-element.49), channel_id=1, source_target_pairs={{0,24},{4,28},{8,16},{12,20},{16,8},{20,12},{24,0},{28,4},{1,25},{... | collective-permute-start | bytes 393224 | tf_op jit(solution)/shard_map/ppermute | solution.py:297
  26.9 7.3 %collective-permute-start.11 = (bf16[2,8,4096]{2,1,0:T(8,128)(2,1)S(1)}, bf16[2,8,4096]{2,1,0:T(8,128)(2,1)S(1)}, u32[]{:S(2)}, u32[]{:S(2)}) collective-permute-start(bf16[2,8,4096]{2,1,0:T(8,128)(2,1)S(1)} %get-tuple-element.50), channel_id=1, source_target_pairs={{0,8},{4,12},{8,0},{12,4},{16,24},{20,28},{24,16},{28,20},{1,9},{5... | collective-permute-start | bytes 393224 | tf_op jit(solution)/shard_map/ppermute | solution.py:297
  27.2 10.5 %collective-permute-start.12 = (bf16[2,8,4096]{2,1,0:T(8,128)(2,1)S(1)}, bf16[2,8,4096]{2,1,0:T(8,128)(2,1)S(1)}, u32[]{:S(2)}, u32[]{:S(2)}) collective-permute-start(bf16[2,8,4096]{2,1,0:T(8,128)(2,1)S(1)} %get-tuple-element.53), channel_id=1, source_target_pairs={{0,16},{4,20},{8,24},{12,28},{16,0},{20,4},{24,8},{28,12},{1,17},{... | collective-permute-start | bytes 393224 | tf_op jit(solution)/shard_map/ppermute | solution.py:297
  27.4 12.0 %collective-permute-start.13 = (bf16[2,8,4096]{2,1,0:T(8,128)(2,1)S(1)}, bf16[2,8,4096]{2,1,0:T(8,128)(2,1)S(1)}, u32[]{:S(2)}, u32[]{:S(2)}) collective-permute-start(bf16[2,8,4096]{2,1,0:T(8,128)(2,1)S(1)} %get-tuple-element.54), channel_id=1, source_target_pairs={{0,20},{4,16},{8,28},{12,24},{16,4},{20,0},{24,12},{28,8},{1,21},{... | collective-permute-start | bytes 393224 | tf_op jit(solution)/shard_map/ppermute | solution.py:297
  31.0 8.5 %collective-permute-start.14 = (bf16[2,8,4096]{2,1,0:T(8,128)(2,1)S(1)}, bf16[2,8,4096]{2,1,0:T(8,128)(2,1)S(1)}, u32[]{:S(2)}, u32[]{:S(2)}) collective-permute-start(bf16[2,8,4096]{2,1,0:T(8,128)(2,1)S(1)} %get-tuple-element.55), channel_id=1, source_target_pairs={{0,28},{4,24},{8,20},{12,16},{16,12},{20,8},{24,4},{28,0},{1,29},{... | collective-permute-start | bytes 393224 | tf_op jit(solution)/shard_map/ppermute | solution.py:297
  31.9 7.5 %collective-permute-start.15 = (bf16[2,8,4096]{2,1,0:T(8,128)(2,1)S(1)}, bf16[2,8,4096]{2,1,0:T(8,128)(2,1)S(1)}, u32[]{:S(2)}, u32[]{:S(2)}) collective-permute-start(bf16[2,8,4096]{2,1,0:T(8,128)(2,1)S(1)} %get-tuple-element.56), channel_id=1, source_target_pairs={{0,12},{4,8},{8,4},{12,0},{16,28},{20,24},{24,20},{28,16},{1,13},{... | collective-permute-start | bytes 393224 | tf_op jit(solution)/shard_map/ppermute | solution.py:297
  34.2 5.3 %collective-permute-start.16 = (bf16[2,8,4096]{2,1,0:T(8,128)(2,1)S(1)}, bf16[2,8,4096]{2,1,0:T(8,128)(2,1)S(1)}, u32[]{:S(2)}, u32[]{:S(2)}) collective-permute-start(bf16[2,8,4096]{2,1,0:T(8,128)(2,1)S(1)} %get-tuple-element.57), channel_id=1, source_target_pairs={{0,4},{4,0},{8,12},{12,8},{16,20},{20,16},{24,28},{28,24},{1,5},{5... | collective-permute-start | bytes 393224 | tf_op jit(solution)/shard_map/ppermute | solution.py:297
